TPU v7x, 256 devices: a whole 4x4x8 slice. The times are simulated.
256 devices in a mesh: wrap: 128 (over z, x_lo, y, core), span: 2 (over x_hi).
Axes of the slice: x: 4 (x_hi: 2, x_lo: 2; x = x_hi * 2 + x_lo), y: 4, z: 8, core: 2. Of those that a mesh axis runs over, the one named last changes fastest.
Arguments:
- cell_xyz: float32 [3, 4096, 16, 128], P(None, 'wrap', 'span'), may hold values from -6 to 6
- panel_xyz: float32 [3, 65536], P(None, 'wrap'), may hold values from -6 to 6
- panel_size: float32 [65536], P('wrap'), may hold values from 1 to 3
- block_lists: int32 [4096, 16, 8], P('wrap', 'span'), may hold values from 0 to 511
- nu_field: float32 [4096, 16, 128], P('wrap', 'span'), may hold values from 0.05 to 1
- vorticity: float32 [4096, 16, 128], P('wrap', 'span'), may hold values from 0.5 to 5
Outputs:
- nu_next: float32 [4096, 16, 128], P('wrap', 'span')
- wall_dist: float32 [4096, 16, 128], P('wrap', 'span')
Inputs may be any that keep to these rules, and one draw needn't show every extreme that they name: `block_lists`: each entry names a panel block.
All inputs are finite; a program needn't handle non-finite values.
Results may differ from a plain program's by a relative error of at most 0.00002.
Values sent between devices are 32-bit elements; how exact they have to be, the bound alone decides.
No kernel may reach another device: no remote copies, remote signals or barrier semaphores. Data moves between devices by JAX's collectives and lax.ppermute only.
A program may use at most 64 MiB of HBM per device.

v0:
```python
import math

import jax
import jax.numpy as jnp
from jax import lax
from jax.sharding import PartitionSpec as P

PBS = 128


coef_cb1 = 0.1355
coef_cb2 = 0.622
coef_sigma = 2.0 / 3.0
coef_kappa = 0.41
coef_cw2 = 0.3
coef_cw3 = 2.0
viscous = 1.0
time_step = 0.03
coef_cw1 = coef_cb1 / coef_kappa**2 + (1.0 + coef_cb2) / coef_sigma


def extended(cells, sides, width):
    for axis, dim in sides:
        count = lax.axis_size(axis)
        ends = count - 1
        head = lax.slice_in_dim(cells, 0, width, axis=dim)
        tail = lax.slice_in_dim(cells, cells.shape[dim] - width, cells.shape[dim], axis=dim)
        cells = jnp.concatenate(
            [
                lax.ppermute(tail, axis, [(i, (i + 1) % count) for i in range(ends)]),
                cells,
                lax.ppermute(head, axis, [((i + 1) % count, i) for i in range(ends)]),
            ],
            axis=dim,
        )
    return cells


def partner_2(block, axis, bit):
    count = lax.axis_size(axis)
    route = []
    for low in range(count):
        high = low | 1 << bit
        if high != low and high < count:
            route += [(low, high), (high, low)]
    return lax.ppermute(block, axis, route)


def group_squares(cells, blocks_xyz, blocks_size, listed):
    nearest = None
    for list_slot in range(listed.shape[1]):
        picked = listed[:, list_slot]
        chosen = blocks_xyz[:, picked, :]
        radius = blocks_size[picked, :]
        summed = (radius * radius)[:, None, :]
        for component in range(3):
            offset = cells[component][:, :, None] - chosen[component][:, None, :]
            summed = summed + offset * offset
        block_min = jnp.min(summed, axis=2)
        nearest = block_min if nearest is None else jnp.minimum(nearest, block_min)
    return nearest


def update_rate(current, neighbours, squares, vorticity):
    face_flux = jnp.zeros_like(current)
    for beside in neighbours:
        change = beside - current
        face_flux = (
            face_flux
            + (1.0 + coef_cb2) * (viscous + 0.5 * (current + beside)) * change
            - coef_cb2 * (viscous + current) * change
        )
    diffusion = face_flux / coef_sigma
    scaled = coef_kappa**2 * squares
    modified = vorticity + current / scaled
    wall_ratio = current / (modified * scaled)
    shaped = wall_ratio + coef_cw2 * (wall_ratio**6 - wall_ratio)
    factor = shaped * ((1.0 + coef_cw3**6) / (shaped**6 + coef_cw3**6)) ** (1.0 / 6.0)
    return (
        diffusion + coef_cb1 * modified * current - coef_cw1 * factor * current * current / squares
    )


def shards(cell_xyz, panel_xyz, panel_size, block_lists, nu_field, vorticity):
    all_xyz, all_size = (
        lax.all_gather(panel_xyz, "wrap", axis=1, tiled=True),
        lax.all_gather(panel_size, "wrap", axis=0, tiled=True),
    )
    blocks_xyz = all_xyz.reshape(3, -1, PBS)
    blocks_size = all_size.reshape(-1, PBS)
    local_wrap = nu_field.shape[0]
    local_span = nu_field.shape[1]
    normal_cells = nu_field.shape[2]
    line_count = local_wrap * local_span
    group_count = math.gcd(line_count, 8)
    group_size = line_count // group_count
    grouped_cells = jnp.moveaxis(cell_xyz.reshape(3, group_count, group_size, normal_cells), 1, 0)
    grouped_lists = block_lists.reshape(group_count, group_size, block_lists.shape[2])

    def per_group(packed):
        return group_squares(packed[0], blocks_xyz, blocks_size, packed[1])

    squares = lax.map(per_group, (grouped_cells, grouped_lists)).reshape(
        local_wrap, local_span, normal_cells
    )
    devices = lax.axis_size("wrap")
    wrap_place = lax.axis_index("wrap")
    span_count = lax.axis_size("span")
    span_place = lax.axis_index("span")
    extent = local_wrap * devices
    global_rows = wrap_place * local_wrap + jnp.arange(local_wrap)
    in_wake = (global_rows < extent // 4) | (global_rows >= extent - extent // 4)
    bit_total = devices.bit_length() - 1
    bit_order = list(range(bit_total))

    def section_rate(current):
        padded = extended(current, (("wrap", 0), ("span", 1)), 1)
        lower_wrap = jnp.concatenate(
            [jnp.where(wrap_place == 0, current[:1], padded[:1, 1:-1]), current[:-1]], axis=0
        )
        upper_wrap = jnp.concatenate(
            [current[1:], jnp.where(wrap_place == devices - 1, current[-1:], padded[-1:, 1:-1])],
            axis=0,
        )
        lower_span = jnp.concatenate(
            [jnp.where(span_place == 0, current[:, :1], padded[1:-1, :1]), current[:, :-1]], axis=1
        )
        upper_span = jnp.concatenate(
            [
                current[:, 1:],
                jnp.where(span_place == span_count - 1, current[:, -1:], padded[1:-1, -1:]),
            ],
            axis=1,
        )
        first_row = current[:, :, 0]
        partner = first_row[::-1]
        for bit_index in bit_order:
            partner = partner_2(partner, "wrap", bit_index)
        ghost_row = jnp.where(in_wake[:, None], partner, -first_row)
        neighbours = (
            lower_wrap,
            upper_wrap,
            lower_span,
            upper_span,
            jnp.concatenate([ghost_row[:, :, None], current[:, :, :-1]], axis=2),
            jnp.concatenate([current[:, :, 1:], current[:, :, -1:]], axis=2),
        )
        return update_rate(current, neighbours, squares, vorticity)

    middle = nu_field + 0.5 * time_step * section_rate(nu_field)
    nu_next = nu_field + time_step * section_rate(middle)
    return (nu_next, jnp.sqrt(squares))


def solution(mesh):
    in_specs = (
        P(None, "wrap", "span", None),
        P(None, "wrap"),
        P("wrap"),
        P("wrap", "span", None),
        P("wrap", "span", None),
        P("wrap", "span", None),
    )
    out_specs = (P("wrap", "span", None), P("wrap", "span", None))
    return jax.shard_map(shards, mesh=mesh, in_specs=in_specs, out_specs=out_specs, check_vma=False)
```

profile of v0, /device:TPU:32, one launch (start us, length us, event | category | flops | bytes accessed | tf_op | source)
XLA Modules:
  0.0 576.1 jit_solution(13957476942990503689)
XLA Ops:
  5.1 6.2 %collective-permute-start.1 = (f32[1,8,128]{2,1,0:T(8,128)S(1)}, f32[1,8,128]{2,1,0:T(8,128)S(1)}, u32[]{:S(2)}, u32[]{:S(2)}) collective-permute-start(f32[1,8,128]{2,1,0:T(8,128)S(1)} %get-tuple-element.176), channel_id=1, source_target_pairs={{2,0},{4,2},{6,4},{8,6},{10,8},{12,10},{14,12},{16,14},{18,16},{20... | collective-permute-start | bytes 12296 | tf_op jit(solution)/shard_map/ppermute | solution.py:32
  12.2 142.7 %all-gather = f32[128,1,512]{2,1,0:T(1,128)S(1)} all-gather(f32[1,1,512]{2,1,0:T(1,128)} %bitcast.192), channel_id=1, replica_groups=mesh['wrap'=128,'span'=2] {'wrap'}, dimensions={0}, use_global_device_ids=true | all-gather | bytes 264192 | tf_op jit(solution)/shard_map/all_gather | solution.py:87
  154.9 153.8 %all_gather.7 = f32[3,65536]{1,0:T(4,128)S(1)} all-gather(f32[3,512]{1,0:T(4,128)S(1)} %copy-done.2), channel_id=1, replica_groups=mesh['wrap'=128,'span'=2] {'wrap'}, dimensions={1}, use_global_device_ids=true | all-gather | bytes 792576 | tf_op jit(solution)/shard_map/all_gather | solution.py:86
  308.7 184.8 %while.10 = (s32[]{:T(128)}, f32[8,32,128]{2,1,0:T(8,128)S(1)}, s32[8,32,8]{1,0,2:T(8,128)S(1)}, f32[512,128]{1,0:T(8,128)S(1)}, f32[8,3,32,128]{3,2,0,1:T(8,128)}, /*index=5*/f32[3,512,128]{2,0,1:T(4,128)S(1)}, s32[]{:T(128)}) while((s32[]{:T(128)}, f32[8,32,128]{2,1,0:T(8,128)S(1)}, s32[8,32,8]{1,0,2:T(8,128)S(1)}, ...), condition=%wide.region_9.10_spmd, body=%wide.region_0.9_spmd.sunk | while | flops 41980672 | bytes 3365985 | solution.py:103
  314.6 6.1 %add_reduce_fusion.10 = (f32[32,128]{1,0:T(8,128)S(1)}, f32[32,128]{1,0:T(8,128)S(1)}, f32[32,128]{1,0:T(8,128)S(1)}, f32[32,128]{1,0:T(8,128)S(1)}) fusion(f32[32,128]{1,0:T(8,128)S(1)} %bitcast.164, f32[32,128]{1,0:T(8,128)S(1)} %get-tuple-element.275, f32[32,128]{1,0:T(8,128)S(1)} %bitcast.163, f32[32,128]{1,0:T(8,128)S(1)} %get-tuple-element.277, ...), kind=kLoop, calls=%fused_computation.23.clone.1 | loop fusion | flops 20955136 | bytes 376832 | tf_op jit(solution)/shard_map/while/body/eval_jaxpr/reduce_min | solution.py:59
  325.7 6.1 %add_reduce_fusion.11 = (f32[32,128]{1,0:T(8,128)S(1)}, f32[32,128]{1,0:T(8,128)S(1)}, f32[32,128]{1,0:T(8,128)S(1)}, f32[32,128]{1,0:T(8,128)S(1)}) fusion(f32[32,128]{1,0:T(8,128)S(1)} %bitcast.167, f32[32,128]{1,0:T(8,128)S(1)} %bitcast.166, f32[32,128]{1,0:T(8,128)S(1)} %bitcast.165, f32[32,128]{1,0:T(8,128)S(1)} %mul.772, ...), kind=kLoop, calls=%fused_computation.22.clone.1 | loop fusion | flops 20955136 | bytes 376832 | tf_op jit(solution)/shard_map/while/body/eval_jaxpr/reduce_min | solution.py:59
  337.7 6.1 %add_reduce_fusion.10 = (f32[32,128]{1,0:T(8,128)S(1)}, f32[32,128]{1,0:T(8,128)S(1)}, f32[32,128]{1,0:T(8,128)S(1)}, f32[32,128]{1,0:T(8,128)S(1)}) fusion(f32[32,128]{1,0:T(8,128)S(1)} %bitcast.164, f32[32,128]{1,0:T(8,128)S(1)} %get-tuple-element.275, f32[32,128]{1,0:T(8,128)S(1)} %bitcast.163, f32[32,128]{1,0:T(8,128)S(1)} %get-tuple-element.277, ...), kind=kLoop, calls=%fused_computation.23.clone.1 | loop fusion | flops 20955136 | bytes 376832 | tf_op jit(solution)/shard_map/while/body/eval_jaxpr/reduce_min | solution.py:59
  348.8 6.1 %add_reduce_fusion.11 = (f32[32,128]{1,0:T(8,128)S(1)}, f32[32,128]{1,0:T(8,128)S(1)}, f32[32,128]{1,0:T(8,128)S(1)}, f32[32,128]{1,0:T(8,128)S(1)}) fusion(f32[32,128]{1,0:T(8,128)S(1)} %bitcast.167, f32[32,128]{1,0:T(8,128)S(1)} %bitcast.166, f32[32,128]{1,0:T(8,128)S(1)} %bitcast.165, f32[32,128]{1,0:T(8,128)S(1)} %mul.772, ...), kind=kLoop, calls=%fused_computation.22.clone.1 | loop fusion | flops 20955136 | bytes 376832 | tf_op jit(solution)/shard_map/while/body/eval_jaxpr/reduce_min | solution.py:59
  360.8 6.1 %add_reduce_fusion.10 = (f32[32,128]{1,0:T(8,128)S(1)}, f32[32,128]{1,0:T(8,128)S(1)}, f32[32,128]{1,0:T(8,128)S(1)}, f32[32,128]{1,0:T(8,128)S(1)}) fusion(f32[32,128]{1,0:T(8,128)S(1)} %bitcast.164, f32[32,128]{1,0:T(8,128)S(1)} %get-tuple-element.275, f32[32,128]{1,0:T(8,128)S(1)} %bitcast.163, f32[32,128]{1,0:T(8,128)S(1)} %get-tuple-element.277, ...), kind=kLoop, calls=%fused_computation.23.clone.1 | loop fusion | flops 20955136 | bytes 376832 | tf_op jit(solution)/shard_map/while/body/eval_jaxpr/reduce_min | solution.py:59
  371.9 6.1 %add_reduce_fusion.11 = (f32[32,128]{1,0:T(8,128)S(1)}, f32[32,128]{1,0:T(8,128)S(1)}, f32[32,128]{1,0:T(8,128)S(1)}, f32[32,128]{1,0:T(8,128)S(1)}) fusion(f32[32,128]{1,0:T(8,128)S(1)} %bitcast.167, f32[32,128]{1,0:T(8,128)S(1)} %bitcast.166, f32[32,128]{1,0:T(8,128)S(1)} %bitcast.165, f32[32,128]{1,0:T(8,128)S(1)} %mul.772, ...), kind=kLoop, calls=%fused_computation.22.clone.1 | loop fusion | flops 20955136 | bytes 376832 | tf_op jit(solution)/shard_map/while/body/eval_jaxpr/reduce_min | solution.py:59
  383.9 6.1 %add_reduce_fusion.10 = (f32[32,128]{1,0:T(8,128)S(1)}, f32[32,128]{1,0:T(8,128)S(1)}, f32[32,128]{1,0:T(8,128)S(1)}, f32[32,128]{1,0:T(8,128)S(1)}) fusion(f32[32,128]{1,0:T(8,128)S(1)} %bitcast.164, f32[32,128]{1,0:T(8,128)S(1)} %get-tuple-element.275, f32[32,128]{1,0:T(8,128)S(1)} %bitcast.163, f32[32,128]{1,0:T(8,128)S(1)} %get-tuple-element.277, ...), kind=kLoop, calls=%fused_computation.23.clone.1 | loop fusion | flops 20955136 | bytes 376832 | tf_op jit(solution)/shard_map/while/body/eval_jaxpr/reduce_min | solution.py:59
  395.0 6.1 %add_reduce_fusion.11 = (f32[32,128]{1,0:T(8,128)S(1)}, f32[32,128]{1,0:T(8,128)S(1)}, f32[32,128]{1,0:T(8,128)S(1)}, f32[32,128]{1,0:T(8,128)S(1)}) fusion(f32[32,128]{1,0:T(8,128)S(1)} %bitcast.167, f32[32,128]{1,0:T(8,128)S(1)} %bitcast.166, f32[32,128]{1,0:T(8,128)S(1)} %bitcast.165, f32[32,128]{1,0:T(8,128)S(1)} %mul.772, ...), kind=kLoop, calls=%fused_computation.22.clone.1 | loop fusion | flops 20955136 | bytes 376832 | tf_op jit(solution)/shard_map/while/body/eval_jaxpr/reduce_min | solution.py:59
  407.0 6.1 %add_reduce_fusion.10 = (f32[32,128]{1,0:T(8,128)S(1)}, f32[32,128]{1,0:T(8,128)S(1)}, f32[32,128]{1,0:T(8,128)S(1)}, f32[32,128]{1,0:T(8,128)S(1)}) fusion(f32[32,128]{1,0:T(8,128)S(1)} %bitcast.164, f32[32,128]{1,0:T(8,128)S(1)} %get-tuple-element.275, f32[32,128]{1,0:T(8,128)S(1)} %bitcast.163, f32[32,128]{1,0:T(8,128)S(1)} %get-tuple-element.277, ...), kind=kLoop, calls=%fused_computation.23.clone.1 | loop fusion | flops 20955136 | bytes 376832 | tf_op jit(solution)/shard_map/while/body/eval_jaxpr/reduce_min | solution.py:59
  418.1 6.1 %add_reduce_fusion.11 = (f32[32,128]{1,0:T(8,128)S(1)}, f32[32,128]{1,0:T(8,128)S(1)}, f32[32,128]{1,0:T(8,128)S(1)}, f32[32,128]{1,0:T(8,128)S(1)}) fusion(f32[32,128]{1,0:T(8,128)S(1)} %bitcast.167, f32[32,128]{1,0:T(8,128)S(1)} %bitcast.166, f32[32,128]{1,0:T(8,128)S(1)} %bitcast.165, f32[32,128]{1,0:T(8,128)S(1)} %mul.772, ...), kind=kLoop, calls=%fused_computation.22.clone.1 | loop fusion | flops 20955136 | bytes 376832 | tf_op jit(solution)/shard_map/while/body/eval_jaxpr/reduce_min | solution.py:59
  430.1 6.1 %add_reduce_fusion.10 = (f32[32,128]{1,0:T(8,128)S(1)}, f32[32,128]{1,0:T(8,128)S(1)}, f32[32,128]{1,0:T(8,128)S(1)}, f32[32,128]{1,0:T(8,128)S(1)}) fusion(f32[32,128]{1,0:T(8,128)S(1)} %bitcast.164, f32[32,128]{1,0:T(8,128)S(1)} %get-tuple-element.275, f32[32,128]{1,0:T(8,128)S(1)} %bitcast.163, f32[32,128]{1,0:T(8,128)S(1)} %get-tuple-element.277, ...), kind=kLoop, calls=%fused_computation.23.clone.1 | loop fusion | flops 20955136 | bytes 376832 | tf_op jit(solution)/shard_map/while/body/eval_jaxpr/reduce_min | solution.py:59
  441.2 6.1 %add_reduce_fusion.11 = (f32[32,128]{1,0:T(8,128)S(1)}, f32[32,128]{1,0:T(8,128)S(1)}, f32[32,128]{1,0:T(8,128)S(1)}, f32[32,128]{1,0:T(8,128)S(1)}) fusion(f32[32,128]{1,0:T(8,128)S(1)} %bitcast.167, f32[32,128]{1,0:T(8,128)S(1)} %bitcast.166, f32[32,128]{1,0:T(8,128)S(1)} %bitcast.165, f32[32,128]{1,0:T(8,128)S(1)} %mul.772, ...), kind=kLoop, calls=%fused_computation.22.clone.1 | loop fusion | flops 20955136 | bytes 376832 | tf_op jit(solution)/shard_map/while/body/eval_jaxpr/reduce_min | solution.py:59
  453.2 6.1 %add_reduce_fusion.10 = (f32[32,128]{1,0:T(8,128)S(1)}, f32[32,128]{1,0:T(8,128)S(1)}, f32[32,128]{1,0:T(8,128)S(1)}, f32[32,128]{1,0:T(8,128)S(1)}) fusion(f32[32,128]{1,0:T(8,128)S(1)} %bitcast.164, f32[32,128]{1,0:T(8,128)S(1)} %get-tuple-element.275, f32[32,128]{1,0:T(8,128)S(1)} %bitcast.163, f32[32,128]{1,0:T(8,128)S(1)} %get-tuple-element.277, ...), kind=kLoop, calls=%fused_computation.23.clone.1 | loop fusion | flops 20955136 | bytes 376832 | tf_op jit(solution)/shard_map/while/body/eval_jaxpr/reduce_min | solution.py:59
  464.3 6.1 %add_reduce_fusion.11 = (f32[32,128]{1,0:T(8,128)S(1)}, f32[32,128]{1,0:T(8,128)S(1)}, f32[32,128]{1,0:T(8,128)S(1)}, f32[32,128]{1,0:T(8,128)S(1)}) fusion(f32[32,128]{1,0:T(8,128)S(1)} %bitcast.167, f32[32,128]{1,0:T(8,128)S(1)} %bitcast.166, f32[32,128]{1,0:T(8,128)S(1)} %bitcast.165, f32[32,128]{1,0:T(8,128)S(1)} %mul.772, ...), kind=kLoop, calls=%fused_computation.22.clone.1 | loop fusion | flops 20955136 | bytes 376832 | tf_op jit(solution)/shard_map/while/body/eval_jaxpr/reduce_min | solution.py:59
  476.3 6.1 %add_reduce_fusion.10 = (f32[32,128]{1,0:T(8,128)S(1)}, f32[32,128]{1,0:T(8,128)S(1)}, f32[32,128]{1,0:T(8,128)S(1)}, f32[32,128]{1,0:T(8,128)S(1)}) fusion(f32[32,128]{1,0:T(8,128)S(1)} %bitcast.164, f32[32,128]{1,0:T(8,128)S(1)} %get-tuple-element.275, f32[32,128]{1,0:T(8,128)S(1)} %bitcast.163, f32[32,128]{1,0:T(8,128)S(1)} %get-tuple-element.277, ...), kind=kLoop, calls=%fused_computation.23.clone.1 | loop fusion | flops 20955136 | bytes 376832 | tf_op jit(solution)/shard_map/while/body/eval_jaxpr/reduce_min | solution.py:59
  487.4 6.1 %add_reduce_fusion.11 = (f32[32,128]{1,0:T(8,128)S(1)}, f32[32,128]{1,0:T(8,128)S(1)}, f32[32,128]{1,0:T(8,128)S(1)}, f32[32,128]{1,0:T(8,128)S(1)}) fusion(f32[32,128]{1,0:T(8,128)S(1)} %bitcast.167, f32[32,128]{1,0:T(8,128)S(1)} %bitcast.166, f32[32,128]{1,0:T(8,128)S(1)} %bitcast.165, f32[32,128]{1,0:T(8,128)S(1)} %mul.772, ...), kind=kLoop, calls=%fused_computation.22.clone.1 | loop fusion | flops 20955136 | bytes 376832 | tf_op jit(solution)/shard_map/while/body/eval_jaxpr/reduce_min | solution.py:59
  497.4 5.1 collective-permute-done.6
  506.1 15.3 %collective-permute-start.8 = (f32[32,8]{0,1:T(8,128)S(1)}, f32[32,8]{0,1:T(8,128)S(1)}, u32[]{:S(2)}, u32[]{:S(2)}) collective-permute-start(f32[32,8]{0,1:T(8,128)S(1)} %collective-permute-done.7), channel_id=1, source_target_pairs={{0,32},{32,0},{2,34},{34,2},{4,36},{36,4},{6,38},{38,6},{8,40},{40... | collective-permute-start | bytes 3080 | tf_op jit(solution)/shard_map/ppermute | solution.py:46
  537.9 5.5 collective-permute-done.3
  549.1 5.1 collective-permute-done.17
  (405 shorter events, 142.1 us)
Async XLA Ops:
  0.6 154.3 %copy-start.2 = (f32[3,512]{1,0:T(4,128)S(1)}, f32[3,512]{1,0:T(4,128)}, u32[]{:S(2)}) copy-start(f32[3,512]{1,0:T(4,128)} %param.9) | copy-start | bytes 18436
  1.9 491.7 %collective-permute-start.4 = (f32[32,8]{0,1:T(8,128)S(1)}, f32[32,8]{0,1:T(8,128)S(1)}, u32[]{:S(2)}, u32[]{:S(2)}) collective-permute-start(f32[32,8]{0,1:T(8,128)S(1)} %rev.6), channel_id=1, source_target_pairs={{0,2},{2,0},{4,6},{6,4},{8,10},{10,8},{12,14},{14,12},{16,18},{18,... | collective-permute-start | bytes 3080 | tf_op jit(solution)/shard_map/ppermute | solution.py:46
  2.7 518.7 %collective-permute-start = (f32[1,8,128]{2,1,0:T(8,128)S(1)}, f32[1,8,128]{2,1,0:T(8,128)S(1)}, u32[]{:S(2)}, u32[]{:S(2)}) collective-permute-start(f32[1,8,128]{2,1,0:T(8,128)S(1)} %get-tuple-element.177), channel_id=1, source_target_pairs={{0,2},{2,4},{4,6},{6,8},{8,10},{10,12},{12,14},{14,16},{16,18},{18... | collective-permute-start | bytes 12296 | tf_op jit(solution)/shard_map/ppermute | solution.py:30
  5.1 517.9 %collective-permute-start.1 = (f32[1,8,128]{2,1,0:T(8,128)S(1)}, f32[1,8,128]{2,1,0:T(8,128)S(1)}, u32[]{:S(2)}, u32[]{:S(2)}) collective-permute-start(f32[1,8,128]{2,1,0:T(8,128)S(1)} %get-tuple-element.176), channel_id=1, source_target_pairs={{2,0},{4,2},{6,4},{8,6},{10,8},{12,10},{14,12},{16,14},{18,16},{20... | collective-permute-start | bytes 12296 | tf_op jit(solution)/shard_map/ppermute | solution.py:32
  308.7 184.8 %copy-start = (f32[32,8,128]{2,1,0:T(8,128)S(1)}, f32[32,8,128]{2,1,0:T(8,128)}, u32[]{:S(2)}) copy-start(f32[32,8,128]{2,1,0:T(8,128)} %param.12) | copy-start | bytes 393220
  493.6 3.7 collective-permute-start.5
  497.3 5.1 collective-permute-start.6
  502.5 3.6 collective-permute-start.7
  506.1 16.9 %collective-permute-start.8 = (f32[32,8]{0,1:T(8,128)S(1)}, f32[32,8]{0,1:T(8,128)S(1)}, u32[]{:S(2)}, u32[]{:S(2)}) collective-permute-start(f32[32,8]{0,1:T(8,128)S(1)} %collective-permute-done.7), channel_id=1, source_target_pairs={{0,32},{32,0},{2,34},{34,2},{4,36},{36,4},{6,38},{38,6},{8,40},{40... | collective-permute-start | bytes 3080 | tf_op jit(solution)/shard_map/ppermute | solution.py:46
  523.0 4.5 collective-permute-start.9
  527.5 10.3 %collective-permute-start.10 = (f32[32,8]{0,1:T(8,128)S(1)}, f32[32,8]{0,1:T(8,128)S(1)}, u32[]{:S(2)}, u32[]{:S(2)}) collective-permute-start(f32[32,8]{0,1:T(8,128)S(1)} %collective-permute-done.9), channel_id=1, source_target_pairs={{0,128},{128,0},{2,130},{130,2},{4,132},{132,4},{6,134},{134,6},{8... | collective-permute-start | bytes 3080 | tf_op jit(solution)/shard_map/ppermute | solution.py:46
  531.3 6.6 %collective-permute-start.2 = (f32[34,1,128]{2,1,0:T(1,128)S(1)}, f32[34,1,128]{2,1,0:T(1,128)S(1)}, u32[]{:S(2)}, u32[]{:S(2)}) collective-permute-start(f32[34,1,128]{2,1,0:T(1,128)S(1)} %get-tuple-element.150), channel_id=1, source_target_pairs={{0,1},{2,3},{4,5},{6,7},{8,9},{10,11},{12,13},{14,15},{16,17},{18,... | collective-permute-start | bytes 52232 | tf_op jit(solution)/shard_map/ppermute | solution.py:30
  536.3 7.1 %collective-permute-start.3 = (f32[34,1,128]{2,1,0:T(1,128)S(1)}, f32[34,1,128]{2,1,0:T(1,128)S(1)}, u32[]{:S(2)}, u32[]{:S(2)}) collective-permute-start(f32[34,1,128]{2,1,0:T(1,128)S(1)} %get-tuple-element.151), channel_id=1, source_target_pairs={{1,0},{3,2},{5,4},{7,6},{9,8},{11,10},{13,12},{15,14},{17,16},{19,... | collective-permute-start | bytes 52232 | tf_op jit(solution)/shard_map/ppermute | solution.py:32
  544.3 1.2 collective-permute-start.15
  545.5 3.6 collective-permute-start.16
  549.1 5.1 collective-permute-start.17
  554.2 4.3 collective-permute-start.18
  554.2 8.0 %collective-permute-start.12 = (f32[1,8,128]{2,1,0:T(8,128)S(1)}, f32[1,8,128]{2,1,0:T(8,128)S(1)}, u32[]{:S(2)}, u32[]{:S(2)}) collective-permute-start(f32[1,8,128]{2,1,0:T(8,128)S(1)} %get-tuple-element.163), channel_id=1, source_target_pairs={{2,0},{4,2},{6,4},{8,6},{10,8},{12,10},{14,12},{16,14},{18,16},{20... | collective-permute-start | bytes 12296 | tf_op jit(solution)/shard_map/ppermute | solution.py:32
  556.1 7.9 %collective-permute-start.11 = (f32[1,8,128]{2,1,0:T(8,128)S(1)}, f32[1,8,128]{2,1,0:T(8,128)S(1)}, u32[]{:S(2)}, u32[]{:S(2)}) collective-permute-start(f32[1,8,128]{2,1,0:T(8,128)S(1)} %get-tuple-element.162), channel_id=1, source_target_pairs={{0,2},{2,4},{4,6},{6,8},{8,10},{10,12},{12,14},{14,16},{16,18},{18... | collective-permute-start | bytes 12296 | tf_op jit(solution)/shard_map/ppermute | solution.py:30
  558.6 3.7 collective-permute-start.19
  562.3 4.8 collective-permute-start.20
  564.1 10.7 %collective-permute-start.13 = (f32[34,1,128]{2,1,0:T(1,128)S(1)}, f32[34,1,128]{2,1,0:T(1,128)S(1)}, u32[]{:S(2)}, u32[]{:S(2)}) collective-permute-start(f32[34,1,128]{2,1,0:T(1,128)S(1)} %get-tuple-element.148), channel_id=1, source_target_pairs={{0,1},{2,3},{4,5},{6,7},{8,9},{10,11},{12,13},{14,15},{16,17},{18,... | collective-permute-start | bytes 52232 | tf_op jit(solution)/shard_map/ppermute | solution.py:30
  565.8 9.1 %collective-permute-start.14 = (f32[34,1,128]{2,1,0:T(1,128)S(1)}, f32[34,1,128]{2,1,0:T(1,128)S(1)}, u32[]{:S(2)}, u32[]{:S(2)}) collective-permute-start(f32[34,1,128]{2,1,0:T(1,128)S(1)} %get-tuple-element.149), channel_id=1, source_target_pairs={{1,0},{3,2},{5,4},{7,6},{9,8},{11,10},{13,12},{15,14},{17,16},{19,... | collective-permute-start | bytes 52232 | tf_op jit(solution)/shard_map/ppermute | solution.py:32
  567.1 7.6 %collective-permute-start.21 = (f32[32,8]{0,1:T(8,128)S(1)}, f32[32,8]{0,1:T(8,128)S(1)}, u32[]{:S(2)}, u32[]{:S(2)}) collective-permute-start(f32[32,8]{0,1:T(8,128)S(1)} %collective-permute-done.20), channel_id=1, source_target_pairs={{0,128},{128,0},{2,130},{130,2},{4,132},{132,4},{6,134},{134,6},{8... | collective-permute-start | bytes 3080 | tf_op jit(solution)/shard_map/ppermute | solution.py:46
  (1 other events, 49.9 us)
where the time goes:
time: 580 us; the launch traced here: 576 us
  blocking collectives  297 us (51%)
  other arithmetic  101 us (17%)
  local copies, waits for them, and re-layouts  88.4 us (15%)
  starting transfers between devices  48.5 us (8%)
  waiting for transfers between devices  39.6 us (7%)
    all_gather x1, blocking collectives, shards(): lax.all_gather(panel_xyz, 'wrap', axis=1, tiled=True)  154 us
    all_gather x1, blocking collectives, shards(): lax.all_gather(panel_size, 'wrap', axis=0, tiled=True)  143 us
    reduce_min x16, other arithmetic, group_squares(): block_min = jnp.min(summed, axis=2)  97.8 us
    gather x64, local copies, waits for them, and re-layouts, group_squares(): chosen = blocks_xyz[:, picked, :]  39 us
    gather x64, local copies, waits for them, and re-layouts, group_squares(): radius = blocks_size[picked, :]  36.7 us
    ppermute x14, waiting for transfers between devices, partner_2(): return lax.ppermute(block, axis, route)  32.3 us
    ppermute x14, starting transfers between devices, partner_2(): return lax.ppermute(block, axis, route)  26.3 us
  transfers between devices with their start and end apart: 22, of which 12 were waited for; matrix products, arithmetic and copies ran while one was open for 32% of the time, Pallas kernels for 0%

commit v1 on v0

v1 whole, which is shorter than its diff:
```python
import functools

import jax
import jax.numpy as jnp
from jax import lax
from jax.experimental import pallas as pl
from jax.experimental.pallas import tpu as pltpu
from jax.sharding import PartitionSpec as P

BF = jnp.bfloat16
F32 = jnp.float32
PBS = 128
FEATS = 48
LINES_PER_STEP = 32
STAGES = ((6, 5), (4, 3), (2, 1), (0,))

coef_cb1 = 0.1355
coef_cb2 = 0.622
coef_sigma = 2.0 / 3.0
coef_kappa = 0.41
coef_cw2 = 0.3
coef_cw3 = 2.0
viscous = 1.0
time_step = 0.03
coef_cw1 = coef_cb1 / coef_kappa**2 + (1.0 + coef_cb2) / coef_sigma


def split_rows(rows):
    high = rows.astype(BF).astype(F32)
    rest = rows - high
    mid = rest.astype(BF).astype(F32)
    return high, mid, rest - mid


def panel_features(rows):
    high, mid, low = split_rows(rows)
    return jnp.concatenate([high, high, high, mid, mid, low], 0).astype(BF)


def cell_features(rows):
    high, mid, low = split_rows(rows)
    return jnp.concatenate([high, mid, low, high, mid, high], 0).astype(BF)


def cells_kernel(rows_ref, out_ref):
    lines = rows_ref.shape[0]
    per_step = 8

    def body(step, carry):
        for part in range(per_step):
            line = step * per_step + part
            feats = cell_features(rows_ref[line])
            out_ref[pl.ds(pl.multiple_of(line * 128, 128), 128), :] = feats.T
        return carry

    lax.fori_loop(0, lines // per_step, body, 0)


def squares_kernel(place_ref, panels_ref, cells_ref, norm_ref, squares_ref, dist_ref, table_ref):
    blocks = table_ref.shape[0]
    per_step = 4

    def build(step, carry):
        for part in range(per_step):
            pair = step * per_step + part
            rows = panels_ref[pl.ds(pl.multiple_of(pair * 8, 8), 8), :]
            table_ref[pair * 2] = panel_features(rows)
            table_ref[pair * 2 + 1] = panel_features(jnp.concatenate([rows[4:], rows[:4]], 0))
        return carry

    lax.fori_loop(0, blocks // 2 // per_step, build, 0)
    tiles = squares_ref.shape[0]
    tiles_per_step = LINES_PER_STEP // 8

    def body(step, carry):
        for part in range(tiles_per_step):
            tile = step * tiles_per_step + part
            found = []
            for sub in range(8):
                line = tile * 8 + sub
                cells = cells_ref[pl.ds(pl.multiple_of(line * 128, 128), 128), :]
                nearest = None
                for slot in range(0, 8, 2):
                    first = place_ref[line * 8 + slot]
                    second = place_ref[line * 8 + slot + 1]
                    panels = jnp.concatenate([table_ref[first], table_ref[second]], 1)
                    value = jnp.dot(cells, panels, preferred_element_type=F32)
                    value = jnp.minimum(value[:, :128], value[:, 128:])
                    nearest = value if nearest is None else jnp.minimum(nearest, value)
                turned = jnp.min(nearest.T.reshape(16, 8, 128), axis=0)
                found.append(jnp.min(turned, axis=0, keepdims=True))
            squares = jnp.concatenate(found, 0) + norm_ref[tile]
            squares_ref[tile] = squares
            dist_ref[tile] = jnp.sqrt(squares)
        return carry

    lax.fori_loop(0, tiles // tiles_per_step, body, 0)


def section_kernel(
    step_size,
    flags_ref,
    current_ref,
    lower_ref,
    upper_ref,
    beside_ref,
    ghost_ref,
    squares_ref,
    vorticity_ref,
    base_ref,
    out_ref,
):
    rows = current_ref.shape[0]
    at_first = flags_ref[0] == 1
    at_last = flags_ref[1] == 1
    at_low_span = flags_ref[2] == 1
    in_wake = flags_ref[3] == 1
    lane = lax.broadcasted_iota(jnp.int32, (8, 128), 1)
    sub = lax.broadcasted_iota(jnp.int32, (8, 128), 0)

    for row in range(rows):
        value = current_ref[row]
        if row == 0:
            below = jnp.where(at_first, value, lower_ref[0])
        else:
            below = current_ref[row - 1]
        if row == rows - 1:
            above = jnp.where(at_last, value, upper_ref[0])
        else:
            above = current_ref[row + 1]
        across = jnp.broadcast_to(beside_ref[row : row + 1, :], (8, 128))
        span_low = jnp.where(at_low_span, value, across)
        span_high = jnp.where(at_low_span, across, value)
        span_below = jnp.where(sub == 0, span_low, pltpu.roll(value, 1, 0))
        span_above = jnp.where(sub == 7, span_high, pltpu.roll(value, 7, 0))
        ghost = jnp.where(in_wake, ghost_ref[row], -value)
        normal_below = jnp.where(lane == 0, ghost, pltpu.roll(value, 1, 1))
        normal_above = jnp.where(lane == 127, value, pltpu.roll(value, 127, 1))
        sums = jnp.zeros_like(value)
        squared = jnp.zeros_like(value)
        for other in (below, above, span_below, span_above, normal_below, normal_above):
            change = other - value
            sums = sums + change
            squared = squared + change * change
        flux = (viscous + value) * sums + (0.5 * (1.0 + coef_cb2)) * squared
        squares = squares_ref[row]
        scaled = coef_kappa**2 * squares
        modified = vorticity_ref[row] + value / scaled
        ratio = value / (modified * scaled)
        ratio2 = ratio * ratio
        shaped = ratio + coef_cw2 * (ratio2 * ratio2 * ratio2 - ratio)
        shaped2 = shaped * shaped
        base = (1.0 + coef_cw3**6) / (shaped2 * shaped2 * shaped2 + coef_cw3**6)
        factor = shaped * jnp.exp(jnp.log(base) * (1.0 / 6.0))
        rate = (
            flux / coef_sigma
            + coef_cb1 * modified * value
            - coef_cw1 * factor * value * value / squares
        )
        out_ref[row] = base_ref[row] + step_size * rate


def section(step_size, flags, current, base, squares, vorticity):
    devices = lax.axis_size("wrap")
    rows = current.shape[0]
    low_span = lax.axis_index("span") == 0
    lower = lax.ppermute(current[-1:], "wrap", [(i, i + 1) for i in range(devices - 1)])
    upper = lax.ppermute(current[:1], "wrap", [(i + 1, i) for i in range(devices - 1)])
    sent = jnp.where(low_span, current[:, -1], current[:, 0])
    beside = lax.ppermute(sent, "span", [(0, 1), (1, 0)])
    partner = lax.ppermute(
        current[:, :, 0], "wrap", [(i, devices - 1 - i) for i in range(devices)]
    )[::-1]
    ghost = jnp.broadcast_to(partner[:, :, None], current.shape)
    smem = pl.BlockSpec(memory_space=pltpu.SMEM)
    vmem = pl.BlockSpec(memory_space=pltpu.VMEM)
    return pl.pallas_call(
        functools.partial(section_kernel, step_size),
        out_shape=jax.ShapeDtypeStruct(current.shape, F32),
        in_specs=[smem] + [vmem] * 8,
        out_specs=vmem,
        name="section",
    )(flags, current, lower, upper, beside, ghost, squares, vorticity, base)


def gather(shard):
    devices = lax.axis_size("wrap")
    for bits in STAGES:
        parts = [shard]
        for choice in range(1, 1 << len(bits)):
            mask = sum(((choice >> n) & 1) << bit for n, bit in enumerate(bits))
            parts.append(lax.ppermute(shard, "wrap", [(i, i ^ mask) for i in range(devices)]))
        shard = jnp.concatenate(parts, 0)
    return shard


def slot_of(device):
    mask = device ^ lax.axis_index("wrap")
    order = [bit for bits in STAGES for bit in bits]
    return sum(((mask >> bit) & 1) << place for place, bit in enumerate(order))


def shards(cell_xyz, panel_xyz, panel_size, block_lists, nu_field, vorticity):
    devices = lax.axis_size("wrap")
    wrap_place = lax.axis_index("wrap")
    local_wrap, local_span, normal_cells = nu_field.shape
    lines = local_wrap * local_span
    own_blocks = panel_size.shape[0] // PBS

    offset = jnp.sum(panel_xyz * panel_xyz, axis=0) + panel_size * panel_size
    packed = jnp.concatenate([panel_xyz, offset[None]], 0).reshape(4, own_blocks, PBS)
    panels = gather(jnp.swapaxes(packed, 0, 1).reshape(own_blocks * 4, PBS))

    places = slot_of(block_lists // own_blocks) * own_blocks + block_lists % own_blocks
    places = places.reshape(lines * block_lists.shape[2])

    norm = jnp.sum(cell_xyz * cell_xyz, axis=0)
    flat = cell_xyz.reshape(3, lines, normal_cells)
    filler = jnp.zeros_like(flat[0])
    cell_rows = jnp.stack(
        [-2.0 * flat[0], -2.0 * flat[1], -2.0 * flat[2], filler + 1.0] + [filler] * 4, 1
    )
    smem = pl.BlockSpec(memory_space=pltpu.SMEM)
    vmem = pl.BlockSpec(memory_space=pltpu.VMEM)
    cells = pl.pallas_call(
        cells_kernel,
        out_shape=jax.ShapeDtypeStruct((lines * normal_cells, FEATS), BF),
        in_specs=[vmem],
        out_specs=vmem,
        compiler_params=pltpu.CompilerParams(vmem_limit_bytes=24 * 2**20),
        name="cells",
    )(cell_rows)
    like = jax.ShapeDtypeStruct(nu_field.shape, F32)
    squares, dist = pl.pallas_call(
        squares_kernel,
        out_shape=(like, like),
        in_specs=[smem, vmem, vmem, vmem],
        out_specs=(vmem, vmem),
        scratch_shapes=[pltpu.VMEM((devices * own_blocks, FEATS, PBS), BF)],
        compiler_params=pltpu.CompilerParams(vmem_limit_bytes=32 * 2**20),
        name="squares",
    )(places, panels, cells, norm)

    wake = (wrap_place < devices // 4) | (wrap_place >= devices - devices // 4)
    flags = jnp.stack(
        [wrap_place == 0, wrap_place == devices - 1, lax.axis_index("span") == 0, wake]
    ).astype(jnp.int32)
    middle = section(0.5 * time_step, flags, nu_field, nu_field, squares, vorticity)
    nu_next = section(time_step, flags, middle, nu_field, squares, vorticity)
    return (nu_next, dist)


def solution(mesh):
    in_specs = (
        P(None, "wrap", "span", None),
        P(None, "wrap"),
        P("wrap"),
        P("wrap", "span", None),
        P("wrap", "span", None),
        P("wrap", "span", None),
    )
    out_specs = (P("wrap", "span", None), P("wrap", "span", None))
    return jax.shard_map(shards, mesh=mesh, in_specs=in_specs, out_specs=out_specs, check_vma=False)
```

time: 580 us -> 118 us (0.20)
  blocking collectives: 297 us -> 0 us
  other arithmetic: 101 us -> 7.57 us
  local copies, waits for them, and re-layouts: 88.4 us -> 25.4 us
  Pallas kernels: 0 us -> 30.3 us
  waiting for transfers between devices: 39.6 us -> 10.8 us
  starting transfers between devices: 48.5 us -> 42.6 us
    all_gather x2 -> x0, blocking collectives: 297 us -> none  [the longest x1 154 us: shards(): lax.all_gather(panel_xyz, 'wrap', axis=1, tiled=True)]
    reduce_min x16 -> x0, other arithmetic: 97.8 us -> none  [group_squares(): block_min = jnp.min(summed, axis=2)]
    gather x128 -> x0, local copies, waits for them, and re-layouts: 75.7 us -> none  [the longest x64 39 us: group_squares(): chosen = blocks_xyz[:, picked, :]]
    pallas_call x0 -> x4, Pallas kernels: none -> 30.3 us  [the longest x1 21.6 us: shards(): pl.pallas_call(squares_kernel, out_shape=(like, like), in_specs=[smem, vm...]
    ppermute x22 -> x18, waiting for transfers between devices: 39.6 us -> 10.8 us  [the longest x2 7.49 us: section(): lax.ppermute(current[:, :, 0], 'wrap', [(i, devices - 1 - i) for i in ran...]
    unnamed x10 -> x26, local copies, waits for them, and re-layouts: 1.01 us -> 14.5 us
    dynamic_slice x16 -> x0, local copies, waits for them, and re-layouts: 6.57 us -> none  [shards(): lax.map(per_group, (grouped_cells, grouped_lists))]
    ppermute x22 -> x18, starting transfers between devices: 48.5 us -> 42.6 us  [the longest x10 16.3 us: gather(): lax.ppermute(shard, 'wrap', [(i, i ^ mask) for i in range(devices)])]
  transfers between devices with their start and end apart: 22 -> 18, of which waited for: 12 -> 4; matrix products, arithmetic and copies ran while one was open for 32% -> 18% of each run, Pallas kernels for 0% -> 22%
where the time goes in v1:
time: 118 us; the launch traced here: 117 us
  starting transfers between devices  42.6 us (36%)
  Pallas kernels  30.3 us (26%)
  local copies, waits for them, and re-layouts  25.4 us (22%)
  waiting for transfers between devices  10.8 us (9%)
  other arithmetic  7.57 us (6%)
    pallas_call x1, Pallas kernels, shards(): pl.pallas_call(squares_kernel, out_shape=(like, like), in_specs=[smem, vm...  21.6 us
    ppermute x10, starting transfers between devices, gather(): lax.ppermute(shard, 'wrap', [(i, i ^ mask) for i in range(devices)])  16.3 us
    unnamed x26, local copies, waits for them, and re-layouts  14.5 us
    ppermute x2, starting transfers between devices, section(): lax.ppermute(current[:1], 'wrap', [(i + 1, i) for i in range(devices - 1)])  13.1 us
    ppermute x2, waiting for transfers between devices, section(): lax.ppermute(current[:, :, 0], 'wrap', [(i, devices - 1 - i) for i in ran...  7.49 us
    ppermute x2, starting transfers between devices, section(): beside = lax.ppermute(sent, 'span', [(0, 1), (1, 0)])  4.63 us
    ppermute x2, starting transfers between devices, section(): lax.ppermute(current[:, :, 0], 'wrap', [(i, devices - 1 - i) for i in ran...  4.49 us
    pallas_call x2, Pallas kernels, section(): pl.pallas_call(functools.partial(section_kernel, step_size), out_shape=ja...  4.4 us
  transfers between devices with their start and end apart: 18, of which 4 were waited for; matrix products, arithmetic and copies ran while one was open for 18% of the time, Pallas kernels for 22%

profile of v1, /device:TPU:32, one launch (start us, length us, event | category | flops | bytes accessed | tf_op | source)
XLA Modules:
  0.0 117.4 jit_solution(11773021828772950473)
XLA Ops:
  2.7 6.3 %collective-permute-start.4 = (f32[16,128]{1,0:T(8,128)S(1)}, f32[16,128]{1,0:T(8,128)S(1)}, u32[]{:S(2)}, u32[]{:S(2)}) collective-permute-start(f32[16,128]{1,0:T(8,128)S(1)} %bitcast.29), channel_id=1, source_target_pairs={{0,128},{2,130},{4,132},{6,134},{8,136},{10,138},{12,140},{14,142}... | collective-permute-start | bytes 24584 | tf_op jit(solution)/shard_map/ppermute | solution.py:192
  9.0 1.5 %collective-permute-start.5 = (f32[16,128]{1,0:T(8,128)S(1)}, f32[16,128]{1,0:T(8,128)S(1)}, u32[]{:S(2)}, u32[]{:S(2)}) collective-permute-start(f32[16,128]{1,0:T(8,128)S(1)} %bitcast.30), channel_id=1, source_target_pairs={{0,64},{2,66},{4,68},{6,70},{8,72},{10,74},{12,76},{14,78},{16,80}... | collective-permute-start | bytes 24584 | tf_op jit(solution)/shard_map/ppermute | solution.py:192
  12.1 3.0 %collective-permute-start.2 = (f32[32,128]{1,0:T(8,128)}, f32[32,128]{1,0:T(8,128)S(1)}, u32[]{:S(2)}, u32[]{:S(2)}) collective-permute-start(f32[32,128]{1,0:T(8,128)} %select_bitcast_fusion.1), channel_id=1, source_target_pairs={{0,1},{1,0},{2,3},{3,2},{4,5},{5,4},{6,7},{7,6},{8,9},{9,8},{10,11... | collective-permute-start | bytes 49160 | tf_op jit(solution)/shard_map/ppermute | solution.py:170
  17.3 1.5 %collective-permute-start.8 = (f32[64,128]{1,0:T(8,128)S(1)}, f32[64,128]{1,0:T(8,128)S(1)}, u32[]{:S(2)}, u32[]{:S(2)}) collective-permute-start(f32[64,128]{1,0:T(8,128)S(1)} %pad_maximum_fusion), channel_id=1, source_target_pairs={{0,16},{2,18},{4,20},{6,22},{8,24},{10,26},{12,28},{14,30},{16,0},... | collective-permute-start | bytes 98312 | tf_op jit(solution)/shard_map/ppermute | solution.py:192
  24.2 3.2 %collective-permute-start.10 = (f32[256,128]{1,0:T(8,128)S(1)}, f32[256,128]{1,0:T(8,128)S(1)}, u32[]{:S(2)}, u32[]{:S(2)}) collective-permute-start(f32[256,128]{1,0:T(8,128)S(1)} %get-tuple-element.25), channel_id=1, source_target_pairs={{0,8},{2,10},{4,12},{6,14},{8,0},{10,2},{12,4},{14,6},{16,24},{18,... | collective-permute-start | bytes 393224 | tf_op jit(solution)/shard_map/ppermute | solution.py:192
  29.4 1.9 %collective-permute-start = (f32[1,8,128]{2,1,0:T(8,128)}, f32[1,8,128]{2,1,0:T(8,128)}, u32[]{:S(2)}, u32[]{:S(2)}) collective-permute-start(f32[1,8,128]{2,1,0:T(8,128)} %get-tuple-element.22), channel_id=1, source_target_pairs={{0,2},{2,4},{4,6},{6,8},{8,10},{10,12},{12,14},{14,16},{16,18},{18... | collective-permute-start | bytes 12296 | tf_op jit(solution)/shard_map/ppermute | solution.py:167
  31.3 6.7 %collective-permute-start.1 = (f32[1,8,128]{2,1,0:T(8,128)}, f32[1,8,128]{2,1,0:T(8,128)}, u32[]{:S(2)}, u32[]{:S(2)}) collective-permute-start(f32[1,8,128]{2,1,0:T(8,128)} %get-tuple-element.21), channel_id=1, source_target_pairs={{2,0},{4,2},{6,4},{8,6},{10,8},{12,10},{14,12},{16,14},{18,16},{20... | collective-permute-start | bytes 12296 | tf_op jit(solution)/shard_map/ppermute | solution.py:168
  38.0 1.6 %copy.25 = f32[32,8,1]{0,1,2:T(8,128)} copy(f32[32,8,1]{2,1,0:T(8,128)} %bitcast.24) | data formatting | bytes 2048
  40.3 2.9 %collective-permute-start.3 = (f32[32,8]{0,1:T(8,128)}, f32[32,8]{0,1:T(8,128)}, u32[]{:S(2)}, u32[]{:S(2)}) collective-permute-start(f32[32,8]{0,1:T(8,128)} %bitcast.5), channel_id=1, source_target_pairs={{0,254},{2,252},{4,250},{6,248},{8,246},{10,244},{12,242},{14,240}... | collective-permute-start | bytes 3080 | tf_op jit(solution)/shard_map/ppermute | solution.py:171
  43.8 2.0 %collective-permute-done.12 = f32[256,128]{1,0:T(8,128)S(1)} collective-permute-done((f32[256,128]{1,0:T(8,128)S(1)}, f32[256,128]{1,0:T(8,128)S(1)}, u32[]{:S(2)}, u32[]{:S(2)}) %collective-permute-start.12) | collective-permute-done | bytes 131104 | tf_op jit(solution)/shard_map/ppermute | solution.py:192
  47.6 1.4 %fusion.1 = s32[32,8,8]{0,2,1:T(8,128)} fusion(s32[32,8,8]{0,2,1:T(8,128)} %param.9, s32[]{:T(128)S(6)} %axis_index.15), kind=kLoop, calls=%fused_computation.38 | loop fusion | flops 100352 | bytes 16388 | tf_op jit(solution)/shard_map/add | solution.py:214
  50.1 1.8 %slice_multiply_fusion = (f32[1,32,8,128]{3,2,1,0:T(8,128)S(1)}, f32[1,32,8,128]{3,2,1,0:T(8,128)}, f32[1,32,8,128]{3,2,1,0:T(8,128)}) fusion(f32[3,32,8,128]{3,2,1,0:T(8,128)} %param.6), kind=kLoop, calls=%fused_computation.1 | loop fusion | flops 98304 | bytes 786432 | tf_op jit(solution)/shard_map/mul | solution.py:221
  52.6 2.3 %stack.34.rows_ref = f32[256,8,128]{2,1,0:T(8,128)S(1)} concatenate(f32[256,1,128]{2,1,0:T(1,128)} %bitcast.28, f32[256,1,128]{2,1,0:T(1,128)} %bitcast.27, f32[256,1,128]{2,1,0:T(1,128)S(1)} %bitcast.26, f32[256,1,128]{2,1,0:T(1,128)S(1)} %stack.32, f32[256,4,128]{2,1,0:T(4,128)S(1)} %stack.33), dimensions={1} | concatenate | bytes 2097152 | tf_op jit(solution)/shard_map/stack | solution.py:220
  55.0 4.3 %cells.1.cells_ref = bf16[32768,48]{1,0:T(8,128)(2,1)S(1)} custom-call(f32[256,8,128]{2,1,0:T(8,128)S(1)} %stack.34.rows_ref), custom_call_target="tpu_custom_call" | custom-call | tf_op jit(solution)/shard_map/cells/pallas_call | solution.py:225
  59.2 3.3 %copy-done = bf16[32768,48]{1,0:T(8,128)(2,1)} copy-done((bf16[32768,48]{1,0:T(8,128)(2,1)}, bf16[32768,48]{1,0:T(8,128)(2,1)S(1)}, u32[]{:S(2)}) %copy-start) | copy-done | bytes 3145752
  63.6 3.4 %copy-done.1 = bf16[32768,48]{1,0:T(8,128)(2,1)S(1)} copy-done((bf16[32768,48]{1,0:T(8,128)(2,1)S(1)}, bf16[32768,48]{1,0:T(8,128)(2,1)}, u32[]{:S(2)}) %copy-start.1) | copy-done | bytes 3145752
  67.0 21.6 %squares.1 = (f32[32,8,128]{2,1,0:T(8,128)S(1)}, f32[32,8,128]{2,1,0:T(8,128)}) custom-call(s32[2048]{0:T(1024)S(1)} %reshape.63.place_ref, f32[2048,128]{1,0:T(8,128)S(1)} %constant_dynamic-update-slice_fusion.17.panels_ref, bf16[32768,48]{1,0:T(8,128)(2,1)S(1)} %copy-done.1, f32[32,8,128]{2,1,0:T(8,128)S(1)} %multiply_reduce_fusion.norm_ref), custom_call_target="tpu_custom_call" | custom-call | tf_op jit(solution)/shard_map/squares/pallas_call | solution.py:234
  90.1 2.2 %section.2.current_ref = f32[32,8,128]{2,1,0:T(8,128)} custom-call(s32[4]{0:T(128)} %add_convert_fusion.flags_ref, f32[32,8,128]{2,1,0:T(8,128)} %base_ref.3, f32[1,8,128]{2,1,0:T(8,128)} %collective-permute-done.lower_ref, f32[1,8,128]{2,1,0:T(8,128)} %collective-permute-done.1.upper_ref, f32[32,128]{1,0:T(8,128)} %copy-done.4, ...), custom_call_target="tpu_custom_call" | custom-call | tf_op jit(solution)/shard_map/section/pallas_call | solution.py:177
  93.3 1.6 %collective-permute-start.16 = (f32[32,128]{1,0:T(8,128)S(1)}, f32[32,128]{1,0:T(8,128)S(1)}, u32[]{:S(2)}, u32[]{:S(2)}) collective-permute-start(f32[32,128]{1,0:T(8,128)S(1)} %select_bitcast_fusion), channel_id=1, source_target_pairs={{0,1},{1,0},{2,3},{3,2},{4,5},{5,4},{6,7},{7,6},{8,9},{9,8},{10,11... | collective-permute-start | bytes 49160 | tf_op jit(solution)/shard_map/ppermute | solution.py:170
  95.6 2.1 %collective-permute-start.14 = (f32[1,8,128]{2,1,0:T(8,128)S(1)}, f32[1,8,128]{2,1,0:T(8,128)S(1)}, u32[]{:S(2)}, u32[]{:S(2)}) collective-permute-start(f32[1,8,128]{2,1,0:T(8,128)S(1)} %get-tuple-element.12), channel_id=1, source_target_pairs={{0,2},{2,4},{4,6},{6,8},{8,10},{10,12},{12,14},{14,16},{16,18},{18... | collective-permute-start | bytes 12296 | tf_op jit(solution)/shard_map/ppermute | solution.py:167
  97.7 6.4 %collective-permute-start.15 = (f32[1,8,128]{2,1,0:T(8,128)S(1)}, f32[1,8,128]{2,1,0:T(8,128)S(1)}, u32[]{:S(2)}, u32[]{:S(2)}) collective-permute-start(f32[1,8,128]{2,1,0:T(8,128)S(1)} %get-tuple-element.11), channel_id=1, source_target_pairs={{2,0},{4,2},{6,4},{8,6},{10,8},{12,10},{14,12},{16,14},{18,16},{20... | collective-permute-start | bytes 12296 | tf_op jit(solution)/shard_map/ppermute | solution.py:168
  105.2 1.6 %collective-permute-start.17 = (f32[32,8]{0,1:T(8,128)S(1)}, f32[32,8]{0,1:T(8,128)S(1)}, u32[]{:S(2)}, u32[]{:S(2)}) collective-permute-start(f32[32,8]{0,1:T(8,128)S(1)} %bitcast.40), channel_id=1, source_target_pairs={{0,254},{2,252},{4,250},{6,248},{8,246},{10,244},{12,242},{14,240}... | collective-permute-start | bytes 3080 | tf_op jit(solution)/shard_map/ppermute | solution.py:171
  106.8 7.5 %collective-permute-done.17 = f32[32,8]{0,1:T(8,128)S(1)} collective-permute-done((f32[32,8]{0,1:T(8,128)S(1)}, f32[32,8]{0,1:T(8,128)S(1)}, u32[]{:S(2)}, u32[]{:S(2)}) %collective-permute-start.17) | collective-permute-done | bytes 1056 | tf_op jit(solution)/shard_map/ppermute | solution.py:171
  115.2 2.2 %section.3 = f32[32,8,128]{2,1,0:T(8,128)} custom-call(s32[4]{0:T(128)} %add_convert_fusion.flags_ref, f32[32,8,128]{2,1,0:T(8,128)} %section.2.current_ref, f32[1,8,128]{2,1,0:T(8,128)} %copy-done.6, f32[1,8,128]{2,1,0:T(8,128)} %copy-done.7, f32[32,128]{1,0:T(8,128)} %copy-done.5, f32[32,8,128]{2,1,0:T(8,128)} %broadcast_in_dim.5.ghost_ref, ...), custom_call_target="tpu_custom_call" | custom-call | tf_op jit(solution)/shard_map/section/pallas_call | solution.py:177
  (70 shorter events, 24.4 us)
Async XLA Ops:
  2.7 13.0 %collective-permute-start.4 = (f32[16,128]{1,0:T(8,128)S(1)}, f32[16,128]{1,0:T(8,128)S(1)}, u32[]{:S(2)}, u32[]{:S(2)}) collective-permute-start(f32[16,128]{1,0:T(8,128)S(1)} %bitcast.29), channel_id=1, source_target_pairs={{0,128},{2,130},{4,132},{6,134},{8,136},{10,138},{12,140},{14,142}... | collective-permute-start | bytes 24584 | tf_op jit(solution)/shard_map/ppermute | solution.py:192
  9.0 6.7 %collective-permute-start.5 = (f32[16,128]{1,0:T(8,128)S(1)}, f32[16,128]{1,0:T(8,128)S(1)}, u32[]{:S(2)}, u32[]{:S(2)}) collective-permute-start(f32[16,128]{1,0:T(8,128)S(1)} %bitcast.30), channel_id=1, source_target_pairs={{0,64},{2,66},{4,68},{6,70},{8,72},{10,74},{12,76},{14,78},{16,80}... | collective-permute-start | bytes 24584 | tf_op jit(solution)/shard_map/ppermute | solution.py:192
  10.5 5.8 %collective-permute-start.6 = (f32[16,128]{1,0:T(8,128)S(1)}, f32[16,128]{1,0:T(8,128)S(1)}, u32[]{:S(2)}, u32[]{:S(2)}) collective-permute-start(f32[16,128]{1,0:T(8,128)S(1)} %bitcast.31), channel_id=1, source_target_pairs={{0,192},{2,194},{4,196},{6,198},{8,200},{10,202},{12,204},{14,206}... | collective-permute-start | bytes 24584 | tf_op jit(solution)/shard_map/ppermute | solution.py:192
  12.1 77.2 %collective-permute-start.2 = (f32[32,128]{1,0:T(8,128)}, f32[32,128]{1,0:T(8,128)S(1)}, u32[]{:S(2)}, u32[]{:S(2)}) collective-permute-start(f32[32,128]{1,0:T(8,128)} %select_bitcast_fusion.1), channel_id=1, source_target_pairs={{0,1},{1,0},{2,3},{3,2},{4,5},{5,4},{6,7},{7,6},{8,9},{9,8},{10,11... | collective-permute-start | bytes 49160 | tf_op jit(solution)/shard_map/ppermute | solution.py:170
  16.3 5.3 %collective-permute-start.7 = (f32[64,128]{1,0:T(8,128)S(1)}, f32[64,128]{1,0:T(8,128)S(1)}, u32[]{:S(2)}, u32[]{:S(2)}) collective-permute-start(f32[64,128]{1,0:T(8,128)S(1)} %pad_maximum_fusion), channel_id=1, source_target_pairs={{0,32},{2,34},{4,36},{6,38},{8,40},{10,42},{12,44},{14,46},{16,48}... | collective-permute-start | bytes 98312 | tf_op jit(solution)/shard_map/ppermute | solution.py:192
  17.3 4.9 %collective-permute-start.8 = (f32[64,128]{1,0:T(8,128)S(1)}, f32[64,128]{1,0:T(8,128)S(1)}, u32[]{:S(2)}, u32[]{:S(2)}) collective-permute-start(f32[64,128]{1,0:T(8,128)S(1)} %pad_maximum_fusion), channel_id=1, source_target_pairs={{0,16},{2,18},{4,20},{6,22},{8,24},{10,26},{12,28},{14,30},{16,0},... | collective-permute-start | bytes 98312 | tf_op jit(solution)/shard_map/ppermute | solution.py:192
  18.8 4.8 %collective-permute-start.9 = (f32[64,128]{1,0:T(8,128)S(1)}, f32[64,128]{1,0:T(8,128)S(1)}, u32[]{:S(2)}, u32[]{:S(2)}) collective-permute-start(f32[64,128]{1,0:T(8,128)S(1)} %pad_maximum_fusion), channel_id=1, source_target_pairs={{0,48},{2,50},{4,52},{6,54},{8,56},{10,58},{12,60},{14,62},{16,32}... | collective-permute-start | bytes 98312 | tf_op jit(solution)/shard_map/ppermute | solution.py:192
  24.2 15.4 %collective-permute-start.10 = (f32[256,128]{1,0:T(8,128)S(1)}, f32[256,128]{1,0:T(8,128)S(1)}, u32[]{:S(2)}, u32[]{:S(2)}) collective-permute-start(f32[256,128]{1,0:T(8,128)S(1)} %get-tuple-element.25), channel_id=1, source_target_pairs={{0,8},{2,10},{4,12},{6,14},{8,0},{10,2},{12,4},{14,6},{16,24},{18,... | collective-permute-start | bytes 393224 | tf_op jit(solution)/shard_map/ppermute | solution.py:192
  27.4 12.9 %collective-permute-start.11 = (f32[256,128]{1,0:T(8,128)S(1)}, f32[256,128]{1,0:T(8,128)S(1)}, u32[]{:S(2)}, u32[]{:S(2)}) collective-permute-start(f32[256,128]{1,0:T(8,128)S(1)} %get-tuple-element.25), channel_id=1, source_target_pairs={{0,4},{2,6},{4,0},{6,2},{8,12},{10,14},{12,8},{14,10},{16,20},{18,... | collective-permute-start | bytes 393224 | tf_op jit(solution)/shard_map/ppermute | solution.py:192
  29.4 59.9 %collective-permute-start = (f32[1,8,128]{2,1,0:T(8,128)}, f32[1,8,128]{2,1,0:T(8,128)}, u32[]{:S(2)}, u32[]{:S(2)}) collective-permute-start(f32[1,8,128]{2,1,0:T(8,128)} %get-tuple-element.22), channel_id=1, source_target_pairs={{0,2},{2,4},{4,6},{6,8},{8,10},{10,12},{12,14},{14,16},{16,18},{18... | collective-permute-start | bytes 12296 | tf_op jit(solution)/shard_map/ppermute | solution.py:167
  31.3 58.0 %collective-permute-start.1 = (f32[1,8,128]{2,1,0:T(8,128)}, f32[1,8,128]{2,1,0:T(8,128)}, u32[]{:S(2)}, u32[]{:S(2)}) collective-permute-start(f32[1,8,128]{2,1,0:T(8,128)} %get-tuple-element.21), channel_id=1, source_target_pairs={{2,0},{4,2},{6,4},{8,6},{10,8},{12,10},{14,12},{16,14},{18,16},{20... | collective-permute-start | bytes 12296 | tf_op jit(solution)/shard_map/ppermute | solution.py:168
  39.6 6.2 %collective-permute-start.12 = (f32[256,128]{1,0:T(8,128)S(1)}, f32[256,128]{1,0:T(8,128)S(1)}, u32[]{:S(2)}, u32[]{:S(2)}) collective-permute-start(f32[256,128]{1,0:T(8,128)S(1)} %get-tuple-element.25), channel_id=1, source_target_pairs={{0,12},{2,14},{4,8},{6,10},{8,4},{10,6},{12,0},{14,2},{16,28},{18,... | collective-permute-start | bytes 393224 | tf_op jit(solution)/shard_map/ppermute | solution.py:192
  40.3 22.5 %collective-permute-start.3 = (f32[32,8]{0,1:T(8,128)}, f32[32,8]{0,1:T(8,128)}, u32[]{:S(2)}, u32[]{:S(2)}) collective-permute-start(f32[32,8]{0,1:T(8,128)} %bitcast.5), channel_id=1, source_target_pairs={{0,254},{2,252},{4,250},{6,248},{8,246},{10,244},{12,242},{14,240}... | collective-permute-start | bytes 3080 | tf_op jit(solution)/shard_map/ppermute | solution.py:171
  46.4 17.2 %collective-permute-start.13 = (f32[1024,128]{1,0:T(8,128)}, f32[1024,128]{1,0:T(8,128)S(1)}, u32[]{:S(2)}, u32[]{:S(2)}) collective-permute-start(f32[1024,128]{1,0:T(8,128)} %get-tuple-element.13), channel_id=1, source_target_pairs={{0,2},{2,0},{4,6},{6,4},{8,10},{10,8},{12,14},{14,12},{16,18},{18,... | collective-permute-start | bytes 1572872 | tf_op jit(solution)/shard_map/ppermute | solution.py:192
  55.0 7.6 %copy-start.3 = (s32[32,8,8]{0,2,1:T(8,128)S(1)}, s32[32,8,8]{0,2,1:T(8,128)}, u32[]{:S(2)}) copy-start(s32[32,8,8]{0,2,1:T(8,128)} %fusion.1) | copy-start | bytes 24580
  59.2 3.3 %copy-start = (bf16[32768,48]{1,0:T(8,128)(2,1)}, bf16[32768,48]{1,0:T(8,128)(2,1)S(1)}, u32[]{:S(2)}) copy-start(bf16[32768,48]{1,0:T(8,128)(2,1)S(1)} %cells.1.cells_ref) | copy-start | bytes 9437188
  63.6 3.4 %copy-start.1 = (bf16[32768,48]{1,0:T(8,128)(2,1)S(1)}, bf16[32768,48]{1,0:T(8,128)(2,1)}, u32[]{:S(2)}) copy-start(bf16[32768,48]{1,0:T(8,128)(2,1)} %copy-done) | copy-start | bytes 9437188
  89.3 0.8 copy-start.4
  93.3 21.2 %collective-permute-start.16 = (f32[32,128]{1,0:T(8,128)S(1)}, f32[32,128]{1,0:T(8,128)S(1)}, u32[]{:S(2)}, u32[]{:S(2)}) collective-permute-start(f32[32,128]{1,0:T(8,128)S(1)} %select_bitcast_fusion), channel_id=1, source_target_pairs={{0,1},{1,0},{2,3},{3,2},{4,5},{5,4},{6,7},{7,6},{8,9},{9,8},{10,11... | collective-permute-start | bytes 49160 | tf_op jit(solution)/shard_map/ppermute | solution.py:170
  95.6 18.9 %collective-permute-start.14 = (f32[1,8,128]{2,1,0:T(8,128)S(1)}, f32[1,8,128]{2,1,0:T(8,128)S(1)}, u32[]{:S(2)}, u32[]{:S(2)}) collective-permute-start(f32[1,8,128]{2,1,0:T(8,128)S(1)} %get-tuple-element.12), channel_id=1, source_target_pairs={{0,2},{2,4},{4,6},{6,8},{8,10},{10,12},{12,14},{14,16},{16,18},{18... | collective-permute-start | bytes 12296 | tf_op jit(solution)/shard_map/ppermute | solution.py:167
  97.7 16.8 %collective-permute-start.15 = (f32[1,8,128]{2,1,0:T(8,128)S(1)}, f32[1,8,128]{2,1,0:T(8,128)S(1)}, u32[]{:S(2)}, u32[]{:S(2)}) collective-permute-start(f32[1,8,128]{2,1,0:T(8,128)S(1)} %get-tuple-element.11), channel_id=1, source_target_pairs={{2,0},{4,2},{6,4},{8,6},{10,8},{12,10},{14,12},{16,14},{18,16},{20... | collective-permute-start | bytes 12296 | tf_op jit(solution)/shard_map/ppermute | solution.py:168
  105.2 9.1 %collective-permute-start.17 = (f32[32,8]{0,1:T(8,128)S(1)}, f32[32,8]{0,1:T(8,128)S(1)}, u32[]{:S(2)}, u32[]{:S(2)}) collective-permute-start(f32[32,8]{0,1:T(8,128)S(1)} %bitcast.40), channel_id=1, source_target_pairs={{0,254},{2,252},{4,250},{6,248},{8,246},{10,244},{12,242},{14,240}... | collective-permute-start | bytes 3080 | tf_op jit(solution)/shard_map/ppermute | solution.py:171
  114.4 0.8 copy-start.6
  114.5 0.8 copy-start.7
  (2 other events, 1.4 us)

commit v2 on v1

v2 whole, which is shorter than its diff:
```python
import functools

import jax
import jax.numpy as jnp
from jax import lax
from jax.experimental import pallas as pl
from jax.experimental.pallas import tpu as pltpu
from jax.sharding import PartitionSpec as P

BF = jnp.bfloat16
F32 = jnp.float32
PBS = 128
FEATS = 48
LINES_PER_STEP = 32
STAGES = ((6, 5), (4, 3), (2, 1), (0,))

coef_cb1 = 0.1355
coef_cb2 = 0.622
coef_sigma = 2.0 / 3.0
coef_kappa = 0.41
coef_cw2 = 0.3
coef_cw3 = 2.0
viscous = 1.0
time_step = 0.03
coef_cw1 = coef_cb1 / coef_kappa**2 + (1.0 + coef_cb2) / coef_sigma

SMEM = pl.BlockSpec(memory_space=pltpu.SMEM)
VMEM = pl.BlockSpec(memory_space=pltpu.VMEM)


def tile_iota(dim):
    return lax.broadcasted_iota(jnp.int32, (8, 128), dim)


def split_rows(rows):
    high = rows.astype(BF).astype(F32)
    rest = rows - high
    mid = rest.astype(BF).astype(F32)
    return high, mid, rest - mid


def panel_features(rows):
    high, mid, low = split_rows(rows)
    return jnp.concatenate([high, high, high, mid, mid, low], 0).astype(BF)


def cell_features(rows):
    high, mid, low = split_rows(rows)
    return jnp.concatenate([high, mid, low, high, mid, high], 0).astype(BF)


def edge_row(value, low_span):
    return jnp.where(low_span, value[7:8], value[0:1])


def first_column(value):
    return jnp.broadcast_to(value[:, 0:1], (8, 128))


def prep_kernel(xyz_ref, size_ref, nu_ref, message_ref, last_ref, first_ref, beside_ref, column_ref):
    low_span = lax.axis_index("span") == 0
    own_blocks = size_ref.shape[1] // PBS
    for block in range(own_blocks):
        lanes = slice(block * PBS, (block + 1) * PBS)
        xyz = xyz_ref[:, lanes]
        size = size_ref[:, lanes]
        offset = jnp.sum(xyz * xyz, axis=0, keepdims=True) + size * size
        message_ref[block * 4 : block * 4 + 3, :] = xyz
        message_ref[block * 4 + 3 : block * 4 + 4, :] = offset
    rows = nu_ref.shape[0]
    last_ref[...] = nu_ref[rows - 1]
    first_ref[...] = nu_ref[0]
    lane = tile_iota(1)
    column = jnp.zeros((8, 128), F32)
    for row in range(rows):
        value = nu_ref[row]
        beside_ref[row : row + 1, :] = edge_row(value, low_span)
        column = jnp.where(lane == row, first_column(value), column)
    column_ref[...] = column


class Halo:
    def __init__(self, nu_ref, last_ref, first_ref, beside_ref, column_ref, padded_ref, ghost_ref):
        devices = lax.axis_size("wrap")
        place = lax.axis_index("wrap")
        rows = nu_ref.shape[0]
        self.rows = rows
        self.low_span = lax.axis_index("span") == 0
        self.padded, self.ghost, self.beside = padded_ref, ghost_ref, beside_ref
        padded_ref[0] = jnp.where(place == 0, nu_ref[0], last_ref[...])
        padded_ref[rows + 1] = jnp.where(place == devices - 1, nu_ref[rows - 1], first_ref[...])
        in_wake = (place < devices // 4) | (place >= devices - devices // 4)
        column = column_ref[...]
        for row in range(rows):
            value = nu_ref[row]
            padded_ref[row + 1] = value
            partner = jnp.broadcast_to(column[:, rows - 1 - row : rows - row], (8, 128))
            ghost_ref[row] = jnp.where(in_wake, partner, -value)

    def rate(self, row, squares, vorticity):
        value = self.padded[row + 1]
        sub, lane = tile_iota(0), tile_iota(1)
        across = jnp.broadcast_to(self.beside[pl.ds(row, 1), :], (8, 128))
        span_low = jnp.where(self.low_span, value, across)
        span_high = jnp.where(self.low_span, across, value)
        others = (
            self.padded[row],
            self.padded[row + 2],
            jnp.where(sub == 0, span_low, pltpu.roll(value, 1, 0)),
            jnp.where(sub == 7, span_high, pltpu.roll(value, 7, 0)),
            jnp.where(lane == 0, self.ghost[row], pltpu.roll(value, 1, 1)),
            jnp.where(lane == 127, value, pltpu.roll(value, 127, 1)),
        )
        sums = jnp.zeros_like(value)
        squared = jnp.zeros_like(value)
        for other in others:
            change = other - value
            sums = sums + change
            squared = squared + change * change
        flux = (viscous + value) * sums + (0.5 * (1.0 + coef_cb2)) * squared
        scaled = coef_kappa**2 * squares
        modified = vorticity + value / scaled
        ratio = value / (modified * scaled)
        ratio2 = ratio * ratio
        shaped = ratio + coef_cw2 * (ratio2 * ratio2 * ratio2 - ratio)
        shaped2 = shaped * shaped
        base = (1.0 + coef_cw3**6) / (shaped2 * shaped2 * shaped2 + coef_cw3**6)
        factor = shaped * jnp.exp(jnp.log(base) * (1.0 / 6.0))
        return (
            flux / coef_sigma
            + coef_cb1 * modified * value
            - coef_cw1 * factor * value * value / squares
        )


def build_table(halves, table_ref):
    place = lax.axis_index("wrap")
    order = [bit for bits in STAGES for bit in bits]
    own_blocks = table_ref.shape[0] // lax.axis_size("wrap")
    slots = halves[0].shape[0] // (4 * own_blocks)
    top = len(order) - 1

    def body(slot, carry):
        for half, ref in enumerate(halves):
            mask = half << order[top]
            for n in range(top):
                mask = mask | (((slot >> n) & 1) << order[n])
            base = (place ^ mask) * own_blocks
            for pair in range(own_blocks // 2):
                start = pl.multiple_of(slot * own_blocks * 4 + pair * 8, 8)
                rows = ref[pl.ds(start, 8), :]
                table_ref[base + pair * 2] = panel_features(rows)
                table_ref[base + pair * 2 + 1] = panel_features(pltpu.roll(rows, 4, 0))
        return carry

    lax.fori_loop(0, slots, body, 0)


def nearest_tile(tile, list_ref, cell_ref, table_ref):
    sub = tile_iota(0)
    unit = jnp.where(sub == 3, 1.0, 0.0)
    xyz = [cell_ref[component, tile] for component in range(3)]
    twice = [-2.0 * part for part in xyz]
    found = []
    for line in range(8):
        rows = unit
        for component in range(3):
            spread = jnp.broadcast_to(twice[component][line : line + 1], (8, 128))
            rows = jnp.where(sub == component, spread, rows)
        cells = cell_features(rows).T
        nearest = None
        for slot in range(0, 8, 2):
            first = list_ref[(tile * 8 + line) * 8 + slot]
            second = list_ref[(tile * 8 + line) * 8 + slot + 1]
            panels = jnp.concatenate([table_ref[first], table_ref[second]], 1)
            value = jnp.dot(cells, panels, preferred_element_type=F32)
            value = jnp.minimum(value[:, :128], value[:, 128:])
            nearest = value if nearest is None else jnp.minimum(nearest, value)
        turned = jnp.min(nearest.T.reshape(16, 8, 128), axis=0)
        found.append(jnp.min(turned, axis=0, keepdims=True))
    norm = xyz[0] * xyz[0] + xyz[1] * xyz[1] + xyz[2] * xyz[2]
    return jnp.concatenate(found, 0) + norm


def main_kernel(
    list_ref,
    own_ref,
    other_ref,
    cell_ref,
    nu_ref,
    vorticity_ref,
    last_ref,
    first_ref,
    beside_ref,
    column_ref,
    dist_ref,
    squares_ref,
    middle_ref,
    last_out,
    first_out,
    beside_out,
    column_out,
    table_ref,
    padded_ref,
    ghost_ref,
):
    halo = Halo(nu_ref, last_ref, first_ref, beside_ref, column_ref, padded_ref, ghost_ref)
    build_table((own_ref, other_ref), table_ref)
    tiles = nu_ref.shape[0]
    per_step = LINES_PER_STEP // 8

    def body(step, column):
        lane = tile_iota(1)
        for part in range(per_step):
            tile = step * per_step + part
            squares = nearest_tile(tile, list_ref, cell_ref, table_ref)
            squares_ref[tile] = squares
            dist_ref[tile] = jnp.sqrt(squares)
            rate = halo.rate(tile, squares, vorticity_ref[tile])
            middle = nu_ref[tile] + 0.5 * time_step * rate
            middle_ref[tile] = middle
            beside_out[pl.ds(tile, 1), :] = edge_row(middle, halo.low_span)
            column = jnp.where(lane == tile, first_column(middle), column)
        return column

    column_out[...] = lax.fori_loop(0, tiles // per_step, body, jnp.zeros((8, 128), F32))
    last_out[...] = middle_ref[tiles - 1]
    first_out[...] = middle_ref[0]


def last_kernel(
    middle_ref,
    nu_ref,
    squares_ref,
    vorticity_ref,
    last_ref,
    first_ref,
    beside_ref,
    column_ref,
    next_ref,
    padded_ref,
    ghost_ref,
):
    halo = Halo(middle_ref, last_ref, first_ref, beside_ref, column_ref, padded_ref, ghost_ref)
    for row in range(nu_ref.shape[0]):
        rate = halo.rate(row, squares_ref[row], vorticity_ref[row])
        next_ref[row] = nu_ref[row] + time_step * rate


def exchange(last, first, beside, column):
    devices = lax.axis_size("wrap")
    column = lax.ppermute(column, "wrap", [(i, devices - 1 - i) for i in range(devices)])
    last = lax.ppermute(last, "wrap", [(i, i + 1) for i in range(devices - 1)])
    first = lax.ppermute(first, "wrap", [(i + 1, i) for i in range(devices - 1)])
    beside = lax.ppermute(beside, "span", [(0, 1), (1, 0)])
    return last, first, beside, column


def gather(shard):
    devices = lax.axis_size("wrap")
    for bits in STAGES[:-1]:
        parts = [shard]
        for choice in range(1, 1 << len(bits)):
            mask = sum(((choice >> n) & 1) << bit for n, bit in enumerate(bits))
            parts.append(lax.ppermute(shard, "wrap", [(i, i ^ mask) for i in range(devices)]))
        shard = jnp.concatenate(parts, 0)
    mask = 1 << STAGES[-1][0]
    return shard, lax.ppermute(shard, "wrap", [(i, i ^ mask) for i in range(devices)])


def shards(cell_xyz, panel_xyz, panel_size, block_lists, nu_field, vorticity):
    devices = lax.axis_size("wrap")
    rows, span, cells = nu_field.shape
    own_blocks = panel_size.shape[0] // PBS
    tile = jax.ShapeDtypeStruct((span, cells), F32)
    field = jax.ShapeDtypeStruct(nu_field.shape, F32)
    side = jax.ShapeDtypeStruct((rows, cells), F32)
    edges = (tile, tile, side, tile)
    scratch = [pltpu.VMEM((rows + 2, span, cells), F32), pltpu.VMEM(nu_field.shape, F32)]

    message, *sent = pl.pallas_call(
        prep_kernel,
        out_shape=(jax.ShapeDtypeStruct((4 * own_blocks, PBS), F32),) + edges,
        in_specs=[VMEM] * 3,
        out_specs=(VMEM,) * 5,
        compiler_params=pltpu.CompilerParams(vmem_limit_bytes=4 * 2**20),
        name="prep",
    )(panel_xyz, panel_size[None], nu_field)
    own, other = gather(message)
    halos = exchange(*sent)

    dist, squares, middle, *sent = pl.pallas_call(
        main_kernel,
        out_shape=(field, field, field) + edges,
        in_specs=[SMEM] + [VMEM] * 9,
        out_specs=(VMEM,) * 7,
        scratch_shapes=[pltpu.VMEM((devices * own_blocks, FEATS, PBS), BF)] + scratch,
        compiler_params=pltpu.CompilerParams(vmem_limit_bytes=24 * 2**20),
        cost_estimate=pl.CostEstimate(
            flops=2 * 128 * rows * span * cells * block_lists.shape[2] * PBS,
            bytes_accessed=4 * 2**20,
            transcendentals=0,
        ),
        name="main",
    )(block_lists.reshape(-1), own, other, cell_xyz, nu_field, vorticity, *halos)
    halos = exchange(*sent)

    nu_next = pl.pallas_call(
        last_kernel,
        out_shape=field,
        in_specs=[VMEM] * 8,
        out_specs=VMEM,
        scratch_shapes=scratch,
        compiler_params=pltpu.CompilerParams(vmem_limit_bytes=8 * 2**20),
        name="last",
    )(middle, nu_field, squares, vorticity, *halos)
    return (nu_next, dist)


def solution(mesh):
    in_specs = (
        P(None, "wrap", "span", None),
        P(None, "wrap"),
        P("wrap"),
        P("wrap", "span", None),
        P("wrap", "span", None),
        P("wrap", "span", None),
    )
    out_specs = (P("wrap", "span", None), P("wrap", "span", None))
    return jax.shard_map(shards, mesh=mesh, in_specs=in_specs, out_specs=out_specs, check_vma=False)
```

time: 118 us -> 99 us (0.84)
  local copies, waits for them, and re-layouts: 25.4 us -> 2.58 us
  waiting for transfers between devices: 10.8 us -> 33.5 us
  other arithmetic: 7.57 us -> 0 us
  starting transfers between devices: 42.6 us -> 36.9 us
  Pallas kernels: 30.3 us -> 24.9 us
    ppermute x10, waiting for transfers between devices: 3.28 us -> 15.7 us  [gather(): lax.ppermute(shard, 'wrap', [(i, i ^ mask) for i in range(devices)])]
    unnamed x26 -> x23, local copies, waits for them, and re-layouts: 14.5 us -> 2.45 us
    ppermute x8, waiting for transfers between devices: 7.51 us -> 17.8 us  [the longest x2 15.7 us: exchange(): lax.ppermute(column, 'wrap', [(i, devices - 1 - i) for i in range(devices)])]
    pallas_call x4 -> x3, Pallas kernels: 30.3 us -> 24.9 us  [the longest x1 23.8 us: shards(): pl.pallas_call(main_kernel, out_shape=(field, field, field) + edges, in_s...]
    ppermute x8, starting transfers between devices: 26.2 us -> 20.9 us  [the longest x2 13.2 us: exchange(): lax.ppermute(first, 'wrap', [(i + 1, i) for i in range(devices - 1)])]
    slice x5 -> x0, local copies, waits for them, and re-layouts: 5.02 us -> none  [the longest x2 2.01 us: section(): sent = jnp.where(low_span, current[:, -1], current[:, 0])]
    another operation x3 -> x0, local copies, waits for them, and re-layouts: 2.45 us -> none  [shards(): jnp.stack([-2.0 * flat[0], -2.0 * flat[1], -2.0 * flat[2], filler + 1.0]...]
    add x2 -> x0, other arithmetic: 2.12 us -> none  [the longest x1 1.44 us: shards(): slot_of(block_lists // own_blocks) * own_blocks + block_lists % own_blocks]
  transfers between devices with their start and end apart: 18 -> 18, of which waited for: 4 -> 10; matrix products, arithmetic and copies ran while one was open for 18% -> 0% of each run, Pallas kernels for 22% -> 0%
where the time goes in v2:
time: 99 us; the launch traced here: 98.7 us
  starting transfers between devices  36.9 us (37%)
  waiting for transfers between devices  33.5 us (34%)
  Pallas kernels  24.9 us (25%)
  local copies, waits for them, and re-layouts  2.58 us (3%)
    pallas_call x1, Pallas kernels, shards(): pl.pallas_call(main_kernel, out_shape=(field, field, field) + edges, in_s...  23.8 us
    ppermute x10, starting transfers between devices, gather(): lax.ppermute(shard, 'wrap', [(i, i ^ mask) for i in range(devices)])  16 us
    ppermute x2, waiting for transfers between devices, exchange(): lax.ppermute(column, 'wrap', [(i, devices - 1 - i) for i in range(devices)])  15.7 us
    ppermute x10, waiting for transfers between devices, gather(): lax.ppermute(shard, 'wrap', [(i, i ^ mask) for i in range(devices)])  15.7 us
    ppermute x2, starting transfers between devices, exchange(): lax.ppermute(first, 'wrap', [(i + 1, i) for i in range(devices - 1)])  13.2 us
    ppermute x2, starting transfers between devices, exchange(): last = lax.ppermute(last, 'wrap', [(i, i + 1) for i in range(devices - 1)])  3.95 us
    ppermute x2, starting transfers between devices, exchange(): beside = lax.ppermute(beside, 'span', [(0, 1), (1, 0)])  3.61 us
    unnamed x23, local copies, waits for them, and re-layouts  2.45 us
  transfers between devices with their start and end apart: 18, of which 10 were waited for; matrix products, arithmetic and copies ran while one was open for 0% of the time, Pallas kernels for 0%

profile of v2, /device:TPU:32, one launch (start us, length us, event | category | flops | bytes accessed | tf_op | source)
XLA Modules:
  0.0 98.7 jit_solution(6702430368300817094)
XLA Ops:
  0.6 0.9 copy-done
  3.0 5.5 %collective-permute-start.2 = (f32[16,128]{1,0:T(8,128)S(1)}, f32[16,128]{1,0:T(8,128)S(1)}, u32[]{:S(2)}, u32[]{:S(2)}) collective-permute-start(f32[16,128]{1,0:T(8,128)S(1)} %get-tuple-element.14), channel_id=1, source_target_pairs={{0,192},{2,194},{4,196},{6,198},{8,200},{10,202},{12,204},{14,206}... | collective-permute-start | bytes 24584 | tf_op jit(solution)/shard_map/ppermute | solution.py:265
  8.5 1.5 %collective-permute-start.1 = (f32[16,128]{1,0:T(8,128)S(1)}, f32[16,128]{1,0:T(8,128)S(1)}, u32[]{:S(2)}, u32[]{:S(2)}) collective-permute-start(f32[16,128]{1,0:T(8,128)S(1)} %get-tuple-element.14), channel_id=1, source_target_pairs={{0,64},{2,66},{4,68},{6,70},{8,72},{10,74},{12,76},{14,78},{16,80}... | collective-permute-start | bytes 24584 | tf_op jit(solution)/shard_map/ppermute | solution.py:265
  10.0 1.0 %collective-permute-start = (f32[16,128]{1,0:T(8,128)S(1)}, f32[16,128]{1,0:T(8,128)S(1)}, u32[]{:S(2)}, u32[]{:S(2)}) collective-permute-start(f32[16,128]{1,0:T(8,128)S(1)} %get-tuple-element.14), channel_id=1, source_target_pairs={{0,128},{2,130},{4,132},{6,134},{8,136},{10,138},{12,140},{14,142}... | collective-permute-start | bytes 24584 | tf_op jit(solution)/shard_map/ppermute | solution.py:265
  11.0 6.5 %collective-permute-done = f32[16,128]{1,0:T(8,128)S(1)} collective-permute-done((f32[16,128]{1,0:T(8,128)S(1)}, f32[16,128]{1,0:T(8,128)S(1)}, u32[]{:S(2)}, u32[]{:S(2)}) %collective-permute-start) | collective-permute-done | bytes 8224 | tf_op jit(solution)/shard_map/ppermute | solution.py:265
  17.6 1.1 %collective-permute-start.3 = (f32[64,128]{1,0:T(8,128)S(1)}, f32[64,128]{1,0:T(8,128)S(1)}, u32[]{:S(2)}, u32[]{:S(2)}) collective-permute-start(f32[64,128]{1,0:T(8,128)S(1)} %get-tuple-element.34), channel_id=1, source_target_pairs={{0,32},{2,34},{4,36},{6,38},{8,40},{10,42},{12,44},{14,46},{16,48}... | collective-permute-start | bytes 98312 | tf_op jit(solution)/shard_map/ppermute | solution.py:265
  18.7 1.9 %collective-permute-start.5 = (f32[64,128]{1,0:T(8,128)S(1)}, f32[64,128]{1,0:T(8,128)S(1)}, u32[]{:S(2)}, u32[]{:S(2)}) collective-permute-start(f32[64,128]{1,0:T(8,128)S(1)} %get-tuple-element.34), channel_id=1, source_target_pairs={{0,48},{2,50},{4,52},{6,54},{8,56},{10,58},{12,60},{14,62},{16,32}... | collective-permute-start | bytes 98312 | tf_op jit(solution)/shard_map/ppermute | solution.py:265
  21.6 2.9 %collective-permute-done.4 = f32[64,128]{1,0:T(8,128)S(1)} collective-permute-done((f32[64,128]{1,0:T(8,128)S(1)}, f32[64,128]{1,0:T(8,128)S(1)}, u32[]{:S(2)}, u32[]{:S(2)}) %collective-permute-start.4) | collective-permute-done | bytes 32800 | tf_op jit(solution)/shard_map/ppermute | solution.py:265
  24.5 3.3 %collective-permute-start.6 = (f32[256,128]{1,0:T(8,128)S(1)}, f32[256,128]{1,0:T(8,128)S(1)}, u32[]{:S(2)}, u32[]{:S(2)}) collective-permute-start(f32[256,128]{1,0:T(8,128)S(1)} %get-tuple-element.26), channel_id=1, source_target_pairs={{0,8},{2,10},{4,12},{6,14},{8,0},{10,2},{12,4},{14,6},{16,24},{18,... | collective-permute-start | bytes 393224 | tf_op jit(solution)/shard_map/ppermute | solution.py:265
  28.9 2.2 %collective-permute-done.6 = f32[256,128]{1,0:T(8,128)S(1)} collective-permute-done((f32[256,128]{1,0:T(8,128)S(1)}, f32[256,128]{1,0:T(8,128)S(1)}, u32[]{:S(2)}, u32[]{:S(2)}) %collective-permute-start.6) | collective-permute-done | bytes 131104 | tf_op jit(solution)/shard_map/ppermute | solution.py:265
  31.1 1.7 %collective-permute-done.7 = f32[256,128]{1,0:T(8,128)S(1)} collective-permute-done((f32[256,128]{1,0:T(8,128)S(1)}, f32[256,128]{1,0:T(8,128)S(1)}, u32[]{:S(2)}, u32[]{:S(2)}) %collective-permute-start.7) | collective-permute-done | bytes 131104 | tf_op jit(solution)/shard_map/ppermute | solution.py:265
  32.9 1.8 %collective-permute-done.8 = f32[256,128]{1,0:T(8,128)S(1)} collective-permute-done((f32[256,128]{1,0:T(8,128)S(1)}, f32[256,128]{1,0:T(8,128)S(1)}, u32[]{:S(2)}, u32[]{:S(2)}) %collective-permute-start.8) | collective-permute-done | bytes 131104 | tf_op jit(solution)/shard_map/ppermute | solution.py:265
  34.8 2.8 %collective-permute-start.12 = (f32[32,128]{1,0:T(8,128)S(1)}, f32[32,128]{1,0:T(8,128)S(1)}, u32[]{:S(2)}, u32[]{:S(2)}) collective-permute-start(f32[32,128]{1,0:T(8,128)S(1)} %get-tuple-element.17), channel_id=1, source_target_pairs={{0,1},{1,0},{2,3},{3,2},{4,5},{5,4},{6,7},{7,6},{8,9},{9,8},{10,11... | collective-permute-start | bytes 49160 | tf_op jit(solution)/shard_map/ppermute | solution.py:255
  37.6 2.0 %collective-permute-start.10 = (f32[8,128]{1,0:T(8,128)S(1)}, f32[8,128]{1,0:T(8,128)S(1)}, u32[]{:S(2)}, u32[]{:S(2)}) collective-permute-start(f32[8,128]{1,0:T(8,128)S(1)} %get-tuple-element.15), channel_id=1, source_target_pairs={{0,2},{2,4},{4,6},{6,8},{8,10},{10,12},{12,14},{14,16},{16,18},{18... | collective-permute-start | bytes 12296 | tf_op jit(solution)/shard_map/ppermute | solution.py:253
  39.7 6.5 %collective-permute-start.11 = (f32[8,128]{1,0:T(8,128)S(1)}, f32[8,128]{1,0:T(8,128)S(1)}, u32[]{:S(2)}, u32[]{:S(2)}) collective-permute-start(f32[8,128]{1,0:T(8,128)S(1)} %get-tuple-element.16), channel_id=1, source_target_pairs={{2,0},{4,2},{6,4},{8,6},{10,8},{12,10},{14,12},{16,14},{18,16},{20... | collective-permute-start | bytes 12296 | tf_op jit(solution)/shard_map/ppermute | solution.py:254
  46.6 0.9 collective-permute-done.11.first_ref
  47.5 7.9 %collective-permute-done.13.column_ref = f32[8,128]{1,0:T(8,128)S(1)} collective-permute-done((f32[8,128]{1,0:T(8,128)S(1)}, f32[8,128]{1,0:T(8,128)S(1)}, u32[]{:S(2)}, u32[]{:S(2)}) %collective-permute-start.13) | collective-permute-done | bytes 4128 | tf_op jit(solution)/shard_map/ppermute | solution.py:252
  55.4 23.8 %main.1 = (f32[32,8,128]{2,1,0:T(8,128)}, f32[32,8,128]{2,1,0:T(8,128)S(1)}, f32[32,8,128]{2,1,0:T(8,128)S(1)}, f32[8,128]{1,0:T(8,128)S(1)}, f32[8,128]{1,0:T(8...) custom-call(s32[2048]{0:T(1024)S(1)} %reshape.7.list_ref, ...), custom_call_target="tpu_custom_call" | custom-call | flops 8589934592 | bytes 4194304 | tf_op jit(solution)/shard_map/main/pallas_call | solution.py:292
  79.1 0.8 collective-permute-start.16
  79.9 1.9 %collective-permute-start.14 = (f32[8,128]{1,0:T(8,128)S(1)}, f32[8,128]{1,0:T(8,128)S(1)}, u32[]{:S(2)}, u32[]{:S(2)}) collective-permute-start(f32[8,128]{1,0:T(8,128)S(1)} %get-tuple-element.21), channel_id=1, source_target_pairs={{0,2},{2,4},{4,6},{6,8},{8,10},{10,12},{12,14},{14,16},{16,18},{18... | collective-permute-start | bytes 12296 | tf_op jit(solution)/shard_map/ppermute | solution.py:253
  81.9 6.7 %collective-permute-start.15 = (f32[8,128]{1,0:T(8,128)S(1)}, f32[8,128]{1,0:T(8,128)S(1)}, u32[]{:S(2)}, u32[]{:S(2)}) collective-permute-start(f32[8,128]{1,0:T(8,128)S(1)} %get-tuple-element.22), channel_id=1, source_target_pairs={{2,0},{4,2},{6,4},{8,6},{10,8},{12,10},{14,12},{16,14},{18,16},{20... | collective-permute-start | bytes 12296 | tf_op jit(solution)/shard_map/ppermute | solution.py:254
  88.6 1.2 %collective-permute-done.15.first_ref = f32[8,128]{1,0:T(8,128)S(1)} collective-permute-done((f32[8,128]{1,0:T(8,128)S(1)}, f32[8,128]{1,0:T(8,128)S(1)}, u32[]{:S(2)}, u32[]{:S(2)}) %collective-permute-start.15) | collective-permute-done | bytes 4128 | tf_op jit(solution)/shard_map/ppermute | solution.py:254
  89.8 7.8 %collective-permute-done.17.column_ref = f32[8,128]{1,0:T(8,128)S(1)} collective-permute-done((f32[8,128]{1,0:T(8,128)S(1)}, f32[8,128]{1,0:T(8,128)S(1)}, u32[]{:S(2)}, u32[]{:S(2)}) %collective-permute-start.17) | collective-permute-done | bytes 4128 | tf_op jit(solution)/shard_map/ppermute | solution.py:252
  97.7 1.0 %last.1 = f32[32,8,128]{2,1,0:T(8,128)} custom-call(f32[32,8,128]{2,1,0:T(8,128)S(1)} %get-tuple-element.19.middle_ref, f32[32,8,128]{2,1,0:T(8,128)S(1)} %copy-done.1, f32[32,8,128]{2,1,0:T(8,128)S(1)} %get-tuple-element.20.squares_ref, f32[32,8,128]{2,1,0:T(8,128)S(1)} %copy-done.2, f32[8,128]{1,0:T(8,128)S(1)} %collective-permute-done.14.last_ref, ...), custom_call_target="tpu_custom_call" | custom-call | tf_op jit(solution)/shard_map/last/pallas_call | solution.py:308
  (41 shorter events, 4.1 us)
Async XLA Ops:
  0.6 0.9 copy-start
  1.5 0.7 copy-start.3
  3.0 14.5 %collective-permute-start.2 = (f32[16,128]{1,0:T(8,128)S(1)}, f32[16,128]{1,0:T(8,128)S(1)}, u32[]{:S(2)}, u32[]{:S(2)}) collective-permute-start(f32[16,128]{1,0:T(8,128)S(1)} %get-tuple-element.14), channel_id=1, source_target_pairs={{0,192},{2,194},{4,196},{6,198},{8,200},{10,202},{12,204},{14,206}... | collective-permute-start | bytes 24584 | tf_op jit(solution)/shard_map/ppermute | solution.py:265
  8.5 9.0 %collective-permute-start.1 = (f32[16,128]{1,0:T(8,128)S(1)}, f32[16,128]{1,0:T(8,128)S(1)}, u32[]{:S(2)}, u32[]{:S(2)}) collective-permute-start(f32[16,128]{1,0:T(8,128)S(1)} %get-tuple-element.14), channel_id=1, source_target_pairs={{0,64},{2,66},{4,68},{6,70},{8,72},{10,74},{12,76},{14,78},{16,80}... | collective-permute-start | bytes 24584 | tf_op jit(solution)/shard_map/ppermute | solution.py:265
  10.0 7.6 %collective-permute-start = (f32[16,128]{1,0:T(8,128)S(1)}, f32[16,128]{1,0:T(8,128)S(1)}, u32[]{:S(2)}, u32[]{:S(2)}) collective-permute-start(f32[16,128]{1,0:T(8,128)S(1)} %get-tuple-element.14), channel_id=1, source_target_pairs={{0,128},{2,130},{4,132},{6,134},{8,136},{10,138},{12,140},{14,142}... | collective-permute-start | bytes 24584 | tf_op jit(solution)/shard_map/ppermute | solution.py:265
  17.6 4.0 %collective-permute-start.3 = (f32[64,128]{1,0:T(8,128)S(1)}, f32[64,128]{1,0:T(8,128)S(1)}, u32[]{:S(2)}, u32[]{:S(2)}) collective-permute-start(f32[64,128]{1,0:T(8,128)S(1)} %get-tuple-element.34), channel_id=1, source_target_pairs={{0,32},{2,34},{4,36},{6,38},{8,40},{10,42},{12,44},{14,46},{16,48}... | collective-permute-start | bytes 98312 | tf_op jit(solution)/shard_map/ppermute | solution.py:265
  18.7 5.9 %collective-permute-start.5 = (f32[64,128]{1,0:T(8,128)S(1)}, f32[64,128]{1,0:T(8,128)S(1)}, u32[]{:S(2)}, u32[]{:S(2)}) collective-permute-start(f32[64,128]{1,0:T(8,128)S(1)} %get-tuple-element.34), channel_id=1, source_target_pairs={{0,48},{2,50},{4,52},{6,54},{8,56},{10,58},{12,60},{14,62},{16,32}... | collective-permute-start | bytes 98312 | tf_op jit(solution)/shard_map/ppermute | solution.py:265
  20.6 3.9 %collective-permute-start.4 = (f32[64,128]{1,0:T(8,128)S(1)}, f32[64,128]{1,0:T(8,128)S(1)}, u32[]{:S(2)}, u32[]{:S(2)}) collective-permute-start(f32[64,128]{1,0:T(8,128)S(1)} %get-tuple-element.34), channel_id=1, source_target_pairs={{0,16},{2,18},{4,20},{6,22},{8,24},{10,26},{12,28},{14,30},{16,0},... | collective-permute-start | bytes 98312 | tf_op jit(solution)/shard_map/ppermute | solution.py:265
  24.5 6.6 %collective-permute-start.6 = (f32[256,128]{1,0:T(8,128)S(1)}, f32[256,128]{1,0:T(8,128)S(1)}, u32[]{:S(2)}, u32[]{:S(2)}) collective-permute-start(f32[256,128]{1,0:T(8,128)S(1)} %get-tuple-element.26), channel_id=1, source_target_pairs={{0,8},{2,10},{4,12},{6,14},{8,0},{10,2},{12,4},{14,6},{16,24},{18,... | collective-permute-start | bytes 393224 | tf_op jit(solution)/shard_map/ppermute | solution.py:265
  27.8 5.0 %collective-permute-start.7 = (f32[256,128]{1,0:T(8,128)S(1)}, f32[256,128]{1,0:T(8,128)S(1)}, u32[]{:S(2)}, u32[]{:S(2)}) collective-permute-start(f32[256,128]{1,0:T(8,128)S(1)} %get-tuple-element.26), channel_id=1, source_target_pairs={{0,4},{2,6},{4,0},{6,2},{8,12},{10,14},{12,8},{14,10},{16,20},{18,... | collective-permute-start | bytes 393224 | tf_op jit(solution)/shard_map/ppermute | solution.py:265
  28.5 6.2 %collective-permute-start.8 = (f32[256,128]{1,0:T(8,128)S(1)}, f32[256,128]{1,0:T(8,128)S(1)}, u32[]{:S(2)}, u32[]{:S(2)}) collective-permute-start(f32[256,128]{1,0:T(8,128)S(1)} %get-tuple-element.26), channel_id=1, source_target_pairs={{0,12},{2,14},{4,8},{6,10},{8,4},{10,6},{12,0},{14,2},{16,28},{18,... | collective-permute-start | bytes 393224 | tf_op jit(solution)/shard_map/ppermute | solution.py:265
  31.1 24.2 %copy-start.5 = (f32[3,32,8,128]{3,2,1,0:T(8,128)S(1)}, f32[3,32,8,128]{3,2,1,0:T(8,128)}, u32[]{:S(2)}) copy-start(f32[3,32,8,128]{3,2,1,0:T(8,128)} %cell_ref.1) | copy-start | bytes 1179652
  32.9 13.5 %copy-start.6 = (s32[32,8,8]{0,2,1:T(8,128)S(1)}, s32[32,8,8]{0,2,1:T(8,128)}, u32[]{:S(2)}) copy-start(s32[32,8,8]{0,2,1:T(8,128)} %param.9) | copy-start | bytes 24580
  34.7 20.7 %collective-permute-start.9 = (f32[1024,128]{1,0:T(8,128)S(1)}, f32[1024,128]{1,0:T(8,128)S(1)}, u32[]{:S(2)}, u32[]{:S(2)}) collective-permute-start(f32[1024,128]{1,0:T(8,128)S(1)} %constant_dynamic-update-slice_fusion.11.own_ref), channel_id=1, source_target_pairs={{0,2},{2,0},{4,6},{6,4},{8,10},{10,8},{12,14},{14,12},{16,18},{18,... | collective-permute-start | bytes 1572872 | tf_op jit(solution)/shard_map/ppermute | solution.py:268
  34.8 20.6 %collective-permute-start.12 = (f32[32,128]{1,0:T(8,128)S(1)}, f32[32,128]{1,0:T(8,128)S(1)}, u32[]{:S(2)}, u32[]{:S(2)}) collective-permute-start(f32[32,128]{1,0:T(8,128)S(1)} %get-tuple-element.17), channel_id=1, source_target_pairs={{0,1},{1,0},{2,3},{3,2},{4,5},{5,4},{6,7},{7,6},{8,9},{9,8},{10,11... | collective-permute-start | bytes 49160 | tf_op jit(solution)/shard_map/ppermute | solution.py:255
  37.6 8.9 %collective-permute-start.10 = (f32[8,128]{1,0:T(8,128)S(1)}, f32[8,128]{1,0:T(8,128)S(1)}, u32[]{:S(2)}, u32[]{:S(2)}) collective-permute-start(f32[8,128]{1,0:T(8,128)S(1)} %get-tuple-element.15), channel_id=1, source_target_pairs={{0,2},{2,4},{4,6},{6,8},{8,10},{10,12},{12,14},{14,16},{16,18},{18... | collective-permute-start | bytes 12296 | tf_op jit(solution)/shard_map/ppermute | solution.py:253
  39.7 7.8 %collective-permute-start.11 = (f32[8,128]{1,0:T(8,128)S(1)}, f32[8,128]{1,0:T(8,128)S(1)}, u32[]{:S(2)}, u32[]{:S(2)}) collective-permute-start(f32[8,128]{1,0:T(8,128)S(1)} %get-tuple-element.16), channel_id=1, source_target_pairs={{2,0},{4,2},{6,4},{8,6},{10,8},{12,10},{14,12},{16,14},{18,16},{20... | collective-permute-start | bytes 12296 | tf_op jit(solution)/shard_map/ppermute | solution.py:254
  46.2 9.2 %copy-start.1 = (f32[32,8,128]{2,1,0:T(8,128)S(1)}, f32[32,8,128]{2,1,0:T(8,128)}, u32[]{:S(2)}) copy-start(f32[32,8,128]{2,1,0:T(8,128)} %nu_ref.5) | copy-start | bytes 393220
  46.2 9.2 %copy-start.2 = (f32[32,8,128]{2,1,0:T(8,128)S(1)}, f32[32,8,128]{2,1,0:T(8,128)}, u32[]{:S(2)}) copy-start(f32[32,8,128]{2,1,0:T(8,128)} %vorticity_ref.3) | copy-start | bytes 393220
  46.2 9.1 %collective-permute-start.13 = (f32[8,128]{1,0:T(8,128)S(1)}, f32[8,128]{1,0:T(8,128)S(1)}, u32[]{:S(2)}, u32[]{:S(2)}) collective-permute-start(f32[8,128]{1,0:T(8,128)S(1)} %get-tuple-element.18), channel_id=1, source_target_pairs={{0,254},{2,252},{4,250},{6,248},{8,246},{10,244},{12,242},{14,240}... | collective-permute-start | bytes 12296 | tf_op jit(solution)/shard_map/ppermute | solution.py:252
  79.1 18.5 %collective-permute-start.16 = (f32[32,128]{1,0:T(8,128)S(1)}, f32[32,128]{1,0:T(8,128)S(1)}, u32[]{:S(2)}, u32[]{:S(2)}) collective-permute-start(f32[32,128]{1,0:T(8,128)S(1)} %get-tuple-element.23), channel_id=1, source_target_pairs={{0,1},{1,0},{2,3},{3,2},{4,5},{5,4},{6,7},{7,6},{8,9},{9,8},{10,11... | collective-permute-start | bytes 49160 | tf_op jit(solution)/shard_map/ppermute | solution.py:255
  79.9 8.7 %collective-permute-start.14 = (f32[8,128]{1,0:T(8,128)S(1)}, f32[8,128]{1,0:T(8,128)S(1)}, u32[]{:S(2)}, u32[]{:S(2)}) collective-permute-start(f32[8,128]{1,0:T(8,128)S(1)} %get-tuple-element.21), channel_id=1, source_target_pairs={{0,2},{2,4},{4,6},{6,8},{8,10},{10,12},{12,14},{14,16},{16,18},{18... | collective-permute-start | bytes 12296 | tf_op jit(solution)/shard_map/ppermute | solution.py:253
  81.9 8.0 %collective-permute-start.15 = (f32[8,128]{1,0:T(8,128)S(1)}, f32[8,128]{1,0:T(8,128)S(1)}, u32[]{:S(2)}, u32[]{:S(2)}) collective-permute-start(f32[8,128]{1,0:T(8,128)S(1)} %get-tuple-element.22), channel_id=1, source_target_pairs={{2,0},{4,2},{6,4},{8,6},{10,8},{12,10},{14,12},{16,14},{18,16},{20... | collective-permute-start | bytes 12296 | tf_op jit(solution)/shard_map/ppermute | solution.py:254
  88.5 9.1 %collective-permute-start.17 = (f32[8,128]{1,0:T(8,128)S(1)}, f32[8,128]{1,0:T(8,128)S(1)}, u32[]{:S(2)}, u32[]{:S(2)}) collective-permute-start(f32[8,128]{1,0:T(8,128)S(1)} %get-tuple-element.24), channel_id=1, source_target_pairs={{0,254},{2,252},{4,250},{6,248},{8,246},{10,244},{12,242},{14,240}... | collective-permute-start | bytes 12296 | tf_op jit(solution)/shard_map/ppermute | solution.py:252
  (1 other events, 0.7 us)

commit v3 on v2

--- a/solution.py
+++ b/solution.py
@@ -57,19 +57,37 @@
     return jnp.broadcast_to(value[:, 0:1], (8, 128))
 
 
-def prep_kernel(xyz_ref, size_ref, nu_ref, message_ref, last_ref, first_ref, beside_ref, column_ref):
-    low_span = lax.axis_index("span") == 0
-    own_blocks = size_ref.shape[1] // PBS
-    for block in range(own_blocks):
+def message_kernel(xyz_hbm, size_hbm, message_ref, xyz_ref, size_ref, sems):
+    copies = [
+        pltpu.make_async_copy(xyz_hbm, xyz_ref, sems.at[0]),
+        pltpu.make_async_copy(size_hbm, size_ref, sems.at[1]),
+    ]
+    for copy in copies:
+        copy.start()
+    for copy in copies:
+        copy.wait()
+    for block in range(size_ref.shape[1] // PBS):
         lanes = slice(block * PBS, (block + 1) * PBS)
         xyz = xyz_ref[:, lanes]
         size = size_ref[:, lanes]
         offset = jnp.sum(xyz * xyz, axis=0, keepdims=True) + size * size
         message_ref[block * 4 : block * 4 + 3, :] = xyz
         message_ref[block * 4 + 3 : block * 4 + 4, :] = offset
+
+
+def even_place():
+    return lax.rem(lax.axis_index("wrap"), 2) == 0
+
+
+def put_edges(first, last, pair_ref, next_ref):
+    pair_ref[...] = jnp.where(even_place(), last, first)
+    next_ref[...] = jnp.where(even_place(), first, last)
+
+
+def edges_kernel(nu_ref, pair_ref, next_ref, beside_ref, column_ref):
+    low_span = lax.axis_index("span") == 0
     rows = nu_ref.shape[0]
-    last_ref[...] = nu_ref[rows - 1]
-    first_ref[...] = nu_ref[0]
+    put_edges(nu_ref[0], nu_ref[rows - 1], pair_ref, next_ref)
     lane = tile_iota(1)
     column = jnp.zeros((8, 128), F32)
     for row in range(rows):
@@ -80,17 +98,18 @@
 
 
 class Halo:
-    def __init__(self, nu_ref, last_ref, first_ref, beside_ref, column_ref, padded_ref, ghost_ref):
+    def __init__(self, nu_ref, pair, after, beside_ref, column, padded_ref, ghost_ref):
         devices = lax.axis_size("wrap")
         place = lax.axis_index("wrap")
         rows = nu_ref.shape[0]
         self.rows = rows
         self.low_span = lax.axis_index("span") == 0
         self.padded, self.ghost, self.beside = padded_ref, ghost_ref, beside_ref
-        padded_ref[0] = jnp.where(place == 0, nu_ref[0], last_ref[...])
-        padded_ref[rows + 1] = jnp.where(place == devices - 1, nu_ref[rows - 1], first_ref[...])
+        lower = jnp.where(even_place(), after, pair)
+        upper = jnp.where(even_place(), pair, after)
+        padded_ref[0] = jnp.where(place == 0, nu_ref[0], lower)
+        padded_ref[rows + 1] = jnp.where(place == devices - 1, nu_ref[rows - 1], upper)
         in_wake = (place < devices // 4) | (place >= devices - devices // 4)
-        column = column_ref[...]
         for row in range(rows):
             value = nu_ref[row]
             padded_ref[row + 1] = value
@@ -189,22 +208,23 @@
     cell_ref,
     nu_ref,
     vorticity_ref,
-    last_ref,
-    first_ref,
+    next_ref,
     beside_ref,
-    column_ref,
     dist_ref,
     squares_ref,
     middle_ref,
-    last_out,
-    first_out,
+    pair_out,
+    next_out,
     beside_out,
     column_out,
     table_ref,
     padded_ref,
     ghost_ref,
 ):
-    halo = Halo(nu_ref, last_ref, first_ref, beside_ref, column_ref, padded_ref, ghost_ref)
+    panel_rows = own_ref.shape[0]
+    column = other_ref[panel_rows : panel_rows + 8]
+    pair = other_ref[panel_rows + 8 : panel_rows + 16]
+    halo = Halo(nu_ref, pair, next_ref[...], beside_ref, column, padded_ref, ghost_ref)
     build_table((own_ref, other_ref), table_ref)
     tiles = nu_ref.shape[0]
     per_step = LINES_PER_STEP // 8
@@ -224,8 +244,7 @@
         return column
 
     column_out[...] = lax.fori_loop(0, tiles // per_step, body, jnp.zeros((8, 128), F32))
-    last_out[...] = middle_ref[tiles - 1]
-    first_out[...] = middle_ref[0]
+    put_edges(middle_ref[0], middle_ref[tiles - 1], pair_out, next_out)
 
 
 def last_kernel(
@@ -233,39 +252,56 @@
     nu_ref,
     squares_ref,
     vorticity_ref,
-    last_ref,
-    first_ref,
+    pair_ref,
+    next_ref,
     beside_ref,
     column_ref,
-    next_ref,
+    out_ref,
     padded_ref,
     ghost_ref,
 ):
-    halo = Halo(middle_ref, last_ref, first_ref, beside_ref, column_ref, padded_ref, ghost_ref)
+    halo = Halo(
+        middle_ref, pair_ref[...], next_ref[...], beside_ref, column_ref[...], padded_ref, ghost_ref
+    )
     for row in range(nu_ref.shape[0]):
         rate = halo.rate(row, squares_ref[row], vorticity_ref[row])
-        next_ref[row] = nu_ref[row] + time_step * rate
-
-
-def exchange(last, first, beside, column):
+        out_ref[row] = nu_ref[row] + time_step * rate
+
+
+def swap_mask(block, mask):
+    return lax.ppermute(block, "wrap", [(i, i ^ mask) for i in range(lax.axis_size("wrap"))])
+
+
+def swap_next(block):
     devices = lax.axis_size("wrap")
-    column = lax.ppermute(column, "wrap", [(i, devices - 1 - i) for i in range(devices)])
-    last = lax.ppermute(last, "wrap", [(i, i + 1) for i in range(devices - 1)])
-    first = lax.ppermute(first, "wrap", [(i + 1, i) for i in range(devices - 1)])
-    beside = lax.ppermute(beside, "span", [(0, 1), (1, 0)])
-    return last, first, beside, column
-
-
-def gather(shard):
-    devices = lax.axis_size("wrap")
-    for bits in STAGES[:-1]:
+    pairs = [(i, i + 1) for i in range(1, devices - 1, 2)]
+    return lax.ppermute(block, "wrap", pairs + [(j, i) for i, j in pairs])
+
+
+def swap_span(block):
+    return lax.ppermute(block, "span", [(0, 1), (1, 0)])
+
+
+def gather(shard, pair, after, beside, column):
+    size = shard.shape[0]
+    for stage, bits in enumerate(STAGES[:-1]):
+        if stage == len(STAGES) - 2:
+            shard, after, beside = lax.optimization_barrier((shard, after, beside))
+            after, beside = swap_next(after), swap_span(beside)
         parts = [shard]
         for choice in range(1, 1 << len(bits)):
             mask = sum(((choice >> n) & 1) << bit for n, bit in enumerate(bits))
-            parts.append(lax.ppermute(shard, "wrap", [(i, i ^ mask) for i in range(devices)]))
+            if choice == (1 << len(bits)) - 1:
+                both = swap_mask(jnp.concatenate([shard, column], 0), mask)
+                parts.append(both[:size])
+                column = both[size:]
+            else:
+                parts.append(swap_mask(shard, mask))
         shard = jnp.concatenate(parts, 0)
-    mask = 1 << STAGES[-1][0]
-    return shard, lax.ppermute(shard, "wrap", [(i, i ^ mask) for i in range(devices)])
+        size = shard.shape[0]
+    shard, after, beside = lax.optimization_barrier((shard, after, beside))
+    other = swap_mask(jnp.concatenate([shard, column, pair], 0), 1 << STAGES[-1][0])
+    return shard, other, after, beside
 
 
 def shards(cell_xyz, panel_xyz, panel_size, block_lists, nu_field, vorticity):
@@ -278,21 +314,33 @@
     edges = (tile, tile, side, tile)
     scratch = [pltpu.VMEM((rows + 2, span, cells), F32), pltpu.VMEM(nu_field.shape, F32)]
 
-    message, *sent = pl.pallas_call(
-        prep_kernel,
-        out_shape=(jax.ShapeDtypeStruct((4 * own_blocks, PBS), F32),) + edges,
-        in_specs=[VMEM] * 3,
-        out_specs=(VMEM,) * 5,
+    message = pl.pallas_call(
+        message_kernel,
+        out_shape=jax.ShapeDtypeStruct((4 * own_blocks, PBS), F32),
+        in_specs=[pl.BlockSpec(memory_space=pltpu.HBM)] * 2,
+        out_specs=VMEM,
+        scratch_shapes=[
+            pltpu.VMEM(panel_xyz.shape, F32),
+            pltpu.VMEM((1,) + panel_size.shape, F32),
+            pltpu.SemaphoreType.DMA((2,)),
+        ],
+        compiler_params=pltpu.CompilerParams(vmem_limit_bytes=2**20),
+        name="message",
+    )(panel_xyz, panel_size[None])
+    sent = pl.pallas_call(
+        edges_kernel,
+        out_shape=edges,
+        in_specs=[VMEM],
+        out_specs=(VMEM,) * 4,
         compiler_params=pltpu.CompilerParams(vmem_limit_bytes=4 * 2**20),
-        name="prep",
-    )(panel_xyz, panel_size[None], nu_field)
-    own, other = gather(message)
-    halos = exchange(*sent)
-
-    dist, squares, middle, *sent = pl.pallas_call(
+        name="edges",
+    )(nu_field)
+    own, other, after, beside = gather(message, *sent)
+
+    dist, squares, middle, pair, next_pair, sides, column = pl.pallas_call(
         main_kernel,
         out_shape=(field, field, field) + edges,
-        in_specs=[SMEM] + [VMEM] * 9,
+        in_specs=[SMEM] + [VMEM] * 7,
         out_specs=(VMEM,) * 7,
         scratch_shapes=[pltpu.VMEM((devices * own_blocks, FEATS, PBS), BF)] + scratch,
         compiler_params=pltpu.CompilerParams(vmem_limit_bytes=24 * 2**20),
@@ -302,8 +350,11 @@
             transcendentals=0,
         ),
         name="main",
-    )(block_lists.reshape(-1), own, other, cell_xyz, nu_field, vorticity, *halos)
-    halos = exchange(*sent)
+    )(block_lists.reshape(-1), own, other, cell_xyz, nu_field, vorticity, after, beside)
+    column = swap_mask(column, devices - 1)
+    next_pair = swap_next(next_pair)
+    sides = swap_span(sides)
+    pair = swap_mask(pair, 1)
 
     nu_next = pl.pallas_call(
         last_kernel,
@@ -313,7 +364,7 @@
         scratch_shapes=scratch,
         compiler_params=pltpu.CompilerParams(vmem_limit_bytes=8 * 2**20),
         name="last",
-    )(middle, nu_field, squares, vorticity, *halos)
+    )(middle, nu_field, squares, vorticity, pair, next_pair, sides, column)
     return (nu_next, dist)
 
 

time: 99 us -> 79 us (0.80)
  waiting for transfers between devices: 33.5 us -> 22 us
  starting transfers between devices: 36.9 us -> 27.3 us
    ppermute x18 -> x16, waiting for transfers between devices: 33.5 us -> 22 us  [the longest x12 15.1 us: swap_mask(): lax.ppermute(block, 'wrap', [(i, i ^ mask) for i in range(lax.axis_size('...]
    ppermute x18 -> x16, starting transfers between devices: 36.9 us -> 27.3 us  [the longest x12 19.5 us: swap_mask(): lax.ppermute(block, 'wrap', [(i, i ^ mask) for i in range(lax.axis_size('...]
    unnamed x23 -> x20, local copies, waits for them, and re-layouts: 2.45 us -> 2.99 us
  transfers between devices with their start and end apart: 18 -> 16, of which waited for: 10 -> 10; matrix products, arithmetic and copies ran while one was open for 0% -> 0% of each run, Pallas kernels for 0% -> 0%
where the time goes in v3:
time: 79 us; the launch traced here: 78.3 us
  starting transfers between devices  27.3 us (35%)
  Pallas kernels  24.9 us (32%)
  waiting for transfers between devices  22 us (28%)
  local copies, waits for them, and re-layouts  3.12 us (4%)
  between operations  0.8 us (1%)
    pallas_call x1, Pallas kernels, shards(): pl.pallas_call(main_kernel, out_shape=(field, field, field) + edges, in_s...  23.8 us
    ppermute x12, starting transfers between devices, swap_mask(): lax.ppermute(block, 'wrap', [(i, i ^ mask) for i in range(lax.axis_size('...  19.5 us
    ppermute x12, waiting for transfers between devices, swap_mask(): lax.ppermute(block, 'wrap', [(i, i ^ mask) for i in range(lax.axis_size('...  15.1 us
    ppermute x2, waiting for transfers between devices, swap_next(): return lax.ppermute(block, 'wrap', pairs + [(j, i) for i, j in pairs])  6.93 us
    ppermute x2, starting transfers between devices, swap_next(): return lax.ppermute(block, 'wrap', pairs + [(j, i) for i, j in pairs])  4.35 us
    ppermute x2, starting transfers between devices, swap_span(): return lax.ppermute(block, 'span', [(0, 1), (1, 0)])  3.53 us
    unnamed x20, local copies, waits for them, and re-layouts  2.99 us
  transfers between devices with their start and end apart: 16, of which 10 were waited for; matrix products, arithmetic and copies ran while one was open for 0% of the time, Pallas kernels for 0%

profile of v3, /device:TPU:32, one launch (start us, length us, event | category | flops | bytes accessed | tf_op | source)
XLA Modules:
  0.0 78.3 jit_solution(11378346272790836631)
XLA Ops:
  0.6 0.7 copy-done.3
  2.1 6.4 %collective-permute-start = (f32[16,128]{1,0:T(8,128)S(1)}, f32[16,128]{1,0:T(8,128)S(1)}, u32[]{:S(2)}, u32[]{:S(2)}) collective-permute-start(f32[16,128]{1,0:T(8,128)S(1)} %message.1), channel_id=1, source_target_pairs={{0,128},{2,130},{4,132},{6,134},{8,136},{10,138},{12,140},{14,142}... | collective-permute-start | bytes 24584 | tf_op jit(solution)/shard_map/ppermute | solution.py:272
  8.4 1.5 %collective-permute-start.1 = (f32[16,128]{1,0:T(8,128)S(1)}, f32[16,128]{1,0:T(8,128)S(1)}, u32[]{:S(2)}, u32[]{:S(2)}) collective-permute-start(f32[16,128]{1,0:T(8,128)S(1)} %message.1), channel_id=1, source_target_pairs={{0,64},{2,66},{4,68},{6,70},{8,72},{10,74},{12,76},{14,78},{16,80}... | collective-permute-start | bytes 24584 | tf_op jit(solution)/shard_map/ppermute | solution.py:272
  9.9 0.9 %copy-done = f32[32,8,128]{2,1,0:T(8,128)S(1)} copy-done((f32[32,8,128]{2,1,0:T(8,128)S(1)}, f32[32,8,128]{2,1,0:T(8,128)}, u32[]{:S(2)}) %copy-start) | copy-done | bytes 131096
  11.1 1.9 %collective-permute-done.1 = f32[16,128]{1,0:T(8,128)S(1)} collective-permute-done((f32[16,128]{1,0:T(8,128)S(1)}, f32[16,128]{1,0:T(8,128)S(1)}, u32[]{:S(2)}, u32[]{:S(2)}) %collective-permute-start.1) | collective-permute-done | bytes 8224 | tf_op jit(solution)/shard_map/ppermute | solution.py:272
  13.0 3.8 %collective-permute-done.2 = f32[24,128]{1,0:T(8,128)S(1)} collective-permute-done((f32[24,128]{1,0:T(8,128)S(1)}, f32[24,128]{1,0:T(8,128)S(1)}, u32[]{:S(2)}, u32[]{:S(2)}) %collective-permute-start.2) | collective-permute-done | bytes 12320 | tf_op jit(solution)/shard_map/ppermute | solution.py:272
  16.8 1.0 %collective-permute-start.3 = (f32[64,128]{1,0:T(8,128)S(1)}, f32[64,128]{1,0:T(8,128)S(1)}, u32[]{:S(2)}, u32[]{:S(2)}) collective-permute-start(f32[64,128]{1,0:T(8,128)S(1)} %pad_maximum_fusion.4), channel_id=1, source_target_pairs={{0,32},{2,34},{4,36},{6,38},{8,40},{10,42},{12,44},{14,46},{16,48}... | collective-permute-start | bytes 98312 | tf_op jit(solution)/shard_map/ppermute | solution.py:272
  17.8 1.5 %collective-permute-start.4 = (f32[64,128]{1,0:T(8,128)S(1)}, f32[64,128]{1,0:T(8,128)S(1)}, u32[]{:S(2)}, u32[]{:S(2)}) collective-permute-start(f32[64,128]{1,0:T(8,128)S(1)} %pad_maximum_fusion.4), channel_id=1, source_target_pairs={{0,16},{2,18},{4,20},{6,22},{8,24},{10,26},{12,28},{14,30},{16,0},... | collective-permute-start | bytes 98312 | tf_op jit(solution)/shard_map/ppermute | solution.py:272
  19.3 1.0 %collective-permute-start.5 = (f32[72,128]{1,0:T(8,128)S(1)}, f32[72,128]{1,0:T(8,128)S(1)}, u32[]{:S(2)}, u32[]{:S(2)}) collective-permute-start(f32[72,128]{1,0:T(8,128)S(1)} %pad_maximum_fusion.3), channel_id=1, source_target_pairs={{0,48},{2,50},{4,52},{6,54},{8,56},{10,58},{12,60},{14,62},{16,32}... | collective-permute-start | bytes 110600 | tf_op jit(solution)/shard_map/ppermute | solution.py:272
  20.7 1.0 %collective-permute-done.4 = f32[64,128]{1,0:T(8,128)S(1)} collective-permute-done((f32[64,128]{1,0:T(8,128)S(1)}, f32[64,128]{1,0:T(8,128)S(1)}, u32[]{:S(2)}, u32[]{:S(2)}) %collective-permute-start.4) | collective-permute-done | bytes 32800 | tf_op jit(solution)/shard_map/ppermute | solution.py:272
  21.8 2.4 %collective-permute-done.5 = f32[72,128]{1,0:T(8,128)S(1)} collective-permute-done((f32[72,128]{1,0:T(8,128)S(1)}, f32[72,128]{1,0:T(8,128)S(1)}, u32[]{:S(2)}, u32[]{:S(2)}) %collective-permute-start.5) | collective-permute-done | bytes 36896 | tf_op jit(solution)/shard_map/ppermute | solution.py:272
  24.2 3.1 %collective-permute-start.8 = (f32[264,128]{1,0:T(8,128)S(1)}, f32[264,128]{1,0:T(8,128)S(1)}, u32[]{:S(2)}, u32[]{:S(2)}) collective-permute-start(f32[264,128]{1,0:T(8,128)S(1)} %pad_maximum_fusion.2), channel_id=1, source_target_pairs={{0,12},{2,14},{4,8},{6,10},{8,4},{10,6},{12,0},{14,2},{16,28},{18,... | collective-permute-start | bytes 405512 | tf_op jit(solution)/shard_map/ppermute | solution.py:272
  28.4 2.7 %collective-permute-start.10 = (f32[32,128]{1,0:T(8,128)S(1)}, f32[32,128]{1,0:T(8,128)S(1)}, u32[]{:S(2)}, u32[]{:S(2)}) collective-permute-start(f32[32,128]{1,0:T(8,128)S(1)} %get-tuple-element.24), channel_id=1, source_target_pairs={{0,1},{1,0},{2,3},{3,2},{4,5},{5,4},{6,7},{7,6},{8,9},{9,8},{10,11... | collective-permute-start | bytes 49160 | tf_op jit(solution)/shard_map/ppermute | solution.py:282
  31.1 1.9 %collective-permute-start.9 = (f32[8,128]{1,0:T(8,128)S(1)}, f32[8,128]{1,0:T(8,128)S(1)}, u32[]{:S(2)}, u32[]{:S(2)}) collective-permute-start(f32[8,128]{1,0:T(8,128)S(1)} %get-tuple-element.23), channel_id=1, source_target_pairs={{2,4},{6,8},{10,12},{14,16},{18,20},{22,24},{26,28},{30,32},{34,36... | collective-permute-start | bytes 12296 | tf_op jit(solution)/shard_map/ppermute | solution.py:278
  33.1 0.7 collective-permute-done.6
  33.8 5.2 %collective-permute-done.9.next_ref = f32[8,128]{1,0:T(8,128)S(1)} collective-permute-done((f32[8,128]{1,0:T(8,128)S(1)}, f32[8,128]{1,0:T(8,128)S(1)}, u32[]{:S(2)}, u32[]{:S(2)}) %collective-permute-start.9) | collective-permute-done | bytes 4128 | tf_op jit(solution)/shard_map/ppermute | solution.py:278
  40.0 1.1 %collective-permute-done.11.other_ref = f32[1040,128]{1,0:T(8,128)S(1)} collective-permute-done((f32[1040,128]{1,0:T(8,128)S(1)}, f32[1040,128]{1,0:T(8,128)S(1)}, u32[]{:S(2)}, u32[]{:S(2)}) %collective-permute-start.11) | collective-permute-done | bytes 532512 | tf_op jit(solution)/shard_map/ppermute | solution.py:272
  41.1 23.8 %main.1 = (f32[32,8,128]{2,1,0:T(8,128)}, f32[32,8,128]{2,1,0:T(8,128)S(1)}, f32[32,8,128]{2,1,0:T(8,128)S(1)}, f32[8,128]{1,0:T(8,128)S(1)}, f32[8,128]{1,0:T(8...) custom-call(s32[2048]{0:T(1024)S(1)} %reshape.7.list_ref, f32[1024,128]{1,0:T(8,128)S(1)} %pad_maximum_fusion.1.own_ref, ...), custom_call_target="tpu_custom_call" | custom-call | flops 8589934592 | bytes 4194304 | tf_op jit(solution)/shard_map/main/pallas_call | solution.py:340
  64.9 0.8 %collective-permute-start.14 = (f32[32,128]{1,0:T(8,128)S(1)}, f32[32,128]{1,0:T(8,128)S(1)}, u32[]{:S(2)}, u32[]{:S(2)}) collective-permute-start(f32[32,128]{1,0:T(8,128)S(1)} %get-tuple-element.33), channel_id=1, source_target_pairs={{0,1},{1,0},{2,3},{3,2},{4,5},{5,4},{6,7},{7,6},{8,9},{9,8},{10,11... | collective-permute-start | bytes 49160 | tf_op jit(solution)/shard_map/ppermute | solution.py:282
  65.7 2.4 %collective-permute-start.13 = (f32[8,128]{1,0:T(8,128)S(1)}, f32[8,128]{1,0:T(8,128)S(1)}, u32[]{:S(2)}, u32[]{:S(2)}) collective-permute-start(f32[8,128]{1,0:T(8,128)S(1)} %get-tuple-element.32), channel_id=1, source_target_pairs={{2,4},{6,8},{10,12},{14,16},{18,20},{22,24},{26,28},{30,32},{34,36... | collective-permute-start | bytes 12296 | tf_op jit(solution)/shard_map/ppermute | solution.py:278
  68.2 3.8 %collective-permute-start.15 = (f32[8,128]{1,0:T(8,128)S(1)}, f32[8,128]{1,0:T(8,128)S(1)}, u32[]{:S(2)}, u32[]{:S(2)}) collective-permute-start(f32[8,128]{1,0:T(8,128)S(1)} %get-tuple-element.34), channel_id=1, source_target_pairs={{0,254},{2,252},{4,250},{6,248},{8,246},{10,244},{12,242},{14,240}... | collective-permute-start | bytes 12296 | tf_op jit(solution)/shard_map/ppermute | solution.py:272
  71.9 1.7 %collective-permute-done.13.next_ref = f32[8,128]{1,0:T(8,128)S(1)} collective-permute-done((f32[8,128]{1,0:T(8,128)S(1)}, f32[8,128]{1,0:T(8,128)S(1)}, u32[]{:S(2)}, u32[]{:S(2)}) %collective-permute-start.13) | collective-permute-done | bytes 4128 | tf_op jit(solution)/shard_map/ppermute | solution.py:278
  73.6 3.7 %collective-permute-done.15.column_ref = f32[8,128]{1,0:T(8,128)S(1)} collective-permute-done((f32[8,128]{1,0:T(8,128)S(1)}, f32[8,128]{1,0:T(8,128)S(1)}, u32[]{:S(2)}, u32[]{:S(2)}) %collective-permute-start.15) | collective-permute-done | bytes 4128 | tf_op jit(solution)/shard_map/ppermute | solution.py:272
  77.3 1.0 %last.1 = f32[32,8,128]{2,1,0:T(8,128)} custom-call(f32[32,8,128]{2,1,0:T(8,128)S(1)} %get-tuple-element.29.middle_ref, f32[32,8,128]{2,1,0:T(8,128)S(1)} %copy-done.1, f32[32,8,128]{2,1,0:T(8,128)S(1)} %get-tuple-element.30.squares_ref, f32[32,8,128]{2,1,0:T(8,128)S(1)} %copy-done.2, f32[8,128]{1,0:T(8,128)S(1)} %collective-permute-done.12.pair_ref, ...), custom_call_target="tpu_custom_call" | custom-call | tf_op jit(solution)/shard_map/last/pallas_call | solution.py:359
  (44 shorter events, 3.5 us)
Async XLA Ops:
  0.6 0.7 copy-start.3
  1.3 0.7 copy-start.4
  2.1 9.0 %collective-permute-start = (f32[16,128]{1,0:T(8,128)S(1)}, f32[16,128]{1,0:T(8,128)S(1)}, u32[]{:S(2)}, u32[]{:S(2)}) collective-permute-start(f32[16,128]{1,0:T(8,128)S(1)} %message.1), channel_id=1, source_target_pairs={{0,128},{2,130},{4,132},{6,134},{8,136},{10,138},{12,140},{14,142}... | collective-permute-start | bytes 24584 | tf_op jit(solution)/shard_map/ppermute | solution.py:272
  8.4 4.5 %collective-permute-start.1 = (f32[16,128]{1,0:T(8,128)S(1)}, f32[16,128]{1,0:T(8,128)S(1)}, u32[]{:S(2)}, u32[]{:S(2)}) collective-permute-start(f32[16,128]{1,0:T(8,128)S(1)} %message.1), channel_id=1, source_target_pairs={{0,64},{2,66},{4,68},{6,70},{8,72},{10,74},{12,76},{14,78},{16,80}... | collective-permute-start | bytes 24584 | tf_op jit(solution)/shard_map/ppermute | solution.py:272
  9.9 0.9 %copy-start = (f32[32,8,128]{2,1,0:T(8,128)S(1)}, f32[32,8,128]{2,1,0:T(8,128)}, u32[]{:S(2)}) copy-start(f32[32,8,128]{2,1,0:T(8,128)} %nu_ref.5) | copy-start | bytes 393220
  10.9 5.9 %collective-permute-start.2 = (f32[24,128]{1,0:T(8,128)S(1)}, f32[24,128]{1,0:T(8,128)S(1)}, u32[]{:S(2)}, u32[]{:S(2)}) collective-permute-start(f32[24,128]{1,0:T(8,128)S(1)} %pad_maximum_fusion.5), channel_id=1, source_target_pairs={{0,192},{2,194},{4,196},{6,198},{8,200},{10,202},{12,204},{14,206}... | collective-permute-start | bytes 36872 | tf_op jit(solution)/shard_map/ppermute | solution.py:272
  16.8 3.9 %collective-permute-start.3 = (f32[64,128]{1,0:T(8,128)S(1)}, f32[64,128]{1,0:T(8,128)S(1)}, u32[]{:S(2)}, u32[]{:S(2)}) collective-permute-start(f32[64,128]{1,0:T(8,128)S(1)} %pad_maximum_fusion.4), channel_id=1, source_target_pairs={{0,32},{2,34},{4,36},{6,38},{8,40},{10,42},{12,44},{14,46},{16,48}... | collective-permute-start | bytes 98312 | tf_op jit(solution)/shard_map/ppermute | solution.py:272
  17.8 3.9 %collective-permute-start.4 = (f32[64,128]{1,0:T(8,128)S(1)}, f32[64,128]{1,0:T(8,128)S(1)}, u32[]{:S(2)}, u32[]{:S(2)}) collective-permute-start(f32[64,128]{1,0:T(8,128)S(1)} %pad_maximum_fusion.4), channel_id=1, source_target_pairs={{0,16},{2,18},{4,20},{6,22},{8,24},{10,26},{12,28},{14,30},{16,0},... | collective-permute-start | bytes 98312 | tf_op jit(solution)/shard_map/ppermute | solution.py:272
  19.3 4.9 %collective-permute-start.5 = (f32[72,128]{1,0:T(8,128)S(1)}, f32[72,128]{1,0:T(8,128)S(1)}, u32[]{:S(2)}, u32[]{:S(2)}) collective-permute-start(f32[72,128]{1,0:T(8,128)S(1)} %pad_maximum_fusion.3), channel_id=1, source_target_pairs={{0,48},{2,50},{4,52},{6,54},{8,56},{10,58},{12,60},{14,62},{16,32}... | collective-permute-start | bytes 110600 | tf_op jit(solution)/shard_map/ppermute | solution.py:272
  24.2 8.8 %collective-permute-start.8 = (f32[264,128]{1,0:T(8,128)S(1)}, f32[264,128]{1,0:T(8,128)S(1)}, u32[]{:S(2)}, u32[]{:S(2)}) collective-permute-start(f32[264,128]{1,0:T(8,128)S(1)} %pad_maximum_fusion.2), channel_id=1, source_target_pairs={{0,12},{2,14},{4,8},{6,10},{8,4},{10,6},{12,0},{14,2},{16,28},{18,... | collective-permute-start | bytes 405512 | tf_op jit(solution)/shard_map/ppermute | solution.py:272
  27.3 6.5 %collective-permute-start.6 = (f32[256,128]{1,0:T(8,128)S(1)}, f32[256,128]{1,0:T(8,128)S(1)}, u32[]{:S(2)}, u32[]{:S(2)}) collective-permute-start(f32[256,128]{1,0:T(8,128)S(1)} %slice_dynamic-update-slice_fusion), channel_id=1, source_target_pairs={{0,8},{2,10},{4,12},{6,14},{8,0},{10,2},{12,4},{14,6},{16,24},{18,... | collective-permute-start | bytes 393224 | tf_op jit(solution)/shard_map/ppermute | solution.py:272
  27.9 5.8 %collective-permute-start.7 = (f32[256,128]{1,0:T(8,128)S(1)}, f32[256,128]{1,0:T(8,128)S(1)}, u32[]{:S(2)}, u32[]{:S(2)}) collective-permute-start(f32[256,128]{1,0:T(8,128)S(1)} %slice_dynamic-update-slice_fusion), channel_id=1, source_target_pairs={{0,4},{2,6},{4,0},{6,2},{8,12},{10,14},{12,8},{14,10},{16,20},{18,... | collective-permute-start | bytes 393224 | tf_op jit(solution)/shard_map/ppermute | solution.py:272
  28.4 10.7 %collective-permute-start.10 = (f32[32,128]{1,0:T(8,128)S(1)}, f32[32,128]{1,0:T(8,128)S(1)}, u32[]{:S(2)}, u32[]{:S(2)}) collective-permute-start(f32[32,128]{1,0:T(8,128)S(1)} %get-tuple-element.24), channel_id=1, source_target_pairs={{0,1},{1,0},{2,3},{3,2},{4,5},{5,4},{6,7},{7,6},{8,9},{9,8},{10,11... | collective-permute-start | bytes 49160 | tf_op jit(solution)/shard_map/ppermute | solution.py:282
  31.1 7.9 %collective-permute-start.9 = (f32[8,128]{1,0:T(8,128)S(1)}, f32[8,128]{1,0:T(8,128)S(1)}, u32[]{:S(2)}, u32[]{:S(2)}) collective-permute-start(f32[8,128]{1,0:T(8,128)S(1)} %get-tuple-element.23), channel_id=1, source_target_pairs={{2,4},{6,8},{10,12},{14,16},{18,20},{22,24},{26,28},{30,32},{34,36... | collective-permute-start | bytes 12296 | tf_op jit(solution)/shard_map/ppermute | solution.py:278
  39.0 0.8 copy-start.6
  39.1 2.1 %copy-start.5 = (f32[3,32,8,128]{3,2,1,0:T(8,128)S(1)}, f32[3,32,8,128]{3,2,1,0:T(8,128)}, u32[]{:S(2)}) copy-start(f32[3,32,8,128]{3,2,1,0:T(8,128)} %cell_ref.1) | copy-start | bytes 1179652
  39.1 2.0 %copy-start.1 = (f32[32,8,128]{2,1,0:T(8,128)S(1)}, f32[32,8,128]{2,1,0:T(8,128)}, u32[]{:S(2)}) copy-start(f32[32,8,128]{2,1,0:T(8,128)} %nu_ref.5) | copy-start | bytes 393220
  39.1 2.0 %copy-start.2 = (f32[32,8,128]{2,1,0:T(8,128)S(1)}, f32[32,8,128]{2,1,0:T(8,128)}, u32[]{:S(2)}) copy-start(f32[32,8,128]{2,1,0:T(8,128)} %vorticity_ref.3) | copy-start | bytes 393220
  39.1 2.0 %collective-permute-start.11 = (f32[1040,128]{1,0:T(8,128)S(1)}, f32[1040,128]{1,0:T(8,128)S(1)}, u32[]{:S(2)}, u32[]{:S(2)}) collective-permute-start(f32[1040,128]{1,0:T(8,128)S(1)} %pad_maximum_fusion), channel_id=1, source_target_pairs={{0,2},{2,0},{4,6},{6,4},{8,10},{10,8},{12,14},{14,12},{16,18},{18,... | collective-permute-start | bytes 1597448 | tf_op jit(solution)/shard_map/ppermute | solution.py:272
  64.9 12.4 %collective-permute-start.14 = (f32[32,128]{1,0:T(8,128)S(1)}, f32[32,128]{1,0:T(8,128)S(1)}, u32[]{:S(2)}, u32[]{:S(2)}) collective-permute-start(f32[32,128]{1,0:T(8,128)S(1)} %get-tuple-element.33), channel_id=1, source_target_pairs={{0,1},{1,0},{2,3},{3,2},{4,5},{5,4},{6,7},{7,6},{8,9},{9,8},{10,11... | collective-permute-start | bytes 49160 | tf_op jit(solution)/shard_map/ppermute | solution.py:282
  65.7 6.2 %collective-permute-start.12 = (f32[8,128]{1,0:T(8,128)S(1)}, f32[8,128]{1,0:T(8,128)S(1)}, u32[]{:S(2)}, u32[]{:S(2)}) collective-permute-start(f32[8,128]{1,0:T(8,128)S(1)} %get-tuple-element.31), channel_id=1, source_target_pairs={{0,2},{2,0},{4,6},{6,4},{8,10},{10,8},{12,14},{14,12},{16,18},{18,... | collective-permute-start | bytes 12296 | tf_op jit(solution)/shard_map/ppermute | solution.py:272
  65.7 7.9 %collective-permute-start.13 = (f32[8,128]{1,0:T(8,128)S(1)}, f32[8,128]{1,0:T(8,128)S(1)}, u32[]{:S(2)}, u32[]{:S(2)}) collective-permute-start(f32[8,128]{1,0:T(8,128)S(1)} %get-tuple-element.32), channel_id=1, source_target_pairs={{2,4},{6,8},{10,12},{14,16},{18,20},{22,24},{26,28},{30,32},{34,36... | collective-permute-start | bytes 12296 | tf_op jit(solution)/shard_map/ppermute | solution.py:278
  68.2 9.1 %collective-permute-start.15 = (f32[8,128]{1,0:T(8,128)S(1)}, f32[8,128]{1,0:T(8,128)S(1)}, u32[]{:S(2)}, u32[]{:S(2)}) collective-permute-start(f32[8,128]{1,0:T(8,128)S(1)} %get-tuple-element.34), channel_id=1, source_target_pairs={{0,254},{2,252},{4,250},{6,248},{8,246},{10,244},{12,242},{14,240}... | collective-permute-start | bytes 12296 | tf_op jit(solution)/shard_map/ppermute | solution.py:272

commit v4 on v3

--- a/solution.py
+++ b/solution.py
@@ -274,7 +274,7 @@
 
 def swap_next(block):
     devices = lax.axis_size("wrap")
-    pairs = [(i, i + 1) for i in range(1, devices - 1, 2)]
+    pairs = [(i, (i + 1) % devices) for i in range(1, devices, 2)]
     return lax.ppermute(block, "wrap", pairs + [(j, i) for i, j in pairs])
 
 

time: 79 us -> 76 us (0.962)
  starting transfers between devices: 27.3 us -> 23.4 us
  waiting for transfers between devices: 22 us -> 23.2 us
    ppermute x12, waiting for transfers between devices: 15.1 us -> 18 us  [swap_mask(): lax.ppermute(block, 'wrap', [(i, i ^ mask) for i in range(lax.axis_size('...]
    ppermute x2, starting transfers between devices: 4.35 us -> 1.65 us  [swap_next(): return lax.ppermute(block, 'wrap', pairs + [(j, i) for i, j in pairs])]
    ppermute x2, waiting for transfers between devices: 6.93 us -> 5.17 us  [swap_next(): return lax.ppermute(block, 'wrap', pairs + [(j, i) for i, j in pairs])]
    ppermute x12, starting transfers between devices: 19.5 us -> 18.3 us  [swap_mask(): lax.ppermute(block, 'wrap', [(i, i ^ mask) for i in range(lax.axis_size('...]
  transfers between devices with their start and end apart: 16 -> 16, of which waited for: 10 -> 11; matrix products, arithmetic and copies ran while one was open for 0% -> 0% of each run, Pallas kernels for 0% -> 0%
where the time goes in v4:
time: 76 us; the launch traced here: 75.6 us
  Pallas kernels  24.9 us (33%)
  starting transfers between devices  23.4 us (31%)
  waiting for transfers between devices  23.2 us (31%)
  local copies, waits for them, and re-layouts  3.12 us (4%)
  between operations  0.78 us (1%)
    pallas_call x1, Pallas kernels, shards(): pl.pallas_call(main_kernel, out_shape=(field, field, field) + edges, in_s...  23.8 us
    ppermute x12, starting transfers between devices, swap_mask(): lax.ppermute(block, 'wrap', [(i, i ^ mask) for i in range(lax.axis_size('...  18.3 us
    ppermute x12, waiting for transfers between devices, swap_mask(): lax.ppermute(block, 'wrap', [(i, i ^ mask) for i in range(lax.axis_size('...  18 us
    ppermute x2, waiting for transfers between devices, swap_next(): return lax.ppermute(block, 'wrap', pairs + [(j, i) for i, j in pairs])  5.17 us
    ppermute x2, starting transfers between devices, swap_span(): return lax.ppermute(block, 'span', [(0, 1), (1, 0)])  3.53 us
    unnamed x20, local copies, waits for them, and re-layouts  2.99 us
    ppermute x2, starting transfers between devices, swap_next(): return lax.ppermute(block, 'wrap', pairs + [(j, i) for i, j in pairs])  1.65 us
  transfers between devices with their start and end apart: 16, of which 11 were waited for; matrix products, arithmetic and copies ran while one was open for 0% of the time, Pallas kernels for 0%

profile of v4, /device:TPU:32, one launch (start us, length us, event | category | flops | bytes accessed | tf_op | source)
XLA Modules:
  0.0 75.6 jit_solution(10152722966695522994)
XLA Ops:
  0.6 0.7 copy-done.3
  1.3 0.7 copy-done.4
  2.1 6.4 %collective-permute-start = (f32[16,128]{1,0:T(8,128)S(1)}, f32[16,128]{1,0:T(8,128)S(1)}, u32[]{:S(2)}, u32[]{:S(2)}) collective-permute-start(f32[16,128]{1,0:T(8,128)S(1)} %message.1), channel_id=1, source_target_pairs={{0,128},{2,130},{4,132},{6,134},{8,136},{10,138},{12,140},{14,142}... | collective-permute-start | bytes 24584 | tf_op jit(solution)/shard_map/ppermute | solution.py:272
  8.4 1.5 %collective-permute-start.1 = (f32[16,128]{1,0:T(8,128)S(1)}, f32[16,128]{1,0:T(8,128)S(1)}, u32[]{:S(2)}, u32[]{:S(2)}) collective-permute-start(f32[16,128]{1,0:T(8,128)S(1)} %message.1), channel_id=1, source_target_pairs={{0,64},{2,66},{4,68},{6,70},{8,72},{10,74},{12,76},{14,78},{16,80}... | collective-permute-start | bytes 24584 | tf_op jit(solution)/shard_map/ppermute | solution.py:272
  9.9 0.9 %copy-done = f32[32,8,128]{2,1,0:T(8,128)S(1)} copy-done((f32[32,8,128]{2,1,0:T(8,128)S(1)}, f32[32,8,128]{2,1,0:T(8,128)}, u32[]{:S(2)}) %copy-start) | copy-done | bytes 131096
  11.1 1.9 %collective-permute-done.1 = f32[16,128]{1,0:T(8,128)S(1)} collective-permute-done((f32[16,128]{1,0:T(8,128)S(1)}, f32[16,128]{1,0:T(8,128)S(1)}, u32[]{:S(2)}, u32[]{:S(2)}) %collective-permute-start.1) | collective-permute-done | bytes 8224 | tf_op jit(solution)/shard_map/ppermute | solution.py:272
  13.0 3.8 %collective-permute-done.2 = f32[24,128]{1,0:T(8,128)S(1)} collective-permute-done((f32[24,128]{1,0:T(8,128)S(1)}, f32[24,128]{1,0:T(8,128)S(1)}, u32[]{:S(2)}, u32[]{:S(2)}) %collective-permute-start.2) | collective-permute-done | bytes 12320 | tf_op jit(solution)/shard_map/ppermute | solution.py:272
  16.8 1.0 %collective-permute-start.3 = (f32[64,128]{1,0:T(8,128)S(1)}, f32[64,128]{1,0:T(8,128)S(1)}, u32[]{:S(2)}, u32[]{:S(2)}) collective-permute-start(f32[64,128]{1,0:T(8,128)S(1)} %pad_maximum_fusion.4), channel_id=1, source_target_pairs={{0,32},{2,34},{4,36},{6,38},{8,40},{10,42},{12,44},{14,46},{16,48}... | collective-permute-start | bytes 98312 | tf_op jit(solution)/shard_map/ppermute | solution.py:272
  17.8 1.5 %collective-permute-start.4 = (f32[64,128]{1,0:T(8,128)S(1)}, f32[64,128]{1,0:T(8,128)S(1)}, u32[]{:S(2)}, u32[]{:S(2)}) collective-permute-start(f32[64,128]{1,0:T(8,128)S(1)} %pad_maximum_fusion.4), channel_id=1, source_target_pairs={{0,16},{2,18},{4,20},{6,22},{8,24},{10,26},{12,28},{14,30},{16,0},... | collective-permute-start | bytes 98312 | tf_op jit(solution)/shard_map/ppermute | solution.py:272
  19.3 1.0 %collective-permute-start.5 = (f32[72,128]{1,0:T(8,128)S(1)}, f32[72,128]{1,0:T(8,128)S(1)}, u32[]{:S(2)}, u32[]{:S(2)}) collective-permute-start(f32[72,128]{1,0:T(8,128)S(1)} %pad_maximum_fusion.3), channel_id=1, source_target_pairs={{0,48},{2,50},{4,52},{6,54},{8,56},{10,58},{12,60},{14,62},{16,32}... | collective-permute-start | bytes 110600 | tf_op jit(solution)/shard_map/ppermute | solution.py:272
  20.7 1.0 %collective-permute-done.4 = f32[64,128]{1,0:T(8,128)S(1)} collective-permute-done((f32[64,128]{1,0:T(8,128)S(1)}, f32[64,128]{1,0:T(8,128)S(1)}, u32[]{:S(2)}, u32[]{:S(2)}) %collective-permute-start.4) | collective-permute-done | bytes 32800 | tf_op jit(solution)/shard_map/ppermute | solution.py:272
  21.8 2.4 %collective-permute-done.5 = f32[72,128]{1,0:T(8,128)S(1)} collective-permute-done((f32[72,128]{1,0:T(8,128)S(1)}, f32[72,128]{1,0:T(8,128)S(1)}, u32[]{:S(2)}, u32[]{:S(2)}) %collective-permute-start.5) | collective-permute-done | bytes 36896 | tf_op jit(solution)/shard_map/ppermute | solution.py:272
  24.2 3.1 %collective-permute-start.8 = (f32[264,128]{1,0:T(8,128)S(1)}, f32[264,128]{1,0:T(8,128)S(1)}, u32[]{:S(2)}, u32[]{:S(2)}) collective-permute-start(f32[264,128]{1,0:T(8,128)S(1)} %pad_maximum_fusion.2), channel_id=1, source_target_pairs={{0,12},{2,14},{4,8},{6,10},{8,4},{10,6},{12,0},{14,2},{16,28},{18,... | collective-permute-start | bytes 405512 | tf_op jit(solution)/shard_map/ppermute | solution.py:272
  28.4 2.7 %collective-permute-start.10 = (f32[32,128]{1,0:T(8,128)S(1)}, f32[32,128]{1,0:T(8,128)S(1)}, u32[]{:S(2)}, u32[]{:S(2)}) collective-permute-start(f32[32,128]{1,0:T(8,128)S(1)} %get-tuple-element.24), channel_id=1, source_target_pairs={{0,1},{1,0},{2,3},{3,2},{4,5},{5,4},{6,7},{7,6},{8,9},{9,8},{10,11... | collective-permute-start | bytes 49160 | tf_op jit(solution)/shard_map/ppermute | solution.py:282
  31.3 2.5 %collective-permute-done.6 = f32[256,128]{1,0:T(8,128)S(1)} collective-permute-done((f32[256,128]{1,0:T(8,128)S(1)}, f32[256,128]{1,0:T(8,128)S(1)}, u32[]{:S(2)}, u32[]{:S(2)}) %collective-permute-start.6) | collective-permute-done | bytes 131104 | tf_op jit(solution)/shard_map/ppermute | solution.py:272
  33.8 3.3 %collective-permute-done.9.next_ref = f32[8,128]{1,0:T(8,128)S(1)} collective-permute-done((f32[8,128]{1,0:T(8,128)S(1)}, f32[8,128]{1,0:T(8,128)S(1)}, u32[]{:S(2)}, u32[]{:S(2)}) %collective-permute-start.9) | collective-permute-done | bytes 4128 | tf_op jit(solution)/shard_map/ppermute | solution.py:278
  38.2 1.1 %collective-permute-done.11.other_ref = f32[1040,128]{1,0:T(8,128)S(1)} collective-permute-done((f32[1040,128]{1,0:T(8,128)S(1)}, f32[1040,128]{1,0:T(8,128)S(1)}, u32[]{:S(2)}, u32[]{:S(2)}) %collective-permute-start.11) | collective-permute-done | bytes 532512 | tf_op jit(solution)/shard_map/ppermute | solution.py:272
  39.3 23.8 %main.1 = (f32[32,8,128]{2,1,0:T(8,128)}, f32[32,8,128]{2,1,0:T(8,128)S(1)}, f32[32,8,128]{2,1,0:T(8,128)S(1)}, f32[8,128]{1,0:T(8,128)S(1)}, f32[8,128]{1,0:T(8...) custom-call(s32[2048]{0:T(1024)S(1)} %reshape.7.list_ref, f32[1024,128]{1,0:T(8,128)S(1)} %pad_maximum_fusion.1.own_ref, ...), custom_call_target="tpu_custom_call" | custom-call | flops 8589934592 | bytes 4194304 | tf_op jit(solution)/shard_map/main/pallas_call | solution.py:340
  63.0 0.8 %collective-permute-start.14 = (f32[32,128]{1,0:T(8,128)S(1)}, f32[32,128]{1,0:T(8,128)S(1)}, u32[]{:S(2)}, u32[]{:S(2)}) collective-permute-start(f32[32,128]{1,0:T(8,128)S(1)} %get-tuple-element.33), channel_id=1, source_target_pairs={{0,1},{1,0},{2,3},{3,2},{4,5},{5,4},{6,7},{7,6},{8,9},{9,8},{10,11... | collective-permute-start | bytes 49160 | tf_op jit(solution)/shard_map/ppermute | solution.py:282
  63.8 1.6 %collective-permute-start.13 = (f32[8,128]{1,0:T(8,128)S(1)}, f32[8,128]{1,0:T(8,128)S(1)}, u32[]{:S(2)}, u32[]{:S(2)}) collective-permute-start(f32[8,128]{1,0:T(8,128)S(1)} %get-tuple-element.32), channel_id=1, source_target_pairs={{2,4},{6,8},{10,12},{14,16},{18,20},{22,24},{26,28},{30,32},{34,36... | collective-permute-start | bytes 12296 | tf_op jit(solution)/shard_map/ppermute | solution.py:278
  65.5 2.6 %collective-permute-start.15 = (f32[8,128]{1,0:T(8,128)S(1)}, f32[8,128]{1,0:T(8,128)S(1)}, u32[]{:S(2)}, u32[]{:S(2)}) collective-permute-start(f32[8,128]{1,0:T(8,128)S(1)} %get-tuple-element.34), channel_id=1, source_target_pairs={{0,254},{2,252},{4,250},{6,248},{8,246},{10,244},{12,242},{14,240}... | collective-permute-start | bytes 12296 | tf_op jit(solution)/shard_map/ppermute | solution.py:272
  68.0 1.8 %collective-permute-done.13.next_ref = f32[8,128]{1,0:T(8,128)S(1)} collective-permute-done((f32[8,128]{1,0:T(8,128)S(1)}, f32[8,128]{1,0:T(8,128)S(1)}, u32[]{:S(2)}, u32[]{:S(2)}) %collective-permute-start.13) | collective-permute-done | bytes 4128 | tf_op jit(solution)/shard_map/ppermute | solution.py:278
  69.9 4.7 %collective-permute-done.15.column_ref = f32[8,128]{1,0:T(8,128)S(1)} collective-permute-done((f32[8,128]{1,0:T(8,128)S(1)}, f32[8,128]{1,0:T(8,128)S(1)}, u32[]{:S(2)}, u32[]{:S(2)}) %collective-permute-start.15) | collective-permute-done | bytes 4128 | tf_op jit(solution)/shard_map/ppermute | solution.py:272
  74.5 1.0 %last.1 = f32[32,8,128]{2,1,0:T(8,128)} custom-call(f32[32,8,128]{2,1,0:T(8,128)S(1)} %get-tuple-element.29.middle_ref, f32[32,8,128]{2,1,0:T(8,128)S(1)} %copy-done.1, f32[32,8,128]{2,1,0:T(8,128)S(1)} %get-tuple-element.30.squares_ref, f32[32,8,128]{2,1,0:T(8,128)S(1)} %copy-done.2, f32[8,128]{1,0:T(8,128)S(1)} %collective-permute-done.12.pair_ref, ...), custom_call_target="tpu_custom_call" | custom-call | tf_op jit(solution)/shard_map/last/pallas_call | solution.py:359
  (44 shorter events, 2.9 us)
Async XLA Ops:
  0.6 0.7 copy-start.3
  1.3 0.7 copy-start.4
  2.1 9.0 %collective-permute-start = (f32[16,128]{1,0:T(8,128)S(1)}, f32[16,128]{1,0:T(8,128)S(1)}, u32[]{:S(2)}, u32[]{:S(2)}) collective-permute-start(f32[16,128]{1,0:T(8,128)S(1)} %message.1), channel_id=1, source_target_pairs={{0,128},{2,130},{4,132},{6,134},{8,136},{10,138},{12,140},{14,142}... | collective-permute-start | bytes 24584 | tf_op jit(solution)/shard_map/ppermute | solution.py:272
  8.4 4.5 %collective-permute-start.1 = (f32[16,128]{1,0:T(8,128)S(1)}, f32[16,128]{1,0:T(8,128)S(1)}, u32[]{:S(2)}, u32[]{:S(2)}) collective-permute-start(f32[16,128]{1,0:T(8,128)S(1)} %message.1), channel_id=1, source_target_pairs={{0,64},{2,66},{4,68},{6,70},{8,72},{10,74},{12,76},{14,78},{16,80}... | collective-permute-start | bytes 24584 | tf_op jit(solution)/shard_map/ppermute | solution.py:272
  9.9 0.9 %copy-start = (f32[32,8,128]{2,1,0:T(8,128)S(1)}, f32[32,8,128]{2,1,0:T(8,128)}, u32[]{:S(2)}) copy-start(f32[32,8,128]{2,1,0:T(8,128)} %nu_ref.5) | copy-start | bytes 393220
  10.9 5.9 %collective-permute-start.2 = (f32[24,128]{1,0:T(8,128)S(1)}, f32[24,128]{1,0:T(8,128)S(1)}, u32[]{:S(2)}, u32[]{:S(2)}) collective-permute-start(f32[24,128]{1,0:T(8,128)S(1)} %pad_maximum_fusion.5), channel_id=1, source_target_pairs={{0,192},{2,194},{4,196},{6,198},{8,200},{10,202},{12,204},{14,206}... | collective-permute-start | bytes 36872 | tf_op jit(solution)/shard_map/ppermute | solution.py:272
  16.8 3.9 %collective-permute-start.3 = (f32[64,128]{1,0:T(8,128)S(1)}, f32[64,128]{1,0:T(8,128)S(1)}, u32[]{:S(2)}, u32[]{:S(2)}) collective-permute-start(f32[64,128]{1,0:T(8,128)S(1)} %pad_maximum_fusion.4), channel_id=1, source_target_pairs={{0,32},{2,34},{4,36},{6,38},{8,40},{10,42},{12,44},{14,46},{16,48}... | collective-permute-start | bytes 98312 | tf_op jit(solution)/shard_map/ppermute | solution.py:272
  17.8 3.9 %collective-permute-start.4 = (f32[64,128]{1,0:T(8,128)S(1)}, f32[64,128]{1,0:T(8,128)S(1)}, u32[]{:S(2)}, u32[]{:S(2)}) collective-permute-start(f32[64,128]{1,0:T(8,128)S(1)} %pad_maximum_fusion.4), channel_id=1, source_target_pairs={{0,16},{2,18},{4,20},{6,22},{8,24},{10,26},{12,28},{14,30},{16,0},... | collective-permute-start | bytes 98312 | tf_op jit(solution)/shard_map/ppermute | solution.py:272
  19.3 4.9 %collective-permute-start.5 = (f32[72,128]{1,0:T(8,128)S(1)}, f32[72,128]{1,0:T(8,128)S(1)}, u32[]{:S(2)}, u32[]{:S(2)}) collective-permute-start(f32[72,128]{1,0:T(8,128)S(1)} %pad_maximum_fusion.3), channel_id=1, source_target_pairs={{0,48},{2,50},{4,52},{6,54},{8,56},{10,58},{12,60},{14,62},{16,32}... | collective-permute-start | bytes 110600 | tf_op jit(solution)/shard_map/ppermute | solution.py:272
  24.2 7.1 %collective-permute-start.8 = (f32[264,128]{1,0:T(8,128)S(1)}, f32[264,128]{1,0:T(8,128)S(1)}, u32[]{:S(2)}, u32[]{:S(2)}) collective-permute-start(f32[264,128]{1,0:T(8,128)S(1)} %pad_maximum_fusion.2), channel_id=1, source_target_pairs={{0,12},{2,14},{4,8},{6,10},{8,4},{10,6},{12,0},{14,2},{16,28},{18,... | collective-permute-start | bytes 405512 | tf_op jit(solution)/shard_map/ppermute | solution.py:272
  27.3 6.5 %collective-permute-start.6 = (f32[256,128]{1,0:T(8,128)S(1)}, f32[256,128]{1,0:T(8,128)S(1)}, u32[]{:S(2)}, u32[]{:S(2)}) collective-permute-start(f32[256,128]{1,0:T(8,128)S(1)} %slice_dynamic-update-slice_fusion), channel_id=1, source_target_pairs={{0,8},{2,10},{4,12},{6,14},{8,0},{10,2},{12,4},{14,6},{16,24},{18,... | collective-permute-start | bytes 393224 | tf_op jit(solution)/shard_map/ppermute | solution.py:272
  27.9 5.8 %collective-permute-start.7 = (f32[256,128]{1,0:T(8,128)S(1)}, f32[256,128]{1,0:T(8,128)S(1)}, u32[]{:S(2)}, u32[]{:S(2)}) collective-permute-start(f32[256,128]{1,0:T(8,128)S(1)} %slice_dynamic-update-slice_fusion), channel_id=1, source_target_pairs={{0,4},{2,6},{4,0},{6,2},{8,12},{10,14},{12,8},{14,10},{16,20},{18,... | collective-permute-start | bytes 393224 | tf_op jit(solution)/shard_map/ppermute | solution.py:272
  28.4 8.8 %collective-permute-start.10 = (f32[32,128]{1,0:T(8,128)S(1)}, f32[32,128]{1,0:T(8,128)S(1)}, u32[]{:S(2)}, u32[]{:S(2)}) collective-permute-start(f32[32,128]{1,0:T(8,128)S(1)} %get-tuple-element.24), channel_id=1, source_target_pairs={{0,1},{1,0},{2,3},{3,2},{4,5},{5,4},{6,7},{7,6},{8,9},{9,8},{10,11... | collective-permute-start | bytes 49160 | tf_op jit(solution)/shard_map/ppermute | solution.py:282
  31.1 6.0 %collective-permute-start.9 = (f32[8,128]{1,0:T(8,128)S(1)}, f32[8,128]{1,0:T(8,128)S(1)}, u32[]{:S(2)}, u32[]{:S(2)}) collective-permute-start(f32[8,128]{1,0:T(8,128)S(1)} %get-tuple-element.23), channel_id=1, source_target_pairs={{2,4},{6,8},{10,12},{14,16},{18,20},{22,24},{26,28},{30,32},{34,36... | collective-permute-start | bytes 12296 | tf_op jit(solution)/shard_map/ppermute | solution.py:278
  37.2 0.8 %copy-start.6 = (s32[32,8,8]{0,2,1:T(8,128)S(1)}, s32[32,8,8]{0,2,1:T(8,128)}, u32[]{:S(2)}) copy-start(s32[32,8,8]{0,2,1:T(8,128)} %param.9) | copy-start | bytes 24580
  37.2 2.1 %copy-start.5 = (f32[3,32,8,128]{3,2,1,0:T(8,128)S(1)}, f32[3,32,8,128]{3,2,1,0:T(8,128)}, u32[]{:S(2)}) copy-start(f32[3,32,8,128]{3,2,1,0:T(8,128)} %cell_ref.1) | copy-start | bytes 1179652
  37.2 2.0 %copy-start.1 = (f32[32,8,128]{2,1,0:T(8,128)S(1)}, f32[32,8,128]{2,1,0:T(8,128)}, u32[]{:S(2)}) copy-start(f32[32,8,128]{2,1,0:T(8,128)} %nu_ref.5) | copy-start | bytes 393220
  37.2 2.0 %copy-start.2 = (f32[32,8,128]{2,1,0:T(8,128)S(1)}, f32[32,8,128]{2,1,0:T(8,128)}, u32[]{:S(2)}) copy-start(f32[32,8,128]{2,1,0:T(8,128)} %vorticity_ref.3) | copy-start | bytes 393220
  37.2 2.0 %collective-permute-start.11 = (f32[1040,128]{1,0:T(8,128)S(1)}, f32[1040,128]{1,0:T(8,128)S(1)}, u32[]{:S(2)}, u32[]{:S(2)}) collective-permute-start(f32[1040,128]{1,0:T(8,128)S(1)} %pad_maximum_fusion), channel_id=1, source_target_pairs={{0,2},{2,0},{4,6},{6,4},{8,10},{10,8},{12,14},{14,12},{16,18},{18,... | collective-permute-start | bytes 1597448 | tf_op jit(solution)/shard_map/ppermute | solution.py:272
  63.0 11.5 %collective-permute-start.14 = (f32[32,128]{1,0:T(8,128)S(1)}, f32[32,128]{1,0:T(8,128)S(1)}, u32[]{:S(2)}, u32[]{:S(2)}) collective-permute-start(f32[32,128]{1,0:T(8,128)S(1)} %get-tuple-element.33), channel_id=1, source_target_pairs={{0,1},{1,0},{2,3},{3,2},{4,5},{5,4},{6,7},{7,6},{8,9},{9,8},{10,11... | collective-permute-start | bytes 49160 | tf_op jit(solution)/shard_map/ppermute | solution.py:282
  63.8 4.2 %collective-permute-start.12 = (f32[8,128]{1,0:T(8,128)S(1)}, f32[8,128]{1,0:T(8,128)S(1)}, u32[]{:S(2)}, u32[]{:S(2)}) collective-permute-start(f32[8,128]{1,0:T(8,128)S(1)} %get-tuple-element.31), channel_id=1, source_target_pairs={{0,2},{2,0},{4,6},{6,4},{8,10},{10,8},{12,14},{14,12},{16,18},{18,... | collective-permute-start | bytes 12296 | tf_op jit(solution)/shard_map/ppermute | solution.py:272
  63.8 6.0 %collective-permute-start.13 = (f32[8,128]{1,0:T(8,128)S(1)}, f32[8,128]{1,0:T(8,128)S(1)}, u32[]{:S(2)}, u32[]{:S(2)}) collective-permute-start(f32[8,128]{1,0:T(8,128)S(1)} %get-tuple-element.32), channel_id=1, source_target_pairs={{2,4},{6,8},{10,12},{14,16},{18,20},{22,24},{26,28},{30,32},{34,36... | collective-permute-start | bytes 12296 | tf_op jit(solution)/shard_map/ppermute | solution.py:278
  65.5 9.0 %collective-permute-start.15 = (f32[8,128]{1,0:T(8,128)S(1)}, f32[8,128]{1,0:T(8,128)S(1)}, u32[]{:S(2)}, u32[]{:S(2)}) collective-permute-start(f32[8,128]{1,0:T(8,128)S(1)} %get-tuple-element.34), channel_id=1, source_target_pairs={{0,254},{2,252},{4,250},{6,248},{8,246},{10,244},{12,242},{14,240}... | collective-permute-start | bytes 12296 | tf_op jit(solution)/shard_map/ppermute | solution.py:272

commit v5 on v4

--- a/solution.py
+++ b/solution.py
@@ -12,7 +12,8 @@
 PBS = 128
 FEATS = 48
 LINES_PER_STEP = 32
-STAGES = ((6, 5), (4, 3), (2, 1), (0,))
+GROUP_BIT = 3
+Y_MASKS = (2, 6, 4)
 
 coef_cb1 = 0.1355
 coef_cb2 = 0.622
@@ -57,44 +58,44 @@
     return jnp.broadcast_to(value[:, 0:1], (8, 128))
 
 
-def message_kernel(xyz_hbm, size_hbm, message_ref, xyz_ref, size_ref, sems):
-    copies = [
-        pltpu.make_async_copy(xyz_hbm, xyz_ref, sems.at[0]),
-        pltpu.make_async_copy(size_hbm, size_ref, sems.at[1]),
-    ]
+def even_place():
+    return lax.rem(lax.axis_index("wrap"), 2) == 0
+
+
+def put_edges(first, last, pair_ref, next_ref):
+    pair_ref[...] = jnp.where(even_place(), last, first)
+    next_ref[...] = jnp.where(even_place(), first, last)
+
+
+def prep_kernel(
+    xyz_hbm, size_hbm, nu_hbm, chunks_ref, pair_ref, beside_ref, xyz_ref, size_ref, nu_ref, sems
+):
+    pairs = ((xyz_hbm, xyz_ref), (size_hbm, size_ref), (nu_hbm, nu_ref))
+    copies = [pltpu.make_async_copy(*pair, sems.at[n]) for n, pair in enumerate(pairs)]
     for copy in copies:
         copy.start()
     for copy in copies:
         copy.wait()
+    parts = []
     for block in range(size_ref.shape[1] // PBS):
         lanes = slice(block * PBS, (block + 1) * PBS)
         xyz = xyz_ref[:, lanes]
         size = size_ref[:, lanes]
-        offset = jnp.sum(xyz * xyz, axis=0, keepdims=True) + size * size
-        message_ref[block * 4 : block * 4 + 3, :] = xyz
-        message_ref[block * 4 + 3 : block * 4 + 4, :] = offset
-
-
-def even_place():
-    return lax.rem(lax.axis_index("wrap"), 2) == 0
-
-
-def put_edges(first, last, pair_ref, next_ref):
-    pair_ref[...] = jnp.where(even_place(), last, first)
-    next_ref[...] = jnp.where(even_place(), first, last)
-
-
-def edges_kernel(nu_ref, pair_ref, next_ref, beside_ref, column_ref):
+        parts += [xyz, jnp.sum(xyz * xyz, axis=0, keepdims=True) + size * size]
     low_span = lax.axis_index("span") == 0
     rows = nu_ref.shape[0]
-    put_edges(nu_ref[0], nu_ref[rows - 1], pair_ref, next_ref)
     lane = tile_iota(1)
     column = jnp.zeros((8, 128), F32)
     for row in range(rows):
         value = nu_ref[row]
         beside_ref[row : row + 1, :] = edge_row(value, low_span)
         column = jnp.where(lane == row, first_column(value), column)
-    column_ref[...] = column
+    first, last = nu_ref[0], nu_ref[rows - 1]
+    pair_ref[...] = jnp.where(even_place(), last, first)
+    parts += [column, jnp.where(even_place(), first, last)]
+    chunk = jnp.concatenate(parts, 0)
+    for n in range(chunks_ref.shape[0]):
+        chunks_ref[n] = chunk
 
 
 class Halo:
@@ -154,19 +155,21 @@
 
 def build_table(halves, table_ref):
     place = lax.axis_index("wrap")
-    order = [bit for bits in STAGES for bit in bits]
     own_blocks = table_ref.shape[0] // lax.axis_size("wrap")
-    slots = halves[0].shape[0] // (4 * own_blocks)
-    top = len(order) - 1
+    groups = lax.axis_size("wrap") >> GROUP_BIT
+    slots = groups * (len(Y_MASKS) + 1)
 
     def body(slot, carry):
+        choice = slot // groups
+        near = jnp.where(choice == 0, 0, Y_MASKS[0])
+        for n in range(1, len(Y_MASKS)):
+            near = jnp.where(choice == n + 1, Y_MASKS[n], near)
+        low = (place & ((1 << GROUP_BIT) - 1)) ^ near
+        skip = jnp.where(choice >= 2, 8, 0) + jnp.where(choice >= 3, 16, 0)
         for half, ref in enumerate(halves):
-            mask = half << order[top]
-            for n in range(top):
-                mask = mask | (((slot >> n) & 1) << order[n])
-            base = (place ^ mask) * own_blocks
+            base = (((slot % groups) << GROUP_BIT) | (low ^ half)) * own_blocks
             for pair in range(own_blocks // 2):
-                start = pl.multiple_of(slot * own_blocks * 4 + pair * 8, 8)
+                start = pl.multiple_of(slot * own_blocks * 4 + skip + pair * 8, 8)
                 rows = ref[pl.ds(start, 8), :]
                 table_ref[base + pair * 2] = panel_features(rows)
                 table_ref[base + pair * 2 + 1] = panel_features(pltpu.roll(rows, 4, 0))
@@ -208,7 +211,6 @@
     cell_ref,
     nu_ref,
     vorticity_ref,
-    next_ref,
     beside_ref,
     dist_ref,
     squares_ref,
@@ -221,10 +223,15 @@
     padded_ref,
     ghost_ref,
 ):
-    panel_rows = own_ref.shape[0]
-    column = other_ref[panel_rows : panel_rows + 8]
-    pair = other_ref[panel_rows + 8 : panel_rows + 16]
-    halo = Halo(nu_ref, pair, next_ref[...], beside_ref, column, padded_ref, ghost_ref)
+    place = lax.axis_index("wrap")
+    total = (other_ref.shape[0] - 32) // 4
+    in_first = (((place >> 1) + (place ^ 1)) & 1) == 0
+    first_edge = other_ref[2 * total : 2 * total + 8]
+    second_edge = other_ref[3 * total + 8 : 3 * total + 16]
+    after = jnp.where(in_first, first_edge, second_edge)
+    column = other_ref[3 * total + 16 : 3 * total + 24]
+    pair = other_ref[4 * total + 24 : 4 * total + 32]
+    halo = Halo(nu_ref, pair, after, beside_ref, column, padded_ref, ghost_ref)
     build_table((own_ref, other_ref), table_ref)
     tiles = nu_ref.shape[0]
     per_step = LINES_PER_STEP // 8
@@ -282,26 +289,27 @@
     return lax.ppermute(block, "span", [(0, 1), (1, 0)])
 
 
-def gather(shard, pair, after, beside, column):
-    size = shard.shape[0]
-    for stage, bits in enumerate(STAGES[:-1]):
-        if stage == len(STAGES) - 2:
-            shard, after, beside = lax.optimization_barrier((shard, after, beside))
-            after, beside = swap_next(after), swap_span(beside)
-        parts = [shard]
-        for choice in range(1, 1 << len(bits)):
-            mask = sum(((choice >> n) & 1) << bit for n, bit in enumerate(bits))
-            if choice == (1 << len(bits)) - 1:
-                both = swap_mask(jnp.concatenate([shard, column], 0), mask)
-                parts.append(both[:size])
-                column = both[size:]
-            else:
-                parts.append(swap_mask(shard, mask))
-        shard = jnp.concatenate(parts, 0)
-        size = shard.shape[0]
-    shard, after, beside = lax.optimization_barrier((shard, after, beside))
-    other = swap_mask(jnp.concatenate([shard, column, pair], 0), 1 << STAGES[-1][0])
-    return shard, other, after, beside
+def gather(chunks, pair, beside):
+    devices = lax.axis_size("wrap")
+    place = lax.axis_index("wrap")
+    groups, rows, lanes = chunks.shape
+    size = rows - 16
+    members = [[low + (n << GROUP_BIT) for n in range(groups)] for low in range(devices // groups)]
+    chunks = lax.all_to_all(chunks, "wrap", 0, 0, tiled=True, axis_index_groups=members)
+    chunks, beside = lax.optimization_barrier((chunks, beside))
+    beside = swap_span(beside)
+    shard = chunks[:, :size].reshape(groups * size, lanes)
+    group, y, core = place >> GROUP_BIT, (place >> 1) & 3, place & 1
+    column = lax.dynamic_slice(chunks, (groups - 1 - group, size, 0), (1, 8, lanes))[0]
+    step = jnp.where(core == 1, jnp.where(y == 3, -1, 0), jnp.where(y == 0, 1, 0))
+    source = (group + step) & (groups - 1)
+    after = lax.dynamic_slice(chunks, (source, size + 8, 0), (1, 8, lanes))[0]
+    first = swap_mask(jnp.concatenate([shard, after], 0), Y_MASKS[0])
+    second = swap_mask(jnp.concatenate([shard, after, column], 0), Y_MASKS[1])
+    third = swap_mask(shard, Y_MASKS[2])
+    shard = jnp.concatenate([shard, first, second, third, pair], 0)
+    shard, beside = lax.optimization_barrier((shard, beside))
+    return shard, swap_mask(shard, 1), beside
 
 
 def shards(cell_xyz, panel_xyz, panel_size, block_lists, nu_field, vorticity):
@@ -314,33 +322,27 @@
     edges = (tile, tile, side, tile)
     scratch = [pltpu.VMEM((rows + 2, span, cells), F32), pltpu.VMEM(nu_field.shape, F32)]
 
-    message = pl.pallas_call(
-        message_kernel,
-        out_shape=jax.ShapeDtypeStruct((4 * own_blocks, PBS), F32),
-        in_specs=[pl.BlockSpec(memory_space=pltpu.HBM)] * 2,
-        out_specs=VMEM,
+    groups = devices >> GROUP_BIT
+    chunks, pair, beside = pl.pallas_call(
+        prep_kernel,
+        out_shape=(jax.ShapeDtypeStruct((groups, 4 * own_blocks + 16, PBS), F32), tile, side),
+        in_specs=[pl.BlockSpec(memory_space=pltpu.HBM)] * 3,
+        out_specs=(VMEM,) * 3,
         scratch_shapes=[
             pltpu.VMEM(panel_xyz.shape, F32),
             pltpu.VMEM((1,) + panel_size.shape, F32),
-            pltpu.SemaphoreType.DMA((2,)),
+            pltpu.VMEM(nu_field.shape, F32),
+            pltpu.SemaphoreType.DMA((3,)),
         ],
-        compiler_params=pltpu.CompilerParams(vmem_limit_bytes=2**20),
-        name="message",
-    )(panel_xyz, panel_size[None])
-    sent = pl.pallas_call(
-        edges_kernel,
-        out_shape=edges,
-        in_specs=[VMEM],
-        out_specs=(VMEM,) * 4,
-        compiler_params=pltpu.CompilerParams(vmem_limit_bytes=4 * 2**20),
-        name="edges",
-    )(nu_field)
-    own, other, after, beside = gather(message, *sent)
+        compiler_params=pltpu.CompilerParams(vmem_limit_bytes=60 * 2**20),
+        name="prep",
+    )(panel_xyz, panel_size[None], nu_field)
+    own, other, beside = gather(chunks, pair, beside)
 
     dist, squares, middle, pair, next_pair, sides, column = pl.pallas_call(
         main_kernel,
         out_shape=(field, field, field) + edges,
-        in_specs=[SMEM] + [VMEM] * 7,
+        in_specs=[SMEM] + [VMEM] * 6,
         out_specs=(VMEM,) * 7,
         scratch_shapes=[pltpu.VMEM((devices * own_blocks, FEATS, PBS), BF)] + scratch,
         compiler_params=pltpu.CompilerParams(vmem_limit_bytes=24 * 2**20),
@@ -350,7 +352,7 @@
             transcendentals=0,
         ),
         name="main",
-    )(block_lists.reshape(-1), own, other, cell_xyz, nu_field, vorticity, after, beside)
+    )(block_lists.reshape(-1), own, other, cell_xyz, nu_field, vorticity, beside)
     column = swap_mask(column, devices - 1)
     next_pair = swap_next(next_pair)
     sides = swap_span(sides)

time: 76 us -> 74.9 us (0.986)
  waiting for transfers between devices: 23.2 us -> 20.7 us
  Pallas kernels: 24.9 us -> 26.9 us
  local copies, waits for them, and re-layouts: 3.12 us -> 1.17 us
  starting transfers between devices: 23.4 us -> 25 us
    all_to_all x0 -> x1, waiting for transfers between devices: none -> 10.6 us  [gather(): lax.all_to_all(chunks, 'wrap', 0, 0, tiled=True, axis_index_groups=members)]
    ppermute x12 -> x6, starting transfers between devices: 18.3 us -> 8.19 us  [swap_mask(): lax.ppermute(block, 'wrap', [(i, i ^ mask) for i in range(lax.axis_size('...]
    all_to_all x0 -> x1, starting transfers between devices: none -> 9.53 us  [gather(): lax.all_to_all(chunks, 'wrap', 0, 0, tiled=True, axis_index_groups=members)]
    ppermute x12 -> x6, waiting for transfers between devices: 18 us -> 9.42 us  [swap_mask(): lax.ppermute(block, 'wrap', [(i, i ^ mask) for i in range(lax.axis_size('...]
    ppermute x2 -> x1, waiting for transfers between devices: 5.17 us -> 0.63 us  [swap_next(): return lax.ppermute(block, 'wrap', pairs + [(j, i) for i, j in pairs])]
    unnamed x20 -> x17, local copies, waits for them, and re-layouts: 2.99 us -> 1.05 us
    ppermute x2, starting transfers between devices: 3.53 us -> 5.46 us  [swap_span(): return lax.ppermute(block, 'span', [(0, 1), (1, 0)])]
    pallas_call x2 -> x1, Pallas kernels: 0.13 us -> 1.76 us  [shards(): pl.pallas_call(prep_kernel, out_shape=(jax.ShapeDtypeStruct((groups, 4 *...]
  transfers between devices with their start and end apart: 16 -> 10, of which waited for: 11 -> 6; matrix products, arithmetic and copies ran while one was open for 0% -> 0% of each run, Pallas kernels for 0% -> 0%
where the time goes in v5:
time: 74.9 us; the launch traced here: 74.5 us
  Pallas kernels  26.9 us (36%)
  starting transfers between devices  25 us (33%)
  waiting for transfers between devices  20.7 us (28%)
  local copies, waits for them, and re-layouts  1.17 us (2%)
  between operations  0.75 us (1%)
    pallas_call x1, Pallas kernels, shards(): pl.pallas_call(main_kernel, out_shape=(field, field, field) + edges, in_s...  24.1 us
    all_to_all x1, waiting for transfers between devices, gather(): lax.all_to_all(chunks, 'wrap', 0, 0, tiled=True, axis_index_groups=members)  10.6 us
    all_to_all x1, starting transfers between devices, gather(): lax.all_to_all(chunks, 'wrap', 0, 0, tiled=True, axis_index_groups=members)  9.53 us
    ppermute x6, waiting for transfers between devices, swap_mask(): lax.ppermute(block, 'wrap', [(i, i ^ mask) for i in range(lax.axis_size('...  9.42 us
    ppermute x6, starting transfers between devices, swap_mask(): lax.ppermute(block, 'wrap', [(i, i ^ mask) for i in range(lax.axis_size('...  8.19 us
    ppermute x2, starting transfers between devices, swap_span(): return lax.ppermute(block, 'span', [(0, 1), (1, 0)])  5.46 us
    ppermute x1, starting transfers between devices, swap_next(): return lax.ppermute(block, 'wrap', pairs + [(j, i) for i, j in pairs])  1.84 us
    pallas_call x1, Pallas kernels, shards(): pl.pallas_call(prep_kernel, out_shape=(jax.ShapeDtypeStruct((groups, 4 *...  1.76 us
  transfers between devices with their start and end apart: 10, of which 6 were waited for; matrix products, arithmetic and copies ran while one was open for 0% of the time, Pallas kernels for 0%

profile of v5, /device:TPU:32, one launch (start us, length us, event | category | flops | bytes accessed | tf_op | source)
XLA Modules:
  0.0 74.5 jit_solution(17881595881936865931)
XLA Ops:
  0.6 1.8 %prep.1 = (f32[16,32,128]{2,1,0:T(8,128)}, f32[8,128]{1,0:T(8,128)}, f32[32,128]{1,0:T(8,128)}) custom-call(f32[3,512]{1,0:T(4,128)} %xyz_hbm.1, f32[1,512]{1,0:T(1,128)} %bitcast.10, f32[32,8,128]{2,1,0:T(8,128)} %nu_ref.3), custom_call_target="tpu_custom_call" | custom-call | tf_op jit(solution)/shard_map/prep/pallas_call | solution.py:326
  2.4 9.5 %all-to-all-start = ((f32[16,32,128]{2,1,0:T(8,128)}), f32[16,32,128]{2,1,0:T(8,128)S(1)}, u32[]{:S(2)}, u32[]{:S(2)}) async-start(f32[16,32,128]{2,1,0:T(8,128)} %get-tuple-element.16), calls=%async_computation | async-start | bytes 524288 | tf_op jit(solution)/shard_map/all_to_all | solution.py:298
  11.9 10.6 %all-to-all-done = f32[16,32,128]{2,1,0:T(8,128)S(1)} async-done(((f32[16,32,128]{2,1,0:T(8,128)}), f32[16,32,128]{2,1,0:T(8,128)S(1)}, u32[]{:S(2)}, u32[]{:S(2)}) %all-to-all-start) | async-done | bytes 262176 | tf_op jit(solution)/shard_map/all_to_all | solution.py:298
  22.6 3.3 %collective-permute-start.2 = (f32[256,128]{1,0:T(8,128)S(1)}, f32[256,128]{1,0:T(8,128)S(1)}, u32[]{:S(2)}, u32[]{:S(2)}) collective-permute-start(f32[256,128]{1,0:T(8,128)S(1)} %bitcast.6), channel_id=1, source_target_pairs={{0,8},{2,10},{4,12},{6,14},{8,0},{10,2},{12,4},{14,6},{16,24},{18,... | collective-permute-start | bytes 393224 | tf_op jit(solution)/shard_map/ppermute | solution.py:279
  25.9 0.8 %collective-permute-start = (f32[264,128]{1,0:T(8,128)S(1)}, f32[264,128]{1,0:T(8,128)S(1)}, u32[]{:S(2)}, u32[]{:S(2)}) collective-permute-start(f32[264,128]{1,0:T(8,128)S(1)} %pad_maximum_fusion.1), channel_id=1, source_target_pairs={{0,4},{2,6},{4,0},{6,2},{8,12},{10,14},{12,8},{14,10},{16,20},{18,... | collective-permute-start | bytes 405512 | tf_op jit(solution)/shard_map/ppermute | solution.py:279
  26.6 0.0 copy-start.5
  26.6 0.5 collective-permute-start.1
  27.1 0.2 copy-done.5
  27.4 2.7 %collective-permute-start.3 = (f32[32,128]{1,0:T(8,128)S(1)}, f32[32,128]{1,0:T(8,128)S(1)}, u32[]{:S(2)}, u32[]{:S(2)}) collective-permute-start(f32[32,128]{1,0:T(8,128)S(1)} %copy-done.5), channel_id=1, source_target_pairs={{0,1},{1,0},{2,3},{3,2},{4,5},{5,4},{6,7},{7,6},{8,9},{9,8},{10,11... | collective-permute-start | bytes 49160 | tf_op jit(solution)/shard_map/ppermute | solution.py:289
  30.1 0.9 %collective-permute-done = f32[264,128]{1,0:T(8,128)S(1)} collective-permute-done((f32[264,128]{1,0:T(8,128)S(1)}, f32[264,128]{1,0:T(8,128)S(1)}, u32[]{:S(2)}, u32[]{:S(2)}) %collective-permute-start) | collective-permute-done | bytes 135200 | tf_op jit(solution)/shard_map/ppermute | solution.py:279
  31.0 2.0 %collective-permute-done.1 = f32[272,128]{1,0:T(8,128)S(1)} collective-permute-done((f32[272,128]{1,0:T(8,128)S(1)}, f32[272,128]{1,0:T(8,128)S(1)}, u32[]{:S(2)}, u32[]{:S(2)}) %collective-permute-start.1) | collective-permute-done | bytes 139296 | tf_op jit(solution)/shard_map/ppermute | solution.py:279
  33.0 0.0 copy-start.4
  33.1 0.7 copy-done.4
  33.7 0.1 collective-permute-start.4
  33.8 0.1 copy.8
  34.0 0.1 reshape.10.list_ref
  34.1 1.7 %collective-permute-done.4.other_ref = f32[1056,128]{1,0:T(8,128)S(1)} collective-permute-done((f32[1056,128]{1,0:T(8,128)S(1)}, f32[1056,128]{1,0:T(8,128)S(1)}, u32[]{:S(2)}, u32[]{:S(2)}) %collective-permute-start.4) | collective-permute-done | bytes 540704 | tf_op jit(solution)/shard_map/ppermute | solution.py:279
  35.8 24.1 %main.1 = (f32[32,8,128]{2,1,0:T(8,128)}, f32[32,8,128]{2,1,0:T(8,128)S(1)}, f32[32,8,128]{2,1,0:T(8,128)S(1)}, f32[8,128]{1,0:T(8,128)S(1)}, f32[8,128]{1,0:T(8...) custom-call(s32[2048]{0:T(1024)S(1)} %reshape.10.list_ref, ...), custom_call_target="tpu_custom_call" | custom-call | flops 8589934592 | bytes 4194304 | tf_op jit(solution)/shard_map/main/pallas_call | solution.py:342
  59.9 2.7 %collective-permute-start.7 = (f32[32,128]{1,0:T(8,128)S(1)}, f32[32,128]{1,0:T(8,128)S(1)}, u32[]{:S(2)}, u32[]{:S(2)}) collective-permute-start(f32[32,128]{1,0:T(8,128)S(1)} %get-tuple-element.27), channel_id=1, source_target_pairs={{0,1},{1,0},{2,3},{3,2},{4,5},{5,4},{6,7},{7,6},{8,9},{9,8},{10,11... | collective-permute-start | bytes 49160 | tf_op jit(solution)/shard_map/ppermute | solution.py:289
  62.6 1.8 %collective-permute-start.6 = (f32[8,128]{1,0:T(8,128)S(1)}, f32[8,128]{1,0:T(8,128)S(1)}, u32[]{:S(2)}, u32[]{:S(2)}) collective-permute-start(f32[8,128]{1,0:T(8,128)S(1)} %get-tuple-element.26), channel_id=1, source_target_pairs={{2,4},{6,8},{10,12},{14,16},{18,20},{22,24},{26,28},{30,32},{34,36... | collective-permute-start | bytes 12296 | tf_op jit(solution)/shard_map/ppermute | solution.py:285
  64.4 3.6 %collective-permute-start.8 = (f32[8,128]{1,0:T(8,128)S(1)}, f32[8,128]{1,0:T(8,128)S(1)}, u32[]{:S(2)}, u32[]{:S(2)}) collective-permute-start(f32[8,128]{1,0:T(8,128)S(1)} %get-tuple-element.28), channel_id=1, source_target_pairs={{0,254},{2,252},{4,250},{6,248},{8,246},{10,244},{12,242},{14,240}... | collective-permute-start | bytes 12296 | tf_op jit(solution)/shard_map/ppermute | solution.py:279
  68.0 0.6 collective-permute-done.6.next_ref
  68.6 4.8 %collective-permute-done.8.column_ref = f32[8,128]{1,0:T(8,128)S(1)} collective-permute-done((f32[8,128]{1,0:T(8,128)S(1)}, f32[8,128]{1,0:T(8,128)S(1)}, u32[]{:S(2)}, u32[]{:S(2)}) %collective-permute-start.8) | collective-permute-done | bytes 4128 | tf_op jit(solution)/shard_map/ppermute | solution.py:279
  73.5 1.0 %last.1 = f32[32,8,128]{2,1,0:T(8,128)} custom-call(f32[32,8,128]{2,1,0:T(8,128)S(1)} %get-tuple-element.23.middle_ref, f32[32,8,128]{2,1,0:T(8,128)S(1)} %copy-done, f32[32,8,128]{2,1,0:T(8,128)S(1)} %get-tuple-element.24.squares_ref, f32[32,8,128]{2,1,0:T(8,128)S(1)} %copy-done.1, f32[8,128]{1,0:T(8,128)S(1)} %collective-permute-done.5.pair_ref, ...), custom_call_target="tpu_custom_call" | custom-call | tf_op jit(solution)/shard_map/last/pallas_call | solution.py:361
  (22 shorter events, 0.1 us)
Async XLA Ops:
  2.4 20.1 %all-to-all-start = ((f32[16,32,128]{2,1,0:T(8,128)}), f32[16,32,128]{2,1,0:T(8,128)S(1)}, u32[]{:S(2)}, u32[]{:S(2)}) async-start(f32[16,32,128]{2,1,0:T(8,128)} %get-tuple-element.16), calls=%async_computation | async-start | bytes 524288 | tf_op jit(solution)/shard_map/all_to_all | solution.py:298
  22.6 10.5 %collective-permute-start.2 = (f32[256,128]{1,0:T(8,128)S(1)}, f32[256,128]{1,0:T(8,128)S(1)}, u32[]{:S(2)}, u32[]{:S(2)}) collective-permute-start(f32[256,128]{1,0:T(8,128)S(1)} %bitcast.6), channel_id=1, source_target_pairs={{0,8},{2,10},{4,12},{6,14},{8,0},{10,2},{12,4},{14,6},{16,24},{18,... | collective-permute-start | bytes 393224 | tf_op jit(solution)/shard_map/ppermute | solution.py:279
  25.9 5.1 %collective-permute-start = (f32[264,128]{1,0:T(8,128)S(1)}, f32[264,128]{1,0:T(8,128)S(1)}, u32[]{:S(2)}, u32[]{:S(2)}) collective-permute-start(f32[264,128]{1,0:T(8,128)S(1)} %pad_maximum_fusion.1), channel_id=1, source_target_pairs={{0,4},{2,6},{4,0},{6,2},{8,12},{10,14},{12,8},{14,10},{16,20},{18,... | collective-permute-start | bytes 405512 | tf_op jit(solution)/shard_map/ppermute | solution.py:279
  26.6 0.7 copy-start.5
  26.6 6.4 %collective-permute-start.1 = (f32[272,128]{1,0:T(8,128)S(1)}, f32[272,128]{1,0:T(8,128)S(1)}, u32[]{:S(2)}, u32[]{:S(2)}) collective-permute-start(f32[272,128]{1,0:T(8,128)S(1)} %pad_maximum_fusion), channel_id=1, source_target_pairs={{0,12},{2,14},{4,8},{6,10},{8,4},{10,6},{12,0},{14,2},{16,28},{18,... | collective-permute-start | bytes 417800 | tf_op jit(solution)/shard_map/ppermute | solution.py:279
  27.4 6.4 %collective-permute-start.3 = (f32[32,128]{1,0:T(8,128)S(1)}, f32[32,128]{1,0:T(8,128)S(1)}, u32[]{:S(2)}, u32[]{:S(2)}) collective-permute-start(f32[32,128]{1,0:T(8,128)S(1)} %copy-done.5), channel_id=1, source_target_pairs={{0,1},{1,0},{2,3},{3,2},{4,5},{5,4},{6,7},{7,6},{8,9},{9,8},{10,11... | collective-permute-start | bytes 49160 | tf_op jit(solution)/shard_map/ppermute | solution.py:289
  31.0 4.8 %copy-start.2 = (f32[3,32,8,128]{3,2,1,0:T(8,128)S(1)}, f32[3,32,8,128]{3,2,1,0:T(8,128)}, u32[]{:S(2)}) copy-start(f32[3,32,8,128]{3,2,1,0:T(8,128)} %cell_ref.1) | copy-start | bytes 1179652
  33.0 0.8 %copy-start.3 = (s32[32,8,8]{0,2,1:T(8,128)S(1)}, s32[32,8,8]{0,2,1:T(8,128)}, u32[]{:S(2)}) copy-start(s32[32,8,8]{0,2,1:T(8,128)} %param.9) | copy-start | bytes 24580
  33.0 0.7 copy-start.4
  33.7 2.0 %copy-start = (f32[32,8,128]{2,1,0:T(8,128)S(1)}, f32[32,8,128]{2,1,0:T(8,128)}, u32[]{:S(2)}) copy-start(f32[32,8,128]{2,1,0:T(8,128)} %nu_ref.3) | copy-start | bytes 393220
  33.7 2.0 %copy-start.1 = (f32[32,8,128]{2,1,0:T(8,128)S(1)}, f32[32,8,128]{2,1,0:T(8,128)}, u32[]{:S(2)}) copy-start(f32[32,8,128]{2,1,0:T(8,128)} %vorticity_ref.3) | copy-start | bytes 393220
  33.7 2.0 %collective-permute-start.4 = (f32[1056,128]{1,0:T(8,128)S(1)}, f32[1056,128]{1,0:T(8,128)S(1)}, u32[]{:S(2)}, u32[]{:S(2)}) collective-permute-start(f32[1056,128]{1,0:T(8,128)S(1)} %constant_dynamic-update-slice_fusion.own_ref), channel_id=1, source_target_pairs={{0,2},{2,0},{4,6},{6,4},{8,10},{10,8},{12,14},{14,12},{16,18},{18,... | collective-permute-start | bytes 1622024 | tf_op jit(solution)/shard_map/ppermute | solution.py:279
  59.9 13.6 %collective-permute-start.7 = (f32[32,128]{1,0:T(8,128)S(1)}, f32[32,128]{1,0:T(8,128)S(1)}, u32[]{:S(2)}, u32[]{:S(2)}) collective-permute-start(f32[32,128]{1,0:T(8,128)S(1)} %get-tuple-element.27), channel_id=1, source_target_pairs={{0,1},{1,0},{2,3},{3,2},{4,5},{5,4},{6,7},{7,6},{8,9},{9,8},{10,11... | collective-permute-start | bytes 49160 | tf_op jit(solution)/shard_map/ppermute | solution.py:289
  62.6 5.4 %collective-permute-start.5 = (f32[8,128]{1,0:T(8,128)S(1)}, f32[8,128]{1,0:T(8,128)S(1)}, u32[]{:S(2)}, u32[]{:S(2)}) collective-permute-start(f32[8,128]{1,0:T(8,128)S(1)} %get-tuple-element.25), channel_id=1, source_target_pairs={{0,2},{2,0},{4,6},{6,4},{8,10},{10,8},{12,14},{14,12},{16,18},{18,... | collective-permute-start | bytes 12296 | tf_op jit(solution)/shard_map/ppermute | solution.py:279
  62.6 6.0 %collective-permute-start.6 = (f32[8,128]{1,0:T(8,128)S(1)}, f32[8,128]{1,0:T(8,128)S(1)}, u32[]{:S(2)}, u32[]{:S(2)}) collective-permute-start(f32[8,128]{1,0:T(8,128)S(1)} %get-tuple-element.26), channel_id=1, source_target_pairs={{2,4},{6,8},{10,12},{14,16},{18,20},{22,24},{26,28},{30,32},{34,36... | collective-permute-start | bytes 12296 | tf_op jit(solution)/shard_map/ppermute | solution.py:285
  64.4 9.0 %collective-permute-start.8 = (f32[8,128]{1,0:T(8,128)S(1)}, f32[8,128]{1,0:T(8,128)S(1)}, u32[]{:S(2)}, u32[]{:S(2)}) collective-permute-start(f32[8,128]{1,0:T(8,128)S(1)} %get-tuple-element.28), channel_id=1, source_target_pairs={{0,254},{2,252},{4,250},{6,248},{8,246},{10,244},{12,242},{14,240}... | collective-permute-start | bytes 12296 | tf_op jit(solution)/shard_map/ppermute | solution.py:279

commit v6 on v5

--- a/solution.py
+++ b/solution.py
@@ -68,7 +68,17 @@
 
 
 def prep_kernel(
-    xyz_hbm, size_hbm, nu_hbm, chunks_ref, pair_ref, beside_ref, xyz_ref, size_ref, nu_ref, sems
+    xyz_hbm,
+    size_hbm,
+    nu_hbm,
+    chunks_ref,
+    pair_ref,
+    next_ref,
+    beside_ref,
+    xyz_ref,
+    size_ref,
+    nu_ref,
+    sems,
 ):
     pairs = ((xyz_hbm, xyz_ref), (size_hbm, size_ref), (nu_hbm, nu_ref))
     copies = [pltpu.make_async_copy(*pair, sems.at[n]) for n, pair in enumerate(pairs)]
@@ -90,10 +100,8 @@
         value = nu_ref[row]
         beside_ref[row : row + 1, :] = edge_row(value, low_span)
         column = jnp.where(lane == row, first_column(value), column)
-    first, last = nu_ref[0], nu_ref[rows - 1]
-    pair_ref[...] = jnp.where(even_place(), last, first)
-    parts += [column, jnp.where(even_place(), first, last)]
-    chunk = jnp.concatenate(parts, 0)
+    put_edges(nu_ref[0], nu_ref[rows - 1], pair_ref, next_ref)
+    chunk = jnp.concatenate(parts + [column], 0)
     for n in range(chunks_ref.shape[0]):
         chunks_ref[n] = chunk
 
@@ -165,7 +173,7 @@
         for n in range(1, len(Y_MASKS)):
             near = jnp.where(choice == n + 1, Y_MASKS[n], near)
         low = (place & ((1 << GROUP_BIT) - 1)) ^ near
-        skip = jnp.where(choice >= 2, 8, 0) + jnp.where(choice >= 3, 16, 0)
+        skip = jnp.where(choice == 3, 8, 0)
         for half, ref in enumerate(halves):
             base = (((slot % groups) << GROUP_BIT) | (low ^ half)) * own_blocks
             for pair in range(own_blocks // 2):
@@ -211,6 +219,7 @@
     cell_ref,
     nu_ref,
     vorticity_ref,
+    next_ref,
     beside_ref,
     dist_ref,
     squares_ref,
@@ -223,15 +232,10 @@
     padded_ref,
     ghost_ref,
 ):
-    place = lax.axis_index("wrap")
-    total = (other_ref.shape[0] - 32) // 4
-    in_first = (((place >> 1) + (place ^ 1)) & 1) == 0
-    first_edge = other_ref[2 * total : 2 * total + 8]
-    second_edge = other_ref[3 * total + 8 : 3 * total + 16]
-    after = jnp.where(in_first, first_edge, second_edge)
-    column = other_ref[3 * total + 16 : 3 * total + 24]
-    pair = other_ref[4 * total + 24 : 4 * total + 32]
-    halo = Halo(nu_ref, pair, after, beside_ref, column, padded_ref, ghost_ref)
+    total = (other_ref.shape[0] - 16) // 4
+    column = other_ref[3 * total : 3 * total + 8]
+    pair = other_ref[4 * total + 8 : 4 * total + 16]
+    halo = Halo(nu_ref, pair, next_ref[...], beside_ref, column, padded_ref, ghost_ref)
     build_table((own_ref, other_ref), table_ref)
     tiles = nu_ref.shape[0]
     per_step = LINES_PER_STEP // 8
@@ -289,27 +293,21 @@
     return lax.ppermute(block, "span", [(0, 1), (1, 0)])
 
 
-def gather(chunks, pair, beside):
+def gather(chunks, pair, after, beside):
     devices = lax.axis_size("wrap")
-    place = lax.axis_index("wrap")
     groups, rows, lanes = chunks.shape
-    size = rows - 16
+    size = rows - 8
     members = [[low + (n << GROUP_BIT) for n in range(groups)] for low in range(devices // groups)]
     chunks = lax.all_to_all(chunks, "wrap", 0, 0, tiled=True, axis_index_groups=members)
-    chunks, beside = lax.optimization_barrier((chunks, beside))
-    beside = swap_span(beside)
+    chunks, after, beside = lax.optimization_barrier((chunks, swap_next(after), swap_span(beside)))
     shard = chunks[:, :size].reshape(groups * size, lanes)
-    group, y, core = place >> GROUP_BIT, (place >> 1) & 3, place & 1
-    column = lax.dynamic_slice(chunks, (groups - 1 - group, size, 0), (1, 8, lanes))[0]
-    step = jnp.where(core == 1, jnp.where(y == 3, -1, 0), jnp.where(y == 0, 1, 0))
-    source = (group + step) & (groups - 1)
-    after = lax.dynamic_slice(chunks, (source, size + 8, 0), (1, 8, lanes))[0]
-    first = swap_mask(jnp.concatenate([shard, after], 0), Y_MASKS[0])
-    second = swap_mask(jnp.concatenate([shard, after, column], 0), Y_MASKS[1])
+    opposite = groups - 1 - (lax.axis_index("wrap") >> GROUP_BIT)
+    column = lax.dynamic_slice(chunks, (opposite, size, 0), (1, 8, lanes))[0]
+    first = swap_mask(shard, Y_MASKS[0])
+    second = swap_mask(jnp.concatenate([shard, column], 0), Y_MASKS[1])
     third = swap_mask(shard, Y_MASKS[2])
     shard = jnp.concatenate([shard, first, second, third, pair], 0)
-    shard, beside = lax.optimization_barrier((shard, beside))
-    return shard, swap_mask(shard, 1), beside
+    return shard, swap_mask(shard, 1), after, beside
 
 
 def shards(cell_xyz, panel_xyz, panel_size, block_lists, nu_field, vorticity):
@@ -323,11 +321,11 @@
     scratch = [pltpu.VMEM((rows + 2, span, cells), F32), pltpu.VMEM(nu_field.shape, F32)]
 
     groups = devices >> GROUP_BIT
-    chunks, pair, beside = pl.pallas_call(
+    chunks, pair, after, beside = pl.pallas_call(
         prep_kernel,
-        out_shape=(jax.ShapeDtypeStruct((groups, 4 * own_blocks + 16, PBS), F32), tile, side),
+        out_shape=(jax.ShapeDtypeStruct((groups, 4 * own_blocks + 8, PBS), F32), tile, tile, side),
         in_specs=[pl.BlockSpec(memory_space=pltpu.HBM)] * 3,
-        out_specs=(VMEM,) * 3,
+        out_specs=(VMEM,) * 4,
         scratch_shapes=[
             pltpu.VMEM(panel_xyz.shape, F32),
             pltpu.VMEM((1,) + panel_size.shape, F32),
@@ -337,12 +335,12 @@
         compiler_params=pltpu.CompilerParams(vmem_limit_bytes=60 * 2**20),
         name="prep",
     )(panel_xyz, panel_size[None], nu_field)
-    own, other, beside = gather(chunks, pair, beside)
+    own, other, after, beside = gather(chunks, pair, after, beside)
 
     dist, squares, middle, pair, next_pair, sides, column = pl.pallas_call(
         main_kernel,
         out_shape=(field, field, field) + edges,
-        in_specs=[SMEM] + [VMEM] * 6,
+        in_specs=[SMEM] + [VMEM] * 7,
         out_specs=(VMEM,) * 7,
         scratch_shapes=[pltpu.VMEM((devices * own_blocks, FEATS, PBS), BF)] + scratch,
         compiler_params=pltpu.CompilerParams(vmem_limit_bytes=24 * 2**20),
@@ -352,7 +350,7 @@
             transcendentals=0,
         ),
         name="main",
-    )(block_lists.reshape(-1), own, other, cell_xyz, nu_field, vorticity, beside)
+    )(block_lists.reshape(-1), own, other, cell_xyz, nu_field, vorticity, after, beside)
     column = swap_mask(column, devices - 1)
     next_pair = swap_next(next_pair)
     sides = swap_span(sides)

time: 74.9 us -> 72.9 us (0.973)
  waiting for transfers between devices: 20.7 us -> 17.1 us
  starting transfers between devices: 25 us -> 27 us
    all_to_all x1, waiting for transfers between devices: 10.6 us -> 0.59 us  [gather(): lax.all_to_all(chunks, 'wrap', 0, 0, tiled=True, axis_index_groups=members)]
    ppermute x1 -> x2, waiting for transfers between devices: 0.63 us -> 4.59 us  [swap_next(): return lax.ppermute(block, 'wrap', pairs + [(j, i) for i, j in pairs])]
    ppermute x6, waiting for transfers between devices: 9.42 us -> 11.9 us  [swap_mask(): lax.ppermute(block, 'wrap', [(i, i ^ mask) for i in range(lax.axis_size('...]
    ppermute x1 -> x2, starting transfers between devices: 1.84 us -> 3.38 us  [swap_next(): return lax.ppermute(block, 'wrap', pairs + [(j, i) for i, j in pairs])]
  transfers between devices with their start and end apart: 10 -> 11, of which waited for: 6 -> 7; matrix products, arithmetic and copies ran while one was open for 0% -> 0% of each run, Pallas kernels for 0% -> 0%
where the time goes in v6:
time: 72.9 us; the launch traced here: 72.6 us
  starting transfers between devices  27 us (37%)
  Pallas kernels  26.7 us (37%)
  waiting for transfers between devices  17.1 us (23%)
  local copies, waits for them, and re-layouts  0.99 us (1%)
  between operations  0.74 us (1%)
    pallas_call x1, Pallas kernels, shards(): pl.pallas_call(main_kernel, out_shape=(field, field, field) + edges, in_s...  23.9 us
    ppermute x6, waiting for transfers between devices, swap_mask(): lax.ppermute(block, 'wrap', [(i, i ^ mask) for i in range(lax.axis_size('...  11.9 us
    all_to_all x1, starting transfers between devices, gather(): lax.all_to_all(chunks, 'wrap', 0, 0, tiled=True, axis_index_groups=members)  9.53 us
    ppermute x6, starting transfers between devices, swap_mask(): lax.ppermute(block, 'wrap', [(i, i ^ mask) for i in range(lax.axis_size('...  8.55 us
    ppermute x2, starting transfers between devices, swap_span(): return lax.ppermute(block, 'span', [(0, 1), (1, 0)])  5.55 us
    ppermute x2, waiting for transfers between devices, swap_next(): return lax.ppermute(block, 'wrap', pairs + [(j, i) for i, j in pairs])  4.59 us
    ppermute x2, starting transfers between devices, swap_next(): return lax.ppermute(block, 'wrap', pairs + [(j, i) for i, j in pairs])  3.38 us
    pallas_call x1, Pallas kernels, shards(): pl.pallas_call(prep_kernel, out_shape=(jax.ShapeDtypeStruct((groups, 4 *...  1.74 us
  transfers between devices with their start and end apart: 11, of which 7 were waited for; matrix products, arithmetic and copies ran while one was open for 0% of the time, Pallas kernels for 0%

profile of v6, /device:TPU:32, one launch (start us, length us, event | category | flops | bytes accessed | tf_op | source)
XLA Modules:
  0.0 72.6 jit_solution(11306793277279349063)
XLA Ops:
  0.6 1.7 %prep.1 = (f32[16,24,128]{2,1,0:T(8,128)}, f32[8,128]{1,0:T(8,128)}, f32[8,128]{1,0:T(8,128)}, f32[32,128]{1,0:T(8,128)}) custom-call(f32[3,512]{1,0:T(4,128)} %xyz_hbm.1, f32[1,512]{1,0:T(1,128)} %bitcast.8, f32[32,8,128]{2,1,0:T(8,128)} %nu_ref.3), custom_call_target="tpu_custom_call" | custom-call | tf_op jit(solution)/shard_map/prep/pallas_call | solution.py:324
  2.4 0.0 copy-start.5
  2.4 9.5 %all-to-all-start = ((f32[16,24,128]{2,1,0:T(8,128)}), f32[16,24,128]{2,1,0:T(8,128)S(1)}, u32[]{:S(2)}, u32[]{:S(2)}) async-start(f32[16,24,128]{2,1,0:T(8,128)} %get-tuple-element.16), calls=%async_computation | async-start | bytes 393216 | tf_op jit(solution)/shard_map/all_to_all | solution.py:301
  11.9 2.8 %collective-permute-start.1 = (f32[32,128]{1,0:T(8,128)S(1)}, f32[32,128]{1,0:T(8,128)S(1)}, u32[]{:S(2)}, u32[]{:S(2)}) collective-permute-start(f32[32,128]{1,0:T(8,128)S(1)} %copy-done.5), channel_id=1, source_target_pairs={{0,1},{1,0},{2,3},{3,2},{4,5},{5,4},{6,7},{7,6},{8,9},{9,8},{10,11... | collective-permute-start | bytes 49160 | tf_op jit(solution)/shard_map/ppermute | solution.py:293
  14.8 1.9 %collective-permute-start = (f32[8,128]{1,0:T(8,128)S(1)}, f32[8,128]{1,0:T(8,128)S(1)}, u32[]{:S(2)}, u32[]{:S(2)}) collective-permute-start(f32[8,128]{1,0:T(8,128)S(1)} %copy-done.6), channel_id=1, source_target_pairs={{2,4},{6,8},{10,12},{14,16},{18,20},{22,24},{26,28},{30,32},{34,36... | collective-permute-start | bytes 12296 | tf_op jit(solution)/shard_map/ppermute | solution.py:289
  16.7 4.1 %collective-permute-done.next_ref = f32[8,128]{1,0:T(8,128)S(1)} collective-permute-done((f32[8,128]{1,0:T(8,128)S(1)}, f32[8,128]{1,0:T(8,128)S(1)}, u32[]{:S(2)}, u32[]{:S(2)}) %collective-permute-start) | collective-permute-done | bytes 4128 | tf_op jit(solution)/shard_map/ppermute | solution.py:289
  20.8 0.6 all-to-all-done
  21.4 3.3 %collective-permute-start.4 = (f32[256,128]{1,0:T(8,128)S(1)}, f32[256,128]{1,0:T(8,128)S(1)}, u32[]{:S(2)}, u32[]{:S(2)}) collective-permute-start(f32[256,128]{1,0:T(8,128)S(1)} %bitcast.4), channel_id=1, source_target_pairs={{0,8},{2,10},{4,12},{6,14},{8,0},{10,2},{12,4},{14,6},{16,24},{18,... | collective-permute-start | bytes 393224 | tf_op jit(solution)/shard_map/ppermute | solution.py:283
  24.7 0.7 collective-permute-start.2
  25.4 0.5 collective-permute-start.3
  25.9 3.9 %collective-permute-done.2 = f32[256,128]{1,0:T(8,128)S(1)} collective-permute-done((f32[256,128]{1,0:T(8,128)S(1)}, f32[256,128]{1,0:T(8,128)S(1)}, u32[]{:S(2)}, u32[]{:S(2)}) %collective-permute-start.2) | collective-permute-done | bytes 131104 | tf_op jit(solution)/shard_map/ppermute | solution.py:283
  29.8 1.9 %collective-permute-done.3 = f32[264,128]{1,0:T(8,128)S(1)} collective-permute-done((f32[264,128]{1,0:T(8,128)S(1)}, f32[264,128]{1,0:T(8,128)S(1)}, u32[]{:S(2)}, u32[]{:S(2)}) %collective-permute-start.3) | collective-permute-done | bytes 135200 | tf_op jit(solution)/shard_map/ppermute | solution.py:283
  31.8 0.7 copy-done.4
  32.4 0.0 copy-done.3
  32.5 0.1 copy.8
  32.6 0.1 reshape.10.list_ref
  32.7 1.7 %collective-permute-done.5.other_ref = f32[1040,128]{1,0:T(8,128)S(1)} collective-permute-done((f32[1040,128]{1,0:T(8,128)S(1)}, f32[1040,128]{1,0:T(8,128)S(1)}, u32[]{:S(2)}, u32[]{:S(2)}) %collective-permute-start.5) | collective-permute-done | bytes 532512 | tf_op jit(solution)/shard_map/ppermute | solution.py:283
  34.4 23.9 %main.1 = (f32[32,8,128]{2,1,0:T(8,128)}, f32[32,8,128]{2,1,0:T(8,128)S(1)}, f32[32,8,128]{2,1,0:T(8,128)S(1)}, f32[8,128]{1,0:T(8,128)S(1)}, f32[8,128]{1,0:T(8...) custom-call(s32[2048]{0:T(1024)S(1)} %reshape.10.list_ref, ...), custom_call_target="tpu_custom_call" | custom-call | flops 8589934592 | bytes 4194304 | tf_op jit(solution)/shard_map/main/pallas_call | solution.py:340
  58.3 2.7 %collective-permute-start.8 = (f32[32,128]{1,0:T(8,128)S(1)}, f32[32,128]{1,0:T(8,128)S(1)}, u32[]{:S(2)}, u32[]{:S(2)}) collective-permute-start(f32[32,128]{1,0:T(8,128)S(1)} %get-tuple-element.27), channel_id=1, source_target_pairs={{0,1},{1,0},{2,3},{3,2},{4,5},{5,4},{6,7},{7,6},{8,9},{9,8},{10,11... | collective-permute-start | bytes 49160 | tf_op jit(solution)/shard_map/ppermute | solution.py:293
  61.0 1.5 %collective-permute-start.7 = (f32[8,128]{1,0:T(8,128)S(1)}, f32[8,128]{1,0:T(8,128)S(1)}, u32[]{:S(2)}, u32[]{:S(2)}) collective-permute-start(f32[8,128]{1,0:T(8,128)S(1)} %get-tuple-element.26), channel_id=1, source_target_pairs={{2,4},{6,8},{10,12},{14,16},{18,20},{22,24},{26,28},{30,32},{34,36... | collective-permute-start | bytes 12296 | tf_op jit(solution)/shard_map/ppermute | solution.py:289
  62.5 4.1 %collective-permute-start.9 = (f32[8,128]{1,0:T(8,128)S(1)}, f32[8,128]{1,0:T(8,128)S(1)}, u32[]{:S(2)}, u32[]{:S(2)}) collective-permute-start(f32[8,128]{1,0:T(8,128)S(1)} %get-tuple-element.28), channel_id=1, source_target_pairs={{0,254},{2,252},{4,250},{6,248},{8,246},{10,244},{12,242},{14,240}... | collective-permute-start | bytes 12296 | tf_op jit(solution)/shard_map/ppermute | solution.py:283
  66.6 0.4 collective-permute-done.7.next_ref
  67.1 4.5 %collective-permute-done.9.column_ref = f32[8,128]{1,0:T(8,128)S(1)} collective-permute-done((f32[8,128]{1,0:T(8,128)S(1)}, f32[8,128]{1,0:T(8,128)S(1)}, u32[]{:S(2)}, u32[]{:S(2)}) %collective-permute-start.9) | collective-permute-done | bytes 4128 | tf_op jit(solution)/shard_map/ppermute | solution.py:283
  71.6 1.0 %last.1 = f32[32,8,128]{2,1,0:T(8,128)} custom-call(f32[32,8,128]{2,1,0:T(8,128)S(1)} %get-tuple-element.23.middle_ref, f32[32,8,128]{2,1,0:T(8,128)S(1)} %copy-done, f32[32,8,128]{2,1,0:T(8,128)S(1)} %get-tuple-element.24.squares_ref, f32[32,8,128]{2,1,0:T(8,128)S(1)} %copy-done.1, f32[8,128]{1,0:T(8,128)S(1)} %collective-permute-done.6.pair_ref, ...), custom_call_target="tpu_custom_call" | custom-call | tf_op jit(solution)/shard_map/last/pallas_call | solution.py:359
  (25 shorter events, 0.1 us)
Async XLA Ops:
  2.4 9.6 %copy-start.5 = (f32[32,128]{1,0:T(8,128)S(1)}, f32[32,128]{1,0:T(8,128)}, u32[]{:S(2)}) copy-start(f32[32,128]{1,0:T(8,128)} %get-tuple-element.18) | copy-start | bytes 49156
  2.4 12.4 %copy-start.6 = (f32[8,128]{1,0:T(8,128)S(1)}, f32[8,128]{1,0:T(8,128)}, u32[]{:S(2)}) copy-start(f32[8,128]{1,0:T(8,128)} %get-tuple-element.17) | copy-start | bytes 12292
  2.4 19.0 %all-to-all-start = ((f32[16,24,128]{2,1,0:T(8,128)}), f32[16,24,128]{2,1,0:T(8,128)S(1)}, u32[]{:S(2)}, u32[]{:S(2)}) async-start(f32[16,24,128]{2,1,0:T(8,128)} %get-tuple-element.16), calls=%async_computation | async-start | bytes 393216 | tf_op jit(solution)/shard_map/all_to_all | solution.py:301
  11.9 8.9 %collective-permute-start.1 = (f32[32,128]{1,0:T(8,128)S(1)}, f32[32,128]{1,0:T(8,128)S(1)}, u32[]{:S(2)}, u32[]{:S(2)}) collective-permute-start(f32[32,128]{1,0:T(8,128)S(1)} %copy-done.5), channel_id=1, source_target_pairs={{0,1},{1,0},{2,3},{3,2},{4,5},{5,4},{6,7},{7,6},{8,9},{9,8},{10,11... | collective-permute-start | bytes 49160 | tf_op jit(solution)/shard_map/ppermute | solution.py:293
  14.8 6.1 %collective-permute-start = (f32[8,128]{1,0:T(8,128)S(1)}, f32[8,128]{1,0:T(8,128)S(1)}, u32[]{:S(2)}, u32[]{:S(2)}) collective-permute-start(f32[8,128]{1,0:T(8,128)S(1)} %copy-done.6), channel_id=1, source_target_pairs={{2,4},{6,8},{10,12},{14,16},{18,20},{22,24},{26,28},{30,32},{34,36... | collective-permute-start | bytes 12296 | tf_op jit(solution)/shard_map/ppermute | solution.py:289
  21.4 10.3 %collective-permute-start.4 = (f32[256,128]{1,0:T(8,128)S(1)}, f32[256,128]{1,0:T(8,128)S(1)}, u32[]{:S(2)}, u32[]{:S(2)}) collective-permute-start(f32[256,128]{1,0:T(8,128)S(1)} %bitcast.4), channel_id=1, source_target_pairs={{0,8},{2,10},{4,12},{6,14},{8,0},{10,2},{12,4},{14,6},{16,24},{18,... | collective-permute-start | bytes 393224 | tf_op jit(solution)/shard_map/ppermute | solution.py:283
  24.7 5.1 %collective-permute-start.2 = (f32[256,128]{1,0:T(8,128)S(1)}, f32[256,128]{1,0:T(8,128)S(1)}, u32[]{:S(2)}, u32[]{:S(2)}) collective-permute-start(f32[256,128]{1,0:T(8,128)S(1)} %bitcast.5), channel_id=1, source_target_pairs={{0,4},{2,6},{4,0},{6,2},{8,12},{10,14},{12,8},{14,10},{16,20},{18,... | collective-permute-start | bytes 393224 | tf_op jit(solution)/shard_map/ppermute | solution.py:283
  25.4 6.3 %collective-permute-start.3 = (f32[264,128]{1,0:T(8,128)S(1)}, f32[264,128]{1,0:T(8,128)S(1)}, u32[]{:S(2)}, u32[]{:S(2)}) collective-permute-start(f32[264,128]{1,0:T(8,128)S(1)} %pad_maximum_fusion), channel_id=1, source_target_pairs={{0,12},{2,14},{4,8},{6,10},{8,4},{10,6},{12,0},{14,2},{16,28},{18,... | collective-permute-start | bytes 405512 | tf_op jit(solution)/shard_map/ppermute | solution.py:283
  29.8 4.5 %copy-start.2 = (f32[3,32,8,128]{3,2,1,0:T(8,128)S(1)}, f32[3,32,8,128]{3,2,1,0:T(8,128)}, u32[]{:S(2)}) copy-start(f32[3,32,8,128]{3,2,1,0:T(8,128)} %cell_ref.1) | copy-start | bytes 1179652
  31.7 0.8 %copy-start.3 = (s32[32,8,8]{0,2,1:T(8,128)S(1)}, s32[32,8,8]{0,2,1:T(8,128)}, u32[]{:S(2)}) copy-start(s32[32,8,8]{0,2,1:T(8,128)} %param.9) | copy-start | bytes 24580
  31.7 0.7 copy-start.4
  32.4 1.9 %copy-start = (f32[32,8,128]{2,1,0:T(8,128)S(1)}, f32[32,8,128]{2,1,0:T(8,128)}, u32[]{:S(2)}) copy-start(f32[32,8,128]{2,1,0:T(8,128)} %nu_ref.3) | copy-start | bytes 393220
  32.4 1.9 %copy-start.1 = (f32[32,8,128]{2,1,0:T(8,128)S(1)}, f32[32,8,128]{2,1,0:T(8,128)}, u32[]{:S(2)}) copy-start(f32[32,8,128]{2,1,0:T(8,128)} %vorticity_ref.3) | copy-start | bytes 393220
  32.4 1.9 %collective-permute-start.5 = (f32[1040,128]{1,0:T(8,128)S(1)}, f32[1040,128]{1,0:T(8,128)S(1)}, u32[]{:S(2)}, u32[]{:S(2)}) collective-permute-start(f32[1040,128]{1,0:T(8,128)S(1)} %constant_dynamic-update-slice_fusion.own_ref), channel_id=1, source_target_pairs={{0,2},{2,0},{4,6},{6,4},{8,10},{10,8},{12,14},{14,12},{16,18},{18,... | collective-permute-start | bytes 1597448 | tf_op jit(solution)/shard_map/ppermute | solution.py:283
  58.3 13.3 %collective-permute-start.8 = (f32[32,128]{1,0:T(8,128)S(1)}, f32[32,128]{1,0:T(8,128)S(1)}, u32[]{:S(2)}, u32[]{:S(2)}) collective-permute-start(f32[32,128]{1,0:T(8,128)S(1)} %get-tuple-element.27), channel_id=1, source_target_pairs={{0,1},{1,0},{2,3},{3,2},{4,5},{5,4},{6,7},{7,6},{8,9},{9,8},{10,11... | collective-permute-start | bytes 49160 | tf_op jit(solution)/shard_map/ppermute | solution.py:293
  61.0 5.6 %collective-permute-start.6 = (f32[8,128]{1,0:T(8,128)S(1)}, f32[8,128]{1,0:T(8,128)S(1)}, u32[]{:S(2)}, u32[]{:S(2)}) collective-permute-start(f32[8,128]{1,0:T(8,128)S(1)} %get-tuple-element.25), channel_id=1, source_target_pairs={{0,2},{2,0},{4,6},{6,4},{8,10},{10,8},{12,14},{14,12},{16,18},{18,... | collective-permute-start | bytes 12296 | tf_op jit(solution)/shard_map/ppermute | solution.py:283
  61.0 6.0 %collective-permute-start.7 = (f32[8,128]{1,0:T(8,128)S(1)}, f32[8,128]{1,0:T(8,128)S(1)}, u32[]{:S(2)}, u32[]{:S(2)}) collective-permute-start(f32[8,128]{1,0:T(8,128)S(1)} %get-tuple-element.26), channel_id=1, source_target_pairs={{2,4},{6,8},{10,12},{14,16},{18,20},{22,24},{26,28},{30,32},{34,36... | collective-permute-start | bytes 12296 | tf_op jit(solution)/shard_map/ppermute | solution.py:289
  62.5 9.0 %collective-permute-start.9 = (f32[8,128]{1,0:T(8,128)S(1)}, f32[8,128]{1,0:T(8,128)S(1)}, u32[]{:S(2)}, u32[]{:S(2)}) collective-permute-start(f32[8,128]{1,0:T(8,128)S(1)} %get-tuple-element.28), channel_id=1, source_target_pairs={{0,254},{2,252},{4,250},{6,248},{8,246},{10,244},{12,242},{14,240}... | collective-permute-start | bytes 12296 | tf_op jit(solution)/shard_map/ppermute | solution.py:283

commit v7 on v6

--- a/solution.py
+++ b/solution.py
@@ -11,7 +11,8 @@
 F32 = jnp.float32
 PBS = 128
 FEATS = 48
-LINES_PER_STEP = 32
+LINES_PER_STEP = 64
+COLUMN_ROWS = 40
 GROUP_BIT = 3
 Y_MASKS = (2, 6, 4)
 
@@ -173,7 +174,7 @@
         for n in range(1, len(Y_MASKS)):
             near = jnp.where(choice == n + 1, Y_MASKS[n], near)
         low = (place & ((1 << GROUP_BIT) - 1)) ^ near
-        skip = jnp.where(choice == 3, 8, 0)
+        skip = jnp.where(choice == 3, 16, 8)
         for half, ref in enumerate(halves):
             base = (((slot % groups) << GROUP_BIT) | (low ^ half)) * own_blocks
             for pair in range(own_blocks // 2):
@@ -233,8 +234,8 @@
     ghost_ref,
 ):
     total = (other_ref.shape[0] - 16) // 4
-    column = other_ref[3 * total : 3 * total + 8]
-    pair = other_ref[4 * total + 8 : 4 * total + 16]
+    column = other_ref[3 * total + 8 : 3 * total + 16]
+    pair = other_ref[0:8]
     halo = Halo(nu_ref, pair, next_ref[...], beside_ref, column, padded_ref, ghost_ref)
     build_table((own_ref, other_ref), table_ref)
     tiles = nu_ref.shape[0]
@@ -254,7 +255,9 @@
             column = jnp.where(lane == tile, first_column(middle), column)
         return column
 
-    column_out[...] = lax.fori_loop(0, tiles // per_step, body, jnp.zeros((8, 128), F32))
+    column = lax.fori_loop(0, tiles // per_step, body, jnp.zeros((8, 128), F32))
+    for row in range(0, column_out.shape[0], 8):
+        column_out[row : row + 8] = column
     put_edges(middle_ref[0], middle_ref[tiles - 1], pair_out, next_out)
 
 
@@ -272,7 +275,7 @@
     ghost_ref,
 ):
     halo = Halo(
-        middle_ref, pair_ref[...], next_ref[...], beside_ref, column_ref[...], padded_ref, ghost_ref
+        middle_ref, pair_ref[...], next_ref[...], beside_ref, column_ref[0:8], padded_ref, ghost_ref
     )
     for row in range(nu_ref.shape[0]):
         rate = halo.rate(row, squares_ref[row], vorticity_ref[row])
@@ -306,7 +309,7 @@
     first = swap_mask(shard, Y_MASKS[0])
     second = swap_mask(jnp.concatenate([shard, column], 0), Y_MASKS[1])
     third = swap_mask(shard, Y_MASKS[2])
-    shard = jnp.concatenate([shard, first, second, third, pair], 0)
+    shard = jnp.concatenate([pair, shard, first, second, third], 0)
     return shard, swap_mask(shard, 1), after, beside
 
 
@@ -317,7 +320,7 @@
     tile = jax.ShapeDtypeStruct((span, cells), F32)
     field = jax.ShapeDtypeStruct(nu_field.shape, F32)
     side = jax.ShapeDtypeStruct((rows, cells), F32)
-    edges = (tile, tile, side, tile)
+    edges = (tile, tile, side, jax.ShapeDtypeStruct((COLUMN_ROWS, cells), F32))
     scratch = [pltpu.VMEM((rows + 2, span, cells), F32), pltpu.VMEM(nu_field.shape, F32)]
 
     groups = devices >> GROUP_BIT

time: 72.9 us -> 71.4 us (0.979)
  Pallas kernels: 26.7 us -> 25.6 us
  starting transfers between devices: 27 us -> 26.2 us
    ppermute x2, waiting for transfers between devices: 4.59 us -> 9.08 us  [swap_next(): return lax.ppermute(block, 'wrap', pairs + [(j, i) for i, j in pairs])]
    ppermute x6, waiting for transfers between devices: 11.9 us -> 7.5 us  [swap_mask(): lax.ppermute(block, 'wrap', [(i, i ^ mask) for i in range(lax.axis_size('...]
    pallas_call x1, Pallas kernels: 23.9 us -> 22.8 us  [shards(): pl.pallas_call(main_kernel, out_shape=(field, field, field) + edges, in_s...]
    ppermute x2, starting transfers between devices: 3.38 us -> 2.55 us  [swap_next(): return lax.ppermute(block, 'wrap', pairs + [(j, i) for i, j in pairs])]
where the time goes in v7:
time: 71.4 us; the launch traced here: 70.6 us
  starting transfers between devices  26.2 us (37%)
  Pallas kernels  25.6 us (36%)
  waiting for transfers between devices  17.2 us (24%)
  local copies, waits for them, and re-layouts  0.9 us (1%)
  between operations  0.76 us (1%)
    pallas_call x1, Pallas kernels, shards(): pl.pallas_call(main_kernel, out_shape=(field, field, field) + edges, in_s...  22.8 us
    all_to_all x1, starting transfers between devices, gather(): lax.all_to_all(chunks, 'wrap', 0, 0, tiled=True, axis_index_groups=members)  9.53 us
    ppermute x2, waiting for transfers between devices, swap_next(): return lax.ppermute(block, 'wrap', pairs + [(j, i) for i, j in pairs])  9.08 us
    ppermute x6, starting transfers between devices, swap_mask(): lax.ppermute(block, 'wrap', [(i, i ^ mask) for i in range(lax.axis_size('...  9.06 us
    ppermute x6, waiting for transfers between devices, swap_mask(): lax.ppermute(block, 'wrap', [(i, i ^ mask) for i in range(lax.axis_size('...  7.5 us
    ppermute x2, starting transfers between devices, swap_span(): return lax.ppermute(block, 'span', [(0, 1), (1, 0)])  5.03 us
    ppermute x2, starting transfers between devices, swap_next(): return lax.ppermute(block, 'wrap', pairs + [(j, i) for i, j in pairs])  2.55 us
    pallas_call x1, Pallas kernels, shards(): pl.pallas_call(prep_kernel, out_shape=(jax.ShapeDtypeStruct((groups, 4 *...  1.74 us
  transfers between devices with their start and end apart: 11, of which 7 were waited for; matrix products, arithmetic and copies ran while one was open for 0% of the time, Pallas kernels for 0%

profile of v7, /device:TPU:32, one launch (start us, length us, event | category | flops | bytes accessed | tf_op | source)
XLA Modules:
  0.0 70.6 jit_solution(11979661540274938017)
XLA Ops:
  0.6 1.7 %prep.1 = (f32[16,24,128]{2,1,0:T(8,128)}, f32[8,128]{1,0:T(8,128)}, f32[8,128]{1,0:T(8,128)}, f32[32,128]{1,0:T(8,128)}) custom-call(f32[3,512]{1,0:T(4,128)} %xyz_hbm.1, f32[1,512]{1,0:T(1,128)} %bitcast.8, f32[32,8,128]{2,1,0:T(8,128)} %nu_ref.3), custom_call_target="tpu_custom_call" | custom-call | tf_op jit(solution)/shard_map/prep/pallas_call | solution.py:327
  2.4 9.5 %all-to-all-start = ((f32[16,24,128]{2,1,0:T(8,128)}), f32[16,24,128]{2,1,0:T(8,128)S(1)}, u32[]{:S(2)}, u32[]{:S(2)}) async-start(f32[16,24,128]{2,1,0:T(8,128)} %get-tuple-element.17), calls=%async_computation | async-start | bytes 393216 | tf_op jit(solution)/shard_map/all_to_all | solution.py:304
  11.9 2.8 %collective-permute-start.1 = (f32[32,128]{1,0:T(8,128)S(1)}, f32[32,128]{1,0:T(8,128)S(1)}, u32[]{:S(2)}, u32[]{:S(2)}) collective-permute-start(f32[32,128]{1,0:T(8,128)S(1)} %copy-done.5), channel_id=1, source_target_pairs={{0,1},{1,0},{2,3},{3,2},{4,5},{5,4},{6,7},{7,6},{8,9},{9,8},{10,11... | collective-permute-start | bytes 49160 | tf_op jit(solution)/shard_map/ppermute | solution.py:296
  14.8 1.9 %collective-permute-start = (f32[8,128]{1,0:T(8,128)S(1)}, f32[8,128]{1,0:T(8,128)S(1)}, u32[]{:S(2)}, u32[]{:S(2)}) collective-permute-start(f32[8,128]{1,0:T(8,128)S(1)} %copy-done.6), channel_id=1, source_target_pairs={{2,4},{6,8},{10,12},{14,16},{18,20},{22,24},{26,28},{30,32},{34,36... | collective-permute-start | bytes 12296 | tf_op jit(solution)/shard_map/ppermute | solution.py:292
  16.7 4.1 %collective-permute-done.next_ref = f32[8,128]{1,0:T(8,128)S(1)} collective-permute-done((f32[8,128]{1,0:T(8,128)S(1)}, f32[8,128]{1,0:T(8,128)S(1)}, u32[]{:S(2)}, u32[]{:S(2)}) %collective-permute-start) | collective-permute-done | bytes 4128 | tf_op jit(solution)/shard_map/ppermute | solution.py:292
  20.8 0.6 all-to-all-done
  21.4 1.7 %collective-permute-start.2 = (f32[256,128]{1,0:T(8,128)S(1)}, f32[256,128]{1,0:T(8,128)S(1)}, u32[]{:S(2)}, u32[]{:S(2)}) collective-permute-start(f32[256,128]{1,0:T(8,128)S(1)} %bitcast.4), channel_id=1, source_target_pairs={{0,4},{2,6},{4,0},{6,2},{8,12},{10,14},{12,8},{14,10},{16,20},{18,... | collective-permute-start | bytes 393224 | tf_op jit(solution)/shard_map/ppermute | solution.py:286
  23.1 2.9 %collective-permute-start.4 = (f32[256,128]{1,0:T(8,128)S(1)}, f32[256,128]{1,0:T(8,128)S(1)}, u32[]{:S(2)}, u32[]{:S(2)}) collective-permute-start(f32[256,128]{1,0:T(8,128)S(1)} %bitcast.5), channel_id=1, source_target_pairs={{0,8},{2,10},{4,12},{6,14},{8,0},{10,2},{12,4},{14,6},{16,24},{18,... | collective-permute-start | bytes 393224 | tf_op jit(solution)/shard_map/ppermute | solution.py:286
  26.0 0.3 collective-permute-start.3
  26.3 1.1 %collective-permute-done.2 = f32[256,128]{1,0:T(8,128)S(1)} collective-permute-done((f32[256,128]{1,0:T(8,128)S(1)}, f32[256,128]{1,0:T(8,128)S(1)}, u32[]{:S(2)}, u32[]{:S(2)}) %collective-permute-start.2) | collective-permute-done | bytes 131104 | tf_op jit(solution)/shard_map/ppermute | solution.py:286
  27.5 4.8 %collective-permute-done.3 = f32[264,128]{1,0:T(8,128)S(1)} collective-permute-done((f32[264,128]{1,0:T(8,128)S(1)}, f32[264,128]{1,0:T(8,128)S(1)}, u32[]{:S(2)}, u32[]{:S(2)}) %collective-permute-start.3) | collective-permute-done | bytes 135200 | tf_op jit(solution)/shard_map/ppermute | solution.py:286
  32.4 0.1 collective-permute-start.5
  32.5 0.6 copy-done.3
  33.1 0.1 copy.8
  33.2 0.1 reshape.10.list_ref
  33.3 1.1 %collective-permute-done.5.other_ref = f32[1040,128]{1,0:T(8,128)S(1)} collective-permute-done((f32[1040,128]{1,0:T(8,128)S(1)}, f32[1040,128]{1,0:T(8,128)S(1)}, u32[]{:S(2)}, u32[]{:S(2)}) %collective-permute-start.5) | collective-permute-done | bytes 532512 | tf_op jit(solution)/shard_map/ppermute | solution.py:286
  34.4 22.8 %main.1 = (f32[32,8,128]{2,1,0:T(8,128)}, f32[32,8,128]{2,1,0:T(8,128)S(1)}, f32[32,8,128]{2,1,0:T(8,128)S(1)}, f32[8,128]{1,0:T(8,128)S(1)}, f32[8,128]{1,0:T(8...) custom-call(s32[2048]{0:T(1024)S(1)} %reshape.10.list_ref, ...), custom_call_target="tpu_custom_call" | custom-call | flops 8589934592 | bytes 4194304 | tf_op jit(solution)/shard_map/main/pallas_call | solution.py:343
  57.2 4.0 %collective-permute-start.9 = (f32[40,128]{1,0:T(8,128)S(1)}, f32[40,128]{1,0:T(8,128)S(1)}, u32[]{:S(2)}, u32[]{:S(2)}) collective-permute-start(f32[40,128]{1,0:T(8,128)S(1)} %get-tuple-element.28), channel_id=1, source_target_pairs={{0,254},{2,252},{4,250},{6,248},{8,246},{10,244},{12,242},{14,240}... | collective-permute-start | bytes 61448 | tf_op jit(solution)/shard_map/ppermute | solution.py:286
  61.3 2.2 %collective-permute-start.8 = (f32[32,128]{1,0:T(8,128)S(1)}, f32[32,128]{1,0:T(8,128)S(1)}, u32[]{:S(2)}, u32[]{:S(2)}) collective-permute-start(f32[32,128]{1,0:T(8,128)S(1)} %get-tuple-element.27), channel_id=1, source_target_pairs={{0,1},{1,0},{2,3},{3,2},{4,5},{5,4},{6,7},{7,6},{8,9},{9,8},{10,11... | collective-permute-start | bytes 49160 | tf_op jit(solution)/shard_map/ppermute | solution.py:296
  63.5 0.1 collective-permute-start.6
  63.5 0.6 collective-permute-start.7
  64.2 0.4 collective-permute-done.6.pair_ref
  64.6 5.0 %collective-permute-done.7.next_ref = f32[8,128]{1,0:T(8,128)S(1)} collective-permute-done((f32[8,128]{1,0:T(8,128)S(1)}, f32[8,128]{1,0:T(8,128)S(1)}, u32[]{:S(2)}, u32[]{:S(2)}) %collective-permute-start.7) | collective-permute-done | bytes 4128 | tf_op jit(solution)/shard_map/ppermute | solution.py:292
  69.6 1.0 %last.1 = f32[32,8,128]{2,1,0:T(8,128)} custom-call(f32[32,8,128]{2,1,0:T(8,128)S(1)} %get-tuple-element.23.middle_ref, f32[32,8,128]{2,1,0:T(8,128)S(1)} %copy-done, f32[32,8,128]{2,1,0:T(8,128)S(1)} %get-tuple-element.24.squares_ref, f32[32,8,128]{2,1,0:T(8,128)S(1)} %copy-done.1, f32[8,128]{1,0:T(8,128)S(1)} %collective-permute-done.6.pair_ref, ...), custom_call_target="tpu_custom_call" | custom-call | tf_op jit(solution)/shard_map/last/pallas_call | solution.py:362
  (25 shorter events, 0.1 us)
Async XLA Ops:
  2.4 9.6 %copy-start.5 = (f32[32,128]{1,0:T(8,128)S(1)}, f32[32,128]{1,0:T(8,128)}, u32[]{:S(2)}) copy-start(f32[32,128]{1,0:T(8,128)} %get-tuple-element.19) | copy-start | bytes 49156
  2.4 12.4 %copy-start.6 = (f32[8,128]{1,0:T(8,128)S(1)}, f32[8,128]{1,0:T(8,128)}, u32[]{:S(2)}) copy-start(f32[8,128]{1,0:T(8,128)} %get-tuple-element.18) | copy-start | bytes 12292
  2.4 19.0 %all-to-all-start = ((f32[16,24,128]{2,1,0:T(8,128)}), f32[16,24,128]{2,1,0:T(8,128)S(1)}, u32[]{:S(2)}, u32[]{:S(2)}) async-start(f32[16,24,128]{2,1,0:T(8,128)} %get-tuple-element.17), calls=%async_computation | async-start | bytes 393216 | tf_op jit(solution)/shard_map/all_to_all | solution.py:304
  11.9 4.7 %copy-start.4 = (f32[8,128]{1,0:T(8,128)S(1)}, f32[8,128]{1,0:T(8,128)}, u32[]{:S(2)}) copy-start(f32[8,128]{1,0:T(8,128)} %get-tuple-element.16) | copy-start | bytes 12292
  11.9 8.9 %collective-permute-start.1 = (f32[32,128]{1,0:T(8,128)S(1)}, f32[32,128]{1,0:T(8,128)S(1)}, u32[]{:S(2)}, u32[]{:S(2)}) collective-permute-start(f32[32,128]{1,0:T(8,128)S(1)} %copy-done.5), channel_id=1, source_target_pairs={{0,1},{1,0},{2,3},{3,2},{4,5},{5,4},{6,7},{7,6},{8,9},{9,8},{10,11... | collective-permute-start | bytes 49160 | tf_op jit(solution)/shard_map/ppermute | solution.py:296
  14.8 6.0 %collective-permute-start = (f32[8,128]{1,0:T(8,128)S(1)}, f32[8,128]{1,0:T(8,128)S(1)}, u32[]{:S(2)}, u32[]{:S(2)}) collective-permute-start(f32[8,128]{1,0:T(8,128)S(1)} %copy-done.6), channel_id=1, source_target_pairs={{2,4},{6,8},{10,12},{14,16},{18,20},{22,24},{26,28},{30,32},{34,36... | collective-permute-start | bytes 12296 | tf_op jit(solution)/shard_map/ppermute | solution.py:292
  21.4 6.0 %collective-permute-start.2 = (f32[256,128]{1,0:T(8,128)S(1)}, f32[256,128]{1,0:T(8,128)S(1)}, u32[]{:S(2)}, u32[]{:S(2)}) collective-permute-start(f32[256,128]{1,0:T(8,128)S(1)} %bitcast.4), channel_id=1, source_target_pairs={{0,4},{2,6},{4,0},{6,2},{8,12},{10,14},{12,8},{14,10},{16,20},{18,... | collective-permute-start | bytes 393224 | tf_op jit(solution)/shard_map/ppermute | solution.py:286
  23.1 9.3 %collective-permute-start.4 = (f32[256,128]{1,0:T(8,128)S(1)}, f32[256,128]{1,0:T(8,128)S(1)}, u32[]{:S(2)}, u32[]{:S(2)}) collective-permute-start(f32[256,128]{1,0:T(8,128)S(1)} %bitcast.5), channel_id=1, source_target_pairs={{0,8},{2,10},{4,12},{6,14},{8,0},{10,2},{12,4},{14,6},{16,24},{18,... | collective-permute-start | bytes 393224 | tf_op jit(solution)/shard_map/ppermute | solution.py:286
  26.0 6.3 %collective-permute-start.3 = (f32[264,128]{1,0:T(8,128)S(1)}, f32[264,128]{1,0:T(8,128)S(1)}, u32[]{:S(2)}, u32[]{:S(2)}) collective-permute-start(f32[264,128]{1,0:T(8,128)S(1)} %pad_maximum_fusion), channel_id=1, source_target_pairs={{0,12},{2,14},{4,8},{6,10},{8,4},{10,6},{12,0},{14,2},{16,28},{18,... | collective-permute-start | bytes 405512 | tf_op jit(solution)/shard_map/ppermute | solution.py:286
  27.5 6.9 %copy-start.2 = (f32[3,32,8,128]{3,2,1,0:T(8,128)S(1)}, f32[3,32,8,128]{3,2,1,0:T(8,128)}, u32[]{:S(2)}) copy-start(f32[3,32,8,128]{3,2,1,0:T(8,128)} %cell_ref.1) | copy-start | bytes 1179652
  32.3 0.8 %copy-start.3 = (s32[32,8,8]{0,2,1:T(8,128)S(1)}, s32[32,8,8]{0,2,1:T(8,128)}, u32[]{:S(2)}) copy-start(s32[32,8,8]{0,2,1:T(8,128)} %param.9) | copy-start | bytes 24580
  32.4 2.0 %copy-start = (f32[32,8,128]{2,1,0:T(8,128)S(1)}, f32[32,8,128]{2,1,0:T(8,128)}, u32[]{:S(2)}) copy-start(f32[32,8,128]{2,1,0:T(8,128)} %nu_ref.3) | copy-start | bytes 393220
  32.4 2.0 %copy-start.1 = (f32[32,8,128]{2,1,0:T(8,128)S(1)}, f32[32,8,128]{2,1,0:T(8,128)}, u32[]{:S(2)}) copy-start(f32[32,8,128]{2,1,0:T(8,128)} %vorticity_ref.3) | copy-start | bytes 393220
  32.4 2.0 %collective-permute-start.5 = (f32[1040,128]{1,0:T(8,128)S(1)}, f32[1040,128]{1,0:T(8,128)S(1)}, u32[]{:S(2)}, u32[]{:S(2)}) collective-permute-start(f32[1040,128]{1,0:T(8,128)S(1)} %constant_dynamic-update-slice_fusion.own_ref), channel_id=1, source_target_pairs={{0,2},{2,0},{4,6},{6,4},{8,10},{10,8},{12,14},{14,12},{16,18},{18,... | collective-permute-start | bytes 1597448 | tf_op jit(solution)/shard_map/ppermute | solution.py:286
  57.2 12.3 %collective-permute-start.9 = (f32[40,128]{1,0:T(8,128)S(1)}, f32[40,128]{1,0:T(8,128)S(1)}, u32[]{:S(2)}, u32[]{:S(2)}) collective-permute-start(f32[40,128]{1,0:T(8,128)S(1)} %get-tuple-element.28), channel_id=1, source_target_pairs={{0,254},{2,252},{4,250},{6,248},{8,246},{10,244},{12,242},{14,240}... | collective-permute-start | bytes 61448 | tf_op jit(solution)/shard_map/ppermute | solution.py:286
  61.3 8.3 %collective-permute-start.8 = (f32[32,128]{1,0:T(8,128)S(1)}, f32[32,128]{1,0:T(8,128)S(1)}, u32[]{:S(2)}, u32[]{:S(2)}) collective-permute-start(f32[32,128]{1,0:T(8,128)S(1)} %get-tuple-element.27), channel_id=1, source_target_pairs={{0,1},{1,0},{2,3},{3,2},{4,5},{5,4},{6,7},{7,6},{8,9},{9,8},{10,11... | collective-permute-start | bytes 49160 | tf_op jit(solution)/shard_map/ppermute | solution.py:296
  63.5 1.2 %collective-permute-start.6 = (f32[8,128]{1,0:T(8,128)S(1)}, f32[8,128]{1,0:T(8,128)S(1)}, u32[]{:S(2)}, u32[]{:S(2)}) collective-permute-start(f32[8,128]{1,0:T(8,128)S(1)} %get-tuple-element.25), channel_id=1, source_target_pairs={{0,2},{2,0},{4,6},{6,4},{8,10},{10,8},{12,14},{14,12},{16,18},{18,... | collective-permute-start | bytes 12296 | tf_op jit(solution)/shard_map/ppermute | solution.py:286
  63.5 6.0 %collective-permute-start.7 = (f32[8,128]{1,0:T(8,128)S(1)}, f32[8,128]{1,0:T(8,128)S(1)}, u32[]{:S(2)}, u32[]{:S(2)}) collective-permute-start(f32[8,128]{1,0:T(8,128)S(1)} %get-tuple-element.26), channel_id=1, source_target_pairs={{2,4},{6,8},{10,12},{14,16},{18,20},{22,24},{26,28},{30,32},{34,36... | collective-permute-start | bytes 12296 | tf_op jit(solution)/shard_map/ppermute | solution.py:292

commit v8 on v7

--- a/solution.py
+++ b/solution.py
@@ -63,9 +63,10 @@
     return lax.rem(lax.axis_index("wrap"), 2) == 0
 
 
-def put_edges(first, last, pair_ref, next_ref):
-    pair_ref[...] = jnp.where(even_place(), last, first)
-    next_ref[...] = jnp.where(even_place(), first, last)
+def missing_term(value, beside):
+    change = beside - value
+    flux = (viscous + value) * change + (0.5 * (1.0 + coef_cb2)) * change * change
+    return (0.5 * time_step / coef_sigma) * flux
 
 
 def prep_kernel(
@@ -74,7 +75,6 @@
     nu_hbm,
     chunks_ref,
     pair_ref,
-    next_ref,
     beside_ref,
     xyz_ref,
     size_ref,
@@ -101,7 +101,7 @@
         value = nu_ref[row]
         beside_ref[row : row + 1, :] = edge_row(value, low_span)
         column = jnp.where(lane == row, first_column(value), column)
-    put_edges(nu_ref[0], nu_ref[rows - 1], pair_ref, next_ref)
+    pair_ref[...] = jnp.where(even_place(), nu_ref[rows - 1], nu_ref[0])
     chunk = jnp.concatenate(parts + [column], 0)
     for n in range(chunks_ref.shape[0]):
         chunks_ref[n] = chunk
@@ -120,6 +120,7 @@
         padded_ref[0] = jnp.where(place == 0, nu_ref[0], lower)
         padded_ref[rows + 1] = jnp.where(place == devices - 1, nu_ref[rows - 1], upper)
         in_wake = (place < devices // 4) | (place >= devices - devices // 4)
+        self.in_wake = in_wake
         for row in range(rows):
             value = nu_ref[row]
             padded_ref[row + 1] = value
@@ -220,7 +221,6 @@
     cell_ref,
     nu_ref,
     vorticity_ref,
-    next_ref,
     beside_ref,
     dist_ref,
     squares_ref,
@@ -236,9 +236,16 @@
     total = (other_ref.shape[0] - 16) // 4
     column = other_ref[3 * total + 8 : 3 * total + 16]
     pair = other_ref[0:8]
-    halo = Halo(nu_ref, pair, next_ref[...], beside_ref, column, padded_ref, ghost_ref)
+    tiles = nu_ref.shape[0]
+    even = even_place()
+    open_row = jnp.where(even, nu_ref[0], nu_ref[tiles - 1])
+    halo = Halo(nu_ref, pair, open_row, beside_ref, column, padded_ref, ghost_ref)
+    open_side = jnp.where(even, beside_ref[0:1], beside_ref[tiles - 1 : tiles])
+    open_partner = jnp.where(even, column[:, tiles - 1 : tiles], column[:, 0:1])
+    next_out[0:8] = open_row
+    next_out[16:24] = jnp.broadcast_to(open_side, (8, 128))
+    next_out[24:32] = jnp.broadcast_to(open_partner, (8, 128))
     build_table((own_ref, other_ref), table_ref)
-    tiles = nu_ref.shape[0]
     per_step = LINES_PER_STEP // 8
 
     def body(step, column):
@@ -258,7 +265,9 @@
     column = lax.fori_loop(0, tiles // per_step, body, jnp.zeros((8, 128), F32))
     for row in range(0, column_out.shape[0], 8):
         column_out[row : row + 8] = column
-    put_edges(middle_ref[0], middle_ref[tiles - 1], pair_out, next_out)
+    first, last = middle_ref[0], middle_ref[tiles - 1]
+    pair_out[...] = jnp.where(even, last, first)
+    next_out[8:16] = jnp.where(even, first, last)
 
 
 def last_kernel(
@@ -267,17 +276,37 @@
     squares_ref,
     vorticity_ref,
     pair_ref,
-    next_ref,
+    mine_ref,
+    theirs_ref,
     beside_ref,
     column_ref,
     out_ref,
     padded_ref,
     ghost_ref,
+    side_ref,
 ):
+    place = lax.axis_index("wrap")
+    rows = nu_ref.shape[0]
+    even = even_place()
+    inner = (place > 0) & (place < lax.axis_size("wrap") - 1)
+    value, partial, side, partner = (mine_ref[n : n + 8] for n in range(0, 32, 8))
+    other, other_partial, other_side, other_partner = (theirs_ref[n : n + 8] for n in range(0, 32, 8))
+    after = other_partial + missing_term(other, value)
     halo = Halo(
-        middle_ref, pair_ref[...], next_ref[...], beside_ref, column_ref[0:8], padded_ref, ghost_ref
+        middle_ref, pair_ref[...], after, beside_ref, column_ref[0:8], padded_ref, ghost_ref
     )
-    for row in range(nu_ref.shape[0]):
+    side_ref[...] = beside_ref[...]
+    halo.beside = side_ref
+    fixed = partial + missing_term(value, other)
+    side_term = missing_term(side, other_side)[0:1]
+    partner_term = missing_term(partner, other_partner)
+    for row, here in ((0, inner & even), (rows - 1, inner & ~even)):
+        own = jnp.where(here, fixed, padded_ref[row + 1])
+        padded_ref[row + 1] = own
+        ghost = ghost_ref[row] + jnp.where(here, partner_term, 0.0)
+        ghost_ref[row] = jnp.where(halo.in_wake, ghost, -own)
+        side_ref[row : row + 1] = side_ref[row : row + 1] + jnp.where(here, side_term, 0.0)
+    for row in range(rows):
         rate = halo.rate(row, squares_ref[row], vorticity_ref[row])
         out_ref[row] = nu_ref[row] + time_step * rate
 
@@ -296,13 +325,13 @@
     return lax.ppermute(block, "span", [(0, 1), (1, 0)])
 
 
-def gather(chunks, pair, after, beside):
+def gather(chunks, pair, beside):
     devices = lax.axis_size("wrap")
     groups, rows, lanes = chunks.shape
     size = rows - 8
     members = [[low + (n << GROUP_BIT) for n in range(groups)] for low in range(devices // groups)]
     chunks = lax.all_to_all(chunks, "wrap", 0, 0, tiled=True, axis_index_groups=members)
-    chunks, after, beside = lax.optimization_barrier((chunks, swap_next(after), swap_span(beside)))
+    chunks, beside = lax.optimization_barrier((chunks, swap_span(beside)))
     shard = chunks[:, :size].reshape(groups * size, lanes)
     opposite = groups - 1 - (lax.axis_index("wrap") >> GROUP_BIT)
     column = lax.dynamic_slice(chunks, (opposite, size, 0), (1, 8, lanes))[0]
@@ -310,7 +339,7 @@
     second = swap_mask(jnp.concatenate([shard, column], 0), Y_MASKS[1])
     third = swap_mask(shard, Y_MASKS[2])
     shard = jnp.concatenate([pair, shard, first, second, third], 0)
-    return shard, swap_mask(shard, 1), after, beside
+    return shard, swap_mask(shard, 1), beside
 
 
 def shards(cell_xyz, panel_xyz, panel_size, block_lists, nu_field, vorticity):
@@ -320,15 +349,16 @@
     tile = jax.ShapeDtypeStruct((span, cells), F32)
     field = jax.ShapeDtypeStruct(nu_field.shape, F32)
     side = jax.ShapeDtypeStruct((rows, cells), F32)
-    edges = (tile, tile, side, jax.ShapeDtypeStruct((COLUMN_ROWS, cells), F32))
+    opened = jax.ShapeDtypeStruct((32, cells), F32)
+    edges = (tile, opened, side, jax.ShapeDtypeStruct((COLUMN_ROWS, cells), F32))
     scratch = [pltpu.VMEM((rows + 2, span, cells), F32), pltpu.VMEM(nu_field.shape, F32)]
 
     groups = devices >> GROUP_BIT
-    chunks, pair, after, beside = pl.pallas_call(
+    chunks, pair, beside = pl.pallas_call(
         prep_kernel,
-        out_shape=(jax.ShapeDtypeStruct((groups, 4 * own_blocks + 8, PBS), F32), tile, tile, side),
+        out_shape=(jax.ShapeDtypeStruct((groups, 4 * own_blocks + 8, PBS), F32), tile, side),
         in_specs=[pl.BlockSpec(memory_space=pltpu.HBM)] * 3,
-        out_specs=(VMEM,) * 4,
+        out_specs=(VMEM,) * 3,
         scratch_shapes=[
             pltpu.VMEM(panel_xyz.shape, F32),
             pltpu.VMEM((1,) + panel_size.shape, F32),
@@ -338,12 +368,12 @@
         compiler_params=pltpu.CompilerParams(vmem_limit_bytes=60 * 2**20),
         name="prep",
     )(panel_xyz, panel_size[None], nu_field)
-    own, other, after, beside = gather(chunks, pair, after, beside)
-
-    dist, squares, middle, pair, next_pair, sides, column = pl.pallas_call(
+    own, other, beside = gather(chunks, pair, beside)
+
+    dist, squares, middle, pair, mine, sides, column = pl.pallas_call(
         main_kernel,
         out_shape=(field, field, field) + edges,
-        in_specs=[SMEM] + [VMEM] * 7,
+        in_specs=[SMEM] + [VMEM] * 6,
         out_specs=(VMEM,) * 7,
         scratch_shapes=[pltpu.VMEM((devices * own_blocks, FEATS, PBS), BF)] + scratch,
         compiler_params=pltpu.CompilerParams(vmem_limit_bytes=24 * 2**20),
@@ -353,21 +383,21 @@
             transcendentals=0,
         ),
         name="main",
-    )(block_lists.reshape(-1), own, other, cell_xyz, nu_field, vorticity, after, beside)
+    )(block_lists.reshape(-1), own, other, cell_xyz, nu_field, vorticity, beside)
     column = swap_mask(column, devices - 1)
-    next_pair = swap_next(next_pair)
+    theirs = swap_next(mine)
     sides = swap_span(sides)
     pair = swap_mask(pair, 1)
 
     nu_next = pl.pallas_call(
         last_kernel,
         out_shape=field,
-        in_specs=[VMEM] * 8,
+        in_specs=[VMEM] * 9,
         out_specs=VMEM,
-        scratch_shapes=scratch,
+        scratch_shapes=scratch + [pltpu.VMEM(side.shape, F32)],
         compiler_params=pltpu.CompilerParams(vmem_limit_bytes=8 * 2**20),
         name="last",
-    )(middle, nu_field, squares, vorticity, pair, next_pair, sides, column)
+    )(middle, nu_field, squares, vorticity, pair, mine, theirs, sides, column)
     return (nu_next, dist)
 
 

time: 71.4 us -> 71 us (level)
  the two profiles are of different devices: /device:TPU:32 before, /device:TPU:1 now
where the time goes in v8:
time: 71 us; the launch traced here: 70.7 us
  starting transfers between devices  30.1 us (42%)
  Pallas kernels  25.6 us (36%)
  waiting for transfers between devices  13.9 us (20%)
  between operations  0.78 us (1%)
    pallas_call x1, Pallas kernels, shards(): pl.pallas_call(main_kernel, out_shape=(field, field, field) + edges, in_s...  22.9 us
    ppermute x6, starting transfers between devices, swap_mask(): lax.ppermute(block, 'wrap', [(i, i ^ mask) for i in range(lax.axis_size('...  15 us
    all_to_all x1, starting transfers between devices, gather(): lax.all_to_all(chunks, 'wrap', 0, 0, tiled=True, axis_index_groups=members)  10.1 us
    ppermute x6, waiting for transfers between devices, swap_mask(): lax.ppermute(block, 'wrap', [(i, i ^ mask) for i in range(lax.axis_size('...  7.18 us
    all_to_all x1, waiting for transfers between devices, gather(): lax.all_to_all(chunks, 'wrap', 0, 0, tiled=True, axis_index_groups=members)  5.07 us
    ppermute x2, starting transfers between devices, swap_span(): return lax.ppermute(block, 'span', [(0, 1), (1, 0)])  5.01 us
    pallas_call x1, Pallas kernels, shards(): pl.pallas_call(prep_kernel, out_shape=(jax.ShapeDtypeStruct((groups, 4 *...  1.76 us
    ppermute x2, waiting for transfers between devices, swap_span(): return lax.ppermute(block, 'span', [(0, 1), (1, 0)])  1.64 us
  transfers between devices with their start and end apart: 10, of which 5 were waited for; matrix products, arithmetic and copies ran while one was open for 0% of the time, Pallas kernels for 0%

profile of v8, /device:TPU:1, one launch (start us, length us, event | category | flops | bytes accessed | tf_op | source)
XLA Modules:
  0.0 70.7 jit_solution(17383827867370832716)
XLA Ops:
  0.6 1.8 %prep.1 = (f32[16,24,128]{2,1,0:T(8,128)}, f32[8,128]{1,0:T(8,128)}, f32[32,128]{1,0:T(8,128)}) custom-call(f32[3,512]{1,0:T(4,128)} %xyz_hbm.1, f32[1,512]{1,0:T(1,128)} %bitcast.8, f32[32,8,128]{2,1,0:T(8,128)} %nu_ref.3), custom_call_target="tpu_custom_call" | custom-call | tf_op jit(solution)/shard_map/prep/pallas_call | solution.py:357
  2.4 0.0 copy-start.5
  2.4 0.0 copy-start.4
  2.4 10.1 %all-to-all-start = ((f32[16,24,128]{2,1,0:T(8,128)}), f32[16,24,128]{2,1,0:T(8,128)S(1)}, u32[]{:S(2)}, u32[]{:S(2)}) async-start(f32[16,24,128]{2,1,0:T(8,128)} %get-tuple-element.15), calls=%async_computation | async-start | bytes 393216 | tf_op jit(solution)/shard_map/all_to_all | solution.py:333
  12.5 2.5 %collective-permute-start = (f32[32,128]{1,0:T(8,128)S(1)}, f32[32,128]{1,0:T(8,128)S(1)}, u32[]{:S(2)}, u32[]{:S(2)}) collective-permute-start(f32[32,128]{1,0:T(8,128)S(1)} %copy-done.5), channel_id=1, source_target_pairs={{0,1},{1,0},{2,3},{3,2},{4,5},{5,4},{6,7},{7,6},{8,9},{9,8},{10,11... | collective-permute-start | bytes 49160 | tf_op jit(solution)/shard_map/ppermute | solution.py:325
  15.0 1.6 %collective-permute-done.beside_ref = f32[32,128]{1,0:T(8,128)S(1)} collective-permute-done((f32[32,128]{1,0:T(8,128)S(1)}, f32[32,128]{1,0:T(8,128)S(1)}, u32[]{:S(2)}, u32[]{:S(2)}) %collective-permute-start) | collective-permute-done | bytes 16416 | tf_op jit(solution)/shard_map/ppermute | solution.py:325
  16.7 5.1 %all-to-all-done = f32[16,24,128]{2,1,0:T(8,128)S(1)} async-done(((f32[16,24,128]{2,1,0:T(8,128)}), f32[16,24,128]{2,1,0:T(8,128)S(1)}, u32[]{:S(2)}, u32[]{:S(2)}) %all-to-all-start) | async-done | bytes 196640 | tf_op jit(solution)/shard_map/all_to_all | solution.py:333
  21.8 1.4 %collective-permute-start.1 = (f32[256,128]{1,0:T(8,128)S(1)}, f32[256,128]{1,0:T(8,128)S(1)}, u32[]{:S(2)}, u32[]{:S(2)}) collective-permute-start(f32[256,128]{1,0:T(8,128)S(1)} %bitcast.4), channel_id=1, source_target_pairs={{0,4},{2,6},{4,0},{6,2},{8,12},{10,14},{12,8},{14,10},{16,20},{18,... | collective-permute-start | bytes 393224 | tf_op jit(solution)/shard_map/ppermute | solution.py:315
  23.1 2.6 %collective-permute-start.3 = (f32[256,128]{1,0:T(8,128)S(1)}, f32[256,128]{1,0:T(8,128)S(1)}, u32[]{:S(2)}, u32[]{:S(2)}) collective-permute-start(f32[256,128]{1,0:T(8,128)S(1)} %bitcast.5), channel_id=1, source_target_pairs={{0,8},{2,10},{4,12},{6,14},{8,0},{10,2},{12,4},{14,6},{16,24},{18,... | collective-permute-start | bytes 393224 | tf_op jit(solution)/shard_map/ppermute | solution.py:315
  25.8 0.1 collective-permute-start.2
  25.9 0.0 copy-start.2
  25.9 5.0 %collective-permute-done.2 = f32[264,128]{1,0:T(8,128)S(1)} collective-permute-done((f32[264,128]{1,0:T(8,128)S(1)}, f32[264,128]{1,0:T(8,128)S(1)}, u32[]{:S(2)}, u32[]{:S(2)}) %collective-permute-start.2) | collective-permute-done | bytes 135200 | tf_op jit(solution)/shard_map/ppermute | solution.py:315
  31.0 0.0 copy-start
  31.0 0.0 copy-start.1
  31.1 4.3 %collective-permute-start.4 = (f32[1040,128]{1,0:T(8,128)S(1)}, f32[1040,128]{1,0:T(8,128)S(1)}, u32[]{:S(2)}, u32[]{:S(2)}) collective-permute-start(f32[1040,128]{1,0:T(8,128)S(1)} %constant_dynamic-update-slice_fusion.own_ref), channel_id=1, source_target_pairs={{0,2},{2,0},{4,6},{6,4},{8,10},{10,8},{12,14},{14,12},{16,18},{18,... | collective-permute-start | bytes 1597448 | tf_op jit(solution)/shard_map/ppermute | solution.py:315
  35.4 0.1 copy.8
  35.5 0.1 reshape.10.list_ref
  35.6 1.3 %collective-permute-done.4.other_ref = f32[1040,128]{1,0:T(8,128)S(1)} collective-permute-done((f32[1040,128]{1,0:T(8,128)S(1)}, f32[1040,128]{1,0:T(8,128)S(1)}, u32[]{:S(2)}, u32[]{:S(2)}) %collective-permute-start.4) | collective-permute-done | bytes 532512 | tf_op jit(solution)/shard_map/ppermute | solution.py:315
  36.9 22.9 %main.1 = (f32[32,8,128]{2,1,0:T(8,128)}, f32[32,8,128]{2,1,0:T(8,128)S(1)}, f32[32,8,128]{2,1,0:T(8,128)S(1)}, f32[8,128]{1,0:T(8,128)S(1)}, f32[32,128]{1,0:T(...) custom-call(s32[2048]{0:T(1024)S(1)} %reshape.10.list_ref, ...), custom_call_target="tpu_custom_call" | custom-call | flops 8589934592 | bytes 4194304 | tf_op jit(solution)/shard_map/main/pallas_call | solution.py:373
  59.8 0.5 collective-permute-start.8
  60.3 2.5 %collective-permute-start.7 = (f32[32,128]{1,0:T(8,128)S(1)}, f32[32,128]{1,0:T(8,128)S(1)}, u32[]{:S(2)}, u32[]{:S(2)}) collective-permute-start(f32[32,128]{1,0:T(8,128)S(1)} %get-tuple-element.23), channel_id=1, source_target_pairs={{0,1},{1,0},{2,3},{3,2},{4,5},{5,4},{6,7},{7,6},{8,9},{9,8},{10,11... | collective-permute-start | bytes 49160 | tf_op jit(solution)/shard_map/ppermute | solution.py:325
  62.8 6.0 %collective-permute-start.5 = (f32[8,128]{1,0:T(8,128)S(1)}, f32[8,128]{1,0:T(8,128)S(1)}, u32[]{:S(2)}, u32[]{:S(2)}) collective-permute-start(f32[8,128]{1,0:T(8,128)S(1)} %get-tuple-element.21), channel_id=1, source_target_pairs={{0,2},{2,0},{4,6},{6,4},{8,10},{10,8},{12,14},{14,12},{16,18},{18,... | collective-permute-start | bytes 12296 | tf_op jit(solution)/shard_map/ppermute | solution.py:315
  68.9 0.8 %collective-permute-done.5.pair_ref = f32[8,128]{1,0:T(8,128)S(1)} collective-permute-done((f32[8,128]{1,0:T(8,128)S(1)}, f32[8,128]{1,0:T(8,128)S(1)}, u32[]{:S(2)}, u32[]{:S(2)}) %collective-permute-start.5) | collective-permute-done | bytes 4128 | tf_op jit(solution)/shard_map/ppermute | solution.py:315
  69.7 1.0 %last.1 = f32[32,8,128]{2,1,0:T(8,128)} custom-call(f32[32,8,128]{2,1,0:T(8,128)S(1)} %get-tuple-element.19.middle_ref, f32[32,8,128]{2,1,0:T(8,128)S(1)} %copy-done, f32[32,8,128]{2,1,0:T(8,128)S(1)} %get-tuple-element.20.squares_ref, f32[32,8,128]{2,1,0:T(8,128)S(1)} %copy-done.1, f32[8,128]{1,0:T(8,128)S(1)} %collective-permute-done.5.pair_ref, ...), custom_call_target="tpu_custom_call" | custom-call | tf_op jit(solution)/shard_map/last/pallas_call | solution.py:392
  (21 shorter events, 0.1 us)
Async XLA Ops:
  2.4 10.1 %copy-start.5 = (f32[32,128]{1,0:T(8,128)S(1)}, f32[32,128]{1,0:T(8,128)}, u32[]{:S(2)}) copy-start(f32[32,128]{1,0:T(8,128)} %get-tuple-element.16) | copy-start | bytes 49156
  2.4 12.6 %copy-start.4 = (f32[8,128]{1,0:T(8,128)S(1)}, f32[8,128]{1,0:T(8,128)}, u32[]{:S(2)}) copy-start(f32[8,128]{1,0:T(8,128)} %get-tuple-element.14) | copy-start | bytes 12292
  2.4 19.3 %all-to-all-start = ((f32[16,24,128]{2,1,0:T(8,128)}), f32[16,24,128]{2,1,0:T(8,128)S(1)}, u32[]{:S(2)}, u32[]{:S(2)}) async-start(f32[16,24,128]{2,1,0:T(8,128)} %get-tuple-element.15), calls=%async_computation | async-start | bytes 393216 | tf_op jit(solution)/shard_map/all_to_all | solution.py:333
  12.5 4.2 %collective-permute-start = (f32[32,128]{1,0:T(8,128)S(1)}, f32[32,128]{1,0:T(8,128)S(1)}, u32[]{:S(2)}, u32[]{:S(2)}) collective-permute-start(f32[32,128]{1,0:T(8,128)S(1)} %copy-done.5), channel_id=1, source_target_pairs={{0,1},{1,0},{2,3},{3,2},{4,5},{5,4},{6,7},{7,6},{8,9},{9,8},{10,11... | collective-permute-start | bytes 49160 | tf_op jit(solution)/shard_map/ppermute | solution.py:325
  21.8 4.1 %collective-permute-start.1 = (f32[256,128]{1,0:T(8,128)S(1)}, f32[256,128]{1,0:T(8,128)S(1)}, u32[]{:S(2)}, u32[]{:S(2)}) collective-permute-start(f32[256,128]{1,0:T(8,128)S(1)} %bitcast.4), channel_id=1, source_target_pairs={{0,4},{2,6},{4,0},{6,2},{8,12},{10,14},{12,8},{14,10},{16,20},{18,... | collective-permute-start | bytes 393224 | tf_op jit(solution)/shard_map/ppermute | solution.py:315
  23.1 7.9 %collective-permute-start.3 = (f32[256,128]{1,0:T(8,128)S(1)}, f32[256,128]{1,0:T(8,128)S(1)}, u32[]{:S(2)}, u32[]{:S(2)}) collective-permute-start(f32[256,128]{1,0:T(8,128)S(1)} %bitcast.5), channel_id=1, source_target_pairs={{0,8},{2,10},{4,12},{6,14},{8,0},{10,2},{12,4},{14,6},{16,24},{18,... | collective-permute-start | bytes 393224 | tf_op jit(solution)/shard_map/ppermute | solution.py:315
  25.8 5.2 %collective-permute-start.2 = (f32[264,128]{1,0:T(8,128)S(1)}, f32[264,128]{1,0:T(8,128)S(1)}, u32[]{:S(2)}, u32[]{:S(2)}) collective-permute-start(f32[264,128]{1,0:T(8,128)S(1)} %pad_maximum_fusion), channel_id=1, source_target_pairs={{0,12},{2,14},{4,8},{6,10},{8,4},{10,6},{12,0},{14,2},{16,28},{18,... | collective-permute-start | bytes 405512 | tf_op jit(solution)/shard_map/ppermute | solution.py:315
  25.9 11.0 %copy-start.2 = (f32[3,32,8,128]{3,2,1,0:T(8,128)S(1)}, f32[3,32,8,128]{3,2,1,0:T(8,128)}, u32[]{:S(2)}) copy-start(f32[3,32,8,128]{3,2,1,0:T(8,128)} %cell_ref.1) | copy-start | bytes 1179652
  31.0 4.4 %copy-start.3 = (s32[32,8,8]{0,2,1:T(8,128)S(1)}, s32[32,8,8]{0,2,1:T(8,128)}, u32[]{:S(2)}) copy-start(s32[32,8,8]{0,2,1:T(8,128)} %param.9) | copy-start | bytes 24580
  31.0 5.9 %copy-start = (f32[32,8,128]{2,1,0:T(8,128)S(1)}, f32[32,8,128]{2,1,0:T(8,128)}, u32[]{:S(2)}) copy-start(f32[32,8,128]{2,1,0:T(8,128)} %nu_ref.3) | copy-start | bytes 393220
  31.0 5.9 %copy-start.1 = (f32[32,8,128]{2,1,0:T(8,128)S(1)}, f32[32,8,128]{2,1,0:T(8,128)}, u32[]{:S(2)}) copy-start(f32[32,8,128]{2,1,0:T(8,128)} %vorticity_ref.3) | copy-start | bytes 393220
  31.1 5.9 %collective-permute-start.4 = (f32[1040,128]{1,0:T(8,128)S(1)}, f32[1040,128]{1,0:T(8,128)S(1)}, u32[]{:S(2)}, u32[]{:S(2)}) collective-permute-start(f32[1040,128]{1,0:T(8,128)S(1)} %constant_dynamic-update-slice_fusion.own_ref), channel_id=1, source_target_pairs={{0,2},{2,0},{4,6},{6,4},{8,10},{10,8},{12,14},{14,12},{16,18},{18,... | collective-permute-start | bytes 1597448 | tf_op jit(solution)/shard_map/ppermute | solution.py:315
  59.8 9.9 %collective-permute-start.8 = (f32[40,128]{1,0:T(8,128)S(1)}, f32[40,128]{1,0:T(8,128)S(1)}, u32[]{:S(2)}, u32[]{:S(2)}) collective-permute-start(f32[40,128]{1,0:T(8,128)S(1)} %get-tuple-element.24), channel_id=1, source_target_pairs={{0,254},{2,252},{4,250},{6,248},{8,246},{10,244},{12,242},{14,240}... | collective-permute-start | bytes 61448 | tf_op jit(solution)/shard_map/ppermute | solution.py:315
  60.3 9.3 %collective-permute-start.6 = (f32[32,128]{1,0:T(8,128)S(1)}, f32[32,128]{1,0:T(8,128)S(1)}, u32[]{:S(2)}, u32[]{:S(2)}) collective-permute-start(f32[32,128]{1,0:T(8,128)S(1)} %get-tuple-element.22.mine_ref), channel_id=1, source_target_pairs={{2,4},{6,8},{10,12},{14,16},{18,20},{22,24},{26,28},{30,32},{34,36... | collective-permute-start | bytes 49160 | tf_op jit(solution)/shard_map/ppermute | solution.py:321
  60.3 9.3 %collective-permute-start.7 = (f32[32,128]{1,0:T(8,128)S(1)}, f32[32,128]{1,0:T(8,128)S(1)}, u32[]{:S(2)}, u32[]{:S(2)}) collective-permute-start(f32[32,128]{1,0:T(8,128)S(1)} %get-tuple-element.23), channel_id=1, source_target_pairs={{0,1},{1,0},{2,3},{3,2},{4,5},{5,4},{6,7},{7,6},{8,9},{9,8},{10,11... | collective-permute-start | bytes 49160 | tf_op jit(solution)/shard_map/ppermute | solution.py:325
  62.8 6.9 %collective-permute-start.5 = (f32[8,128]{1,0:T(8,128)S(1)}, f32[8,128]{1,0:T(8,128)S(1)}, u32[]{:S(2)}, u32[]{:S(2)}) collective-permute-start(f32[8,128]{1,0:T(8,128)S(1)} %get-tuple-element.21), channel_id=1, source_target_pairs={{0,2},{2,0},{4,6},{6,4},{8,10},{10,8},{12,14},{14,12},{16,18},{18,... | collective-permute-start | bytes 12296 | tf_op jit(solution)/shard_map/ppermute | solution.py:315

commit v9 on v8

--- a/solution.py
+++ b/solution.py
@@ -11,8 +11,9 @@
 F32 = jnp.float32
 PBS = 128
 FEATS = 48
-LINES_PER_STEP = 64
-COLUMN_ROWS = 40
+LINES_PER_STEP = 128
+COLUMN_ROWS = 48
+SIDE_ROWS = 40
 GROUP_BIT = 3
 Y_MASKS = (2, 6, 4)
 
@@ -185,7 +186,7 @@
                 table_ref[base + pair * 2 + 1] = panel_features(pltpu.roll(rows, 4, 0))
         return carry
 
-    lax.fori_loop(0, slots, body, 0)
+    lax.fori_loop(0, slots, body, 0, unroll=4)
 
 
 def nearest_tile(tile, list_ref, cell_ref, table_ref):
@@ -265,6 +266,7 @@
     column = lax.fori_loop(0, tiles // per_step, body, jnp.zeros((8, 128), F32))
     for row in range(0, column_out.shape[0], 8):
         column_out[row : row + 8] = column
+    beside_out[tiles:] = jnp.zeros((beside_out.shape[0] - tiles, 128), F32)
     first, last = middle_ref[0], middle_ref[tiles - 1]
     pair_out[...] = jnp.where(even, last, first)
     next_out[8:16] = jnp.where(even, first, last)
@@ -295,7 +297,7 @@
     halo = Halo(
         middle_ref, pair_ref[...], after, beside_ref, column_ref[0:8], padded_ref, ghost_ref
     )
-    side_ref[...] = beside_ref[...]
+    side_ref[...] = beside_ref[0:rows]
     halo.beside = side_ref
     fixed = partial + missing_term(value, other)
     side_term = missing_term(side, other_side)[0:1]
@@ -350,7 +352,12 @@
     field = jax.ShapeDtypeStruct(nu_field.shape, F32)
     side = jax.ShapeDtypeStruct((rows, cells), F32)
     opened = jax.ShapeDtypeStruct((32, cells), F32)
-    edges = (tile, opened, side, jax.ShapeDtypeStruct((COLUMN_ROWS, cells), F32))
+    edges = (
+        tile,
+        opened,
+        jax.ShapeDtypeStruct((SIDE_ROWS, cells), F32),
+        jax.ShapeDtypeStruct((COLUMN_ROWS, cells), F32),
+    )
     scratch = [pltpu.VMEM((rows + 2, span, cells), F32), pltpu.VMEM(nu_field.shape, F32)]
 
     groups = devices >> GROUP_BIT

time: 71 us -> 69.2 us (0.975)
  the two profiles are of different devices: /device:TPU:1 before, /device:TPU:32 now
where the time goes in v9:
time: 69.2 us; the launch traced here: 68.9 us
  Pallas kernels  24.4 us (35%)
  starting transfers between devices  23.8 us (34%)
  waiting for transfers between devices  19.2 us (28%)
  between operations  0.75 us (1%)
  local copies, waits for them, and re-layouts  0.72 us (1%)
    pallas_call x1, Pallas kernels, shards(): pl.pallas_call(main_kernel, out_shape=(field, field, field) + edges, in_s...  21.6 us
    all_to_all x1, starting transfers between devices, gather(): lax.all_to_all(chunks, 'wrap', 0, 0, tiled=True, axis_index_groups=members)  9.53 us
    ppermute x6, waiting for transfers between devices, swap_mask(): lax.ppermute(block, 'wrap', [(i, i ^ mask) for i in range(lax.axis_size('...  8.4 us
    ppermute x6, starting transfers between devices, swap_mask(): lax.ppermute(block, 'wrap', [(i, i ^ mask) for i in range(lax.axis_size('...  7.86 us
    ppermute x2, starting transfers between devices, swap_span(): return lax.ppermute(block, 'span', [(0, 1), (1, 0)])  5.58 us
    ppermute x1, waiting for transfers between devices, swap_next(): return lax.ppermute(block, 'wrap', pairs + [(j, i) for i, j in pairs])  4.2 us
    all_to_all x1, waiting for transfers between devices, gather(): lax.all_to_all(chunks, 'wrap', 0, 0, tiled=True, axis_index_groups=members)  4.13 us
    ppermute x2, waiting for transfers between devices, swap_span(): return lax.ppermute(block, 'span', [(0, 1), (1, 0)])  2.51 us
  transfers between devices with their start and end apart: 10, of which 7 were waited for; matrix products, arithmetic and copies ran while one was open for 0% of the time, Pallas kernels for 0%

profile of v9, /device:TPU:32, one launch (start us, length us, event | category | flops | bytes accessed | tf_op | source)
XLA Modules:
  0.0 68.9 jit_solution(14047016668719380995)
XLA Ops:
  0.6 1.8 %prep.1 = (f32[16,24,128]{2,1,0:T(8,128)}, f32[8,128]{1,0:T(8,128)}, f32[32,128]{1,0:T(8,128)}) custom-call(f32[3,512]{1,0:T(4,128)} %xyz_hbm.1, f32[1,512]{1,0:T(1,128)} %bitcast.8, f32[32,8,128]{2,1,0:T(8,128)} %nu_ref.3), custom_call_target="tpu_custom_call" | custom-call | tf_op jit(solution)/shard_map/prep/pallas_call | solution.py:364
  2.4 0.0 copy-start.4
  2.4 9.5 %all-to-all-start = ((f32[16,24,128]{2,1,0:T(8,128)}), f32[16,24,128]{2,1,0:T(8,128)S(1)}, u32[]{:S(2)}, u32[]{:S(2)}) async-start(f32[16,24,128]{2,1,0:T(8,128)} %get-tuple-element.15), calls=%async_computation | async-start | bytes 393216 | tf_op jit(solution)/shard_map/all_to_all | solution.py:335
  12.0 2.8 %collective-permute-start = (f32[32,128]{1,0:T(8,128)S(1)}, f32[32,128]{1,0:T(8,128)S(1)}, u32[]{:S(2)}, u32[]{:S(2)}) collective-permute-start(f32[32,128]{1,0:T(8,128)S(1)} %copy-done.5), channel_id=1, source_target_pairs={{0,1},{1,0},{2,3},{3,2},{4,5},{5,4},{6,7},{7,6},{8,9},{9,8},{10,11... | collective-permute-start | bytes 49160 | tf_op jit(solution)/shard_map/ppermute | solution.py:327
  14.8 2.5 %collective-permute-done.beside_ref = f32[32,128]{1,0:T(8,128)S(1)} collective-permute-done((f32[32,128]{1,0:T(8,128)S(1)}, f32[32,128]{1,0:T(8,128)S(1)}, u32[]{:S(2)}, u32[]{:S(2)}) %collective-permute-start) | collective-permute-done | bytes 16416 | tf_op jit(solution)/shard_map/ppermute | solution.py:327
  17.3 4.1 %all-to-all-done = f32[16,24,128]{2,1,0:T(8,128)S(1)} async-done(((f32[16,24,128]{2,1,0:T(8,128)}), f32[16,24,128]{2,1,0:T(8,128)S(1)}, u32[]{:S(2)}, u32[]{:S(2)}) %all-to-all-start) | async-done | bytes 196640 | tf_op jit(solution)/shard_map/all_to_all | solution.py:335
  21.4 1.7 %collective-permute-start.1 = (f32[256,128]{1,0:T(8,128)S(1)}, f32[256,128]{1,0:T(8,128)S(1)}, u32[]{:S(2)}, u32[]{:S(2)}) collective-permute-start(f32[256,128]{1,0:T(8,128)S(1)} %bitcast.4), channel_id=1, source_target_pairs={{0,4},{2,6},{4,0},{6,2},{8,12},{10,14},{12,8},{14,10},{16,20},{18,... | collective-permute-start | bytes 393224 | tf_op jit(solution)/shard_map/ppermute | solution.py:317
  23.1 2.9 %collective-permute-start.3 = (f32[256,128]{1,0:T(8,128)S(1)}, f32[256,128]{1,0:T(8,128)S(1)}, u32[]{:S(2)}, u32[]{:S(2)}) collective-permute-start(f32[256,128]{1,0:T(8,128)S(1)} %bitcast.5), channel_id=1, source_target_pairs={{0,8},{2,10},{4,12},{6,14},{8,0},{10,2},{12,4},{14,6},{16,24},{18,... | collective-permute-start | bytes 393224 | tf_op jit(solution)/shard_map/ppermute | solution.py:317
  26.0 0.3 collective-permute-start.2
  26.3 1.1 %collective-permute-done.1 = f32[256,128]{1,0:T(8,128)S(1)} collective-permute-done((f32[256,128]{1,0:T(8,128)S(1)}, f32[256,128]{1,0:T(8,128)S(1)}, u32[]{:S(2)}, u32[]{:S(2)}) %collective-permute-start.1) | collective-permute-done | bytes 131104 | tf_op jit(solution)/shard_map/ppermute | solution.py:317
  27.5 4.8 %collective-permute-done.2 = f32[264,128]{1,0:T(8,128)S(1)} collective-permute-done((f32[264,128]{1,0:T(8,128)S(1)}, f32[264,128]{1,0:T(8,128)S(1)}, u32[]{:S(2)}, u32[]{:S(2)}) %collective-permute-start.2) | collective-permute-done | bytes 135200 | tf_op jit(solution)/shard_map/ppermute | solution.py:317
  32.3 0.0 copy-start.3
  32.4 0.3 collective-permute-start.4
  32.7 0.4 copy-done.3
  33.1 0.1 copy.8
  33.2 0.1 reshape.10.list_ref
  33.3 1.3 %collective-permute-done.4.other_ref = f32[1040,128]{1,0:T(8,128)S(1)} collective-permute-done((f32[1040,128]{1,0:T(8,128)S(1)}, f32[1040,128]{1,0:T(8,128)S(1)}, u32[]{:S(2)}, u32[]{:S(2)}) %collective-permute-start.4) | collective-permute-done | bytes 532512 | tf_op jit(solution)/shard_map/ppermute | solution.py:317
  34.6 21.6 %main.1 = (f32[32,8,128]{2,1,0:T(8,128)}, f32[32,8,128]{2,1,0:T(8,128)S(1)}, f32[32,8,128]{2,1,0:T(8,128)S(1)}, f32[8,128]{1,0:T(8,128)S(1)}, f32[32,128]{1,0:T(...) custom-call(s32[2048]{0:T(1024)S(1)} %reshape.10.list_ref, ...), custom_call_target="tpu_custom_call" | custom-call | flops 8589934592 | bytes 4194304 | tf_op jit(solution)/shard_map/main/pallas_call | solution.py:380
  56.2 2.7 %collective-permute-start.8 = (f32[48,128]{1,0:T(8,128)S(1)}, f32[48,128]{1,0:T(8,128)S(1)}, u32[]{:S(2)}, u32[]{:S(2)}) collective-permute-start(f32[48,128]{1,0:T(8,128)S(1)} %get-tuple-element.24), channel_id=1, source_target_pairs={{0,254},{2,252},{4,250},{6,248},{8,246},{10,244},{12,242},{14,240}... | collective-permute-start | bytes 73736 | tf_op jit(solution)/shard_map/ppermute | solution.py:317
  58.9 2.8 %collective-permute-start.7 = (f32[40,128]{1,0:T(8,128)S(1)}, f32[40,128]{1,0:T(8,128)S(1)}, u32[]{:S(2)}, u32[]{:S(2)}) collective-permute-start(f32[40,128]{1,0:T(8,128)S(1)} %get-tuple-element.23), channel_id=1, source_target_pairs={{0,1},{1,0},{2,3},{3,2},{4,5},{5,4},{6,7},{7,6},{8,9},{9,8},{10,11... | collective-permute-start | bytes 61448 | tf_op jit(solution)/shard_map/ppermute | solution.py:327
  61.7 0.8 %collective-permute-start.6 = (f32[32,128]{1,0:T(8,128)S(1)}, f32[32,128]{1,0:T(8,128)S(1)}, u32[]{:S(2)}, u32[]{:S(2)}) collective-permute-start(f32[32,128]{1,0:T(8,128)S(1)} %get-tuple-element.22.mine_ref), channel_id=1, source_target_pairs={{2,4},{6,8},{10,12},{14,16},{18,20},{22,24},{26,28},{30,32},{34,36... | collective-permute-start | bytes 49160 | tf_op jit(solution)/shard_map/ppermute | solution.py:323
  62.5 1.2 %collective-permute-done.5.pair_ref = f32[8,128]{1,0:T(8,128)S(1)} collective-permute-done((f32[8,128]{1,0:T(8,128)S(1)}, f32[8,128]{1,0:T(8,128)S(1)}, u32[]{:S(2)}, u32[]{:S(2)}) %collective-permute-start.5) | collective-permute-done | bytes 4128 | tf_op jit(solution)/shard_map/ppermute | solution.py:317
  63.7 4.2 %collective-permute-done.6.theirs_ref = f32[32,128]{1,0:T(8,128)S(1)} collective-permute-done((f32[32,128]{1,0:T(8,128)S(1)}, f32[32,128]{1,0:T(8,128)S(1)}, u32[]{:S(2)}, u32[]{:S(2)}) %collective-permute-start.6) | collective-permute-done | bytes 16416 | tf_op jit(solution)/shard_map/ppermute | solution.py:323
  67.9 1.0 %last.1 = f32[32,8,128]{2,1,0:T(8,128)} custom-call(f32[32,8,128]{2,1,0:T(8,128)S(1)} %get-tuple-element.19.middle_ref, f32[32,8,128]{2,1,0:T(8,128)S(1)} %copy-done, f32[32,8,128]{2,1,0:T(8,128)S(1)} %get-tuple-element.20.squares_ref, f32[32,8,128]{2,1,0:T(8,128)S(1)} %copy-done.1, f32[8,128]{1,0:T(8,128)S(1)} %collective-permute-done.5.pair_ref, ...), custom_call_target="tpu_custom_call" | custom-call | tf_op jit(solution)/shard_map/last/pallas_call | solution.py:399
  (21 shorter events, 0.1 us)
Async XLA Ops:
  2.4 9.6 %copy-start.5 = (f32[32,128]{1,0:T(8,128)S(1)}, f32[32,128]{1,0:T(8,128)}, u32[]{:S(2)}) copy-start(f32[32,128]{1,0:T(8,128)} %get-tuple-element.16) | copy-start | bytes 49156
  2.4 12.4 %copy-start.4 = (f32[8,128]{1,0:T(8,128)S(1)}, f32[8,128]{1,0:T(8,128)}, u32[]{:S(2)}) copy-start(f32[8,128]{1,0:T(8,128)} %get-tuple-element.14) | copy-start | bytes 12292
  2.4 19.0 %all-to-all-start = ((f32[16,24,128]{2,1,0:T(8,128)}), f32[16,24,128]{2,1,0:T(8,128)S(1)}, u32[]{:S(2)}, u32[]{:S(2)}) async-start(f32[16,24,128]{2,1,0:T(8,128)} %get-tuple-element.15), calls=%async_computation | async-start | bytes 393216 | tf_op jit(solution)/shard_map/all_to_all | solution.py:335
  12.0 5.3 %collective-permute-start = (f32[32,128]{1,0:T(8,128)S(1)}, f32[32,128]{1,0:T(8,128)S(1)}, u32[]{:S(2)}, u32[]{:S(2)}) collective-permute-start(f32[32,128]{1,0:T(8,128)S(1)} %copy-done.5), channel_id=1, source_target_pairs={{0,1},{1,0},{2,3},{3,2},{4,5},{5,4},{6,7},{7,6},{8,9},{9,8},{10,11... | collective-permute-start | bytes 49160 | tf_op jit(solution)/shard_map/ppermute | solution.py:327
  21.4 6.0 %collective-permute-start.1 = (f32[256,128]{1,0:T(8,128)S(1)}, f32[256,128]{1,0:T(8,128)S(1)}, u32[]{:S(2)}, u32[]{:S(2)}) collective-permute-start(f32[256,128]{1,0:T(8,128)S(1)} %bitcast.4), channel_id=1, source_target_pairs={{0,4},{2,6},{4,0},{6,2},{8,12},{10,14},{12,8},{14,10},{16,20},{18,... | collective-permute-start | bytes 393224 | tf_op jit(solution)/shard_map/ppermute | solution.py:317
  23.1 9.3 %collective-permute-start.3 = (f32[256,128]{1,0:T(8,128)S(1)}, f32[256,128]{1,0:T(8,128)S(1)}, u32[]{:S(2)}, u32[]{:S(2)}) collective-permute-start(f32[256,128]{1,0:T(8,128)S(1)} %bitcast.5), channel_id=1, source_target_pairs={{0,8},{2,10},{4,12},{6,14},{8,0},{10,2},{12,4},{14,6},{16,24},{18,... | collective-permute-start | bytes 393224 | tf_op jit(solution)/shard_map/ppermute | solution.py:317
  26.0 6.3 %collective-permute-start.2 = (f32[264,128]{1,0:T(8,128)S(1)}, f32[264,128]{1,0:T(8,128)S(1)}, u32[]{:S(2)}, u32[]{:S(2)}) collective-permute-start(f32[264,128]{1,0:T(8,128)S(1)} %pad_maximum_fusion), channel_id=1, source_target_pairs={{0,12},{2,14},{4,8},{6,10},{8,4},{10,6},{12,0},{14,2},{16,28},{18,... | collective-permute-start | bytes 405512 | tf_op jit(solution)/shard_map/ppermute | solution.py:317
  27.5 7.1 %copy-start.2 = (f32[3,32,8,128]{3,2,1,0:T(8,128)S(1)}, f32[3,32,8,128]{3,2,1,0:T(8,128)}, u32[]{:S(2)}) copy-start(f32[3,32,8,128]{3,2,1,0:T(8,128)} %cell_ref.1) | copy-start | bytes 1179652
  32.3 0.8 %copy-start.3 = (s32[32,8,8]{0,2,1:T(8,128)S(1)}, s32[32,8,8]{0,2,1:T(8,128)}, u32[]{:S(2)}) copy-start(s32[32,8,8]{0,2,1:T(8,128)} %param.9) | copy-start | bytes 24580
  32.4 2.2 %copy-start = (f32[32,8,128]{2,1,0:T(8,128)S(1)}, f32[32,8,128]{2,1,0:T(8,128)}, u32[]{:S(2)}) copy-start(f32[32,8,128]{2,1,0:T(8,128)} %nu_ref.3) | copy-start | bytes 393220
  32.4 2.2 %copy-start.1 = (f32[32,8,128]{2,1,0:T(8,128)S(1)}, f32[32,8,128]{2,1,0:T(8,128)}, u32[]{:S(2)}) copy-start(f32[32,8,128]{2,1,0:T(8,128)} %vorticity_ref.3) | copy-start | bytes 393220
  32.4 2.2 %collective-permute-start.4 = (f32[1040,128]{1,0:T(8,128)S(1)}, f32[1040,128]{1,0:T(8,128)S(1)}, u32[]{:S(2)}, u32[]{:S(2)}) collective-permute-start(f32[1040,128]{1,0:T(8,128)S(1)} %constant_dynamic-update-slice_fusion.own_ref), channel_id=1, source_target_pairs={{0,2},{2,0},{4,6},{6,4},{8,10},{10,8},{12,14},{14,12},{16,18},{18,... | collective-permute-start | bytes 1597448 | tf_op jit(solution)/shard_map/ppermute | solution.py:317
  56.2 11.6 %collective-permute-start.8 = (f32[48,128]{1,0:T(8,128)S(1)}, f32[48,128]{1,0:T(8,128)S(1)}, u32[]{:S(2)}, u32[]{:S(2)}) collective-permute-start(f32[48,128]{1,0:T(8,128)S(1)} %get-tuple-element.24), channel_id=1, source_target_pairs={{0,254},{2,252},{4,250},{6,248},{8,246},{10,244},{12,242},{14,240}... | collective-permute-start | bytes 73736 | tf_op jit(solution)/shard_map/ppermute | solution.py:317
  58.9 8.9 %collective-permute-start.7 = (f32[40,128]{1,0:T(8,128)S(1)}, f32[40,128]{1,0:T(8,128)S(1)}, u32[]{:S(2)}, u32[]{:S(2)}) collective-permute-start(f32[40,128]{1,0:T(8,128)S(1)} %get-tuple-element.23), channel_id=1, source_target_pairs={{0,1},{1,0},{2,3},{3,2},{4,5},{5,4},{6,7},{7,6},{8,9},{9,8},{10,11... | collective-permute-start | bytes 61448 | tf_op jit(solution)/shard_map/ppermute | solution.py:327
  61.7 6.2 %collective-permute-start.6 = (f32[32,128]{1,0:T(8,128)S(1)}, f32[32,128]{1,0:T(8,128)S(1)}, u32[]{:S(2)}, u32[]{:S(2)}) collective-permute-start(f32[32,128]{1,0:T(8,128)S(1)} %get-tuple-element.22.mine_ref), channel_id=1, source_target_pairs={{2,4},{6,8},{10,12},{14,16},{18,20},{22,24},{26,28},{30,32},{34,36... | collective-permute-start | bytes 49160 | tf_op jit(solution)/shard_map/ppermute | solution.py:323
  62.5 1.2 %collective-permute-start.5 = (f32[8,128]{1,0:T(8,128)S(1)}, f32[8,128]{1,0:T(8,128)S(1)}, u32[]{:S(2)}, u32[]{:S(2)}) collective-permute-start(f32[8,128]{1,0:T(8,128)S(1)} %get-tuple-element.21), channel_id=1, source_target_pairs={{0,2},{2,0},{4,6},{6,4},{8,10},{10,8},{12,14},{14,12},{16,18},{18,... | collective-permute-start | bytes 12296 | tf_op jit(solution)/shard_map/ppermute | solution.py:317

commit v10 on v9

--- a/solution.py
+++ b/solution.py
@@ -168,25 +168,20 @@
     place = lax.axis_index("wrap")
     own_blocks = table_ref.shape[0] // lax.axis_size("wrap")
     groups = lax.axis_size("wrap") >> GROUP_BIT
-    slots = groups * (len(Y_MASKS) + 1)
-
-    def body(slot, carry):
-        choice = slot // groups
-        near = jnp.where(choice == 0, 0, Y_MASKS[0])
-        for n in range(1, len(Y_MASKS)):
-            near = jnp.where(choice == n + 1, Y_MASKS[n], near)
-        low = (place & ((1 << GROUP_BIT) - 1)) ^ near
-        skip = jnp.where(choice == 3, 16, 8)
-        for half, ref in enumerate(halves):
-            base = (((slot % groups) << GROUP_BIT) | (low ^ half)) * own_blocks
-            for pair in range(own_blocks // 2):
-                start = pl.multiple_of(slot * own_blocks * 4 + skip + pair * 8, 8)
-                rows = ref[pl.ds(start, 8), :]
-                table_ref[base + pair * 2] = panel_features(rows)
-                table_ref[base + pair * 2 + 1] = panel_features(pltpu.roll(rows, 4, 0))
+    low = place & ((1 << GROUP_BIT) - 1)
+
+    def body(group, carry):
+        for half, pieces in enumerate(halves):
+            for ref, mask in zip(pieces, (0,) + Y_MASKS):
+                base = ((group << GROUP_BIT) | (low ^ mask ^ half)) * own_blocks
+                for pair in range(own_blocks // 2):
+                    start = pl.multiple_of(group * own_blocks * 4 + pair * 8, 8)
+                    rows = ref[pl.ds(start, 8), :]
+                    table_ref[base + pair * 2] = panel_features(rows)
+                    table_ref[base + pair * 2 + 1] = panel_features(pltpu.roll(rows, 4, 0))
         return carry
 
-    lax.fori_loop(0, slots, body, 0, unroll=4)
+    lax.fori_loop(0, groups, body, 0)
 
 
 def nearest_tile(tile, list_ref, cell_ref, table_ref):
@@ -217,8 +212,14 @@
 
 def main_kernel(
     list_ref,
-    own_ref,
-    other_ref,
+    own0_ref,
+    own1_ref,
+    own2_ref,
+    own3_ref,
+    other0_ref,
+    other1_ref,
+    other2_ref,
+    other3_ref,
     cell_ref,
     nu_ref,
     vorticity_ref,
@@ -234,9 +235,9 @@
     padded_ref,
     ghost_ref,
 ):
-    total = (other_ref.shape[0] - 16) // 4
-    column = other_ref[3 * total + 8 : 3 * total + 16]
-    pair = other_ref[0:8]
+    total = own0_ref.shape[0]
+    column = other2_ref[total : total + 8]
+    pair = other0_ref[total : total + 8]
     tiles = nu_ref.shape[0]
     even = even_place()
     open_row = jnp.where(even, nu_ref[0], nu_ref[tiles - 1])
@@ -246,7 +247,9 @@
     next_out[0:8] = open_row
     next_out[16:24] = jnp.broadcast_to(open_side, (8, 128))
     next_out[24:32] = jnp.broadcast_to(open_partner, (8, 128))
-    build_table((own_ref, other_ref), table_ref)
+    own = (own0_ref, own1_ref, own2_ref, own3_ref)
+    other = (other0_ref, other1_ref, other2_ref, other3_ref)
+    build_table((own, other), table_ref)
     per_step = LINES_PER_STEP // 8
 
     def body(step, column):
@@ -337,11 +340,15 @@
     shard = chunks[:, :size].reshape(groups * size, lanes)
     opposite = groups - 1 - (lax.axis_index("wrap") >> GROUP_BIT)
     column = lax.dynamic_slice(chunks, (opposite, size, 0), (1, 8, lanes))[0]
-    first = swap_mask(shard, Y_MASKS[0])
-    second = swap_mask(jnp.concatenate([shard, column], 0), Y_MASKS[1])
-    third = swap_mask(shard, Y_MASKS[2])
-    shard = jnp.concatenate([pair, shard, first, second, third], 0)
-    return shard, swap_mask(shard, 1), beside
+    own = [
+        shard,
+        swap_mask(shard, Y_MASKS[0]),
+        swap_mask(jnp.concatenate([shard, column], 0), Y_MASKS[1]),
+        swap_mask(shard, Y_MASKS[2]),
+    ]
+    other = [swap_mask(jnp.concatenate([shard, pair], 0), 1)]
+    other += [swap_mask(piece, 1) for piece in own[1:]]
+    return own, other, beside
 
 
 def shards(cell_xyz, panel_xyz, panel_size, block_lists, nu_field, vorticity):
@@ -380,7 +387,7 @@
     dist, squares, middle, pair, mine, sides, column = pl.pallas_call(
         main_kernel,
         out_shape=(field, field, field) + edges,
-        in_specs=[SMEM] + [VMEM] * 6,
+        in_specs=[SMEM] + [VMEM] * 12,
         out_specs=(VMEM,) * 7,
         scratch_shapes=[pltpu.VMEM((devices * own_blocks, FEATS, PBS), BF)] + scratch,
         compiler_params=pltpu.CompilerParams(vmem_limit_bytes=24 * 2**20),
@@ -390,7 +397,7 @@
             transcendentals=0,
         ),
         name="main",
-    )(block_lists.reshape(-1), own, other, cell_xyz, nu_field, vorticity, beside)
+    )(block_lists.reshape(-1), *own, *other, cell_xyz, nu_field, vorticity, beside)
     column = swap_mask(column, devices - 1)
     theirs = swap_next(mine)
     sides = swap_span(sides)

time: 69.2 us -> 68.7 us (level)
    ppermute x6 -> x9, waiting for transfers between devices: 8.4 us -> 7.19 us  [swap_mask(): lax.ppermute(block, 'wrap', [(i, i ^ mask) for i in range(lax.axis_size('...]
    ppermute x1, waiting for transfers between devices: 4.2 us -> 5 us  [swap_next(): return lax.ppermute(block, 'wrap', pairs + [(j, i) for i, j in pairs])]
    ppermute x1, starting transfers between devices: 0.8 us -> 0.01 us  [swap_next(): return lax.ppermute(block, 'wrap', pairs + [(j, i) for i, j in pairs])]
    ppermute x6 -> x9, starting transfers between devices: 7.86 us -> 8.36 us  [swap_mask(): lax.ppermute(block, 'wrap', [(i, i ^ mask) for i in range(lax.axis_size('...]
  transfers between devices with their start and end apart: 10 -> 13, of which waited for: 7 -> 8; matrix products, arithmetic and copies ran while one was open for 0% -> 0% of each run, Pallas kernels for 0% -> 0%
where the time goes in v10:
time: 68.7 us; the launch traced here: 68.4 us
  Pallas kernels  24.5 us (36%)
  starting transfers between devices  23.4 us (34%)
  waiting for transfers between devices  18.8 us (27%)
  local copies, waits for them, and re-layouts  0.9 us (1%)
  between operations  0.72 us (1%)
    pallas_call x1, Pallas kernels, shards(): pl.pallas_call(main_kernel, out_shape=(field, field, field) + edges, in_s...  21.7 us
    all_to_all x1, starting transfers between devices, gather(): lax.all_to_all(chunks, 'wrap', 0, 0, tiled=True, axis_index_groups=members)  9.53 us
    ppermute x9, starting transfers between devices, swap_mask(): lax.ppermute(block, 'wrap', [(i, i ^ mask) for i in range(lax.axis_size('...  8.36 us
    ppermute x9, waiting for transfers between devices, swap_mask(): lax.ppermute(block, 'wrap', [(i, i ^ mask) for i in range(lax.axis_size('...  7.19 us
    ppermute x2, starting transfers between devices, swap_span(): return lax.ppermute(block, 'span', [(0, 1), (1, 0)])  5.55 us
    ppermute x1, waiting for transfers between devices, swap_next(): return lax.ppermute(block, 'wrap', pairs + [(j, i) for i, j in pairs])  5 us
    all_to_all x1, waiting for transfers between devices, gather(): lax.all_to_all(chunks, 'wrap', 0, 0, tiled=True, axis_index_groups=members)  4.13 us
    ppermute x2, waiting for transfers between devices, swap_span(): return lax.ppermute(block, 'span', [(0, 1), (1, 0)])  2.52 us
  transfers between devices with their start and end apart: 13, of which 8 were waited for; matrix products, arithmetic and copies ran while one was open for 0% of the time, Pallas kernels for 0%

profile of v10, /device:TPU:32, one launch (start us, length us, event | category | flops | bytes accessed | tf_op | source)
XLA Modules:
  0.0 68.4 jit_solution(3648818555871313612)
XLA Ops:
  0.6 1.7 %prep.1 = (f32[16,24,128]{2,1,0:T(8,128)}, f32[8,128]{1,0:T(8,128)}, f32[32,128]{1,0:T(8,128)}) custom-call(f32[3,512]{1,0:T(4,128)} %xyz_hbm.1, f32[1,512]{1,0:T(1,128)} %bitcast.8, f32[32,8,128]{2,1,0:T(8,128)} %nu_ref.3), custom_call_target="tpu_custom_call" | custom-call | tf_op jit(solution)/shard_map/prep/pallas_call | solution.py:371
  2.4 0.0 copy-start.5
  2.4 9.5 %all-to-all-start = ((f32[16,24,128]{2,1,0:T(8,128)}), f32[16,24,128]{2,1,0:T(8,128)S(1)}, u32[]{:S(2)}, u32[]{:S(2)}) async-start(f32[16,24,128]{2,1,0:T(8,128)} %get-tuple-element.14), calls=%async_computation | async-start | bytes 393216 | tf_op jit(solution)/shard_map/all_to_all | solution.py:338
  11.9 2.8 %collective-permute-start = (f32[32,128]{1,0:T(8,128)S(1)}, f32[32,128]{1,0:T(8,128)S(1)}, u32[]{:S(2)}, u32[]{:S(2)}) collective-permute-start(f32[32,128]{1,0:T(8,128)S(1)} %copy-done.5), channel_id=1, source_target_pairs={{0,1},{1,0},{2,3},{3,2},{4,5},{5,4},{6,7},{7,6},{8,9},{9,8},{10,11... | collective-permute-start | bytes 49160 | tf_op jit(solution)/shard_map/ppermute | solution.py:330
  14.7 2.5 %collective-permute-done.beside_ref = f32[32,128]{1,0:T(8,128)S(1)} collective-permute-done((f32[32,128]{1,0:T(8,128)S(1)}, f32[32,128]{1,0:T(8,128)S(1)}, u32[]{:S(2)}, u32[]{:S(2)}) %collective-permute-start) | collective-permute-done | bytes 16416 | tf_op jit(solution)/shard_map/ppermute | solution.py:330
  17.3 4.1 %all-to-all-done = f32[16,24,128]{2,1,0:T(8,128)S(1)} async-done(((f32[16,24,128]{2,1,0:T(8,128)}), f32[16,24,128]{2,1,0:T(8,128)S(1)}, u32[]{:S(2)}, u32[]{:S(2)}) %all-to-all-start) | async-done | bytes 196640 | tf_op jit(solution)/shard_map/all_to_all | solution.py:338
  21.4 0.6 copy-done.4
  22.1 3.1 %collective-permute-start.2 = (f32[264,128]{1,0:T(8,128)S(1)}, f32[264,128]{1,0:T(8,128)S(1)}, u32[]{:S(2)}, u32[]{:S(2)}) collective-permute-start(f32[264,128]{1,0:T(8,128)S(1)} %get-tuple-element.27), channel_id=1, source_target_pairs={{0,12},{2,14},{4,8},{6,10},{8,4},{10,6},{12,0},{14,2},{16,28},{18,... | collective-permute-start | bytes 405512 | tf_op jit(solution)/shard_map/ppermute | solution.py:320
  25.2 0.6 collective-permute-start.3
  25.8 0.5 collective-permute-start.1
  26.3 3.5 %collective-permute-done.2.own2_ref = f32[264,128]{1,0:T(8,128)S(1)} collective-permute-done((f32[264,128]{1,0:T(8,128)S(1)}, f32[264,128]{1,0:T(8,128)S(1)}, u32[]{:S(2)}, u32[]{:S(2)}) %collective-permute-start.2) | collective-permute-done | bytes 135200 | tf_op jit(solution)/shard_map/ppermute | solution.py:320
  29.8 1.9 %collective-permute-done.3.own3_ref = f32[256,128]{1,0:T(8,128)S(1)} collective-permute-done((f32[256,128]{1,0:T(8,128)S(1)}, f32[256,128]{1,0:T(8,128)S(1)}, u32[]{:S(2)}, u32[]{:S(2)}) %collective-permute-start.3) | collective-permute-done | bytes 131104 | tf_op jit(solution)/shard_map/ppermute | solution.py:320
  31.7 0.5 collective-permute-start.5
  32.2 0.1 copy.8
  32.3 0.1 reshape.10.list_ref
  32.4 0.6 collective-permute-done.7.other3_ref
  33.0 0.2 collective-permute-done.5.other1_ref
  33.2 21.7 %main.1 = (f32[32,8,128]{2,1,0:T(8,128)}, f32[32,8,128]{2,1,0:T(8,128)S(1)}, f32[32,8,128]{2,1,0:T(8,128)S(1)}, f32[8,128]{1,0:T(8,128)S(1)}, f32[32,128]{1,0:T(...) custom-call(s32[2048]{0:T(1024)S(1)} %reshape.10.list_ref, f32[256,128]{1,0:T(8,128)S(1)} %bitcast.7, ...), custom_call_target="tpu_custom_call" | custom-call | flops 8589934592 | bytes 4194304 | tf_op jit(solution)/shard_map/main/pallas_call | solution.py:387
  54.9 3.5 %collective-permute-start.11 = (f32[48,128]{1,0:T(8,128)S(1)}, f32[48,128]{1,0:T(8,128)S(1)}, u32[]{:S(2)}, u32[]{:S(2)}) collective-permute-start(f32[48,128]{1,0:T(8,128)S(1)} %get-tuple-element.24), channel_id=1, source_target_pairs={{0,254},{2,252},{4,250},{6,248},{8,246},{10,244},{12,242},{14,240}... | collective-permute-start | bytes 73736 | tf_op jit(solution)/shard_map/ppermute | solution.py:320
  58.4 2.7 %collective-permute-start.10 = (f32[40,128]{1,0:T(8,128)S(1)}, f32[40,128]{1,0:T(8,128)S(1)}, u32[]{:S(2)}, u32[]{:S(2)}) collective-permute-start(f32[40,128]{1,0:T(8,128)S(1)} %get-tuple-element.23), channel_id=1, source_target_pairs={{0,1},{1,0},{2,3},{3,2},{4,5},{5,4},{6,7},{7,6},{8,9},{9,8},{10,11... | collective-permute-start | bytes 61448 | tf_op jit(solution)/shard_map/ppermute | solution.py:330
  61.2 0.1 collective-permute-start.8
  61.3 1.0 %collective-permute-done.8.pair_ref = f32[8,128]{1,0:T(8,128)S(1)} collective-permute-done((f32[8,128]{1,0:T(8,128)S(1)}, f32[8,128]{1,0:T(8,128)S(1)}, u32[]{:S(2)}, u32[]{:S(2)}) %collective-permute-start.8) | collective-permute-done | bytes 4128 | tf_op jit(solution)/shard_map/ppermute | solution.py:320
  62.3 5.0 %collective-permute-done.9.theirs_ref = f32[32,128]{1,0:T(8,128)S(1)} collective-permute-done((f32[32,128]{1,0:T(8,128)S(1)}, f32[32,128]{1,0:T(8,128)S(1)}, u32[]{:S(2)}, u32[]{:S(2)}) %collective-permute-start.9) | collective-permute-done | bytes 16416 | tf_op jit(solution)/shard_map/ppermute | solution.py:326
  67.3 1.0 %last.1 = f32[32,8,128]{2,1,0:T(8,128)} custom-call(f32[32,8,128]{2,1,0:T(8,128)S(1)} %get-tuple-element.19.middle_ref, f32[32,8,128]{2,1,0:T(8,128)S(1)} %copy-done, f32[32,8,128]{2,1,0:T(8,128)S(1)} %get-tuple-element.20.squares_ref, f32[32,8,128]{2,1,0:T(8,128)S(1)} %copy-done.1, f32[8,128]{1,0:T(8,128)S(1)} %collective-permute-done.8.pair_ref, ...), custom_call_target="tpu_custom_call" | custom-call | tf_op jit(solution)/shard_map/last/pallas_call | solution.py:406
  (22 shorter events, 0.1 us)
Async XLA Ops:
  2.4 9.5 %copy-start.5 = (f32[32,128]{1,0:T(8,128)S(1)}, f32[32,128]{1,0:T(8,128)}, u32[]{:S(2)}) copy-start(f32[32,128]{1,0:T(8,128)} %get-tuple-element.15) | copy-start | bytes 49156
  2.4 19.0 %all-to-all-start = ((f32[16,24,128]{2,1,0:T(8,128)}), f32[16,24,128]{2,1,0:T(8,128)S(1)}, u32[]{:S(2)}, u32[]{:S(2)}) async-start(f32[16,24,128]{2,1,0:T(8,128)} %get-tuple-element.14), calls=%async_computation | async-start | bytes 393216 | tf_op jit(solution)/shard_map/all_to_all | solution.py:338
  11.9 5.3 %collective-permute-start = (f32[32,128]{1,0:T(8,128)S(1)}, f32[32,128]{1,0:T(8,128)S(1)}, u32[]{:S(2)}, u32[]{:S(2)}) collective-permute-start(f32[32,128]{1,0:T(8,128)S(1)} %copy-done.5), channel_id=1, source_target_pairs={{0,1},{1,0},{2,3},{3,2},{4,5},{5,4},{6,7},{7,6},{8,9},{9,8},{10,11... | collective-permute-start | bytes 49160 | tf_op jit(solution)/shard_map/ppermute | solution.py:330
  21.4 0.7 %copy-start.4 = (f32[8,128]{1,0:T(8,128)S(1)}, f32[8,128]{1,0:T(8,128)}, u32[]{:S(2)}) copy-start(f32[8,128]{1,0:T(8,128)} %get-tuple-element.17) | copy-start | bytes 12292
  21.4 11.8 %copy-start.2 = (f32[3,32,8,128]{3,2,1,0:T(8,128)S(1)}, f32[3,32,8,128]{3,2,1,0:T(8,128)}, u32[]{:S(2)}) copy-start(f32[3,32,8,128]{3,2,1,0:T(8,128)} %cell_ref.1) | copy-start | bytes 1179652
  22.1 10.1 %copy-start.3 = (s32[32,8,8]{0,2,1:T(8,128)S(1)}, s32[32,8,8]{0,2,1:T(8,128)}, u32[]{:S(2)}) copy-start(s32[32,8,8]{0,2,1:T(8,128)} %param.9) | copy-start | bytes 24580
  22.1 7.7 %collective-permute-start.2 = (f32[264,128]{1,0:T(8,128)S(1)}, f32[264,128]{1,0:T(8,128)S(1)}, u32[]{:S(2)}, u32[]{:S(2)}) collective-permute-start(f32[264,128]{1,0:T(8,128)S(1)} %get-tuple-element.27), channel_id=1, source_target_pairs={{0,12},{2,14},{4,8},{6,10},{8,4},{10,6},{12,0},{14,2},{16,28},{18,... | collective-permute-start | bytes 405512 | tf_op jit(solution)/shard_map/ppermute | solution.py:320
  25.2 6.5 %collective-permute-start.3 = (f32[256,128]{1,0:T(8,128)S(1)}, f32[256,128]{1,0:T(8,128)S(1)}, u32[]{:S(2)}, u32[]{:S(2)}) collective-permute-start(f32[256,128]{1,0:T(8,128)S(1)} %bitcast.5), channel_id=1, source_target_pairs={{0,8},{2,10},{4,12},{6,14},{8,0},{10,2},{12,4},{14,6},{16,24},{18,... | collective-permute-start | bytes 393224 | tf_op jit(solution)/shard_map/ppermute | solution.py:320
  25.8 5.8 %collective-permute-start.1 = (f32[256,128]{1,0:T(8,128)S(1)}, f32[256,128]{1,0:T(8,128)S(1)}, u32[]{:S(2)}, u32[]{:S(2)}) collective-permute-start(f32[256,128]{1,0:T(8,128)S(1)} %bitcast.6), channel_id=1, source_target_pairs={{0,4},{2,6},{4,0},{6,2},{8,12},{10,14},{12,8},{14,10},{16,20},{18,... | collective-permute-start | bytes 393224 | tf_op jit(solution)/shard_map/ppermute | solution.py:320
  26.3 6.9 %copy-start = (f32[32,8,128]{2,1,0:T(8,128)S(1)}, f32[32,8,128]{2,1,0:T(8,128)}, u32[]{:S(2)}) copy-start(f32[32,8,128]{2,1,0:T(8,128)} %nu_ref.3) | copy-start | bytes 393220
  26.3 6.9 %copy-start.1 = (f32[32,8,128]{2,1,0:T(8,128)S(1)}, f32[32,8,128]{2,1,0:T(8,128)}, u32[]{:S(2)}) copy-start(f32[32,8,128]{2,1,0:T(8,128)} %vorticity_ref.3) | copy-start | bytes 393220
  26.3 6.1 %collective-permute-start.4 = (f32[264,128]{1,0:T(8,128)S(1)}, f32[264,128]{1,0:T(8,128)S(1)}, u32[]{:S(2)}, u32[]{:S(2)}) collective-permute-start(f32[264,128]{1,0:T(8,128)S(1)} %get-tuple-element.26), channel_id=1, source_target_pairs={{0,2},{2,0},{4,6},{6,4},{8,10},{10,8},{12,14},{14,12},{16,18},{18,... | collective-permute-start | bytes 405512 | tf_op jit(solution)/shard_map/ppermute | solution.py:320
  29.8 3.4 %collective-permute-start.6 = (f32[264,128]{1,0:T(8,128)S(1)}, f32[264,128]{1,0:T(8,128)S(1)}, u32[]{:S(2)}, u32[]{:S(2)}) collective-permute-start(f32[264,128]{1,0:T(8,128)S(1)} %collective-permute-done.2.own2_ref), channel_id=1, source_target_pairs={{0,2},{2,0},{4,6},{6,4},{8,10},{10,8},{12,14},{14,12},{16,18},{18,... | collective-permute-start | bytes 405512 | tf_op jit(solution)/shard_map/ppermute | solution.py:320
  31.7 1.3 %collective-permute-start.7 = (f32[256,128]{1,0:T(8,128)S(1)}, f32[256,128]{1,0:T(8,128)S(1)}, u32[]{:S(2)}, u32[]{:S(2)}) collective-permute-start(f32[256,128]{1,0:T(8,128)S(1)} %collective-permute-done.3.own3_ref), channel_id=1, source_target_pairs={{0,2},{2,0},{4,6},{6,4},{8,10},{10,8},{12,14},{14,12},{16,18},{18,... | collective-permute-start | bytes 393224 | tf_op jit(solution)/shard_map/ppermute | solution.py:320
  31.7 1.5 %collective-permute-start.5 = (f32[256,128]{1,0:T(8,128)S(1)}, f32[256,128]{1,0:T(8,128)S(1)}, u32[]{:S(2)}, u32[]{:S(2)}) collective-permute-start(f32[256,128]{1,0:T(8,128)S(1)} %collective-permute-done.1.own1_ref), channel_id=1, source_target_pairs={{0,2},{2,0},{4,6},{6,4},{8,10},{10,8},{12,14},{14,12},{16,18},{18,... | collective-permute-start | bytes 393224 | tf_op jit(solution)/shard_map/ppermute | solution.py:320
  54.9 12.4 %collective-permute-start.11 = (f32[48,128]{1,0:T(8,128)S(1)}, f32[48,128]{1,0:T(8,128)S(1)}, u32[]{:S(2)}, u32[]{:S(2)}) collective-permute-start(f32[48,128]{1,0:T(8,128)S(1)} %get-tuple-element.24), channel_id=1, source_target_pairs={{0,254},{2,252},{4,250},{6,248},{8,246},{10,244},{12,242},{14,240}... | collective-permute-start | bytes 73736 | tf_op jit(solution)/shard_map/ppermute | solution.py:320
  58.4 8.9 %collective-permute-start.10 = (f32[40,128]{1,0:T(8,128)S(1)}, f32[40,128]{1,0:T(8,128)S(1)}, u32[]{:S(2)}, u32[]{:S(2)}) collective-permute-start(f32[40,128]{1,0:T(8,128)S(1)} %get-tuple-element.23), channel_id=1, source_target_pairs={{0,1},{1,0},{2,3},{3,2},{4,5},{5,4},{6,7},{7,6},{8,9},{9,8},{10,11... | collective-permute-start | bytes 61448 | tf_op jit(solution)/shard_map/ppermute | solution.py:330
  61.2 6.2 %collective-permute-start.9 = (f32[32,128]{1,0:T(8,128)S(1)}, f32[32,128]{1,0:T(8,128)S(1)}, u32[]{:S(2)}, u32[]{:S(2)}) collective-permute-start(f32[32,128]{1,0:T(8,128)S(1)} %get-tuple-element.22.mine_ref), channel_id=1, source_target_pairs={{2,4},{6,8},{10,12},{14,16},{18,20},{22,24},{26,28},{30,32},{34,36... | collective-permute-start | bytes 49160 | tf_op jit(solution)/shard_map/ppermute | solution.py:326
  61.2 1.2 %collective-permute-start.8 = (f32[8,128]{1,0:T(8,128)S(1)}, f32[8,128]{1,0:T(8,128)S(1)}, u32[]{:S(2)}, u32[]{:S(2)}) collective-permute-start(f32[8,128]{1,0:T(8,128)S(1)} %get-tuple-element.21), channel_id=1, source_target_pairs={{0,2},{2,0},{4,6},{6,4},{8,10},{10,8},{12,14},{14,12},{16,18},{18,... | collective-permute-start | bytes 12296 | tf_op jit(solution)/shard_map/ppermute | solution.py:320

commit v11 on v10

--- a/solution.py
+++ b/solution.py
@@ -368,6 +368,7 @@
     scratch = [pltpu.VMEM((rows + 2, span, cells), F32), pltpu.VMEM(nu_field.shape, F32)]
 
     groups = devices >> GROUP_BIT
+    inputs = (panel_xyz, panel_size[None], nu_field)
     chunks, pair, beside = pl.pallas_call(
         prep_kernel,
         out_shape=(jax.ShapeDtypeStruct((groups, 4 * own_blocks + 8, PBS), F32), tile, side),
@@ -379,9 +380,9 @@
             pltpu.VMEM(nu_field.shape, F32),
             pltpu.SemaphoreType.DMA((3,)),
         ],
-        compiler_params=pltpu.CompilerParams(vmem_limit_bytes=60 * 2**20),
+        compiler_params=pltpu.CompilerParams(vmem_limit_bytes=4 * 2**20),
         name="prep",
-    )(panel_xyz, panel_size[None], nu_field)
+    )(*(pltpu.with_memory_space_constraint(x, pltpu.HBM) for x in inputs))
     own, other, beside = gather(chunks, pair, beside)
 
     dist, squares, middle, pair, mine, sides, column = pl.pallas_call(

time: 68.7 us -> 68 us (0.990)
  no operation moved by 1% of the time
where the time goes in v11:
time: 68 us; the launch traced here: 67.7 us
  Pallas kernels  24.4 us (36%)
  starting transfers between devices  23.4 us (34%)
  waiting for transfers between devices  18.9 us (28%)
  between operations  0.71 us (1%)
    pallas_call x1, Pallas kernels, shards(): pl.pallas_call(main_kernel, out_shape=(field, field, field) + edges, in_s...  21.7 us
    all_to_all x1, starting transfers between devices, gather(): lax.all_to_all(chunks, 'wrap', 0, 0, tiled=True, axis_index_groups=members)  9.53 us
    ppermute x9, starting transfers between devices, swap_mask(): lax.ppermute(block, 'wrap', [(i, i ^ mask) for i in range(lax.axis_size('...  8.38 us
    ppermute x9, waiting for transfers between devices, swap_mask(): lax.ppermute(block, 'wrap', [(i, i ^ mask) for i in range(lax.axis_size('...  7.18 us
    ppermute x2, starting transfers between devices, swap_span(): return lax.ppermute(block, 'span', [(0, 1), (1, 0)])  5.47 us
    ppermute x1, waiting for transfers between devices, swap_next(): return lax.ppermute(block, 'wrap', pairs + [(j, i) for i, j in pairs])  5 us
    all_to_all x1, waiting for transfers between devices, gather(): lax.all_to_all(chunks, 'wrap', 0, 0, tiled=True, axis_index_groups=members)  4.23 us
    ppermute x2, waiting for transfers between devices, swap_span(): return lax.ppermute(block, 'span', [(0, 1), (1, 0)])  2.52 us
  transfers between devices with their start and end apart: 13, of which 8 were waited for; matrix products, arithmetic and copies ran while one was open for 0% of the time, Pallas kernels for 0%

profile of v11, /device:TPU:32, one launch (start us, length us, event | category | flops | bytes accessed | tf_op | source)
XLA Modules:
  0.0 67.7 jit_solution(5142921698284037584)
XLA Ops:
  0.6 1.7 %prep.1 = (f32[16,24,128]{2,1,0:T(8,128)}, f32[8,128]{1,0:T(8,128)S(1)}, f32[32,128]{1,0:T(8,128)S(1)}) custom-call(f32[3,512]{1,0:T(4,128)} %xyz_hbm.1, f32[1,512]{1,0:T(1,128)} %bitcast.8, f32[32,8,128]{2,1,0:T(8,128)} %nu_ref.3), custom_call_target="tpu_custom_call" | custom-call | tf_op jit(solution)/shard_map/prep/pallas_call | solution.py:372
  2.4 9.5 %all-to-all-start = ((f32[16,24,128]{2,1,0:T(8,128)}), f32[16,24,128]{2,1,0:T(8,128)S(1)}, u32[]{:S(2)}, u32[]{:S(2)}) async-start(f32[16,24,128]{2,1,0:T(8,128)} %get-tuple-element.14), calls=%async_computation | async-start | bytes 393216 | tf_op jit(solution)/shard_map/all_to_all | solution.py:338
  11.9 2.7 %collective-permute-start = (f32[32,128]{1,0:T(8,128)S(1)}, f32[32,128]{1,0:T(8,128)S(1)}, u32[]{:S(2)}, u32[]{:S(2)}) collective-permute-start(f32[32,128]{1,0:T(8,128)S(1)} %get-tuple-element.15), channel_id=1, source_target_pairs={{0,1},{1,0},{2,3},{3,2},{4,5},{5,4},{6,7},{7,6},{8,9},{9,8},{10,11... | collective-permute-start | bytes 49160 | tf_op jit(solution)/shard_map/ppermute | solution.py:330
  14.6 2.5 %collective-permute-done.beside_ref = f32[32,128]{1,0:T(8,128)S(1)} collective-permute-done((f32[32,128]{1,0:T(8,128)S(1)}, f32[32,128]{1,0:T(8,128)S(1)}, u32[]{:S(2)}, u32[]{:S(2)}) %collective-permute-start) | collective-permute-done | bytes 16416 | tf_op jit(solution)/shard_map/ppermute | solution.py:330
  17.1 4.2 %all-to-all-done = f32[16,24,128]{2,1,0:T(8,128)S(1)} async-done(((f32[16,24,128]{2,1,0:T(8,128)}), f32[16,24,128]{2,1,0:T(8,128)S(1)}, u32[]{:S(2)}, u32[]{:S(2)}) %all-to-all-start) | async-done | bytes 196640 | tf_op jit(solution)/shard_map/all_to_all | solution.py:338
  21.4 0.0 copy-start.2
  21.4 0.0 copy-start.3
  21.5 3.1 %collective-permute-start.2 = (f32[264,128]{1,0:T(8,128)S(1)}, f32[264,128]{1,0:T(8,128)S(1)}, u32[]{:S(2)}, u32[]{:S(2)}) collective-permute-start(f32[264,128]{1,0:T(8,128)S(1)} %get-tuple-element.27), channel_id=1, source_target_pairs={{0,12},{2,14},{4,8},{6,10},{8,4},{10,6},{12,0},{14,2},{16,28},{18,... | collective-permute-start | bytes 405512 | tf_op jit(solution)/shard_map/ppermute | solution.py:320
  24.6 0.6 collective-permute-start.3
  25.2 0.5 collective-permute-start.1
  25.6 3.5 %collective-permute-done.2.own2_ref = f32[264,128]{1,0:T(8,128)S(1)} collective-permute-done((f32[264,128]{1,0:T(8,128)S(1)}, f32[264,128]{1,0:T(8,128)S(1)}, u32[]{:S(2)}, u32[]{:S(2)}) %collective-permute-start.2) | collective-permute-done | bytes 135200 | tf_op jit(solution)/shard_map/ppermute | solution.py:320
  29.2 1.9 %collective-permute-done.3.own3_ref = f32[256,128]{1,0:T(8,128)S(1)} collective-permute-done((f32[256,128]{1,0:T(8,128)S(1)}, f32[256,128]{1,0:T(8,128)S(1)}, u32[]{:S(2)}, u32[]{:S(2)}) %collective-permute-start.3) | collective-permute-done | bytes 131104 | tf_op jit(solution)/shard_map/ppermute | solution.py:320
  31.0 0.5 collective-permute-start.5
  31.5 0.1 copy.8
  31.7 0.1 reshape.10.list_ref
  31.8 0.6 collective-permute-done.7.other3_ref
  32.4 0.2 collective-permute-done.5.other1_ref
  32.6 21.7 %main.1 = (f32[32,8,128]{2,1,0:T(8,128)}, f32[32,8,128]{2,1,0:T(8,128)S(1)}, f32[32,8,128]{2,1,0:T(8,128)S(1)}, f32[8,128]{1,0:T(8,128)S(1)}, f32[32,128]{1,0:T(...) custom-call(s32[2048]{0:T(1024)S(1)} %reshape.10.list_ref, f32[256,128]{1,0:T(8,128)S(1)} %bitcast.7, ...), custom_call_target="tpu_custom_call" | custom-call | flops 8589934592 | bytes 4194304 | tf_op jit(solution)/shard_map/main/pallas_call | solution.py:388
  54.3 3.5 %collective-permute-start.11 = (f32[48,128]{1,0:T(8,128)S(1)}, f32[48,128]{1,0:T(8,128)S(1)}, u32[]{:S(2)}, u32[]{:S(2)}) collective-permute-start(f32[48,128]{1,0:T(8,128)S(1)} %get-tuple-element.24), channel_id=1, source_target_pairs={{0,254},{2,252},{4,250},{6,248},{8,246},{10,244},{12,242},{14,240}... | collective-permute-start | bytes 73736 | tf_op jit(solution)/shard_map/ppermute | solution.py:320
  57.8 2.7 %collective-permute-start.10 = (f32[40,128]{1,0:T(8,128)S(1)}, f32[40,128]{1,0:T(8,128)S(1)}, u32[]{:S(2)}, u32[]{:S(2)}) collective-permute-start(f32[40,128]{1,0:T(8,128)S(1)} %get-tuple-element.23), channel_id=1, source_target_pairs={{0,1},{1,0},{2,3},{3,2},{4,5},{5,4},{6,7},{7,6},{8,9},{9,8},{10,11... | collective-permute-start | bytes 61448 | tf_op jit(solution)/shard_map/ppermute | solution.py:330
  60.5 0.2 collective-permute-start.8
  60.7 1.0 %collective-permute-done.8.pair_ref = f32[8,128]{1,0:T(8,128)S(1)} collective-permute-done((f32[8,128]{1,0:T(8,128)S(1)}, f32[8,128]{1,0:T(8,128)S(1)}, u32[]{:S(2)}, u32[]{:S(2)}) %collective-permute-start.8) | collective-permute-done | bytes 4128 | tf_op jit(solution)/shard_map/ppermute | solution.py:320
  61.7 5.0 %collective-permute-done.9.theirs_ref = f32[32,128]{1,0:T(8,128)S(1)} collective-permute-done((f32[32,128]{1,0:T(8,128)S(1)}, f32[32,128]{1,0:T(8,128)S(1)}, u32[]{:S(2)}, u32[]{:S(2)}) %collective-permute-start.9) | collective-permute-done | bytes 16416 | tf_op jit(solution)/shard_map/ppermute | solution.py:326
  66.7 1.0 %last.1 = f32[32,8,128]{2,1,0:T(8,128)} custom-call(f32[32,8,128]{2,1,0:T(8,128)S(1)} %get-tuple-element.19.middle_ref, f32[32,8,128]{2,1,0:T(8,128)S(1)} %copy-done, f32[32,8,128]{2,1,0:T(8,128)S(1)} %get-tuple-element.20.squares_ref, f32[32,8,128]{2,1,0:T(8,128)S(1)} %copy-done.1, f32[8,128]{1,0:T(8,128)S(1)} %collective-permute-done.8.pair_ref, ...), custom_call_target="tpu_custom_call" | custom-call | tf_op jit(solution)/shard_map/last/pallas_call | solution.py:407
  (18 shorter events, 0.1 us)
Async XLA Ops:
  2.4 19.0 %all-to-all-start = ((f32[16,24,128]{2,1,0:T(8,128)}), f32[16,24,128]{2,1,0:T(8,128)S(1)}, u32[]{:S(2)}, u32[]{:S(2)}) async-start(f32[16,24,128]{2,1,0:T(8,128)} %get-tuple-element.14), calls=%async_computation | async-start | bytes 393216 | tf_op jit(solution)/shard_map/all_to_all | solution.py:338
  11.9 5.2 %collective-permute-start = (f32[32,128]{1,0:T(8,128)S(1)}, f32[32,128]{1,0:T(8,128)S(1)}, u32[]{:S(2)}, u32[]{:S(2)}) collective-permute-start(f32[32,128]{1,0:T(8,128)S(1)} %get-tuple-element.15), channel_id=1, source_target_pairs={{0,1},{1,0},{2,3},{3,2},{4,5},{5,4},{6,7},{7,6},{8,9},{9,8},{10,11... | collective-permute-start | bytes 49160 | tf_op jit(solution)/shard_map/ppermute | solution.py:330
  21.4 11.2 %copy-start.2 = (f32[3,32,8,128]{3,2,1,0:T(8,128)S(1)}, f32[3,32,8,128]{3,2,1,0:T(8,128)}, u32[]{:S(2)}) copy-start(f32[3,32,8,128]{3,2,1,0:T(8,128)} %cell_ref.1) | copy-start | bytes 1179652
  21.4 10.1 %copy-start.3 = (s32[32,8,8]{0,2,1:T(8,128)S(1)}, s32[32,8,8]{0,2,1:T(8,128)}, u32[]{:S(2)}) copy-start(s32[32,8,8]{0,2,1:T(8,128)} %param.9) | copy-start | bytes 24580
  21.5 7.7 %collective-permute-start.2 = (f32[264,128]{1,0:T(8,128)S(1)}, f32[264,128]{1,0:T(8,128)S(1)}, u32[]{:S(2)}, u32[]{:S(2)}) collective-permute-start(f32[264,128]{1,0:T(8,128)S(1)} %get-tuple-element.27), channel_id=1, source_target_pairs={{0,12},{2,14},{4,8},{6,10},{8,4},{10,6},{12,0},{14,2},{16,28},{18,... | collective-permute-start | bytes 405512 | tf_op jit(solution)/shard_map/ppermute | solution.py:320
  24.6 6.5 %collective-permute-start.3 = (f32[256,128]{1,0:T(8,128)S(1)}, f32[256,128]{1,0:T(8,128)S(1)}, u32[]{:S(2)}, u32[]{:S(2)}) collective-permute-start(f32[256,128]{1,0:T(8,128)S(1)} %bitcast.5), channel_id=1, source_target_pairs={{0,8},{2,10},{4,12},{6,14},{8,0},{10,2},{12,4},{14,6},{16,24},{18,... | collective-permute-start | bytes 393224 | tf_op jit(solution)/shard_map/ppermute | solution.py:320
  25.2 5.8 %collective-permute-start.1 = (f32[256,128]{1,0:T(8,128)S(1)}, f32[256,128]{1,0:T(8,128)S(1)}, u32[]{:S(2)}, u32[]{:S(2)}) collective-permute-start(f32[256,128]{1,0:T(8,128)S(1)} %bitcast.6), channel_id=1, source_target_pairs={{0,4},{2,6},{4,0},{6,2},{8,12},{10,14},{12,8},{14,10},{16,20},{18,... | collective-permute-start | bytes 393224 | tf_op jit(solution)/shard_map/ppermute | solution.py:320
  25.6 6.9 %copy-start = (f32[32,8,128]{2,1,0:T(8,128)S(1)}, f32[32,8,128]{2,1,0:T(8,128)}, u32[]{:S(2)}) copy-start(f32[32,8,128]{2,1,0:T(8,128)} %nu_ref.3) | copy-start | bytes 393220
  25.6 6.9 %copy-start.1 = (f32[32,8,128]{2,1,0:T(8,128)S(1)}, f32[32,8,128]{2,1,0:T(8,128)}, u32[]{:S(2)}) copy-start(f32[32,8,128]{2,1,0:T(8,128)} %vorticity_ref.3) | copy-start | bytes 393220
  25.6 6.1 %collective-permute-start.4 = (f32[264,128]{1,0:T(8,128)S(1)}, f32[264,128]{1,0:T(8,128)S(1)}, u32[]{:S(2)}, u32[]{:S(2)}) collective-permute-start(f32[264,128]{1,0:T(8,128)S(1)} %get-tuple-element.26), channel_id=1, source_target_pairs={{0,2},{2,0},{4,6},{6,4},{8,10},{10,8},{12,14},{14,12},{16,18},{18,... | collective-permute-start | bytes 405512 | tf_op jit(solution)/shard_map/ppermute | solution.py:320
  29.2 3.4 %collective-permute-start.6 = (f32[264,128]{1,0:T(8,128)S(1)}, f32[264,128]{1,0:T(8,128)S(1)}, u32[]{:S(2)}, u32[]{:S(2)}) collective-permute-start(f32[264,128]{1,0:T(8,128)S(1)} %collective-permute-done.2.own2_ref), channel_id=1, source_target_pairs={{0,2},{2,0},{4,6},{6,4},{8,10},{10,8},{12,14},{14,12},{16,18},{18,... | collective-permute-start | bytes 405512 | tf_op jit(solution)/shard_map/ppermute | solution.py:320
  31.0 1.3 %collective-permute-start.7 = (f32[256,128]{1,0:T(8,128)S(1)}, f32[256,128]{1,0:T(8,128)S(1)}, u32[]{:S(2)}, u32[]{:S(2)}) collective-permute-start(f32[256,128]{1,0:T(8,128)S(1)} %collective-permute-done.3.own3_ref), channel_id=1, source_target_pairs={{0,2},{2,0},{4,6},{6,4},{8,10},{10,8},{12,14},{14,12},{16,18},{18,... | collective-permute-start | bytes 393224 | tf_op jit(solution)/shard_map/ppermute | solution.py:320
  31.0 1.5 %collective-permute-start.5 = (f32[256,128]{1,0:T(8,128)S(1)}, f32[256,128]{1,0:T(8,128)S(1)}, u32[]{:S(2)}, u32[]{:S(2)}) collective-permute-start(f32[256,128]{1,0:T(8,128)S(1)} %collective-permute-done.1.own1_ref), channel_id=1, source_target_pairs={{0,2},{2,0},{4,6},{6,4},{8,10},{10,8},{12,14},{14,12},{16,18},{18,... | collective-permute-start | bytes 393224 | tf_op jit(solution)/shard_map/ppermute | solution.py:320
  54.3 12.4 %collective-permute-start.11 = (f32[48,128]{1,0:T(8,128)S(1)}, f32[48,128]{1,0:T(8,128)S(1)}, u32[]{:S(2)}, u32[]{:S(2)}) collective-permute-start(f32[48,128]{1,0:T(8,128)S(1)} %get-tuple-element.24), channel_id=1, source_target_pairs={{0,254},{2,252},{4,250},{6,248},{8,246},{10,244},{12,242},{14,240}... | collective-permute-start | bytes 73736 | tf_op jit(solution)/shard_map/ppermute | solution.py:320
  57.8 8.9 %collective-permute-start.10 = (f32[40,128]{1,0:T(8,128)S(1)}, f32[40,128]{1,0:T(8,128)S(1)}, u32[]{:S(2)}, u32[]{:S(2)}) collective-permute-start(f32[40,128]{1,0:T(8,128)S(1)} %get-tuple-element.23), channel_id=1, source_target_pairs={{0,1},{1,0},{2,3},{3,2},{4,5},{5,4},{6,7},{7,6},{8,9},{9,8},{10,11... | collective-permute-start | bytes 61448 | tf_op jit(solution)/shard_map/ppermute | solution.py:330
  60.5 6.2 %collective-permute-start.9 = (f32[32,128]{1,0:T(8,128)S(1)}, f32[32,128]{1,0:T(8,128)S(1)}, u32[]{:S(2)}, u32[]{:S(2)}) collective-permute-start(f32[32,128]{1,0:T(8,128)S(1)} %get-tuple-element.22.mine_ref), channel_id=1, source_target_pairs={{2,4},{6,8},{10,12},{14,16},{18,20},{22,24},{26,28},{30,32},{34,36... | collective-permute-start | bytes 49160 | tf_op jit(solution)/shard_map/ppermute | solution.py:326
  60.5 1.2 %collective-permute-start.8 = (f32[8,128]{1,0:T(8,128)S(1)}, f32[8,128]{1,0:T(8,128)S(1)}, u32[]{:S(2)}, u32[]{:S(2)}) collective-permute-start(f32[8,128]{1,0:T(8,128)S(1)} %get-tuple-element.21), channel_id=1, source_target_pairs={{0,2},{2,0},{4,6},{6,4},{8,10},{10,8},{12,14},{14,12},{16,18},{18,... | collective-permute-start | bytes 12296 | tf_op jit(solution)/shard_map/ppermute | solution.py:320

commit v12 on v11

--- a/solution.py
+++ b/solution.py
@@ -12,8 +12,8 @@
 PBS = 128
 FEATS = 48
 LINES_PER_STEP = 128
-COLUMN_ROWS = 48
-SIDE_ROWS = 40
+NEXT_ROWS = 48
+COLUMN_ROWS = 40
 GROUP_BIT = 3
 Y_MASKS = (2, 6, 4)
 
@@ -247,6 +247,7 @@
     next_out[0:8] = open_row
     next_out[16:24] = jnp.broadcast_to(open_side, (8, 128))
     next_out[24:32] = jnp.broadcast_to(open_partner, (8, 128))
+    next_out[32:] = jnp.zeros((next_out.shape[0] - 32, 128), F32)
     own = (own0_ref, own1_ref, own2_ref, own3_ref)
     other = (other0_ref, other1_ref, other2_ref, other3_ref)
     build_table((own, other), table_ref)
@@ -269,7 +270,6 @@
     column = lax.fori_loop(0, tiles // per_step, body, jnp.zeros((8, 128), F32))
     for row in range(0, column_out.shape[0], 8):
         column_out[row : row + 8] = column
-    beside_out[tiles:] = jnp.zeros((beside_out.shape[0] - tiles, 128), F32)
     first, last = middle_ref[0], middle_ref[tiles - 1]
     pair_out[...] = jnp.where(even, last, first)
     next_out[8:16] = jnp.where(even, first, last)
@@ -300,7 +300,7 @@
     halo = Halo(
         middle_ref, pair_ref[...], after, beside_ref, column_ref[0:8], padded_ref, ghost_ref
     )
-    side_ref[...] = beside_ref[0:rows]
+    side_ref[...] = beside_ref[...]
     halo.beside = side_ref
     fixed = partial + missing_term(value, other)
     side_term = missing_term(side, other_side)[0:1]
@@ -322,8 +322,9 @@
 
 def swap_next(block):
     devices = lax.axis_size("wrap")
-    pairs = [(i, (i + 1) % devices) for i in range(1, devices, 2)]
-    return lax.ppermute(block, "wrap", pairs + [(j, i) for i, j in pairs])
+    pairs = [(i, i + 1) for i in range(1, devices - 1, 2)]
+    pairs += [(j, i) for i, j in pairs] + [(0, 0), (devices - 1, devices - 1)]
+    return lax.ppermute(block, "wrap", pairs)
 
 
 def swap_span(block):
@@ -344,7 +345,7 @@
         shard,
         swap_mask(shard, Y_MASKS[0]),
         swap_mask(jnp.concatenate([shard, column], 0), Y_MASKS[1]),
-        swap_mask(shard, Y_MASKS[2]),
+        swap_mask(jnp.concatenate([shard, column, column], 0), Y_MASKS[2]),
     ]
     other = [swap_mask(jnp.concatenate([shard, pair], 0), 1)]
     other += [swap_mask(piece, 1) for piece in own[1:]]
@@ -358,11 +359,11 @@
     tile = jax.ShapeDtypeStruct((span, cells), F32)
     field = jax.ShapeDtypeStruct(nu_field.shape, F32)
     side = jax.ShapeDtypeStruct((rows, cells), F32)
-    opened = jax.ShapeDtypeStruct((32, cells), F32)
+    opened = jax.ShapeDtypeStruct((NEXT_ROWS, cells), F32)
     edges = (
         tile,
         opened,
-        jax.ShapeDtypeStruct((SIDE_ROWS, cells), F32),
+        side,
         jax.ShapeDtypeStruct((COLUMN_ROWS, cells), F32),
     )
     scratch = [pltpu.VMEM((rows + 2, span, cells), F32), pltpu.VMEM(nu_field.shape, F32)]

time: 68 us -> 69.5 us (1.022)
  starting transfers between devices: 23.4 us -> 27.7 us
  waiting for transfers between devices: 18.9 us -> 16.1 us
    ppermute x1, waiting for transfers between devices: 5 us -> 0.01 us  [swap_next(): return lax.ppermute(block, 'wrap', pairs)]
    ppermute x1, starting transfers between devices: 0.01 us -> 4.65 us  [swap_next(): return lax.ppermute(block, 'wrap', pairs)]
    ppermute x2, waiting for transfers between devices: 2.52 us -> 3.85 us  [swap_span(): return lax.ppermute(block, 'span', [(0, 1), (1, 0)])]
    ppermute x9, waiting for transfers between devices: 7.18 us -> 8.05 us  [swap_mask(): lax.ppermute(block, 'wrap', [(i, i ^ mask) for i in range(lax.axis_size('...]
where the time goes in v12:
time: 69.5 us; the launch traced here: 69.3 us
  starting transfers between devices  27.7 us (40%)
  Pallas kernels  24.4 us (35%)
  waiting for transfers between devices  16.1 us (23%)
  between operations  0.73 us (1%)
    pallas_call x1, Pallas kernels, shards(): pl.pallas_call(main_kernel, out_shape=(field, field, field) + edges, in_s...  21.6 us
    all_to_all x1, starting transfers between devices, gather(): lax.all_to_all(chunks, 'wrap', 0, 0, tiled=True, axis_index_groups=members)  9.53 us
    ppermute x9, starting transfers between devices, swap_mask(): lax.ppermute(block, 'wrap', [(i, i ^ mask) for i in range(lax.axis_size('...  8.08 us
    ppermute x9, waiting for transfers between devices, swap_mask(): lax.ppermute(block, 'wrap', [(i, i ^ mask) for i in range(lax.axis_size('...  8.05 us
    ppermute x2, starting transfers between devices, swap_span(): return lax.ppermute(block, 'span', [(0, 1), (1, 0)])  5.46 us
    ppermute x1, starting transfers between devices, swap_next(): return lax.ppermute(block, 'wrap', pairs)  4.65 us
    all_to_all x1, waiting for transfers between devices, gather(): lax.all_to_all(chunks, 'wrap', 0, 0, tiled=True, axis_index_groups=members)  4.23 us
    ppermute x2, waiting for transfers between devices, swap_span(): return lax.ppermute(block, 'span', [(0, 1), (1, 0)])  3.85 us
  transfers between devices with their start and end apart: 13, of which 8 were waited for; matrix products, arithmetic and copies ran while one was open for 0% of the time, Pallas kernels for 0%

profile of v12, /device:TPU:32, one launch (start us, length us, event | category | flops | bytes accessed | tf_op | source)
XLA Modules:
  0.0 69.3 jit_solution(12424947982803922247)
XLA Ops:
  0.6 1.7 %prep.1 = (f32[16,24,128]{2,1,0:T(8,128)}, f32[8,128]{1,0:T(8,128)S(1)}, f32[32,128]{1,0:T(8,128)S(1)}) custom-call(f32[3,512]{1,0:T(4,128)} %xyz_hbm.1, f32[1,512]{1,0:T(1,128)} %bitcast.8, f32[32,8,128]{2,1,0:T(8,128)} %nu_ref.3), custom_call_target="tpu_custom_call" | custom-call | tf_op jit(solution)/shard_map/prep/pallas_call | solution.py:373
  2.4 9.5 %all-to-all-start = ((f32[16,24,128]{2,1,0:T(8,128)}), f32[16,24,128]{2,1,0:T(8,128)S(1)}, u32[]{:S(2)}, u32[]{:S(2)}) async-start(f32[16,24,128]{2,1,0:T(8,128)} %get-tuple-element.14), calls=%async_computation | async-start | bytes 393216 | tf_op jit(solution)/shard_map/all_to_all | solution.py:339
  11.9 2.7 %collective-permute-start = (f32[32,128]{1,0:T(8,128)S(1)}, f32[32,128]{1,0:T(8,128)S(1)}, u32[]{:S(2)}, u32[]{:S(2)}) collective-permute-start(f32[32,128]{1,0:T(8,128)S(1)} %get-tuple-element.15), channel_id=1, source_target_pairs={{0,1},{1,0},{2,3},{3,2},{4,5},{5,4},{6,7},{7,6},{8,9},{9,8},{10,11... | collective-permute-start | bytes 49160 | tf_op jit(solution)/shard_map/ppermute | solution.py:331
  14.6 2.5 %collective-permute-done.beside_ref = f32[32,128]{1,0:T(8,128)S(1)} collective-permute-done((f32[32,128]{1,0:T(8,128)S(1)}, f32[32,128]{1,0:T(8,128)S(1)}, u32[]{:S(2)}, u32[]{:S(2)}) %collective-permute-start) | collective-permute-done | bytes 16416 | tf_op jit(solution)/shard_map/ppermute | solution.py:331
  17.1 4.2 %all-to-all-done = f32[16,24,128]{2,1,0:T(8,128)S(1)} async-done(((f32[16,24,128]{2,1,0:T(8,128)}), f32[16,24,128]{2,1,0:T(8,128)S(1)}, u32[]{:S(2)}, u32[]{:S(2)}) %all-to-all-start) | async-done | bytes 196640 | tf_op jit(solution)/shard_map/all_to_all | solution.py:339
  21.4 0.0 copy-start.3
  21.4 0.0 copy-start.2
  21.4 3.3 %collective-permute-start.3 = (f32[272,128]{1,0:T(8,128)S(1)}, f32[272,128]{1,0:T(8,128)S(1)}, u32[]{:S(2)}, u32[]{:S(2)}) collective-permute-start(f32[272,128]{1,0:T(8,128)S(1)} %pad_maximum_fusion), channel_id=1, source_target_pairs={{0,8},{2,10},{4,12},{6,14},{8,0},{10,2},{12,4},{14,6},{16,24},{18,... | collective-permute-start | bytes 417800 | tf_op jit(solution)/shard_map/ppermute | solution.py:320
  24.7 1.1 %collective-permute-start.2 = (f32[264,128]{1,0:T(8,128)S(1)}, f32[264,128]{1,0:T(8,128)S(1)}, u32[]{:S(2)}, u32[]{:S(2)}) collective-permute-start(f32[264,128]{1,0:T(8,128)S(1)} %get-tuple-element.27), channel_id=1, source_target_pairs={{0,12},{2,14},{4,8},{6,10},{8,4},{10,6},{12,0},{14,2},{16,28},{18,... | collective-permute-start | bytes 405512 | tf_op jit(solution)/shard_map/ppermute | solution.py:320
  25.9 2.5 %collective-permute-done.3.own3_ref = f32[272,128]{1,0:T(8,128)S(1)} collective-permute-done((f32[272,128]{1,0:T(8,128)S(1)}, f32[272,128]{1,0:T(8,128)S(1)}, u32[]{:S(2)}, u32[]{:S(2)}) %collective-permute-start.3) | collective-permute-done | bytes 139296 | tf_op jit(solution)/shard_map/ppermute | solution.py:320
  28.4 0.5 collective-permute-start.4
  28.9 2.2 %collective-permute-done.2.own2_ref = f32[264,128]{1,0:T(8,128)S(1)} collective-permute-done((f32[264,128]{1,0:T(8,128)S(1)}, f32[264,128]{1,0:T(8,128)S(1)}, u32[]{:S(2)}, u32[]{:S(2)}) %collective-permute-start.2) | collective-permute-done | bytes 135200 | tf_op jit(solution)/shard_map/ppermute | solution.py:320
  31.1 0.5 collective-permute-start.5
  31.6 0.1 copy.8
  31.7 0.1 reshape.10.list_ref
  31.8 0.8 %collective-permute-done.5.other1_ref = f32[256,128]{1,0:T(8,128)S(1)} collective-permute-done((f32[256,128]{1,0:T(8,128)S(1)}, f32[256,128]{1,0:T(8,128)S(1)}, u32[]{:S(2)}, u32[]{:S(2)}) %collective-permute-start.5) | collective-permute-done | bytes 131104 | tf_op jit(solution)/shard_map/ppermute | solution.py:320
  32.6 21.6 %main.1 = (f32[32,8,128]{2,1,0:T(8,128)}, f32[32,8,128]{2,1,0:T(8,128)S(1)}, f32[32,8,128]{2,1,0:T(8,128)S(1)}, f32[8,128]{1,0:T(8,128)S(1)}, f32[48,128]{1,0:T(...) custom-call(s32[2048]{0:T(1024)S(1)} %reshape.10.list_ref, f32[256,128]{1,0:T(8,128)S(1)} %bitcast.7, ...), custom_call_target="tpu_custom_call" | custom-call | flops 8589934592 | bytes 4194304 | tf_op jit(solution)/shard_map/main/pallas_call | solution.py:389
  54.3 4.6 %collective-permute-start.9 = (f32[48,128]{1,0:T(8,128)S(1)}, f32[48,128]{1,0:T(8,128)S(1)}, u32[]{:S(2)}, u32[]{:S(2)}) collective-permute-start(f32[48,128]{1,0:T(8,128)S(1)} %get-tuple-element.22.mine_ref), channel_id=1, source_target_pairs={{2,4},{6,8},{10,12},{14,16},{18,20},{22,24},{26,28},{30,32},{34,36... | collective-permute-start | bytes 73736 | tf_op jit(solution)/shard_map/ppermute | solution.py:327
  58.9 2.6 %collective-permute-start.11 = (f32[40,128]{1,0:T(8,128)S(1)}, f32[40,128]{1,0:T(8,128)S(1)}, u32[]{:S(2)}, u32[]{:S(2)}) collective-permute-start(f32[40,128]{1,0:T(8,128)S(1)} %get-tuple-element.24), channel_id=1, source_target_pairs={{0,254},{2,252},{4,250},{6,248},{8,246},{10,244},{12,242},{14,240}... | collective-permute-start | bytes 61448 | tf_op jit(solution)/shard_map/ppermute | solution.py:320
  61.5 2.7 %collective-permute-start.10 = (f32[32,128]{1,0:T(8,128)S(1)}, f32[32,128]{1,0:T(8,128)S(1)}, u32[]{:S(2)}, u32[]{:S(2)}) collective-permute-start(f32[32,128]{1,0:T(8,128)S(1)} %get-tuple-element.23), channel_id=1, source_target_pairs={{0,1},{1,0},{2,3},{3,2},{4,5},{5,4},{6,7},{7,6},{8,9},{9,8},{10,11... | collective-permute-start | bytes 49160 | tf_op jit(solution)/shard_map/ppermute | solution.py:331
  64.3 1.2 %collective-permute-done.8.pair_ref = f32[8,128]{1,0:T(8,128)S(1)} collective-permute-done((f32[8,128]{1,0:T(8,128)S(1)}, f32[8,128]{1,0:T(8,128)S(1)}, u32[]{:S(2)}, u32[]{:S(2)}) %collective-permute-start.8) | collective-permute-done | bytes 4128 | tf_op jit(solution)/shard_map/ppermute | solution.py:320
  65.4 1.3 %collective-permute-done.10.beside_ref = f32[32,128]{1,0:T(8,128)S(1)} collective-permute-done((f32[32,128]{1,0:T(8,128)S(1)}, f32[32,128]{1,0:T(8,128)S(1)}, u32[]{:S(2)}, u32[]{:S(2)}) %collective-permute-start.10) | collective-permute-done | bytes 16416 | tf_op jit(solution)/shard_map/ppermute | solution.py:331
  66.8 1.4 %collective-permute-done.11.column_ref = f32[40,128]{1,0:T(8,128)S(1)} collective-permute-done((f32[40,128]{1,0:T(8,128)S(1)}, f32[40,128]{1,0:T(8,128)S(1)}, u32[]{:S(2)}, u32[]{:S(2)}) %collective-permute-start.11) | collective-permute-done | bytes 20512 | tf_op jit(solution)/shard_map/ppermute | solution.py:320
  68.2 1.0 %last.1 = f32[32,8,128]{2,1,0:T(8,128)} custom-call(f32[32,8,128]{2,1,0:T(8,128)S(1)} %get-tuple-element.19.middle_ref, f32[32,8,128]{2,1,0:T(8,128)S(1)} %copy-done, f32[32,8,128]{2,1,0:T(8,128)S(1)} %get-tuple-element.20.squares_ref, f32[32,8,128]{2,1,0:T(8,128)S(1)} %copy-done.1, f32[8,128]{1,0:T(8,128)S(1)} %collective-permute-done.8.pair_ref, ...), custom_call_target="tpu_custom_call" | custom-call | tf_op jit(solution)/shard_map/last/pallas_call | solution.py:408
  (19 shorter events, 0.1 us)
Async XLA Ops:
  2.4 19.0 %all-to-all-start = ((f32[16,24,128]{2,1,0:T(8,128)}), f32[16,24,128]{2,1,0:T(8,128)S(1)}, u32[]{:S(2)}, u32[]{:S(2)}) async-start(f32[16,24,128]{2,1,0:T(8,128)} %get-tuple-element.14), calls=%async_computation | async-start | bytes 393216 | tf_op jit(solution)/shard_map/all_to_all | solution.py:339
  11.9 5.2 %collective-permute-start = (f32[32,128]{1,0:T(8,128)S(1)}, f32[32,128]{1,0:T(8,128)S(1)}, u32[]{:S(2)}, u32[]{:S(2)}) collective-permute-start(f32[32,128]{1,0:T(8,128)S(1)} %get-tuple-element.15), channel_id=1, source_target_pairs={{0,1},{1,0},{2,3},{3,2},{4,5},{5,4},{6,7},{7,6},{8,9},{9,8},{10,11... | collective-permute-start | bytes 49160 | tf_op jit(solution)/shard_map/ppermute | solution.py:331
  21.4 10.2 %copy-start.3 = (s32[32,8,8]{0,2,1:T(8,128)S(1)}, s32[32,8,8]{0,2,1:T(8,128)}, u32[]{:S(2)}) copy-start(s32[32,8,8]{0,2,1:T(8,128)} %param.9) | copy-start | bytes 24580
  21.4 11.2 %copy-start.2 = (f32[3,32,8,128]{3,2,1,0:T(8,128)S(1)}, f32[3,32,8,128]{3,2,1,0:T(8,128)}, u32[]{:S(2)}) copy-start(f32[3,32,8,128]{3,2,1,0:T(8,128)} %cell_ref.1) | copy-start | bytes 1179652
  21.4 6.9 %collective-permute-start.3 = (f32[272,128]{1,0:T(8,128)S(1)}, f32[272,128]{1,0:T(8,128)S(1)}, u32[]{:S(2)}, u32[]{:S(2)}) collective-permute-start(f32[272,128]{1,0:T(8,128)S(1)} %pad_maximum_fusion), channel_id=1, source_target_pairs={{0,8},{2,10},{4,12},{6,14},{8,0},{10,2},{12,4},{14,6},{16,24},{18,... | collective-permute-start | bytes 417800 | tf_op jit(solution)/shard_map/ppermute | solution.py:320
  24.7 6.3 %collective-permute-start.2 = (f32[264,128]{1,0:T(8,128)S(1)}, f32[264,128]{1,0:T(8,128)S(1)}, u32[]{:S(2)}, u32[]{:S(2)}) collective-permute-start(f32[264,128]{1,0:T(8,128)S(1)} %get-tuple-element.27), channel_id=1, source_target_pairs={{0,12},{2,14},{4,8},{6,10},{8,4},{10,6},{12,0},{14,2},{16,28},{18,... | collective-permute-start | bytes 405512 | tf_op jit(solution)/shard_map/ppermute | solution.py:320
  25.9 5.2 %collective-permute-start.1 = (f32[256,128]{1,0:T(8,128)S(1)}, f32[256,128]{1,0:T(8,128)S(1)}, u32[]{:S(2)}, u32[]{:S(2)}) collective-permute-start(f32[256,128]{1,0:T(8,128)S(1)} %bitcast.6), channel_id=1, source_target_pairs={{0,4},{2,6},{4,0},{6,2},{8,12},{10,14},{12,8},{14,10},{16,20},{18,... | collective-permute-start | bytes 393224 | tf_op jit(solution)/shard_map/ppermute | solution.py:320
  28.4 4.2 %collective-permute-start.7 = (f32[272,128]{1,0:T(8,128)S(1)}, f32[272,128]{1,0:T(8,128)S(1)}, u32[]{:S(2)}, u32[]{:S(2)}) collective-permute-start(f32[272,128]{1,0:T(8,128)S(1)} %collective-permute-done.3.own3_ref), channel_id=1, source_target_pairs={{0,2},{2,0},{4,6},{6,4},{8,10},{10,8},{12,14},{14,12},{16,18},{18,... | collective-permute-start | bytes 417800 | tf_op jit(solution)/shard_map/ppermute | solution.py:320
  28.4 4.2 %copy-start = (f32[32,8,128]{2,1,0:T(8,128)S(1)}, f32[32,8,128]{2,1,0:T(8,128)}, u32[]{:S(2)}) copy-start(f32[32,8,128]{2,1,0:T(8,128)} %nu_ref.3) | copy-start | bytes 393220
  28.4 4.2 %copy-start.1 = (f32[32,8,128]{2,1,0:T(8,128)S(1)}, f32[32,8,128]{2,1,0:T(8,128)}, u32[]{:S(2)}) copy-start(f32[32,8,128]{2,1,0:T(8,128)} %vorticity_ref.3) | copy-start | bytes 393220
  28.4 3.4 %collective-permute-start.4 = (f32[264,128]{1,0:T(8,128)S(1)}, f32[264,128]{1,0:T(8,128)S(1)}, u32[]{:S(2)}, u32[]{:S(2)}) collective-permute-start(f32[264,128]{1,0:T(8,128)S(1)} %get-tuple-element.26), channel_id=1, source_target_pairs={{0,2},{2,0},{4,6},{6,4},{8,10},{10,8},{12,14},{14,12},{16,18},{18,... | collective-permute-start | bytes 405512 | tf_op jit(solution)/shard_map/ppermute | solution.py:320
  31.1 1.5 %collective-permute-start.6 = (f32[264,128]{1,0:T(8,128)S(1)}, f32[264,128]{1,0:T(8,128)S(1)}, u32[]{:S(2)}, u32[]{:S(2)}) collective-permute-start(f32[264,128]{1,0:T(8,128)S(1)} %collective-permute-done.2.own2_ref), channel_id=1, source_target_pairs={{0,2},{2,0},{4,6},{6,4},{8,10},{10,8},{12,14},{14,12},{16,18},{18,... | collective-permute-start | bytes 405512 | tf_op jit(solution)/shard_map/ppermute | solution.py:320
  31.1 1.5 %collective-permute-start.5 = (f32[256,128]{1,0:T(8,128)S(1)}, f32[256,128]{1,0:T(8,128)S(1)}, u32[]{:S(2)}, u32[]{:S(2)}) collective-permute-start(f32[256,128]{1,0:T(8,128)S(1)} %collective-permute-done.1.own1_ref), channel_id=1, source_target_pairs={{0,2},{2,0},{4,6},{6,4},{8,10},{10,8},{12,14},{14,12},{16,18},{18,... | collective-permute-start | bytes 393224 | tf_op jit(solution)/shard_map/ppermute | solution.py:320
  54.3 14.0 %collective-permute-start.9 = (f32[48,128]{1,0:T(8,128)S(1)}, f32[48,128]{1,0:T(8,128)S(1)}, u32[]{:S(2)}, u32[]{:S(2)}) collective-permute-start(f32[48,128]{1,0:T(8,128)S(1)} %get-tuple-element.22.mine_ref), channel_id=1, source_target_pairs={{2,4},{6,8},{10,12},{14,16},{18,20},{22,24},{26,28},{30,32},{34,36... | collective-permute-start | bytes 73736 | tf_op jit(solution)/shard_map/ppermute | solution.py:327
  58.9 9.3 %collective-permute-start.11 = (f32[40,128]{1,0:T(8,128)S(1)}, f32[40,128]{1,0:T(8,128)S(1)}, u32[]{:S(2)}, u32[]{:S(2)}) collective-permute-start(f32[40,128]{1,0:T(8,128)S(1)} %get-tuple-element.24), channel_id=1, source_target_pairs={{0,254},{2,252},{4,250},{6,248},{8,246},{10,244},{12,242},{14,240}... | collective-permute-start | bytes 61448 | tf_op jit(solution)/shard_map/ppermute | solution.py:320
  61.5 5.2 %collective-permute-start.10 = (f32[32,128]{1,0:T(8,128)S(1)}, f32[32,128]{1,0:T(8,128)S(1)}, u32[]{:S(2)}, u32[]{:S(2)}) collective-permute-start(f32[32,128]{1,0:T(8,128)S(1)} %get-tuple-element.23), channel_id=1, source_target_pairs={{0,1},{1,0},{2,3},{3,2},{4,5},{5,4},{6,7},{7,6},{8,9},{9,8},{10,11... | collective-permute-start | bytes 49160 | tf_op jit(solution)/shard_map/ppermute | solution.py:331
  64.3 1.2 %collective-permute-start.8 = (f32[8,128]{1,0:T(8,128)S(1)}, f32[8,128]{1,0:T(8,128)S(1)}, u32[]{:S(2)}, u32[]{:S(2)}) collective-permute-start(f32[8,128]{1,0:T(8,128)S(1)} %get-tuple-element.21), channel_id=1, source_target_pairs={{0,2},{2,0},{4,6},{6,4},{8,10},{10,8},{12,14},{14,12},{16,18},{18,... | collective-permute-start | bytes 12296 | tf_op jit(solution)/shard_map/ppermute | solution.py:320

commit v13 on v11

--- a/solution.py
+++ b/solution.py
@@ -344,7 +344,7 @@
         shard,
         swap_mask(shard, Y_MASKS[0]),
         swap_mask(jnp.concatenate([shard, column], 0), Y_MASKS[1]),
-        swap_mask(shard, Y_MASKS[2]),
+        swap_mask(jnp.concatenate([shard, column, column], 0), Y_MASKS[2]),
     ]
     other = [swap_mask(jnp.concatenate([shard, pair], 0), 1)]
     other += [swap_mask(piece, 1) for piece in own[1:]]

time: 68 us -> 68.2 us (level)
  starting transfers between devices: 23.4 us -> 24.1 us
    ppermute x9, starting transfers between devices: 8.38 us -> 9.08 us  [swap_mask(): lax.ppermute(block, 'wrap', [(i, i ^ mask) for i in range(lax.axis_size('...]
  transfers between devices with their start and end apart: 13 -> 13, of which waited for: 8 -> 7; matrix products, arithmetic and copies ran while one was open for 0% -> 0% of each run, Pallas kernels for 0% -> 0%
where the time goes in v13:
time: 68.2 us; the launch traced here: 68 us
  Pallas kernels  24.5 us (36%)
  starting transfers between devices  24.1 us (35%)
  waiting for transfers between devices  18.4 us (27%)
  between operations  0.73 us (1%)
    pallas_call x1, Pallas kernels, shards(): pl.pallas_call(main_kernel, out_shape=(field, field, field) + edges, in_s...  21.7 us
    all_to_all x1, starting transfers between devices, gather(): lax.all_to_all(chunks, 'wrap', 0, 0, tiled=True, axis_index_groups=members)  9.53 us
    ppermute x9, starting transfers between devices, swap_mask(): lax.ppermute(block, 'wrap', [(i, i ^ mask) for i in range(lax.axis_size('...  9.08 us
    ppermute x9, waiting for transfers between devices, swap_mask(): lax.ppermute(block, 'wrap', [(i, i ^ mask) for i in range(lax.axis_size('...  6.62 us
    ppermute x2, starting transfers between devices, swap_span(): return lax.ppermute(block, 'span', [(0, 1), (1, 0)])  5.5 us
    ppermute x1, waiting for transfers between devices, swap_next(): return lax.ppermute(block, 'wrap', pairs + [(j, i) for i, j in pairs])  5 us
    all_to_all x1, waiting for transfers between devices, gather(): lax.all_to_all(chunks, 'wrap', 0, 0, tiled=True, axis_index_groups=members)  4.23 us
    ppermute x2, waiting for transfers between devices, swap_span(): return lax.ppermute(block, 'span', [(0, 1), (1, 0)])  2.52 us
  transfers between devices with their start and end apart: 13, of which 7 were waited for; matrix products, arithmetic and copies ran while one was open for 0% of the time, Pallas kernels for 0%

profile of v13, /device:TPU:32, one launch (start us, length us, event | category | flops | bytes accessed | tf_op | source)
XLA Modules:
  0.0 68.0 jit_solution(16992144049951031507)
XLA Ops:
  0.6 1.7 %prep.1 = (f32[16,24,128]{2,1,0:T(8,128)}, f32[8,128]{1,0:T(8,128)S(1)}, f32[32,128]{1,0:T(8,128)S(1)}) custom-call(f32[3,512]{1,0:T(4,128)} %xyz_hbm.1, f32[1,512]{1,0:T(1,128)} %bitcast.8, f32[32,8,128]{2,1,0:T(8,128)} %nu_ref.3), custom_call_target="tpu_custom_call" | custom-call | tf_op jit(solution)/shard_map/prep/pallas_call | solution.py:372
  2.4 9.5 %all-to-all-start = ((f32[16,24,128]{2,1,0:T(8,128)}), f32[16,24,128]{2,1,0:T(8,128)S(1)}, u32[]{:S(2)}, u32[]{:S(2)}) async-start(f32[16,24,128]{2,1,0:T(8,128)} %get-tuple-element.14), calls=%async_computation | async-start | bytes 393216 | tf_op jit(solution)/shard_map/all_to_all | solution.py:338
  11.9 2.7 %collective-permute-start = (f32[32,128]{1,0:T(8,128)S(1)}, f32[32,128]{1,0:T(8,128)S(1)}, u32[]{:S(2)}, u32[]{:S(2)}) collective-permute-start(f32[32,128]{1,0:T(8,128)S(1)} %get-tuple-element.15), channel_id=1, source_target_pairs={{0,1},{1,0},{2,3},{3,2},{4,5},{5,4},{6,7},{7,6},{8,9},{9,8},{10,11... | collective-permute-start | bytes 49160 | tf_op jit(solution)/shard_map/ppermute | solution.py:330
  14.6 2.5 %collective-permute-done.beside_ref = f32[32,128]{1,0:T(8,128)S(1)} collective-permute-done((f32[32,128]{1,0:T(8,128)S(1)}, f32[32,128]{1,0:T(8,128)S(1)}, u32[]{:S(2)}, u32[]{:S(2)}) %collective-permute-start) | collective-permute-done | bytes 16416 | tf_op jit(solution)/shard_map/ppermute | solution.py:330
  17.1 4.2 %all-to-all-done = f32[16,24,128]{2,1,0:T(8,128)S(1)} async-done(((f32[16,24,128]{2,1,0:T(8,128)}), f32[16,24,128]{2,1,0:T(8,128)S(1)}, u32[]{:S(2)}, u32[]{:S(2)}) %all-to-all-start) | async-done | bytes 196640 | tf_op jit(solution)/shard_map/all_to_all | solution.py:338
  21.4 0.0 copy-start.3
  21.4 0.0 copy-start.2
  21.4 3.3 %collective-permute-start.3 = (f32[272,128]{1,0:T(8,128)S(1)}, f32[272,128]{1,0:T(8,128)S(1)}, u32[]{:S(2)}, u32[]{:S(2)}) collective-permute-start(f32[272,128]{1,0:T(8,128)S(1)} %pad_maximum_fusion), channel_id=1, source_target_pairs={{0,8},{2,10},{4,12},{6,14},{8,0},{10,2},{12,4},{14,6},{16,24},{18,... | collective-permute-start | bytes 417800 | tf_op jit(solution)/shard_map/ppermute | solution.py:320
  24.7 1.1 %collective-permute-start.2 = (f32[264,128]{1,0:T(8,128)S(1)}, f32[264,128]{1,0:T(8,128)S(1)}, u32[]{:S(2)}, u32[]{:S(2)}) collective-permute-start(f32[264,128]{1,0:T(8,128)S(1)} %get-tuple-element.27), channel_id=1, source_target_pairs={{0,12},{2,14},{4,8},{6,10},{8,4},{10,6},{12,0},{14,2},{16,28},{18,... | collective-permute-start | bytes 405512 | tf_op jit(solution)/shard_map/ppermute | solution.py:320
  25.9 2.5 %collective-permute-done.3.own3_ref = f32[272,128]{1,0:T(8,128)S(1)} collective-permute-done((f32[272,128]{1,0:T(8,128)S(1)}, f32[272,128]{1,0:T(8,128)S(1)}, u32[]{:S(2)}, u32[]{:S(2)}) %collective-permute-start.3) | collective-permute-done | bytes 139296 | tf_op jit(solution)/shard_map/ppermute | solution.py:320
  28.4 0.0 collective-permute-start.7
  28.4 0.5 collective-permute-start.4
  28.9 2.2 %collective-permute-done.2.own2_ref = f32[264,128]{1,0:T(8,128)S(1)} collective-permute-done((f32[264,128]{1,0:T(8,128)S(1)}, f32[264,128]{1,0:T(8,128)S(1)}, u32[]{:S(2)}, u32[]{:S(2)}) %collective-permute-start.2) | collective-permute-done | bytes 135200 | tf_op jit(solution)/shard_map/ppermute | solution.py:320
  31.1 0.0 collective-permute-start.6
  31.1 0.5 collective-permute-start.5
  31.6 0.1 copy.8
  31.7 0.1 reshape.10.list_ref
  31.8 0.8 %collective-permute-done.5.other1_ref = f32[256,128]{1,0:T(8,128)S(1)} collective-permute-done((f32[256,128]{1,0:T(8,128)S(1)}, f32[256,128]{1,0:T(8,128)S(1)}, u32[]{:S(2)}, u32[]{:S(2)}) %collective-permute-start.5) | collective-permute-done | bytes 131104 | tf_op jit(solution)/shard_map/ppermute | solution.py:320
  32.6 21.7 %main.1 = (f32[32,8,128]{2,1,0:T(8,128)}, f32[32,8,128]{2,1,0:T(8,128)S(1)}, f32[32,8,128]{2,1,0:T(8,128)S(1)}, f32[8,128]{1,0:T(8,128)S(1)}, f32[32,128]{1,0:T(...) custom-call(s32[2048]{0:T(1024)S(1)} %reshape.10.list_ref, f32[256,128]{1,0:T(8,128)S(1)} %bitcast.7, ...), custom_call_target="tpu_custom_call" | custom-call | flops 8589934592 | bytes 4194304 | tf_op jit(solution)/shard_map/main/pallas_call | solution.py:388
  54.3 3.6 %collective-permute-start.11 = (f32[48,128]{1,0:T(8,128)S(1)}, f32[48,128]{1,0:T(8,128)S(1)}, u32[]{:S(2)}, u32[]{:S(2)}) collective-permute-start(f32[48,128]{1,0:T(8,128)S(1)} %get-tuple-element.24), channel_id=1, source_target_pairs={{0,254},{2,252},{4,250},{6,248},{8,246},{10,244},{12,242},{14,240}... | collective-permute-start | bytes 73736 | tf_op jit(solution)/shard_map/ppermute | solution.py:320
  58.0 2.8 %collective-permute-start.10 = (f32[40,128]{1,0:T(8,128)S(1)}, f32[40,128]{1,0:T(8,128)S(1)}, u32[]{:S(2)}, u32[]{:S(2)}) collective-permute-start(f32[40,128]{1,0:T(8,128)S(1)} %get-tuple-element.23), channel_id=1, source_target_pairs={{0,1},{1,0},{2,3},{3,2},{4,5},{5,4},{6,7},{7,6},{8,9},{9,8},{10,11... | collective-permute-start | bytes 61448 | tf_op jit(solution)/shard_map/ppermute | solution.py:330
  60.7 1.2 %collective-permute-done.8.pair_ref = f32[8,128]{1,0:T(8,128)S(1)} collective-permute-done((f32[8,128]{1,0:T(8,128)S(1)}, f32[8,128]{1,0:T(8,128)S(1)}, u32[]{:S(2)}, u32[]{:S(2)}) %collective-permute-start.8) | collective-permute-done | bytes 4128 | tf_op jit(solution)/shard_map/ppermute | solution.py:320
  61.9 5.0 %collective-permute-done.9.theirs_ref = f32[32,128]{1,0:T(8,128)S(1)} collective-permute-done((f32[32,128]{1,0:T(8,128)S(1)}, f32[32,128]{1,0:T(8,128)S(1)}, u32[]{:S(2)}, u32[]{:S(2)}) %collective-permute-start.9) | collective-permute-done | bytes 16416 | tf_op jit(solution)/shard_map/ppermute | solution.py:326
  66.9 1.0 %last.1 = f32[32,8,128]{2,1,0:T(8,128)} custom-call(f32[32,8,128]{2,1,0:T(8,128)S(1)} %get-tuple-element.19.middle_ref, f32[32,8,128]{2,1,0:T(8,128)S(1)} %copy-done, f32[32,8,128]{2,1,0:T(8,128)S(1)} %get-tuple-element.20.squares_ref, f32[32,8,128]{2,1,0:T(8,128)S(1)} %copy-done.1, f32[8,128]{1,0:T(8,128)S(1)} %collective-permute-done.8.pair_ref, ...), custom_call_target="tpu_custom_call" | custom-call | tf_op jit(solution)/shard_map/last/pallas_call | solution.py:407
  (19 shorter events, 0.1 us)
Async XLA Ops:
  2.4 19.0 %all-to-all-start = ((f32[16,24,128]{2,1,0:T(8,128)}), f32[16,24,128]{2,1,0:T(8,128)S(1)}, u32[]{:S(2)}, u32[]{:S(2)}) async-start(f32[16,24,128]{2,1,0:T(8,128)} %get-tuple-element.14), calls=%async_computation | async-start | bytes 393216 | tf_op jit(solution)/shard_map/all_to_all | solution.py:338
  11.9 5.2 %collective-permute-start = (f32[32,128]{1,0:T(8,128)S(1)}, f32[32,128]{1,0:T(8,128)S(1)}, u32[]{:S(2)}, u32[]{:S(2)}) collective-permute-start(f32[32,128]{1,0:T(8,128)S(1)} %get-tuple-element.15), channel_id=1, source_target_pairs={{0,1},{1,0},{2,3},{3,2},{4,5},{5,4},{6,7},{7,6},{8,9},{9,8},{10,11... | collective-permute-start | bytes 49160 | tf_op jit(solution)/shard_map/ppermute | solution.py:330
  21.4 10.2 %copy-start.3 = (s32[32,8,8]{0,2,1:T(8,128)S(1)}, s32[32,8,8]{0,2,1:T(8,128)}, u32[]{:S(2)}) copy-start(s32[32,8,8]{0,2,1:T(8,128)} %param.9) | copy-start | bytes 24580
  21.4 11.2 %copy-start.2 = (f32[3,32,8,128]{3,2,1,0:T(8,128)S(1)}, f32[3,32,8,128]{3,2,1,0:T(8,128)}, u32[]{:S(2)}) copy-start(f32[3,32,8,128]{3,2,1,0:T(8,128)} %cell_ref.1) | copy-start | bytes 1179652
  21.4 6.9 %collective-permute-start.3 = (f32[272,128]{1,0:T(8,128)S(1)}, f32[272,128]{1,0:T(8,128)S(1)}, u32[]{:S(2)}, u32[]{:S(2)}) collective-permute-start(f32[272,128]{1,0:T(8,128)S(1)} %pad_maximum_fusion), channel_id=1, source_target_pairs={{0,8},{2,10},{4,12},{6,14},{8,0},{10,2},{12,4},{14,6},{16,24},{18,... | collective-permute-start | bytes 417800 | tf_op jit(solution)/shard_map/ppermute | solution.py:320
  24.7 6.3 %collective-permute-start.2 = (f32[264,128]{1,0:T(8,128)S(1)}, f32[264,128]{1,0:T(8,128)S(1)}, u32[]{:S(2)}, u32[]{:S(2)}) collective-permute-start(f32[264,128]{1,0:T(8,128)S(1)} %get-tuple-element.27), channel_id=1, source_target_pairs={{0,12},{2,14},{4,8},{6,10},{8,4},{10,6},{12,0},{14,2},{16,28},{18,... | collective-permute-start | bytes 405512 | tf_op jit(solution)/shard_map/ppermute | solution.py:320
  25.9 5.2 %collective-permute-start.1 = (f32[256,128]{1,0:T(8,128)S(1)}, f32[256,128]{1,0:T(8,128)S(1)}, u32[]{:S(2)}, u32[]{:S(2)}) collective-permute-start(f32[256,128]{1,0:T(8,128)S(1)} %bitcast.6), channel_id=1, source_target_pairs={{0,4},{2,6},{4,0},{6,2},{8,12},{10,14},{12,8},{14,10},{16,20},{18,... | collective-permute-start | bytes 393224 | tf_op jit(solution)/shard_map/ppermute | solution.py:320
  28.4 4.2 %collective-permute-start.7 = (f32[272,128]{1,0:T(8,128)S(1)}, f32[272,128]{1,0:T(8,128)S(1)}, u32[]{:S(2)}, u32[]{:S(2)}) collective-permute-start(f32[272,128]{1,0:T(8,128)S(1)} %collective-permute-done.3.own3_ref), channel_id=1, source_target_pairs={{0,2},{2,0},{4,6},{6,4},{8,10},{10,8},{12,14},{14,12},{16,18},{18,... | collective-permute-start | bytes 417800 | tf_op jit(solution)/shard_map/ppermute | solution.py:320
  28.4 4.2 %copy-start = (f32[32,8,128]{2,1,0:T(8,128)S(1)}, f32[32,8,128]{2,1,0:T(8,128)}, u32[]{:S(2)}) copy-start(f32[32,8,128]{2,1,0:T(8,128)} %nu_ref.3) | copy-start | bytes 393220
  28.4 4.2 %copy-start.1 = (f32[32,8,128]{2,1,0:T(8,128)S(1)}, f32[32,8,128]{2,1,0:T(8,128)}, u32[]{:S(2)}) copy-start(f32[32,8,128]{2,1,0:T(8,128)} %vorticity_ref.3) | copy-start | bytes 393220
  28.4 3.4 %collective-permute-start.4 = (f32[264,128]{1,0:T(8,128)S(1)}, f32[264,128]{1,0:T(8,128)S(1)}, u32[]{:S(2)}, u32[]{:S(2)}) collective-permute-start(f32[264,128]{1,0:T(8,128)S(1)} %get-tuple-element.26), channel_id=1, source_target_pairs={{0,2},{2,0},{4,6},{6,4},{8,10},{10,8},{12,14},{14,12},{16,18},{18,... | collective-permute-start | bytes 405512 | tf_op jit(solution)/shard_map/ppermute | solution.py:320
  31.1 1.5 %collective-permute-start.6 = (f32[264,128]{1,0:T(8,128)S(1)}, f32[264,128]{1,0:T(8,128)S(1)}, u32[]{:S(2)}, u32[]{:S(2)}) collective-permute-start(f32[264,128]{1,0:T(8,128)S(1)} %collective-permute-done.2.own2_ref), channel_id=1, source_target_pairs={{0,2},{2,0},{4,6},{6,4},{8,10},{10,8},{12,14},{14,12},{16,18},{18,... | collective-permute-start | bytes 405512 | tf_op jit(solution)/shard_map/ppermute | solution.py:320
  31.1 1.5 %collective-permute-start.5 = (f32[256,128]{1,0:T(8,128)S(1)}, f32[256,128]{1,0:T(8,128)S(1)}, u32[]{:S(2)}, u32[]{:S(2)}) collective-permute-start(f32[256,128]{1,0:T(8,128)S(1)} %collective-permute-done.1.own1_ref), channel_id=1, source_target_pairs={{0,2},{2,0},{4,6},{6,4},{8,10},{10,8},{12,14},{14,12},{16,18},{18,... | collective-permute-start | bytes 393224 | tf_op jit(solution)/shard_map/ppermute | solution.py:320
  54.3 12.6 %collective-permute-start.11 = (f32[48,128]{1,0:T(8,128)S(1)}, f32[48,128]{1,0:T(8,128)S(1)}, u32[]{:S(2)}, u32[]{:S(2)}) collective-permute-start(f32[48,128]{1,0:T(8,128)S(1)} %get-tuple-element.24), channel_id=1, source_target_pairs={{0,254},{2,252},{4,250},{6,248},{8,246},{10,244},{12,242},{14,240}... | collective-permute-start | bytes 73736 | tf_op jit(solution)/shard_map/ppermute | solution.py:320
  58.0 8.9 %collective-permute-start.10 = (f32[40,128]{1,0:T(8,128)S(1)}, f32[40,128]{1,0:T(8,128)S(1)}, u32[]{:S(2)}, u32[]{:S(2)}) collective-permute-start(f32[40,128]{1,0:T(8,128)S(1)} %get-tuple-element.23), channel_id=1, source_target_pairs={{0,1},{1,0},{2,3},{3,2},{4,5},{5,4},{6,7},{7,6},{8,9},{9,8},{10,11... | collective-permute-start | bytes 61448 | tf_op jit(solution)/shard_map/ppermute | solution.py:330
  60.7 6.2 %collective-permute-start.9 = (f32[32,128]{1,0:T(8,128)S(1)}, f32[32,128]{1,0:T(8,128)S(1)}, u32[]{:S(2)}, u32[]{:S(2)}) collective-permute-start(f32[32,128]{1,0:T(8,128)S(1)} %get-tuple-element.22.mine_ref), channel_id=1, source_target_pairs={{2,4},{6,8},{10,12},{14,16},{18,20},{22,24},{26,28},{30,32},{34,36... | collective-permute-start | bytes 49160 | tf_op jit(solution)/shard_map/ppermute | solution.py:326
  60.7 1.2 %collective-permute-start.8 = (f32[8,128]{1,0:T(8,128)S(1)}, f32[8,128]{1,0:T(8,128)S(1)}, u32[]{:S(2)}, u32[]{:S(2)}) collective-permute-start(f32[8,128]{1,0:T(8,128)S(1)} %get-tuple-element.21), channel_id=1, source_target_pairs={{0,2},{2,0},{4,6},{6,4},{8,10},{10,8},{12,14},{14,12},{16,18},{18,... | collective-permute-start | bytes 12296 | tf_op jit(solution)/shard_map/ppermute | solution.py:320

commit v14 on v13

--- a/solution.py
+++ b/solution.py
@@ -224,7 +224,6 @@
     nu_ref,
     vorticity_ref,
     beside_ref,
-    dist_ref,
     squares_ref,
     middle_ref,
     pair_out,
@@ -258,7 +257,6 @@
             tile = step * per_step + part
             squares = nearest_tile(tile, list_ref, cell_ref, table_ref)
             squares_ref[tile] = squares
-            dist_ref[tile] = jnp.sqrt(squares)
             rate = halo.rate(tile, squares, vorticity_ref[tile])
             middle = nu_ref[tile] + 0.5 * time_step * rate
             middle_ref[tile] = middle
@@ -385,11 +383,11 @@
     )(*(pltpu.with_memory_space_constraint(x, pltpu.HBM) for x in inputs))
     own, other, beside = gather(chunks, pair, beside)
 
-    dist, squares, middle, pair, mine, sides, column = pl.pallas_call(
+    squares, middle, pair, mine, sides, column = pl.pallas_call(
         main_kernel,
-        out_shape=(field, field, field) + edges,
+        out_shape=(field, field) + edges,
         in_specs=[SMEM] + [VMEM] * 12,
-        out_specs=(VMEM,) * 7,
+        out_specs=(VMEM,) * 6,
         scratch_shapes=[pltpu.VMEM((devices * own_blocks, FEATS, PBS), BF)] + scratch,
         compiler_params=pltpu.CompilerParams(vmem_limit_bytes=24 * 2**20),
         cost_estimate=pl.CostEstimate(
@@ -413,7 +411,7 @@
         compiler_params=pltpu.CompilerParams(vmem_limit_bytes=8 * 2**20),
         name="last",
     )(middle, nu_field, squares, vorticity, pair, mine, theirs, sides, column)
-    return (nu_next, dist)
+    return (nu_next, jnp.sqrt(squares))
 
 
 def solution(mesh):

time: 68.2 us -> 67.6 us (level)
  Pallas kernels: 24.5 us -> 23.8 us
  waiting for transfers between devices: 18.4 us -> 17.7 us
  local copies, waits for them, and re-layouts: 0.26 us -> 0.95 us
    pallas_call x1, Pallas kernels: 21.7 us -> 21 us  [shards(): pl.pallas_call(main_kernel, out_shape=(field, field) + edges, in_specs=[S...]
    ppermute x9, waiting for transfers between devices: 6.62 us -> 5.92 us  [swap_mask(): lax.ppermute(block, 'wrap', [(i, i ^ mask) for i in range(lax.axis_size('...]
    sqrt x0 -> x1, local copies, waits for them, and re-layouts: none -> 0.69 us  [shards(): return (nu_next, jnp.sqrt(squares))]
  transfers between devices with their start and end apart: 13 -> 13, of which waited for: 7 -> 7; matrix products, arithmetic and copies ran while one was open for 0% -> 1% of each run, Pallas kernels for 0% -> 0%
where the time goes in v14:
time: 67.6 us; the launch traced here: 67.3 us
  starting transfers between devices  24.1 us (36%)
  Pallas kernels  23.8 us (35%)
  waiting for transfers between devices  17.7 us (26%)
  local copies, waits for them, and re-layouts  0.95 us (1%)
  between operations  0.73 us (1%)
    pallas_call x1, Pallas kernels, shards(): pl.pallas_call(main_kernel, out_shape=(field, field) + edges, in_specs=[S...  21 us
    all_to_all x1, starting transfers between devices, gather(): lax.all_to_all(chunks, 'wrap', 0, 0, tiled=True, axis_index_groups=members)  9.53 us
    ppermute x9, starting transfers between devices, swap_mask(): lax.ppermute(block, 'wrap', [(i, i ^ mask) for i in range(lax.axis_size('...  9.15 us
    ppermute x9, waiting for transfers between devices, swap_mask(): lax.ppermute(block, 'wrap', [(i, i ^ mask) for i in range(lax.axis_size('...  5.92 us
    ppermute x2, starting transfers between devices, swap_span(): return lax.ppermute(block, 'span', [(0, 1), (1, 0)])  5.47 us
    ppermute x1, waiting for transfers between devices, swap_next(): return lax.ppermute(block, 'wrap', pairs + [(j, i) for i, j in pairs])  5 us
    all_to_all x1, waiting for transfers between devices, gather(): lax.all_to_all(chunks, 'wrap', 0, 0, tiled=True, axis_index_groups=members)  4.23 us
    ppermute x2, waiting for transfers between devices, swap_span(): return lax.ppermute(block, 'span', [(0, 1), (1, 0)])  2.52 us
  transfers between devices with their start and end apart: 13, of which 7 were waited for; matrix products, arithmetic and copies ran while one was open for 1% of the time, Pallas kernels for 0%

profile of v14, /device:TPU:32, one launch (start us, length us, event | category | flops | bytes accessed | tf_op | source)
XLA Modules:
  0.0 67.3 jit_solution(5932279924318947571)
XLA Ops:
  0.6 1.7 %prep.1 = (f32[16,24,128]{2,1,0:T(8,128)}, f32[8,128]{1,0:T(8,128)S(1)}, f32[32,128]{1,0:T(8,128)S(1)}) custom-call(f32[3,512]{1,0:T(4,128)} %xyz_hbm.1, f32[1,512]{1,0:T(1,128)} %bitcast.8, f32[32,8,128]{2,1,0:T(8,128)} %nu_ref.3), custom_call_target="tpu_custom_call" | custom-call | tf_op jit(solution)/shard_map/prep/pallas_call | solution.py:370
  2.4 9.5 %all-to-all-start = ((f32[16,24,128]{2,1,0:T(8,128)}), f32[16,24,128]{2,1,0:T(8,128)S(1)}, u32[]{:S(2)}, u32[]{:S(2)}) async-start(f32[16,24,128]{2,1,0:T(8,128)} %get-tuple-element.13), calls=%async_computation | async-start | bytes 393216 | tf_op jit(solution)/shard_map/all_to_all | solution.py:336
  11.9 2.7 %collective-permute-start = (f32[32,128]{1,0:T(8,128)S(1)}, f32[32,128]{1,0:T(8,128)S(1)}, u32[]{:S(2)}, u32[]{:S(2)}) collective-permute-start(f32[32,128]{1,0:T(8,128)S(1)} %get-tuple-element.14), channel_id=1, source_target_pairs={{0,1},{1,0},{2,3},{3,2},{4,5},{5,4},{6,7},{7,6},{8,9},{9,8},{10,11... | collective-permute-start | bytes 49160 | tf_op jit(solution)/shard_map/ppermute | solution.py:328
  14.6 2.5 %collective-permute-done.beside_ref = f32[32,128]{1,0:T(8,128)S(1)} collective-permute-done((f32[32,128]{1,0:T(8,128)S(1)}, f32[32,128]{1,0:T(8,128)S(1)}, u32[]{:S(2)}, u32[]{:S(2)}) %collective-permute-start) | collective-permute-done | bytes 16416 | tf_op jit(solution)/shard_map/ppermute | solution.py:328
  17.1 4.2 %all-to-all-done = f32[16,24,128]{2,1,0:T(8,128)S(1)} async-done(((f32[16,24,128]{2,1,0:T(8,128)}), f32[16,24,128]{2,1,0:T(8,128)S(1)}, u32[]{:S(2)}, u32[]{:S(2)}) %all-to-all-start) | async-done | bytes 196640 | tf_op jit(solution)/shard_map/all_to_all | solution.py:336
  21.4 0.0 copy-start.3
  21.4 0.0 copy-start.2
  21.4 3.3 %collective-permute-start.3 = (f32[272,128]{1,0:T(8,128)S(1)}, f32[272,128]{1,0:T(8,128)S(1)}, u32[]{:S(2)}, u32[]{:S(2)}) collective-permute-start(f32[272,128]{1,0:T(8,128)S(1)} %pad_maximum_fusion), channel_id=1, source_target_pairs={{0,8},{2,10},{4,12},{6,14},{8,0},{10,2},{12,4},{14,6},{16,24},{18,... | collective-permute-start | bytes 417800 | tf_op jit(solution)/shard_map/ppermute | solution.py:318
  24.7 1.1 %collective-permute-start.2 = (f32[264,128]{1,0:T(8,128)S(1)}, f32[264,128]{1,0:T(8,128)S(1)}, u32[]{:S(2)}, u32[]{:S(2)}) collective-permute-start(f32[264,128]{1,0:T(8,128)S(1)} %get-tuple-element.25), channel_id=1, source_target_pairs={{0,12},{2,14},{4,8},{6,10},{8,4},{10,6},{12,0},{14,2},{16,28},{18,... | collective-permute-start | bytes 405512 | tf_op jit(solution)/shard_map/ppermute | solution.py:318
  25.9 0.0 collective-permute-start.1
  25.9 2.5 %collective-permute-done.3.own3_ref = f32[272,128]{1,0:T(8,128)S(1)} collective-permute-done((f32[272,128]{1,0:T(8,128)S(1)}, f32[272,128]{1,0:T(8,128)S(1)}, u32[]{:S(2)}, u32[]{:S(2)}) %collective-permute-start.3) | collective-permute-done | bytes 139296 | tf_op jit(solution)/shard_map/ppermute | solution.py:318
  28.4 0.5 collective-permute-start.4
  28.9 2.2 %collective-permute-done.2.own2_ref = f32[264,128]{1,0:T(8,128)S(1)} collective-permute-done((f32[264,128]{1,0:T(8,128)S(1)}, f32[264,128]{1,0:T(8,128)S(1)}, u32[]{:S(2)}, u32[]{:S(2)}) %collective-permute-start.2) | collective-permute-done | bytes 135200 | tf_op jit(solution)/shard_map/ppermute | solution.py:318
  31.1 0.5 collective-permute-start.5
  31.6 0.1 copy.8
  31.7 0.1 reshape.10.list_ref
  31.8 0.8 %collective-permute-done.5.other1_ref = f32[256,128]{1,0:T(8,128)S(1)} collective-permute-done((f32[256,128]{1,0:T(8,128)S(1)}, f32[256,128]{1,0:T(8,128)S(1)}, u32[]{:S(2)}, u32[]{:S(2)}) %collective-permute-start.5) | collective-permute-done | bytes 131104 | tf_op jit(solution)/shard_map/ppermute | solution.py:318
  32.6 21.0 %main.1 = (f32[32,8,128]{2,1,0:T(8,128)S(1)}, f32[32,8,128]{2,1,0:T(8,128)S(1)}, f32[8,128]{1,0:T(8,128)S(1)}, f32[32,128]{1,0:T(8,128)S(1)}, f32[40,128]{1,0:T(8,128)S(1)}, /*index=5*/f32[48,128]{1,0:T(8,128)S(1)}) custom-call(s32[2048]{0:T(1024)S(1)} %reshape.10.list_ref, f32[256,128]{1,0:T(8,128)S(1)} %bitcast.7, ...), custom_call_target="tpu_custom_call" | custom-call | flops 8589934592 | bytes 4194304 | tf_op jit(solution)/shard_map/main/pallas_call | solution.py:386
  53.6 3.7 %collective-permute-start.11 = (f32[48,128]{1,0:T(8,128)S(1)}, f32[48,128]{1,0:T(8,128)S(1)}, u32[]{:S(2)}, u32[]{:S(2)}) collective-permute-start(f32[48,128]{1,0:T(8,128)S(1)} %get-tuple-element.23), channel_id=1, source_target_pairs={{0,254},{2,252},{4,250},{6,248},{8,246},{10,244},{12,242},{14,240}... | collective-permute-start | bytes 73736 | tf_op jit(solution)/shard_map/ppermute | solution.py:318
  57.3 2.7 %collective-permute-start.10 = (f32[40,128]{1,0:T(8,128)S(1)}, f32[40,128]{1,0:T(8,128)S(1)}, u32[]{:S(2)}, u32[]{:S(2)}) collective-permute-start(f32[40,128]{1,0:T(8,128)S(1)} %get-tuple-element.22), channel_id=1, source_target_pairs={{0,1},{1,0},{2,3},{3,2},{4,5},{5,4},{6,7},{7,6},{8,9},{9,8},{10,11... | collective-permute-start | bytes 61448 | tf_op jit(solution)/shard_map/ppermute | solution.py:328
  60.1 0.7 %sqrt.3 = f32[32,8,128]{2,1,0:T(8,128)} sqrt(f32[32,8,128]{2,1,0:T(8,128)S(1)} %get-tuple-element.19.squares_ref) | non-fusion elementwise | bytes 262144 | tf_op jit(solution)/shard_map/sqrt | solution.py:414
  60.8 0.5 collective-permute-done.8.pair_ref
  61.2 5.0 %collective-permute-done.9.theirs_ref = f32[32,128]{1,0:T(8,128)S(1)} collective-permute-done((f32[32,128]{1,0:T(8,128)S(1)}, f32[32,128]{1,0:T(8,128)S(1)}, u32[]{:S(2)}, u32[]{:S(2)}) %collective-permute-start.9) | collective-permute-done | bytes 16416 | tf_op jit(solution)/shard_map/ppermute | solution.py:324
  66.3 1.0 %last.1 = f32[32,8,128]{2,1,0:T(8,128)} custom-call(f32[32,8,128]{2,1,0:T(8,128)S(1)} %get-tuple-element.18.middle_ref, f32[32,8,128]{2,1,0:T(8,128)S(1)} %copy-done, f32[32,8,128]{2,1,0:T(8,128)S(1)} %get-tuple-element.19.squares_ref, f32[32,8,128]{2,1,0:T(8,128)S(1)} %copy-done.1, f32[8,128]{1,0:T(8,128)S(1)} %collective-permute-done.8.pair_ref, ...), custom_call_target="tpu_custom_call" | custom-call | tf_op jit(solution)/shard_map/last/pallas_call | solution.py:405
  (20 shorter events, 0.1 us)
Async XLA Ops:
  2.4 19.0 %all-to-all-start = ((f32[16,24,128]{2,1,0:T(8,128)}), f32[16,24,128]{2,1,0:T(8,128)S(1)}, u32[]{:S(2)}, u32[]{:S(2)}) async-start(f32[16,24,128]{2,1,0:T(8,128)} %get-tuple-element.13), calls=%async_computation | async-start | bytes 393216 | tf_op jit(solution)/shard_map/all_to_all | solution.py:336
  11.9 5.2 %collective-permute-start = (f32[32,128]{1,0:T(8,128)S(1)}, f32[32,128]{1,0:T(8,128)S(1)}, u32[]{:S(2)}, u32[]{:S(2)}) collective-permute-start(f32[32,128]{1,0:T(8,128)S(1)} %get-tuple-element.14), channel_id=1, source_target_pairs={{0,1},{1,0},{2,3},{3,2},{4,5},{5,4},{6,7},{7,6},{8,9},{9,8},{10,11... | collective-permute-start | bytes 49160 | tf_op jit(solution)/shard_map/ppermute | solution.py:328
  21.4 10.2 %copy-start.3 = (s32[32,8,8]{0,2,1:T(8,128)S(1)}, s32[32,8,8]{0,2,1:T(8,128)}, u32[]{:S(2)}) copy-start(s32[32,8,8]{0,2,1:T(8,128)} %param.9) | copy-start | bytes 24580
  21.4 11.2 %copy-start.2 = (f32[3,32,8,128]{3,2,1,0:T(8,128)S(1)}, f32[3,32,8,128]{3,2,1,0:T(8,128)}, u32[]{:S(2)}) copy-start(f32[3,32,8,128]{3,2,1,0:T(8,128)} %cell_ref.1) | copy-start | bytes 1179652
  21.4 6.9 %collective-permute-start.3 = (f32[272,128]{1,0:T(8,128)S(1)}, f32[272,128]{1,0:T(8,128)S(1)}, u32[]{:S(2)}, u32[]{:S(2)}) collective-permute-start(f32[272,128]{1,0:T(8,128)S(1)} %pad_maximum_fusion), channel_id=1, source_target_pairs={{0,8},{2,10},{4,12},{6,14},{8,0},{10,2},{12,4},{14,6},{16,24},{18,... | collective-permute-start | bytes 417800 | tf_op jit(solution)/shard_map/ppermute | solution.py:318
  24.7 6.3 %collective-permute-start.2 = (f32[264,128]{1,0:T(8,128)S(1)}, f32[264,128]{1,0:T(8,128)S(1)}, u32[]{:S(2)}, u32[]{:S(2)}) collective-permute-start(f32[264,128]{1,0:T(8,128)S(1)} %get-tuple-element.25), channel_id=1, source_target_pairs={{0,12},{2,14},{4,8},{6,10},{8,4},{10,6},{12,0},{14,2},{16,28},{18,... | collective-permute-start | bytes 405512 | tf_op jit(solution)/shard_map/ppermute | solution.py:318
  25.9 5.2 %collective-permute-start.1 = (f32[256,128]{1,0:T(8,128)S(1)}, f32[256,128]{1,0:T(8,128)S(1)}, u32[]{:S(2)}, u32[]{:S(2)}) collective-permute-start(f32[256,128]{1,0:T(8,128)S(1)} %bitcast.6), channel_id=1, source_target_pairs={{0,4},{2,6},{4,0},{6,2},{8,12},{10,14},{12,8},{14,10},{16,20},{18,... | collective-permute-start | bytes 393224 | tf_op jit(solution)/shard_map/ppermute | solution.py:318
  28.4 4.2 %collective-permute-start.7 = (f32[272,128]{1,0:T(8,128)S(1)}, f32[272,128]{1,0:T(8,128)S(1)}, u32[]{:S(2)}, u32[]{:S(2)}) collective-permute-start(f32[272,128]{1,0:T(8,128)S(1)} %collective-permute-done.3.own3_ref), channel_id=1, source_target_pairs={{0,2},{2,0},{4,6},{6,4},{8,10},{10,8},{12,14},{14,12},{16,18},{18,... | collective-permute-start | bytes 417800 | tf_op jit(solution)/shard_map/ppermute | solution.py:318
  28.4 4.2 %copy-start = (f32[32,8,128]{2,1,0:T(8,128)S(1)}, f32[32,8,128]{2,1,0:T(8,128)}, u32[]{:S(2)}) copy-start(f32[32,8,128]{2,1,0:T(8,128)} %nu_ref.3) | copy-start | bytes 393220
  28.4 4.2 %copy-start.1 = (f32[32,8,128]{2,1,0:T(8,128)S(1)}, f32[32,8,128]{2,1,0:T(8,128)}, u32[]{:S(2)}) copy-start(f32[32,8,128]{2,1,0:T(8,128)} %vorticity_ref.3) | copy-start | bytes 393220
  28.4 3.4 %collective-permute-start.4 = (f32[264,128]{1,0:T(8,128)S(1)}, f32[264,128]{1,0:T(8,128)S(1)}, u32[]{:S(2)}, u32[]{:S(2)}) collective-permute-start(f32[264,128]{1,0:T(8,128)S(1)} %get-tuple-element.24), channel_id=1, source_target_pairs={{0,2},{2,0},{4,6},{6,4},{8,10},{10,8},{12,14},{14,12},{16,18},{18,... | collective-permute-start | bytes 405512 | tf_op jit(solution)/shard_map/ppermute | solution.py:318
  31.1 1.5 %collective-permute-start.6 = (f32[264,128]{1,0:T(8,128)S(1)}, f32[264,128]{1,0:T(8,128)S(1)}, u32[]{:S(2)}, u32[]{:S(2)}) collective-permute-start(f32[264,128]{1,0:T(8,128)S(1)} %collective-permute-done.2.own2_ref), channel_id=1, source_target_pairs={{0,2},{2,0},{4,6},{6,4},{8,10},{10,8},{12,14},{14,12},{16,18},{18,... | collective-permute-start | bytes 405512 | tf_op jit(solution)/shard_map/ppermute | solution.py:318
  31.1 1.5 %collective-permute-start.5 = (f32[256,128]{1,0:T(8,128)S(1)}, f32[256,128]{1,0:T(8,128)S(1)}, u32[]{:S(2)}, u32[]{:S(2)}) collective-permute-start(f32[256,128]{1,0:T(8,128)S(1)} %collective-permute-done.1.own1_ref), channel_id=1, source_target_pairs={{0,2},{2,0},{4,6},{6,4},{8,10},{10,8},{12,14},{14,12},{16,18},{18,... | collective-permute-start | bytes 393224 | tf_op jit(solution)/shard_map/ppermute | solution.py:318
  53.6 12.6 %collective-permute-start.11 = (f32[48,128]{1,0:T(8,128)S(1)}, f32[48,128]{1,0:T(8,128)S(1)}, u32[]{:S(2)}, u32[]{:S(2)}) collective-permute-start(f32[48,128]{1,0:T(8,128)S(1)} %get-tuple-element.23), channel_id=1, source_target_pairs={{0,254},{2,252},{4,250},{6,248},{8,246},{10,244},{12,242},{14,240}... | collective-permute-start | bytes 73736 | tf_op jit(solution)/shard_map/ppermute | solution.py:318
  57.3 8.9 %collective-permute-start.10 = (f32[40,128]{1,0:T(8,128)S(1)}, f32[40,128]{1,0:T(8,128)S(1)}, u32[]{:S(2)}, u32[]{:S(2)}) collective-permute-start(f32[40,128]{1,0:T(8,128)S(1)} %get-tuple-element.22), channel_id=1, source_target_pairs={{0,1},{1,0},{2,3},{3,2},{4,5},{5,4},{6,7},{7,6},{8,9},{9,8},{10,11... | collective-permute-start | bytes 61448 | tf_op jit(solution)/shard_map/ppermute | solution.py:328
  60.1 6.2 %collective-permute-start.9 = (f32[32,128]{1,0:T(8,128)S(1)}, f32[32,128]{1,0:T(8,128)S(1)}, u32[]{:S(2)}, u32[]{:S(2)}) collective-permute-start(f32[32,128]{1,0:T(8,128)S(1)} %get-tuple-element.21.mine_ref), channel_id=1, source_target_pairs={{2,4},{6,8},{10,12},{14,16},{18,20},{22,24},{26,28},{30,32},{34,36... | collective-permute-start | bytes 49160 | tf_op jit(solution)/shard_map/ppermute | solution.py:324
  60.1 1.2 %collective-permute-start.8 = (f32[8,128]{1,0:T(8,128)S(1)}, f32[8,128]{1,0:T(8,128)S(1)}, u32[]{:S(2)}, u32[]{:S(2)}) collective-permute-start(f32[8,128]{1,0:T(8,128)S(1)} %get-tuple-element.20), channel_id=1, source_target_pairs={{0,2},{2,0},{4,6},{6,4},{8,10},{10,8},{12,14},{14,12},{16,18},{18,... | collective-permute-start | bytes 12296 | tf_op jit(solution)/shard_map/ppermute | solution.py:318

commit v15 on v14

--- a/solution.py
+++ b/solution.py
@@ -181,7 +181,7 @@
                     table_ref[base + pair * 2 + 1] = panel_features(pltpu.roll(rows, 4, 0))
         return carry
 
-    lax.fori_loop(0, groups, body, 0)
+    lax.fori_loop(0, groups, body, 0, unroll=2)
 
 
 def nearest_tile(tile, list_ref, cell_ref, table_ref):

time: 67.6 us -> 67.6 us (level)
  no operation moved by 1% of the time
where the time goes in v15:
time: 67.6 us; the launch traced here: 67.3 us
  starting transfers between devices  24.1 us (36%)
  Pallas kernels  23.8 us (35%)
  waiting for transfers between devices  17.7 us (26%)
  local copies, waits for them, and re-layouts  0.95 us (1%)
  between operations  0.73 us (1%)
    pallas_call x1, Pallas kernels, shards(): pl.pallas_call(main_kernel, out_shape=(field, field) + edges, in_specs=[S...  21 us
    all_to_all x1, starting transfers between devices, gather(): lax.all_to_all(chunks, 'wrap', 0, 0, tiled=True, axis_index_groups=members)  9.53 us
    ppermute x9, starting transfers between devices, swap_mask(): lax.ppermute(block, 'wrap', [(i, i ^ mask) for i in range(lax.axis_size('...  9.15 us
    ppermute x9, waiting for transfers between devices, swap_mask(): lax.ppermute(block, 'wrap', [(i, i ^ mask) for i in range(lax.axis_size('...  5.92 us
    ppermute x2, starting transfers between devices, swap_span(): return lax.ppermute(block, 'span', [(0, 1), (1, 0)])  5.45 us
    ppermute x1, waiting for transfers between devices, swap_next(): return lax.ppermute(block, 'wrap', pairs + [(j, i) for i, j in pairs])  5 us
    all_to_all x1, waiting for transfers between devices, gather(): lax.all_to_all(chunks, 'wrap', 0, 0, tiled=True, axis_index_groups=members)  4.23 us
    ppermute x2, waiting for transfers between devices, swap_span(): return lax.ppermute(block, 'span', [(0, 1), (1, 0)])  2.52 us
  transfers between devices with their start and end apart: 13, of which 7 were waited for; matrix products, arithmetic and copies ran while one was open for 1% of the time, Pallas kernels for 0%

profile of v15, /device:TPU:32, one launch (start us, length us, event | category | flops | bytes accessed | tf_op | source)
XLA Modules:
  0.0 67.3 jit_solution(10085668860040766265)
XLA Ops:
  0.6 1.7 %prep.1 = (f32[16,24,128]{2,1,0:T(8,128)}, f32[8,128]{1,0:T(8,128)S(1)}, f32[32,128]{1,0:T(8,128)S(1)}) custom-call(f32[3,512]{1,0:T(4,128)} %xyz_hbm.1, f32[1,512]{1,0:T(1,128)} %bitcast.8, f32[32,8,128]{2,1,0:T(8,128)} %nu_ref.3), custom_call_target="tpu_custom_call" | custom-call | tf_op jit(solution)/shard_map/prep/pallas_call | solution.py:370
  2.4 9.5 %all-to-all-start = ((f32[16,24,128]{2,1,0:T(8,128)}), f32[16,24,128]{2,1,0:T(8,128)S(1)}, u32[]{:S(2)}, u32[]{:S(2)}) async-start(f32[16,24,128]{2,1,0:T(8,128)} %get-tuple-element.13), calls=%async_computation | async-start | bytes 393216 | tf_op jit(solution)/shard_map/all_to_all | solution.py:336
  11.9 2.7 %collective-permute-start = (f32[32,128]{1,0:T(8,128)S(1)}, f32[32,128]{1,0:T(8,128)S(1)}, u32[]{:S(2)}, u32[]{:S(2)}) collective-permute-start(f32[32,128]{1,0:T(8,128)S(1)} %get-tuple-element.14), channel_id=1, source_target_pairs={{0,1},{1,0},{2,3},{3,2},{4,5},{5,4},{6,7},{7,6},{8,9},{9,8},{10,11... | collective-permute-start | bytes 49160 | tf_op jit(solution)/shard_map/ppermute | solution.py:328
  14.6 2.5 %collective-permute-done.beside_ref = f32[32,128]{1,0:T(8,128)S(1)} collective-permute-done((f32[32,128]{1,0:T(8,128)S(1)}, f32[32,128]{1,0:T(8,128)S(1)}, u32[]{:S(2)}, u32[]{:S(2)}) %collective-permute-start) | collective-permute-done | bytes 16416 | tf_op jit(solution)/shard_map/ppermute | solution.py:328
  17.1 4.2 %all-to-all-done = f32[16,24,128]{2,1,0:T(8,128)S(1)} async-done(((f32[16,24,128]{2,1,0:T(8,128)}), f32[16,24,128]{2,1,0:T(8,128)S(1)}, u32[]{:S(2)}, u32[]{:S(2)}) %all-to-all-start) | async-done | bytes 196640 | tf_op jit(solution)/shard_map/all_to_all | solution.py:336
  21.4 0.0 copy-start.3
  21.4 0.0 copy-start.2
  21.4 3.3 %collective-permute-start.3 = (f32[272,128]{1,0:T(8,128)S(1)}, f32[272,128]{1,0:T(8,128)S(1)}, u32[]{:S(2)}, u32[]{:S(2)}) collective-permute-start(f32[272,128]{1,0:T(8,128)S(1)} %pad_maximum_fusion), channel_id=1, source_target_pairs={{0,8},{2,10},{4,12},{6,14},{8,0},{10,2},{12,4},{14,6},{16,24},{18,... | collective-permute-start | bytes 417800 | tf_op jit(solution)/shard_map/ppermute | solution.py:318
  24.7 1.1 %collective-permute-start.2 = (f32[264,128]{1,0:T(8,128)S(1)}, f32[264,128]{1,0:T(8,128)S(1)}, u32[]{:S(2)}, u32[]{:S(2)}) collective-permute-start(f32[264,128]{1,0:T(8,128)S(1)} %get-tuple-element.25), channel_id=1, source_target_pairs={{0,12},{2,14},{4,8},{6,10},{8,4},{10,6},{12,0},{14,2},{16,28},{18,... | collective-permute-start | bytes 405512 | tf_op jit(solution)/shard_map/ppermute | solution.py:318
  25.9 0.0 collective-permute-start.1
  25.9 2.5 %collective-permute-done.3.own3_ref = f32[272,128]{1,0:T(8,128)S(1)} collective-permute-done((f32[272,128]{1,0:T(8,128)S(1)}, f32[272,128]{1,0:T(8,128)S(1)}, u32[]{:S(2)}, u32[]{:S(2)}) %collective-permute-start.3) | collective-permute-done | bytes 139296 | tf_op jit(solution)/shard_map/ppermute | solution.py:318
  28.4 0.5 collective-permute-start.4
  28.9 2.2 %collective-permute-done.2.own2_ref = f32[264,128]{1,0:T(8,128)S(1)} collective-permute-done((f32[264,128]{1,0:T(8,128)S(1)}, f32[264,128]{1,0:T(8,128)S(1)}, u32[]{:S(2)}, u32[]{:S(2)}) %collective-permute-start.2) | collective-permute-done | bytes 135200 | tf_op jit(solution)/shard_map/ppermute | solution.py:318
  31.1 0.5 collective-permute-start.5
  31.6 0.1 copy.8
  31.7 0.1 reshape.10.list_ref
  31.8 0.8 %collective-permute-done.5.other1_ref = f32[256,128]{1,0:T(8,128)S(1)} collective-permute-done((f32[256,128]{1,0:T(8,128)S(1)}, f32[256,128]{1,0:T(8,128)S(1)}, u32[]{:S(2)}, u32[]{:S(2)}) %collective-permute-start.5) | collective-permute-done | bytes 131104 | tf_op jit(solution)/shard_map/ppermute | solution.py:318
  32.6 21.0 %main.1 = (f32[32,8,128]{2,1,0:T(8,128)S(1)}, f32[32,8,128]{2,1,0:T(8,128)S(1)}, f32[8,128]{1,0:T(8,128)S(1)}, f32[32,128]{1,0:T(8,128)S(1)}, f32[40,128]{1,0:T(8,128)S(1)}, /*index=5*/f32[48,128]{1,0:T(8,128)S(1)}) custom-call(s32[2048]{0:T(1024)S(1)} %reshape.10.list_ref, f32[256,128]{1,0:T(8,128)S(1)} %bitcast.7, ...), custom_call_target="tpu_custom_call" | custom-call | flops 8589934592 | bytes 4194304 | tf_op jit(solution)/shard_map/main/pallas_call | solution.py:386
  53.7 3.7 %collective-permute-start.11 = (f32[48,128]{1,0:T(8,128)S(1)}, f32[48,128]{1,0:T(8,128)S(1)}, u32[]{:S(2)}, u32[]{:S(2)}) collective-permute-start(f32[48,128]{1,0:T(8,128)S(1)} %get-tuple-element.23), channel_id=1, source_target_pairs={{0,254},{2,252},{4,250},{6,248},{8,246},{10,244},{12,242},{14,240}... | collective-permute-start | bytes 73736 | tf_op jit(solution)/shard_map/ppermute | solution.py:318
  57.4 2.7 %collective-permute-start.10 = (f32[40,128]{1,0:T(8,128)S(1)}, f32[40,128]{1,0:T(8,128)S(1)}, u32[]{:S(2)}, u32[]{:S(2)}) collective-permute-start(f32[40,128]{1,0:T(8,128)S(1)} %get-tuple-element.22), channel_id=1, source_target_pairs={{0,1},{1,0},{2,3},{3,2},{4,5},{5,4},{6,7},{7,6},{8,9},{9,8},{10,11... | collective-permute-start | bytes 61448 | tf_op jit(solution)/shard_map/ppermute | solution.py:328
  60.1 0.7 %sqrt.3 = f32[32,8,128]{2,1,0:T(8,128)} sqrt(f32[32,8,128]{2,1,0:T(8,128)S(1)} %get-tuple-element.19.squares_ref) | non-fusion elementwise | bytes 262144 | tf_op jit(solution)/shard_map/sqrt | solution.py:414
  60.8 0.5 collective-permute-done.8.pair_ref
  61.3 5.0 %collective-permute-done.9.theirs_ref = f32[32,128]{1,0:T(8,128)S(1)} collective-permute-done((f32[32,128]{1,0:T(8,128)S(1)}, f32[32,128]{1,0:T(8,128)S(1)}, u32[]{:S(2)}, u32[]{:S(2)}) %collective-permute-start.9) | collective-permute-done | bytes 16416 | tf_op jit(solution)/shard_map/ppermute | solution.py:324
  66.3 1.0 %last.1 = f32[32,8,128]{2,1,0:T(8,128)} custom-call(f32[32,8,128]{2,1,0:T(8,128)S(1)} %get-tuple-element.18.middle_ref, f32[32,8,128]{2,1,0:T(8,128)S(1)} %copy-done, f32[32,8,128]{2,1,0:T(8,128)S(1)} %get-tuple-element.19.squares_ref, f32[32,8,128]{2,1,0:T(8,128)S(1)} %copy-done.1, f32[8,128]{1,0:T(8,128)S(1)} %collective-permute-done.8.pair_ref, ...), custom_call_target="tpu_custom_call" | custom-call | tf_op jit(solution)/shard_map/last/pallas_call | solution.py:405
  (20 shorter events, 0.1 us)
Async XLA Ops:
  2.4 19.0 %all-to-all-start = ((f32[16,24,128]{2,1,0:T(8,128)}), f32[16,24,128]{2,1,0:T(8,128)S(1)}, u32[]{:S(2)}, u32[]{:S(2)}) async-start(f32[16,24,128]{2,1,0:T(8,128)} %get-tuple-element.13), calls=%async_computation | async-start | bytes 393216 | tf_op jit(solution)/shard_map/all_to_all | solution.py:336
  11.9 5.2 %collective-permute-start = (f32[32,128]{1,0:T(8,128)S(1)}, f32[32,128]{1,0:T(8,128)S(1)}, u32[]{:S(2)}, u32[]{:S(2)}) collective-permute-start(f32[32,128]{1,0:T(8,128)S(1)} %get-tuple-element.14), channel_id=1, source_target_pairs={{0,1},{1,0},{2,3},{3,2},{4,5},{5,4},{6,7},{7,6},{8,9},{9,8},{10,11... | collective-permute-start | bytes 49160 | tf_op jit(solution)/shard_map/ppermute | solution.py:328
  21.4 10.2 %copy-start.3 = (s32[32,8,8]{0,2,1:T(8,128)S(1)}, s32[32,8,8]{0,2,1:T(8,128)}, u32[]{:S(2)}) copy-start(s32[32,8,8]{0,2,1:T(8,128)} %param.9) | copy-start | bytes 24580
  21.4 11.2 %copy-start.2 = (f32[3,32,8,128]{3,2,1,0:T(8,128)S(1)}, f32[3,32,8,128]{3,2,1,0:T(8,128)}, u32[]{:S(2)}) copy-start(f32[3,32,8,128]{3,2,1,0:T(8,128)} %cell_ref.1) | copy-start | bytes 1179652
  21.4 6.9 %collective-permute-start.3 = (f32[272,128]{1,0:T(8,128)S(1)}, f32[272,128]{1,0:T(8,128)S(1)}, u32[]{:S(2)}, u32[]{:S(2)}) collective-permute-start(f32[272,128]{1,0:T(8,128)S(1)} %pad_maximum_fusion), channel_id=1, source_target_pairs={{0,8},{2,10},{4,12},{6,14},{8,0},{10,2},{12,4},{14,6},{16,24},{18,... | collective-permute-start | bytes 417800 | tf_op jit(solution)/shard_map/ppermute | solution.py:318
  24.7 6.3 %collective-permute-start.2 = (f32[264,128]{1,0:T(8,128)S(1)}, f32[264,128]{1,0:T(8,128)S(1)}, u32[]{:S(2)}, u32[]{:S(2)}) collective-permute-start(f32[264,128]{1,0:T(8,128)S(1)} %get-tuple-element.25), channel_id=1, source_target_pairs={{0,12},{2,14},{4,8},{6,10},{8,4},{10,6},{12,0},{14,2},{16,28},{18,... | collective-permute-start | bytes 405512 | tf_op jit(solution)/shard_map/ppermute | solution.py:318
  25.9 5.2 %collective-permute-start.1 = (f32[256,128]{1,0:T(8,128)S(1)}, f32[256,128]{1,0:T(8,128)S(1)}, u32[]{:S(2)}, u32[]{:S(2)}) collective-permute-start(f32[256,128]{1,0:T(8,128)S(1)} %bitcast.6), channel_id=1, source_target_pairs={{0,4},{2,6},{4,0},{6,2},{8,12},{10,14},{12,8},{14,10},{16,20},{18,... | collective-permute-start | bytes 393224 | tf_op jit(solution)/shard_map/ppermute | solution.py:318
  28.4 4.2 %collective-permute-start.7 = (f32[272,128]{1,0:T(8,128)S(1)}, f32[272,128]{1,0:T(8,128)S(1)}, u32[]{:S(2)}, u32[]{:S(2)}) collective-permute-start(f32[272,128]{1,0:T(8,128)S(1)} %collective-permute-done.3.own3_ref), channel_id=1, source_target_pairs={{0,2},{2,0},{4,6},{6,4},{8,10},{10,8},{12,14},{14,12},{16,18},{18,... | collective-permute-start | bytes 417800 | tf_op jit(solution)/shard_map/ppermute | solution.py:318
  28.4 4.2 %copy-start = (f32[32,8,128]{2,1,0:T(8,128)S(1)}, f32[32,8,128]{2,1,0:T(8,128)}, u32[]{:S(2)}) copy-start(f32[32,8,128]{2,1,0:T(8,128)} %nu_ref.3) | copy-start | bytes 393220
  28.4 4.2 %copy-start.1 = (f32[32,8,128]{2,1,0:T(8,128)S(1)}, f32[32,8,128]{2,1,0:T(8,128)}, u32[]{:S(2)}) copy-start(f32[32,8,128]{2,1,0:T(8,128)} %vorticity_ref.3) | copy-start | bytes 393220
  28.4 3.4 %collective-permute-start.4 = (f32[264,128]{1,0:T(8,128)S(1)}, f32[264,128]{1,0:T(8,128)S(1)}, u32[]{:S(2)}, u32[]{:S(2)}) collective-permute-start(f32[264,128]{1,0:T(8,128)S(1)} %get-tuple-element.24), channel_id=1, source_target_pairs={{0,2},{2,0},{4,6},{6,4},{8,10},{10,8},{12,14},{14,12},{16,18},{18,... | collective-permute-start | bytes 405512 | tf_op jit(solution)/shard_map/ppermute | solution.py:318
  31.1 1.5 %collective-permute-start.6 = (f32[264,128]{1,0:T(8,128)S(1)}, f32[264,128]{1,0:T(8,128)S(1)}, u32[]{:S(2)}, u32[]{:S(2)}) collective-permute-start(f32[264,128]{1,0:T(8,128)S(1)} %collective-permute-done.2.own2_ref), channel_id=1, source_target_pairs={{0,2},{2,0},{4,6},{6,4},{8,10},{10,8},{12,14},{14,12},{16,18},{18,... | collective-permute-start | bytes 405512 | tf_op jit(solution)/shard_map/ppermute | solution.py:318
  31.1 1.5 %collective-permute-start.5 = (f32[256,128]{1,0:T(8,128)S(1)}, f32[256,128]{1,0:T(8,128)S(1)}, u32[]{:S(2)}, u32[]{:S(2)}) collective-permute-start(f32[256,128]{1,0:T(8,128)S(1)} %collective-permute-done.1.own1_ref), channel_id=1, source_target_pairs={{0,2},{2,0},{4,6},{6,4},{8,10},{10,8},{12,14},{14,12},{16,18},{18,... | collective-permute-start | bytes 393224 | tf_op jit(solution)/shard_map/ppermute | solution.py:318
  53.7 12.6 %collective-permute-start.11 = (f32[48,128]{1,0:T(8,128)S(1)}, f32[48,128]{1,0:T(8,128)S(1)}, u32[]{:S(2)}, u32[]{:S(2)}) collective-permute-start(f32[48,128]{1,0:T(8,128)S(1)} %get-tuple-element.23), channel_id=1, source_target_pairs={{0,254},{2,252},{4,250},{6,248},{8,246},{10,244},{12,242},{14,240}... | collective-permute-start | bytes 73736 | tf_op jit(solution)/shard_map/ppermute | solution.py:318
  57.4 8.9 %collective-permute-start.10 = (f32[40,128]{1,0:T(8,128)S(1)}, f32[40,128]{1,0:T(8,128)S(1)}, u32[]{:S(2)}, u32[]{:S(2)}) collective-permute-start(f32[40,128]{1,0:T(8,128)S(1)} %get-tuple-element.22), channel_id=1, source_target_pairs={{0,1},{1,0},{2,3},{3,2},{4,5},{5,4},{6,7},{7,6},{8,9},{9,8},{10,11... | collective-permute-start | bytes 61448 | tf_op jit(solution)/shard_map/ppermute | solution.py:328
  60.1 6.2 %collective-permute-start.9 = (f32[32,128]{1,0:T(8,128)S(1)}, f32[32,128]{1,0:T(8,128)S(1)}, u32[]{:S(2)}, u32[]{:S(2)}) collective-permute-start(f32[32,128]{1,0:T(8,128)S(1)} %get-tuple-element.21.mine_ref), channel_id=1, source_target_pairs={{2,4},{6,8},{10,12},{14,16},{18,20},{22,24},{26,28},{30,32},{34,36... | collective-permute-start | bytes 49160 | tf_op jit(solution)/shard_map/ppermute | solution.py:324
  60.1 1.2 %collective-permute-start.8 = (f32[8,128]{1,0:T(8,128)S(1)}, f32[8,128]{1,0:T(8,128)S(1)}, u32[]{:S(2)}, u32[]{:S(2)}) collective-permute-start(f32[8,128]{1,0:T(8,128)S(1)} %get-tuple-element.20), channel_id=1, source_target_pairs={{0,2},{2,0},{4,6},{6,4},{8,10},{10,8},{12,14},{14,12},{16,18},{18,... | collective-permute-start | bytes 12296 | tf_op jit(solution)/shard_map/ppermute | solution.py:318
